TPU v7x, 32 devices: a whole 2x2x4 slice. The times are simulated.
32 devices in a mesh: grp: 2 (over y), tile: 4 (over z), slc: 2 (over x), pos: 2 (over core).
Axes of the slice: x: 2, y: 2, z: 4, core: 2. Of those that a mesh axis runs over, the one named last changes fastest.
Arguments:
- object_field: bfloat16 [8, 1024, 2, 512], P(('grp', 'slc'), 'tile'), parts along dimension 0
- offsets: int32 [2, 64], P(None, ('grp', 'tile', 'pos')), parts along dimension 1, may hold values from 0 to 1023, as said below
- counts: int32 [8], P(('grp', 'tile')), parts along dimension 0, may hold values from 1 to 8, as said below
- measured: float32 [64, 256, 256], P(('grp', 'tile', 'pos')), parts along dimension 0, may hold values from 0 to 2
- probe_wave: bfloat16 [512, 512], P('grp'), parts along dimension 0, may hold values from -5 to 5
Outputs:
- object_grad: float32 [8, 1024, 2, 512], P(('grp', 'slc'), 'tile', None, 'pos'), parts along dimension 0
There are 2 independent parts, one for each index of `grp`. A program takes and returns all parts, laid end to end along the dimension named above; each array names one. Nothing has to cross between parts.
Inputs may be any that keep to these rules, and one draw needn't show every extreme that they name: Slot s belongs to tile s // 8; offsets[0, s] is an absolute object row among the 256 rows of that tile, offsets[1, s] an object column. Slots t * 8 to t * 8 + counts[t] - 1 of tile t are live; the other slots of the tile carry no position. In every draw some tile has all 8 slots live.
All inputs are finite; a program needn't handle non-finite values.
Results may differ from a plain program's by a relative error of at most 0.029.
Values may be sent and summed in bfloat16 or wider, within the bound.
No kernel may reach another device: no remote copies, remote signals or barrier semaphores. Data moves between devices by JAX's collectives and lax.ppermute only.
A program may use at most 320 MiB of HBM per device.

v0:
```python
import math

import jax
import jax.numpy as jnp
from jax import lax
from jax.sharding import PartitionSpec as P


def passed_along(array, axis, by):
    peers = lax.axis_size(axis)
    return lax.ppermute(array, axis, [(i, (i + by) % peers) for i in range(peers)])


def passed_along_2(array, axis, by):
    peers = lax.axis_size(axis)
    pairs = [(i, i + by) for i in range(peers) if 0 <= i + by < peers]
    return lax.ppermute(array, axis, pairs)


def halves(values):
    middle = values.shape[-1] // 2
    return (values[..., :middle], values[..., middle:])


def complex_product(left_arg, right_arg):
    left_re, left_im = halves(left_arg.astype(jnp.float32))
    right_re, right_im = halves(right_arg.astype(jnp.float32))
    return jnp.concatenate(
        [left_re * right_re - left_im * right_im, left_re * right_im + left_im * right_re], axis=-1
    )


def conj_product(left_arg, right_arg):
    left_re, left_im = halves(left_arg.astype(jnp.float32))
    right_re, right_im = halves(right_arg)
    return jnp.concatenate(
        [left_re * right_re + left_im * right_im, left_re * right_im - left_im * right_re], axis=-1
    )


def dft_tables(pixels):
    indices = jnp.arange(pixels, dtype=jnp.int32)
    product = indices[:, None] * indices[None, :] % pixels
    angles = 2.0 * math.pi / pixels * product.astype(jnp.float32)
    norm_scale = 1.0 / math.sqrt(pixels)
    real_part = (jnp.cos(angles) * norm_scale).astype(jnp.bfloat16)
    imag_part = (-jnp.sin(angles) * norm_scale).astype(jnp.bfloat16)
    fwd_left = jnp.concatenate([real_part, imag_part], axis=0)
    fwd_right = jnp.concatenate(
        [
            jnp.concatenate([real_part, imag_part], axis=1),
            jnp.concatenate([-imag_part, real_part], axis=1),
        ],
        axis=0,
    )
    inv_left = jnp.concatenate([real_part, -imag_part], axis=0)
    inv_right = jnp.concatenate(
        [
            jnp.concatenate([real_part, -imag_part], axis=1),
            jnp.concatenate([imag_part, real_part], axis=1),
        ],
        axis=0,
    )
    return (fwd_left, fwd_right, inv_left, inv_right)


def propagator(pixels):
    indices = jnp.arange(pixels, dtype=jnp.int32)
    frequency = (indices + pixels // 2) % pixels - pixels // 2
    squared = frequency * frequency
    phases = -0.4 * math.pi / pixels * (squared[:, None] + squared[None, :]).astype(jnp.float32)
    return jnp.concatenate([jnp.cos(phases), jnp.sin(phases)], axis=1)


def apply_left(values, table):
    pixels = values.shape[0]
    products = jnp.dot(table, values, preferred_element_type=jnp.float32)
    real_part = products[:pixels, :pixels] - products[pixels:, pixels:]
    imag_part = products[pixels:, :pixels] + products[:pixels, pixels:]
    return jnp.concatenate([real_part, imag_part], axis=1)


def apply_right(values, table):
    return jnp.dot(values, table, preferred_element_type=jnp.float32)


def slice_forward(wave_in, patch, tables, prop_field):
    fwd_left, fwd_right, inv_left, inv_right = tables
    entrance = complex_product(patch, wave_in).astype(jnp.bfloat16)
    half_way = apply_left(entrance, fwd_left).astype(jnp.bfloat16)
    spectrum = complex_product(apply_right(half_way, fwd_right), prop_field)
    returning = apply_left(spectrum.astype(jnp.bfloat16), inv_left).astype(jnp.bfloat16)
    wave_out = apply_right(returning, inv_right).astype(jnp.bfloat16)
    return (wave_out, spectrum)


def spectrum_grad(wave_grad, tables):
    fwd_left, fwd_right, inv_left, inv_right = tables
    half_way = apply_left(wave_grad, fwd_left).astype(jnp.bfloat16)
    return apply_right(half_way, fwd_right)


def detector_grad(spectrum, light):
    real_part, imag_part = halves(spectrum)
    excess = real_part * real_part + imag_part * imag_part - light
    return jnp.concatenate([excess * real_part, excess * imag_part], axis=1)


def slice_backward(spec_grad, wave_in, patch, tables, prop_field):
    fwd_left, fwd_right, inv_left, inv_right = tables
    tilted = conj_product(prop_field, spec_grad).astype(jnp.bfloat16)
    half_way = apply_left(tilted, inv_left).astype(jnp.bfloat16)
    entrance_grad = apply_right(half_way, inv_right)
    patch_grad = conj_product(wave_in, entrance_grad)
    wave_grad = conj_product(patch, entrance_grad).astype(jnp.bfloat16)
    return (wave_grad, patch_grad)


def body(object_field, offsets, counts, measured, probe_wave):
    slices_here, tile_rows, unused_two, object_cols = object_field.shape
    pixels = probe_wave.shape[0]
    slot_count = offsets.shape[1]
    slice_groups = lax.axis_size("slc")
    slice_rank = lax.axis_index("slc")
    tile_rank = lax.axis_index("tile")
    pos_rank = lax.axis_index("pos")
    tables = dft_tables(pixels)
    prop_field = propagator(pixels)
    anchor = jnp.zeros((), jnp.int32)
    in_tile = pos_rank * slot_count + jnp.arange(slot_count, dtype=jnp.int32)
    live_flag = (in_tile < counts[0]).astype(jnp.int32)
    places = jnp.stack([offsets[0] - tile_rank * tile_rows, offsets[1], live_flag], axis=1)
    rim_below = passed_along(object_field, "tile", -1)
    widened = jnp.concatenate([object_field, rim_below], axis=1)
    widened = jnp.concatenate([widened, widened[..., :pixels]], axis=3)
    patch_shape = (slices_here, pixels, 2, pixels)

    def patches_at(place_row):
        corner = (anchor, place_row[0], anchor, place_row[1])
        return lax.dynamic_slice(widened, corner, patch_shape).reshape(
            slices_here, pixels, 2 * pixels
        )

    block_count = slot_count // slot_count
    step_count = block_count + slice_groups - 1
    wave_shape = (slot_count, pixels, 2 * pixels)
    entry_waves = jnp.broadcast_to(probe_wave, wave_shape)

    def forward_run(operands):
        wave_in, patches = operands
        stored = []
        spectrum = jnp.zeros((pixels, 2 * pixels), jnp.float32)
        for layer_index in range(slices_here):
            stored.append(wave_in)
            wave_in, spectrum = slice_forward(wave_in, patches[layer_index], tables, prop_field)
        return (wave_in, jnp.stack(stored), spectrum)

    def forward_skip(operands):
        wave_in, patches = operands
        return (
            jnp.zeros_like(wave_in),
            jnp.zeros((slices_here,) + wave_in.shape, jnp.bfloat16),
            jnp.zeros(wave_in.shape, jnp.float32),
        )

    def forward_step(step_index, state_in):
        incoming, stored_all, spectra = state_in
        block_index = step_index - slice_rank
        active = (block_index >= 0) & (block_index < block_count)
        first_slot = jnp.clip(block_index, 0, block_count - 1) * slot_count
        entering = jnp.where(slice_rank == 0, entry_waves, incoming)

        def forward_per_slot(member, inner_state):
            leaving, stored_all, spectra = inner_state
            slot_index = first_slot + member
            place_row = places[slot_index]
            running = active & (place_row[2] > 0)
            wave_out, stored, spectrum = lax.cond(
                running, forward_run, forward_skip, (entering[member], patches_at(place_row))
            )
            stored = jnp.where(active, stored, stored_all[slot_index])
            spectrum = jnp.where(active, spectrum, spectra[slot_index])
            stored_all = lax.dynamic_update_index_in_dim(stored_all, stored, slot_index, 0)
            spectra = lax.dynamic_update_index_in_dim(spectra, spectrum, slot_index, 0)
            leaving = lax.dynamic_update_index_in_dim(leaving, wave_out, member, 0)
            return (leaving, stored_all, spectra)

        leaving, stored_all, spectra = lax.fori_loop(
            0,
            slot_count,
            forward_per_slot,
            (jnp.zeros(wave_shape, jnp.bfloat16), stored_all, spectra),
        )
        incoming = passed_along_2(leaving, "slc", 1)
        return (incoming, stored_all, spectra)

    stored_init = jnp.zeros((slot_count, slices_here, pixels, 2 * pixels), jnp.bfloat16)
    spectra_init = jnp.zeros((slot_count, pixels, 2 * pixels), jnp.float32)
    forward_state = lax.fori_loop(
        0,
        step_count,
        forward_step,
        (jnp.zeros(wave_shape, jnp.bfloat16), stored_init, spectra_init),
    )
    stored_all = forward_state[1]
    spectra = forward_state[2]
    at_end = slice_rank == slice_groups - 1

    def end_grad(bundle):
        return detector_grad(bundle[1], bundle[2])

    def chain_grad(bundle):
        return spectrum_grad(bundle[0], tables)

    def backward_run(operands):
        incoming_grad, stored, spectrum, light, patches = operands
        spec_grad = lax.cond(at_end, end_grad, chain_grad, (incoming_grad, spectrum, light))
        layer_grads = [None] * slices_here
        wave_grad = incoming_grad
        for layer_index in reversed(range(slices_here)):
            wave_grad, layer_grads[layer_index] = slice_backward(
                spec_grad, stored[layer_index], patches[layer_index], tables, prop_field
            )
            if layer_index > 0:
                spec_grad = spectrum_grad(wave_grad, tables)
        return (wave_grad, jnp.stack(layer_grads).reshape(patch_shape))

    def backward_skip(operands):
        return (jnp.zeros_like(operands[0]), jnp.zeros(patch_shape, jnp.float32))

    def backward_step(step_index, state_in):
        incoming, grad_wide = state_in
        block_index = step_index - (slice_groups - 1 - slice_rank)
        active = (block_index >= 0) & (block_index < block_count)
        first_slot = jnp.clip(block_index, 0, block_count - 1) * slot_count

        def backward_per_slot(member, inner_state):
            leaving, grad_wide = inner_state
            slot_index = first_slot + member
            place_row = places[slot_index]
            running = active & (place_row[2] > 0)
            operands = (
                incoming[member],
                stored_all[slot_index],
                spectra[slot_index],
                measured[slot_index],
                patches_at(place_row),
            )
            wave_grad, patch_grad = lax.cond(running, backward_run, backward_skip, operands)
            corner = (anchor, place_row[0], anchor, place_row[1])
            current = lax.dynamic_slice(grad_wide, corner, patch_shape)
            grad_wide = lax.dynamic_update_slice(grad_wide, current + patch_grad, corner)
            leaving = lax.dynamic_update_index_in_dim(leaving, wave_grad, member, 0)
            return (leaving, grad_wide)

        leaving, grad_wide = lax.fori_loop(
            0, slot_count, backward_per_slot, (jnp.zeros(wave_shape, jnp.bfloat16), grad_wide)
        )
        incoming = passed_along_2(leaving, "slc", -1)
        return (incoming, grad_wide)

    grad_init = jnp.zeros((slices_here, tile_rows + pixels, 2, object_cols + pixels), jnp.float32)
    final_grad, grad_wide = lax.fori_loop(
        0, step_count, backward_step, (jnp.zeros(wave_shape, jnp.bfloat16), grad_init)
    )
    folded = grad_wide[..., :object_cols].at[..., :pixels].add(grad_wide[..., object_cols:])
    rim_back = passed_along(folded[:, tile_rows:].astype(jnp.bfloat16), "tile", 1).astype(
        jnp.float32
    )
    own_rows = folded[:, :tile_rows].at[:, :pixels].add(rim_back)
    result = lax.psum_scatter(
        own_rows.astype(jnp.bfloat16), "pos", scatter_dimension=3, tiled=True
    ).astype(jnp.float32)
    return result


def solution(mesh):
    placed = (
        P(("grp", "slc"), "tile", None, None),
        P(None, ("grp", "tile", "pos")),
        P(("grp", "tile")),
        P(("grp", "tile", "pos"), None, None),
        P("grp", None),
    )
    return jax.shard_map(
        body,
        mesh=mesh,
        in_specs=placed,
        out_specs=P(("grp", "slc"), "tile", None, "pos"),
        check_vma=False,
    )
```

profile of v0, /device:TPU:0, one launch (start us, length us, event | category | flops | bytes accessed | tf_op | source)
XLA Modules:
  0.0 1546.1 jit_solution(1572896542263571716)
XLA Ops:
  16.1 18.2 %collective-permute-done.2 = bf16[2,256,2,512]{3,2,1,0:T(2,128)(2,1)} collective-permute-done((bf16[2,256,2,512]{3,2,1,0:T(2,128)(2,1)}, bf16[2,256,2,512]{3,2,1,0:T(2,128)(2,1)}, u32[]{:S(2)}, u32[]{:S(2)}) %collective-permute-start.2) | collective-permute-done | bytes 1048608 | tf_op jit(solution)/shard_map/ppermute | solution.py:11
  44.7 209.8 %while.124 = (s32[]{:T(128)}, bf16[4,256,512]{2,1,0:T(8,128)(2,1)S(1)}, bf16[4,2,256,512]{3,2,1,0:T(8,128)(2,1)}, f32[4,256,512]{2,1,0:T(8,128)}, s32[]{:T(128)}...) while((s32[]{:T(128)}, ...), condition=%wide.region_5.6_spmd.clone.clone.clone, body=%wide.region_0.5_spmd.clone.clone.clone.sunk | while | flops 1082851328 | bytes 43257336 | solution.py:199
  47.7 86.4 %while.127 = (s32[]{:T(128)}, bf16[4,256,512]{2,1,0:T(8,128)(2,1)}, bf16[4,2,256,512]{3,2,1,0:T(8,128)(2,1)}, f32[4,256,512]{2,1,0:T(8,128)}, s32[]{:T(128)}, /*...) while((s32[]{:T(128)}, bf16[4,256,512]{2,1,0:T(8,128)(2,1)}, ...), condition=%wide.region_4.4_spmd.clone, body=%wide.region_1.3_spmd.clone.sunk | while | flops 1082130432 | bytes 36177968 | solution.py:188
  151.1 35.0 %while.127 = (s32[]{:T(128)}, bf16[4,256,512]{2,1,0:T(8,128)(2,1)}, bf16[4,2,256,512]{3,2,1,0:T(8,128)(2,1)}, f32[4,256,512]{2,1,0:T(8,128)}, s32[]{:T(128)}, /*...) while((s32[]{:T(128)}, bf16[4,256,512]{2,1,0:T(8,128)(2,1)}, ...), condition=%wide.region_4.4_spmd.clone, body=%wide.region_1.3_spmd.clone.sunk | while | flops 1082130432 | bytes 36177968 | solution.py:188
  186.1 55.8 %collective-permute-start.1 = (bf16[4,256,512]{2,1,0:T(8,128)(2,1)}, bf16[4,256,512]{2,1,0:T(8,128)(2,1)S(1)}, u32[]{:S(2)}, u32[]{:S(2)}) collective-permute-start(bf16[4,256,512]{2,1,0:T(8,128)(2,1)} %get-tuple-element.2741), channel_id=1, source_target_pairs={{0,2},{1,3},{4,6},{5,7},{8,10},{9,11},{12,14},{13,15},{16,18},{17,... | collective-permute-start | bytes 3145736 | tf_op jit(solution)/shard_map/while/body/eval_jaxpr/ppermute | solution.py:17
  259.8 825.0 %while.126 = (s32[]{:T(128)}, bf16[4,256,512]{2,1,0:T(8,128)(2,1)}, f32[2,512,2,768]{3,2,1,0:T(2,128)}, s32[]{:T(128)}, s32[4,3]{1,0:T(4,128)S(1)}, /*index=5*/b...) while((s32[]{:T(128)}, bf16[4,256,512]{2,1,0:T(8,128)(2,1)}, ...), condition=%wide.region_13.14_spmd.clone.clone.clone, body=%wide.region_6.13_spmd.clone.clone.clone.sunk | while | flops 1083375616 | bytes 63442300 | solution.py:263
  260.8 331.3 %while.128 = (s32[]{:T(128)}, bf16[4,256,512]{2,1,0:T(8,128)(2,1)}, f32[2,512,2,768]{3,2,1,0:T(2,128)}, s32[]{:T(128)}, s32[4,3]{1,0:T(4,128)S(1)}, /*index=5*/p...) while((s32[]{:T(128)}, bf16[4,256,512]{2,1,0:T(8,128)(2,1)}, ...), condition=%wide.region_12.12_spmd.clone, body=%wide.region_7.11_spmd.clone.sunk | while | flops 1083179008 | bytes 54527832 | solution.py:256
  270.8 24.0 %dynamic_update_slice.53 = f32[2,512,2,768]{3,2,1,0:T(2,128)} dynamic-update-slice(f32[2,512,2,768]{3,2,1,0:T(2,128)} %get-tuple-element.2840, f32[2,256,2,256]{3,2,1,0:T(2,128)S(1)} %dynamic-slice_add_fusion.2, s32[]{:T(128)} %constant.312.clone.1..sunk.3..sunk, s32[]{:T(128)} %select_n.250, s32[]{:T(128)} %constant.312.clone.1..sunk.3..sunk, s32[]{:T(128)} %select_n.251) | dynamic-update-slice | bytes 2097156 | tf_op jit(solution)/shard_map/while/body/eval_jaxpr/while/body/eval_jaxpr/dynamic_update_slice | solution.py:252
  304.7 89.2 %dynamic_update_slice.53 = f32[2,512,2,768]{3,2,1,0:T(2,128)} dynamic-update-slice(f32[2,512,2,768]{3,2,1,0:T(2,128)} %get-tuple-element.2840, f32[2,256,2,256]{3,2,1,0:T(2,128)S(1)} %dynamic-slice_add_fusion.2, s32[]{:T(128)} %constant.312.clone.1..sunk.3..sunk, s32[]{:T(128)} %select_n.250, s32[]{:T(128)} %constant.312.clone.1..sunk.3..sunk, s32[]{:T(128)} %select_n.251) | dynamic-update-slice | bytes 2097156 | tf_op jit(solution)/shard_map/while/body/eval_jaxpr/while/body/eval_jaxpr/dynamic_update_slice | solution.py:252
  403.9 89.1 %dynamic_update_slice.53 = f32[2,512,2,768]{3,2,1,0:T(2,128)} dynamic-update-slice(f32[2,512,2,768]{3,2,1,0:T(2,128)} %get-tuple-element.2840, f32[2,256,2,256]{3,2,1,0:T(2,128)S(1)} %dynamic-slice_add_fusion.2, s32[]{:T(128)} %constant.312.clone.1..sunk.3..sunk, s32[]{:T(128)} %select_n.250, s32[]{:T(128)} %constant.312.clone.1..sunk.3..sunk, s32[]{:T(128)} %select_n.251) | dynamic-update-slice | bytes 2097156 | tf_op jit(solution)/shard_map/while/body/eval_jaxpr/while/body/eval_jaxpr/dynamic_update_slice | solution.py:252
  502.9 89.2 %dynamic_update_slice.53 = f32[2,512,2,768]{3,2,1,0:T(2,128)} dynamic-update-slice(f32[2,512,2,768]{3,2,1,0:T(2,128)} %get-tuple-element.2840, f32[2,256,2,256]{3,2,1,0:T(2,128)S(1)} %dynamic-slice_add_fusion.2, s32[]{:T(128)} %constant.312.clone.1..sunk.3..sunk, s32[]{:T(128)} %select_n.250, s32[]{:T(128)} %constant.312.clone.1..sunk.3..sunk, s32[]{:T(128)} %select_n.251) | dynamic-update-slice | bytes 2097156 | tf_op jit(solution)/shard_map/while/body/eval_jaxpr/while/body/eval_jaxpr/dynamic_update_slice | solution.py:252
  593.4 78.6 %collective-permute-done = bf16[4,256,512]{2,1,0:T(8,128)(2,1)S(1)} collective-permute-done((bf16[4,256,512]{2,1,0:T(8,128)(2,1)}, bf16[4,256,512]{2,1,0:T(8,128)(2,1)S(1)}, u32[]{:S(2)}, u32[]{:S(2)}) %collective-permute-start) | collective-permute-done | bytes 1048608 | tf_op jit(solution)/shard_map/while/body/eval_jaxpr/ppermute | solution.py:17
  674.0 393.0 %while.128 = (s32[]{:T(128)}, bf16[4,256,512]{2,1,0:T(8,128)(2,1)}, f32[2,512,2,768]{3,2,1,0:T(2,128)}, s32[]{:T(128)}, s32[4,3]{1,0:T(4,128)S(1)}, /*index=5*/p...) while((s32[]{:T(128)}, bf16[4,256,512]{2,1,0:T(8,128)(2,1)}, ...), condition=%wide.region_12.12_spmd.clone, body=%wide.region_7.11_spmd.clone.sunk | while | flops 1083179008 | bytes 54527832 | solution.py:256
  699.3 24.0 %dynamic_update_slice.53 = f32[2,512,2,768]{3,2,1,0:T(2,128)} dynamic-update-slice(f32[2,512,2,768]{3,2,1,0:T(2,128)} %get-tuple-element.2840, f32[2,256,2,256]{3,2,1,0:T(2,128)S(1)} %dynamic-slice_add_fusion.2, s32[]{:T(128)} %constant.312.clone.1..sunk.3..sunk, s32[]{:T(128)} %select_n.250, s32[]{:T(128)} %constant.312.clone.1..sunk.3..sunk, s32[]{:T(128)} %select_n.251) | dynamic-update-slice | bytes 2097156 | tf_op jit(solution)/shard_map/while/body/eval_jaxpr/while/body/eval_jaxpr/dynamic_update_slice | solution.py:252
  728.4 15.8 %conditional.7 = (f32[2,256,2,256]{3,2,1,0:T(2,128)S(1)}, bf16[1,256,512]{2,1,0:T(8,128)(2,1)S(1)}) conditional(s32[]{:T(128)} %convert_element_type.329, () %tuple.271, (bf16[4,2,256,512]{3,2,1,0:T(8,128)(2,1)}, s32[]{:T(128)}, bf16[2,512,2,768]{3,2,1,0:T(2,128)(2,1)}, s32[]{:T(128)}, s32[]{:T(128)}, /*index=5*/pred[]{:T(512)}, ...), branch_computations={%region_8.7_spmd, %region_9.10_spmd} | conditional | flops 1082916864 | bytes 44565228 | solution.py:249
  748.8 89.2 %dynamic_update_slice.53 = f32[2,512,2,768]{3,2,1,0:T(2,128)} dynamic-update-slice(f32[2,512,2,768]{3,2,1,0:T(2,128)} %get-tuple-element.2840, f32[2,256,2,256]{3,2,1,0:T(2,128)S(1)} %dynamic-slice_add_fusion.2, s32[]{:T(128)} %constant.312.clone.1..sunk.3..sunk, s32[]{:T(128)} %select_n.250, s32[]{:T(128)} %constant.312.clone.1..sunk.3..sunk, s32[]{:T(128)} %select_n.251) | dynamic-update-slice | bytes 2097156 | tf_op jit(solution)/shard_map/while/body/eval_jaxpr/while/body/eval_jaxpr/dynamic_update_slice | solution.py:252
  863.3 89.1 %dynamic_update_slice.53 = f32[2,512,2,768]{3,2,1,0:T(2,128)} dynamic-update-slice(f32[2,512,2,768]{3,2,1,0:T(2,128)} %get-tuple-element.2840, f32[2,256,2,256]{3,2,1,0:T(2,128)S(1)} %dynamic-slice_add_fusion.2, s32[]{:T(128)} %constant.312.clone.1..sunk.3..sunk, s32[]{:T(128)} %select_n.250, s32[]{:T(128)} %constant.312.clone.1..sunk.3..sunk, s32[]{:T(128)} %select_n.251) | dynamic-update-slice | bytes 2097156 | tf_op jit(solution)/shard_map/while/body/eval_jaxpr/while/body/eval_jaxpr/dynamic_update_slice | solution.py:252
  977.8 89.2 %dynamic_update_slice.53 = f32[2,512,2,768]{3,2,1,0:T(2,128)} dynamic-update-slice(f32[2,512,2,768]{3,2,1,0:T(2,128)} %get-tuple-element.2840, f32[2,256,2,256]{3,2,1,0:T(2,128)S(1)} %dynamic-slice_add_fusion.2, s32[]{:T(128)} %constant.312.clone.1..sunk.3..sunk, s32[]{:T(128)} %select_n.250, s32[]{:T(128)} %constant.312.clone.1..sunk.3..sunk, s32[]{:T(128)} %select_n.251) | dynamic-update-slice | bytes 2097156 | tf_op jit(solution)/shard_map/while/body/eval_jaxpr/while/body/eval_jaxpr/dynamic_update_slice | solution.py:252
  1091.0 130.8 %collective-permute-start.3 = (bf16[2,256,2,512]{3,2,1,0:T(2,128)(2,1)S(1)}, bf16[2,256,2,512]{3,2,1,0:T(2,128)(2,1)S(1)}, u32[]{:S(2)}, u32[]{:S(2)}) collective-permute-start(bf16[2,256,2,512]{3,2,1,0:T(2,128)(2,1)S(1)} %slice.723), channel_id=1, source_target_pairs={{0,4},{4,8},{8,12},{12,0},{1,5},{5,9},{9,13},{13,1},{2,6},{6,10},{... | collective-permute-start | bytes 3145736 | tf_op jit(solution)/shard_map/ppermute | solution.py:11
  1221.8 55.9 %collective-permute-done.3 = bf16[2,256,2,512]{3,2,1,0:T(2,128)(2,1)S(1)} collective-permute-done((bf16[2,256,2,512]{3,2,1,0:T(2,128)(2,1)S(1)}, bf16[2,256,2,512]{3,2,1,0:T(2,128)(2,1)S(1)}, u32[]{:S(2)}, u32[]{:S(2)}) %collective-permute-start.3) | collective-permute-done | bytes 1048608 | tf_op jit(solution)/shard_map/ppermute | solution.py:11
  1278.9 48.6 %copy.10 = bf16[2,256,2,512]{2,1,0,3:T(8,128)(2,1)} copy(bf16[2,256,2,512]{3,2,1,0:T(2,128)(2,1)S(1)} %fusion.103) | data formatting | bytes 2097152
  1327.5 97.6 %reshape.239 = bf16[512,1024]{1,0:T(8,128)(2,1)} reshape(bf16[512,2,256,2]{3,2,1,0:T(8,128)(2,1)} %bitcast.34) | data formatting | bytes 2097152
  1432.2 73.9 %reshape.240 = bf16[256,2,256,2]{3,2,1,0:T(8,128)(2,1)} reshape(bf16[256,1024]{1,0:T(8,128)(2,1)} %reduce-scatter.4.cloned.1.call-done) | data formatting | bytes 1048576
  1506.1 31.9 %copy.11 = bf16[2,256,2,256]{3,2,1,0:T(2,128)(2,1)S(1)} copy(bf16[2,256,2,256]{2,1,0,3:T(8,128)(2,1)} %bitcast.128) | data formatting | bytes 1048576
  (426 shorter events, 413.7 us)
Async XLA Ops:
  6.5 8.8 copy-start.7
  6.5 1425.7 %reduce-scatter.4.cloned.1.call-start = ((), (), s32[]{:S(2)}) async-start(), calls=%async_computation.1 | async-start | bytes 1572864
  6.5 27.8 %collective-permute-start.2 = (bf16[2,256,2,512]{3,2,1,0:T(2,128)(2,1)}, bf16[2,256,2,512]{3,2,1,0:T(2,128)(2,1)}, u32[]{:S(2)}, u32[]{:S(2)}) collective-permute-start(bf16[2,256,2,512]{3,2,1,0:T(2,128)(2,1)} %param.25), channel_id=1, source_target_pairs={{0,12},{4,0},{8,4},{12,8},{1,13},{5,1},{9,5},{13,9},{2,14},{6,2},{... | collective-permute-start | bytes 3145736 | tf_op jit(solution)/shard_map/ppermute | solution.py:11
  134.2 13.9 collective-permute-start.1
  186.1 68.3 %collective-permute-start.1 = (bf16[4,256,512]{2,1,0:T(8,128)(2,1)}, bf16[4,256,512]{2,1,0:T(8,128)(2,1)S(1)}, u32[]{:S(2)}, u32[]{:S(2)}) collective-permute-start(bf16[4,256,512]{2,1,0:T(8,128)(2,1)} %get-tuple-element.2741), channel_id=1, source_target_pairs={{0,2},{1,3},{4,6},{5,7},{8,10},{9,11},{12,14},{13,15},{16,18},{17,... | collective-permute-start | bytes 3145736 | tf_op jit(solution)/shard_map/while/body/eval_jaxpr/ppermute | solution.py:17
  592.1 79.9 %collective-permute-start = (bf16[4,256,512]{2,1,0:T(8,128)(2,1)}, bf16[4,256,512]{2,1,0:T(8,128)(2,1)S(1)}, u32[]{:S(2)}, u32[]{:S(2)}) collective-permute-start(bf16[4,256,512]{2,1,0:T(8,128)(2,1)} %get-tuple-element.2762), channel_id=1, source_target_pairs={{2,0},{3,1},{6,4},{7,5},{10,8},{11,9},{14,12},{15,13},{18,16},{19,... | collective-permute-start | bytes 3145736 | tf_op jit(solution)/shard_map/while/body/eval_jaxpr/ppermute | solution.py:17
  686.7 1.0 copy-start.2
  689.5 1.0 copy-start.1
  690.5 1.4 copy-start.3
  690.5 1.4 copy-start.4
  736.1 1.0 copy-start.2
  738.9 1.0 copy-start.1
  739.9 1.4 copy-start.3
  739.9 1.4 copy-start.4
  850.6 1.0 copy-start.2
  854.5 1.4 copy-start.3
  854.5 1.4 copy-start.4
  965.1 1.0 copy-start.2
  967.9 1.0 copy-start.1
  969.0 1.4 copy-start.3
  969.0 1.4 copy-start.4
  1067.0 16.9 %collective-permute-start = (bf16[4,256,512]{2,1,0:T(8,128)(2,1)}, bf16[4,256,512]{2,1,0:T(8,128)(2,1)S(1)}, u32[]{:S(2)}, u32[]{:S(2)}) collective-permute-start(bf16[4,256,512]{2,1,0:T(8,128)(2,1)} %get-tuple-element.2762), channel_id=1, source_target_pairs={{2,0},{3,1},{6,4},{7,5},{10,8},{11,9},{14,12},{15,13},{18,16},{19,... | collective-permute-start | bytes 3145736 | tf_op jit(solution)/shard_map/while/body/eval_jaxpr/ppermute | solution.py:17
  1084.8 4.0 copy-start.5
  1091.0 186.7 %collective-permute-start.3 = (bf16[2,256,2,512]{3,2,1,0:T(2,128)(2,1)S(1)}, bf16[2,256,2,512]{3,2,1,0:T(2,128)(2,1)S(1)}, u32[]{:S(2)}, u32[]{:S(2)}) collective-permute-start(bf16[2,256,2,512]{3,2,1,0:T(2,128)(2,1)S(1)} %slice.723), channel_id=1, source_target_pairs={{0,4},{4,8},{8,12},{12,0},{1,5},{5,9},{9,13},{13,1},{2,6},{6,10},{... | collective-permute-start | bytes 3145736 | tf_op jit(solution)/shard_map/ppermute | solution.py:11
  (11 other events, 10.9 us)
Sparse Core Ops, SparseCore 0:
  1425.3 6.8 reduce-scatter.3
where the time goes:
time: 1550 us
  local copies, waits for them, and re-layouts  929 us (60%)
  waiting for transfers between devices  200 us (13%)
  starting transfers between devices  195 us (13%)
  other arithmetic  120 us (8%)
  loops' own time  57.1 us (4%)
  matrix products  29.3 us (2%)
    dynamic_update_slice x8, local copies, waits for them, and re-layouts, backward_per_slot(): lax.dynamic_update_slice(grad_wide, current + patch_grad, corner)  583 us
    unnamed x10, local copies, waits for them, and re-layouts  253 us
    ppermute x2, starting transfers between devices, passed_along(): lax.ppermute(array, axis, [(i, (i + by) % peers) for i in range(peers)])  136 us
    ppermute x4, waiting for transfers between devices, passed_along_2(): return lax.ppermute(array, axis, pairs)  119 us
    ppermute x2, waiting for transfers between devices, passed_along(): lax.ppermute(array, axis, [(i, (i + by) % peers) for i in range(peers)])  74.1 us
    ppermute x4, starting transfers between devices, passed_along_2(): return lax.ppermute(array, axis, pairs)  59.7 us
    another operation x2, loops' own time, backward_step(): lax.fori_loop(0, slot_count, backward_per_slot, (jnp.zeros(wave_shape, jn...  35.3 us
  transfers between devices with their start and end apart: 7, of which 7 were waited for; matrix products, arithmetic and copies ran while one was open for 0% of the time, Pallas kernels for 0%

commit v1 on v0

v1 whole, which is shorter than its diff:
```python
import functools
import math

import jax
import jax.numpy as jnp
import ml_dtypes
import numpy as np
from jax import lax
from jax.experimental import pallas as pl
from jax.experimental.pallas import tpu as pltpu
from jax.sharding import PartitionSpec as P

VMEM_LIMIT = 58 * 1024 * 1024


def passed(array, axis, by):
    peers = lax.axis_size(axis)
    return lax.ppermute(array, axis, [(i, (i + by) % peers) for i in range(peers)])


def base_tables(pix):
    index = np.arange(pix)
    angles = 2.0 * math.pi / pix * (np.outer(index, index) % pix)
    scale = 1.0 / math.sqrt(pix)
    rounded = lambda v: v.astype(np.float32).astype(ml_dtypes.bfloat16)
    wide = lambda v: rounded(v).astype(np.float64)
    w = wide(np.cos(angles) * scale) + 1j * wide(-np.sin(angles) * scale)
    freq = (index + pix // 2) % pix - pix // 2
    h = np.exp(-0.4j * math.pi / pix * (freq * freq))
    planes = []
    for factor in (np.ones_like(h), h, np.conj(h)):
        b = factor[:, None] * w
        planes += [b.real, b.imag]
    stack = np.stack(planes)
    return rounded(np.stack([stack, stack.transpose(0, 2, 1)]))


def prep_kernel(mine, pix, info, base, probe, tabs, psi0):
    def put(m, slot, re, im, transposed):
        upper, lower = (im, -im) if transposed else (-im, im)
        tabs[m, slot, :pix, :pix] = re.astype(jnp.bfloat16)
        tabs[m, slot, :pix, pix:] = upper.astype(jnp.bfloat16)
        tabs[m, slot, pix:, :pix] = lower.astype(jnp.bfloat16)
        tabs[m, slot, pix:, pix:] = re.astype(jnp.bfloat16)

    for m in range(mine):
        r0 = info[2 + 4 * m]
        c0 = info[4 + 4 * m]

        def rolled(side, f, shift, axis):
            re = pltpu.roll(base[side, 2 * f].astype(jnp.float32), shift, axis)
            im = pltpu.roll(base[side, 2 * f + 1].astype(jnp.float32), shift, axis)
            return re, im

        for f in range(3):
            put(m, f, *rolled(0, f, r0, 1), False)
            put(m, 4 + f, *rolled(1, f, c0, 0), True)
        put(m, 3, *rolled(1, 0, r0, 0), True)
        put(m, 7, *rolled(0, 0, c0, 1), False)
        for part in range(2):
            plane = probe[:, part * pix : (part + 1) * pix].astype(jnp.float32)
            plane = pltpu.roll(pltpu.roll(plane, r0, 0), c0, 1)
            psi0[m, part] = plane.astype(jnp.bfloat16)


def main_kernel(
    groups, depth, mine, pix, info, own, nown, nown_x, oth, oth_x, noth, noth_x,
    tabs_any, psi0_any, light_any, keep, send, obj, tp, psi, tabs, light, sems
):
    layers = groups * depth
    rank = info[0]
    core = info[1]
    copies = []

    def fetch(src, dst):
        copy = pltpu.make_async_copy(src, dst, sems.at[len(copies)])
        copy.start()
        copies.append(copy)

    def layer_of(s, i):
        group = lax.rem(rank - s + groups, groups)
        return group * depth + i

    for i in range(depth):
        for col in range(2):
            fetch(own.at[col, i], obj.at[layer_of(0, i), 0, col])
        fetch(nown.at[i], obj.at[layer_of(0, i), 1, core])
        fetch(nown_x.at[i], obj.at[layer_of(0, i), 1, 1 - core])
        for s in range(1, groups):
            fetch(oth.at[s - 1, i], obj.at[layer_of(s, i), 0, core])
            fetch(oth_x.at[s - 1, i], obj.at[layer_of(s, i), 0, 1 - core])
            fetch(noth.at[s - 1, i], obj.at[layer_of(s, i), 1, core])
            fetch(noth_x.at[s - 1, i], obj.at[layer_of(s, i), 1, 1 - core])
    fetch(tabs_any, tabs)
    fetch(psi0_any, psi.at[0])
    fetch(light_any, light)
    for copy in copies:
        copy.wait()

    row_at = lax.broadcasted_iota(jnp.int32, (pix, pix), 0)
    col_at = lax.broadcasted_iota(jnp.int32, (pix, pix), 1)
    members = range(mine)
    r0 = [info[2 + 4 * m] for m in members]
    q = [info[3 + 4 * m] for m in members]
    c0 = [info[4 + 4 * m] for m in members]
    live = [info[5 + 4 * m].astype(jnp.float32) for m in members]
    f32 = jnp.float32
    bf16 = jnp.bfloat16

    def patch(j, m, part):
        right = col_at >= c0[m]
        here = jnp.where(right, obj[j, 0, q[m], part].astype(f32), obj[j, 0, 1 - q[m], part].astype(f32))
        there = jnp.where(right, obj[j, 1, q[m], part].astype(f32), obj[j, 1, 1 - q[m], part].astype(f32))
        return jnp.where(row_at >= r0[m], here, there).astype(bf16)

    def left(m, slot, re, im):
        out = jnp.dot(tabs[m, slot], jnp.concatenate([re, im], axis=0), preferred_element_type=f32)
        return out[:pix], out[pix:]

    def right(m, slot, re, im):
        out = jnp.dot(
            jnp.concatenate([re.astype(bf16), im.astype(bf16)], axis=1), tabs[m, slot],
            preferred_element_type=f32,
        )
        return out[:, :pix], out[:, pix:]

    def both(slots, pairs):
        lf, rf = slots
        halfway = [left(m, lf, re.astype(bf16), im.astype(bf16)) for m, (re, im) in zip(members, pairs)]
        return [right(m, rf, re, im) for m, (re, im) in zip(members, halfway)]

    def entrance(j):
        pairs = []
        for m in members:
            tr, ti = patch(j, m, 0), patch(j, m, 1)
            tp[j, m, 0] = tr
            tp[j, m, 1] = ti
            tr, ti = tr.astype(f32), ti.astype(f32)
            pr, pi = psi[j, m, 0].astype(f32), psi[j, m, 1].astype(f32)
            pairs.append((tr * pr - ti * pi, tr * pi + ti * pr))
        return pairs

    def forward(j, carry):
        spectra = both((1, 5), entrance(j))
        for m, (re, im) in enumerate(both((3, 7), spectra)):
            psi[j + 1, m, 0] = re.astype(bf16)
            psi[j + 1, m, 1] = im.astype(bf16)
        return carry

    lax.fori_loop(0, layers - 1, forward, 0)
    spectra = both((0, 4), entrance(layers - 1))
    tilted = []
    for m, (re, im) in enumerate(spectra):
        excess = (re * re + im * im - light[m]) * live[m]
        tilted.append((excess * re, excess * im))
    exits = both((3, 7), tilted)

    def scatter(j, exits):
        place = lax.rem(j // depth - rank + groups, groups)
        place = lax.rem(groups - place, groups) * depth + lax.rem(j, depth)
        grads = []
        for m, (re, im) in enumerate(exits):
            pr, pi = psi[j, m, 0].astype(f32), psi[j, m, 1].astype(f32)
            grads.append((pr * re + pi * im, pr * im - pi * re))
        for below in range(2):
            for away in range(2):
                target = (1 - core) if away else core
                ref = send if away else keep
                for part in range(2):
                    total = None
                    for m in members:
                        rows = (row_at < r0[m]) if below else (row_at >= r0[m])
                        same = target == q[m]
                        low = jnp.where(same, c0[m], 0)
                        high = jnp.where(same, pix, c0[m])
                        mask = rows & (col_at >= low) & (col_at < high)
                        term = jnp.where(mask, grads[m][part], 0.0)
                        total = term if total is None else total + term
                    ref[below, place, part] = total.astype(bf16)

    def wave_grads(j, exits):
        pairs = []
        for m, (re, im) in enumerate(exits):
            tr, ti = tp[j, m, 0].astype(f32), tp[j, m, 1].astype(f32)
            pairs.append((tr * re + ti * im, tr * im - ti * re))
        return pairs

    hold = tuple(part for pair in exits for part in pair)

    def backward(step, flat):
        j = layers - 1 - step
        exits = [(flat[2 * m], flat[2 * m + 1]) for m in members]
        scatter(j, exits)
        tilted = both((2, 6), wave_grads(j, exits))
        exits = both((3, 7), tilted)
        return tuple(part for pair in exits for part in pair)

    hold = lax.fori_loop(0, layers - 1, backward, hold)
    scatter(0, [(hold[2 * m], hold[2 * m + 1]) for m in members])


def body(object_field, offsets, counts, measured, probe_wave):
    depth, rows, _, cols = object_field.shape
    pix = probe_wave.shape[0]
    slots_here = offsets.shape[1]
    groups = lax.axis_size("slc")
    rank = lax.axis_index("slc").astype(jnp.int32)
    tile = lax.axis_index("tile").astype(jnp.int32)
    core = lax.axis_index("pos").astype(jnp.int32)
    mine = slots_here // groups
    layers = groups * depth
    first = rank * mine
    bf16 = jnp.bfloat16

    off = lax.dynamic_slice(offsets, (jnp.int32(0), first), (2, mine))
    in_tile = core * slots_here + first + jnp.arange(mine, dtype=jnp.int32)
    alive = (in_tile < counts[0]).astype(jnp.int32)
    places = jnp.stack([off[0] - tile * rows, off[1] // pix, off[1] % pix, alive], axis=1)
    info = jnp.concatenate([jnp.stack([rank, core]), places.reshape(-1)])
    light = lax.dynamic_slice(measured, (first, jnp.int32(0), jnp.int32(0)), (mine, pix, pix))

    blocks = object_field.reshape(depth, rows, 2, 2, pix).transpose(3, 0, 2, 1, 4)
    part = lax.dynamic_index_in_dim(blocks, core, 0, keepdims=False)
    half = depth // 2

    nown_hi = passed(part[half:], "tile", -1)
    oth_lo = [passed(part[:half], "slc", s) for s in range(1, groups)]
    nown_lo = passed(part[:half], "tile", -1)
    oth_hi = [passed(part[half:], "slc", s) for s in range(1, groups)]
    noth_lo = [passed(o, "tile", -1) for o in oth_lo]
    noth_hi = [passed(nown_hi, "slc", s) for s in range(1, groups)]
    nown = jnp.concatenate([nown_lo, nown_hi])
    oth = jnp.stack([jnp.concatenate(p) for p in zip(oth_lo, oth_hi)])
    noth = jnp.stack([jnp.concatenate(p) for p in zip(noth_lo, noth_hi)])
    nown_x = passed(nown, "pos", 1)
    oth_x = passed(oth, "pos", 1)
    noth_x = passed(noth, "pos", 1)

    smem = pl.BlockSpec(memory_space=pltpu.SMEM)
    vmem = pl.BlockSpec(memory_space=pltpu.VMEM)
    anywhere = pl.BlockSpec(memory_space=pl.ANY)
    tabs, psi0 = pl.pallas_call(
        functools.partial(prep_kernel, mine, pix),
        out_shape=(
            jax.ShapeDtypeStruct((mine, 8, 2 * pix, 2 * pix), bf16),
            jax.ShapeDtypeStruct((mine, 2, pix, pix), bf16),
        ),
        in_specs=[smem, vmem, vmem],
        out_specs=(vmem, vmem),
        compiler_params=pltpu.CompilerParams(vmem_limit_bytes=VMEM_LIMIT),
        name="tables",
    )(info, jnp.asarray(base_tables(pix)), probe_wave)

    grads_shape = (2, layers, 2, pix, pix)
    fetches = depth * (4 + 4 * (groups - 1)) + 3
    keep, send = pl.pallas_call(
        functools.partial(main_kernel, groups, depth, mine, pix),
        out_shape=(jax.ShapeDtypeStruct(grads_shape, bf16),) * 2,
        in_specs=[smem] + [anywhere] * 10,
        out_specs=(vmem, vmem),
        scratch_shapes=[
            pltpu.VMEM((layers, 2, 2, 2, pix, pix), bf16),
            pltpu.VMEM((layers, mine, 2, pix, pix), bf16),
            pltpu.VMEM((layers, mine, 2, pix, pix), bf16),
            pltpu.VMEM((mine, 8, 2 * pix, 2 * pix), bf16),
            pltpu.VMEM((mine, pix, pix), jnp.float32),
            pltpu.SemaphoreType.DMA((fetches,)),
        ],
        compiler_params=pltpu.CompilerParams(vmem_limit_bytes=VMEM_LIMIT),
        name="waves",
    )(info, blocks, nown, nown_x, oth, oth_x, noth, noth_x, tabs, psi0, light)

    total = (keep.astype(jnp.float32) + passed(send, "pos", 1).astype(jnp.float32)).astype(bf16)
    here = total[0].reshape(groups, depth, 2, pix, pix)
    rim = total[1].reshape(groups, depth, 2, pix, pix)
    wide = lambda v: v.astype(jnp.float32)
    rim_lo = wide(rim[0, :half])
    tile_lo = wide(here[0, :half])
    tile_hi = wide(here[0, half:])
    for s in range(1, groups):
        rim_lo += wide(passed(rim[s, :half], "slc", -s))
        tile_lo += wide(passed(here[s, :half], "slc", -s))
        other_hi = wide(here[s, half:]) + wide(passed(rim[s, half:], "tile", 1))
        tile_hi += wide(passed(other_hi.astype(bf16), "slc", -s))
    tile_hi += wide(passed(rim[0, half:], "tile", 1))
    tile_lo += wide(passed(rim_lo.astype(bf16), "tile", 1))
    return jnp.concatenate([tile_lo, tile_hi]).transpose(0, 2, 1, 3)


def solution(mesh):
    placed = (
        P(("grp", "slc"), "tile", None, None),
        P(None, ("grp", "tile", "pos")),
        P(("grp", "tile")),
        P(("grp", "tile", "pos"), None, None),
        P("grp", None),
    )
    return jax.shard_map(
        body,
        mesh=mesh,
        in_specs=placed,
        out_specs=P(("grp", "slc"), "tile", None, "pos"),
        check_vma=False,
    )
```

time: 1550 us -> 94.2 us (0.06)
  local copies, waits for them, and re-layouts: 929 us -> 6.39 us
  starting transfers between devices: 195 us -> 19.3 us
  waiting for transfers between devices: 200 us -> 30.7 us
  other arithmetic: 120 us -> 7.21 us
  loops' own time: 57.1 us -> 0 us
  Pallas kernels: 0 us -> 29.4 us
  matrix products: 29.3 us -> 0 us
    dynamic_update_slice x24 -> x0, local copies, waits for them, and re-layouts: 595 us -> none  [the longest x8 583 us: backward_per_slot(): lax.dynamic_update_slice(grad_wide, current + patch_grad, corner)]
    unnamed x10 -> x20, local copies, waits for them, and re-layouts: 253 us -> 4.4 us
    ppermute x6 -> x16, starting transfers between devices: 195 us -> 19.3 us  [passed(): lax.ppermute(array, axis, [(i, (i + by) % peers) for i in range(peers)])]
    ppermute x6 -> x16, waiting for transfers between devices: 193 us -> 30.7 us  [passed(): lax.ppermute(array, axis, [(i, (i + by) % peers) for i in range(peers)])]
    another operation x26 -> x0, loops' own time: 57.1 us -> none  [the longest x2 35.3 us: backward_step(): lax.fori_loop(0, slot_count, backward_per_slot, (jnp.zeros(wave_shape, jn...]
    pallas_call x0 -> x2, Pallas kernels: none -> 29.4 us  [the longest x1 21.6 us: body(): pl.pallas_call(functools.partial(main_kernel, groups, depth, mine, pix),...]
    dot_general x64 -> x0, matrix products: 29.3 us -> none  [the longest x32 19.2 us: apply_left(): products = jnp.dot(table, values, preferred_element_type=jnp.float32)]
    convert_element_type x20 -> x4, other arithmetic: 31.2 us -> 2.96 us  [the longest x1 2.22 us: body(): (keep.astype(jnp.float32) + passed(send, 'pos', 1).astype(jnp.float32)).a...]
  transfers between devices with their start and end apart: 7 -> 16, of which waited for: 7 -> 8; matrix products, arithmetic and copies ran while one was open for 0% -> 5% of each run, Pallas kernels for 0% -> 8%
where the time goes in v1:
time: 94.2 us; the launch traced here: 93.9 us
  waiting for transfers between devices  30.7 us (33%)
  Pallas kernels  29.4 us (31%)
  starting transfers between devices  19.3 us (20%)
  other arithmetic  7.21 us (8%)
  local copies, waits for them, and re-layouts  6.39 us (7%)
  between operations  0.95 us (1%)
    ppermute x16, waiting for transfers between devices, passed(): lax.ppermute(array, axis, [(i, (i + by) % peers) for i in range(peers)])  30.7 us
    pallas_call x1, Pallas kernels, body(): pl.pallas_call(functools.partial(main_kernel, groups, depth, mine, pix),...  21.6 us
    ppermute x16, starting transfers between devices, passed(): lax.ppermute(array, axis, [(i, (i + by) % peers) for i in range(peers)])  19.3 us
    pallas_call x1, Pallas kernels, body(): pl.pallas_call(functools.partial(prep_kernel, mine, pix), out_shape=(jax....  7.77 us
    unnamed x20, local copies, waits for them, and re-layouts  4.4 us
    convert_element_type x1, other arithmetic, body(): (keep.astype(jnp.float32) + passed(send, 'pos', 1).astype(jnp.float32)).a...  2.22 us
  transfers between devices with their start and end apart: 16, of which 8 were waited for; matrix products, arithmetic and copies ran while one was open for 5% of the time, Pallas kernels for 8%

profile of v1, /device:TPU:0, one launch (start us, length us, event | category | flops | bytes accessed | tf_op | source)
XLA Modules:
  0.0 93.9 jit_solution(14828198000670565670)
XLA Ops:
  0.0 2.5 %copy.17 = bf16[2,256,2,512]{1,3,2,0:T(8,128)(2,1)S(1)} copy(bf16[2,256,2,512]{3,2,1,0:T(2,128)(2,1)} %param.6) | data formatting | bytes 2097152 | tf_op args[0]
  3.2 3.0 %collective-permute-start.4 = (bf16[1,2,256,256]{3,2,1,0:T(8,128)(2,1)S(1)}, bf16[1,2,256,256]{3,2,1,0:T(8,128)(2,1)}, u32[]{:S(2)}, u32[]{:S(2)}) collective-permute-start(bf16[1,2,256,256]{3,2,1,0:T(8,128)(2,1)S(1)} %get-tuple-element.25), channel_id=1, source_target_pairs={{0,2},{2,0},{1,3},{3,1},{4,6},{6,4},{5,7},{7,5},{8,10},{10,8},{9,1... | collective-permute-start | bytes 786440 | tf_op jit(solution)/shard_map/ppermute | solution.py:18
  6.2 3.6 %collective-permute-start.1 = (bf16[1,2,256,256]{3,2,1,0:T(8,128)(2,1)S(1)}, bf16[1,2,256,256]{3,2,1,0:T(8,128)(2,1)S(1)}, u32[]{:S(2)}, u32[]{:S(2)}) collective-permute-start(bf16[1,2,256,256]{3,2,1,0:T(8,128)(2,1)S(1)} %get-tuple-element.25), channel_id=1, source_target_pairs={{0,12},{4,0},{8,4},{12,8},{1,13},{5,1},{9,5},{13,9},{2,14},{6,2},{... | collective-permute-start | bytes 786440 | tf_op jit(solution)/shard_map/ppermute | solution.py:18
  11.5 5.0 %collective-permute-done.1 = bf16[1,2,256,256]{3,2,1,0:T(8,128)(2,1)S(1)} collective-permute-done((bf16[1,2,256,256]{3,2,1,0:T(8,128)(2,1)S(1)}, bf16[1,2,256,256]{3,2,1,0:T(8,128)(2,1)S(1)}, u32[]{:S(2)}, u32[]{:S(2)}) %collective-permute-start.1) | collective-permute-done | bytes 262176 | tf_op jit(solution)/shard_map/ppermute | solution.py:18
  17.1 2.1 %collective-permute-done.3 = bf16[1,2,256,256]{3,2,1,0:T(8,128)(2,1)} collective-permute-done((bf16[1,2,256,256]{3,2,1,0:T(8,128)(2,1)S(1)}, bf16[1,2,256,256]{3,2,1,0:T(8,128)(2,1)}, u32[]{:S(2)}, u32[]{:S(2)}) %collective-permute-start.3) | collective-permute-done | bytes 262176 | tf_op jit(solution)/shard_map/ppermute | solution.py:18
  19.1 4.1 %collective-permute-start.6 = (bf16[1,2,256,256]{3,2,1,0:T(8,128)(2,1)}, bf16[1,2,256,256]{3,2,1,0:T(8,128)(2,1)S(1)}, u32[]{:S(2)}, u32[]{:S(2)}) collective-permute-start(bf16[1,2,256,256]{3,2,1,0:T(8,128)(2,1)} %collective-permute-done.3), channel_id=1, source_target_pairs={{0,12},{4,0},{8,4},{12,8},{1,13},{5,1},{9,5},{13,9},{2,14},{6,2},{... | collective-permute-start | bytes 786440 | tf_op jit(solution)/shard_map/ppermute | solution.py:18
  23.4 1.2 %maximum_bitcast_fusion.1.oth = bf16[1,2,2,256,256]{4,3,2,1,0:T(8,128)(2,1)S(1)} fusion(bf16[1,2,256,256]{3,2,1,0:T(8,128)(2,1)} %collective-permute-done.4, bf16[1,2,256,256]{3,2,1,0:T(8,128)(2,1)} %collective-permute-done.3), kind=kLoop, calls=%fused_computation.2 | loop fusion | flops 262144 | bytes 1048576 | tf_op jit(solution)/shard_map/stack | solution.py:233
  25.0 2.4 %collective-permute-done.6 = bf16[1,2,256,256]{3,2,1,0:T(8,128)(2,1)S(1)} collective-permute-done((bf16[1,2,256,256]{3,2,1,0:T(8,128)(2,1)}, bf16[1,2,256,256]{3,2,1,0:T(8,128)(2,1)S(1)}, u32[]{:S(2)}, u32[]{:S(2)}) %collective-permute-start.6) | collective-permute-done | bytes 262176 | tf_op jit(solution)/shard_map/ppermute | solution.py:18
  27.8 0.6 pad_add_fusion.1.info
  28.4 7.8 %tables.1 = (bf16[2,8,512,512]{3,2,1,0:T(8,128)(2,1)}, bf16[2,2,256,256]{3,2,1,0:T(8,128)(2,1)}) custom-call(s32[10]{0:T(128)} %pad_add_fusion.1.info, bf16[2,6,256,256]{3,2,1,0:T(8,128)(2,1)} %constant.50.clone.base, bf16[256,512]{1,0:T(8,128)(2,1)} %probe.1), custom_call_target="tpu_custom_call" | custom-call | tf_op jit(solution)/shard_map/tables/pallas_call | solution.py:242
  36.1 0.8 constant_dynamic-slice_fusion.light_any
  37.0 0.8 copy-done.5
  37.8 21.6 %waves.1 = (bf16[2,4,2,256,256]{4,3,2,1,0:T(8,128)(2,1)}, bf16[2,4,2,256,256]{4,3,2,1,0:T(8,128)(2,1)}) custom-call(s32[10]{0:T(128)} %pad_add_fusion.1.info, bf16[2,2,2,256,256]{4,3,2,1,0:T(8,128)(2,1)} %bitcast.66, bf16[2,2,256,256]{3,2,1,0:T(8,128)(2,1)} %copy-done.4, bf16[2,2,256,256]{3,2,1,0:T(8,128)(2,1)} %collective-permute-done.2.nown_x, ...), custom_call_target="tpu_custom_call" | custom-call | tf_op jit(solution)/shard_map/waves/pallas_call | solution.py:256
  59.9 4.0 %collective-permute-done.9 = bf16[2,4,2,256,256]{4,3,2,1,0:T(8,128)(2,1)S(1)} collective-permute-done((bf16[2,4,2,256,256]{4,3,2,1,0:T(8,128)(2,1)}, bf16[2,4,2,256,256]{4,3,2,1,0:T(8,128)(2,1)S(1)}, u32[]{:S(2)}, u32[]{:S(2)}) %collective-permute-start.9) | collective-permute-done | bytes 2097184 | tf_op jit(solution)/shard_map/ppermute | solution.py:18
  63.9 2.2 %add_convert_fusion = bf16[2,4,2,256,256]{4,3,2,1,0:T(8,128)(2,1)S(1)} fusion(bf16[2,4,2,256,256]{4,3,2,1,0:T(8,128)(2,1)S(1)} %collective-permute-done.9, bf16[2,4,2,256,256]{4,3,2,1,0:T(8,128)(2,1)} %get-tuple-element.11), kind=kLoop, calls=%fused_computation | loop fusion | flops 4194304 | bytes 6291456 | tf_op jit(solution)/shard_map/convert_element_type | solution.py:273
  66.7 0.6 collective-permute-start.13
  67.5 1.6 %collective-permute-start.11 = (bf16[1,2,256,256]{3,1,2,0:T(2,128)(2,1)S(1)}, bf16[1,2,256,256]{3,1,2,0:T(2,128)(2,1)S(1)}, u32[]{:S(2)}, u32[]{:S(2)}) collective-permute-start(bf16[1,2,256,256]{3,1,2,0:T(2,128)(2,1)S(1)} %bitcast.70), channel_id=1, source_target_pairs={{0,2},{2,0},{1,3},{3,1},{4,6},{6,4},{5,7},{7,5},{8,10},{10,8},{9,1... | collective-permute-start | bytes 786440 | tf_op jit(solution)/shard_map/ppermute | solution.py:18
  69.5 1.6 %collective-permute-start.15 = (bf16[1,2,256,256]{3,1,2,0:T(2,128)(2,1)S(1)}, bf16[1,2,256,256]{3,1,2,0:T(2,128)(2,1)S(1)}, u32[]{:S(2)}, u32[]{:S(2)}) collective-permute-start(bf16[1,2,256,256]{3,1,2,0:T(2,128)(2,1)S(1)} %bitcast.71), channel_id=1, source_target_pairs={{0,4},{4,8},{8,12},{12,0},{1,5},{5,9},{9,13},{13,1},{2,6},{6,10},{... | collective-permute-start | bytes 786440 | tf_op jit(solution)/shard_map/ppermute | solution.py:18
  71.1 7.2 %collective-permute-done.13 = bf16[1,2,256,256]{3,1,2,0:T(2,128)(2,1)S(1)} collective-permute-done((bf16[1,2,256,256]{3,1,2,0:T(2,128)(2,1)S(1)}, bf16[1,2,256,256]{3,1,2,0:T(2,128)(2,1)S(1)}, u32[]{:S(2)}, u32[]{:S(2)}) %collective-permute-start.13) | collective-permute-done | bytes 262176 | tf_op jit(solution)/shard_map/ppermute | solution.py:18
  78.6 1.6 %collective-permute-start.14 = (bf16[1,2,256,256]{3,1,2,0:T(2,128)(2,1)S(1)}, bf16[1,2,256,256]{3,1,2,0:T(2,128)(2,1)S(1)}, u32[]{:S(2)}, u32[]{:S(2)}) collective-permute-start(bf16[1,2,256,256]{3,1,2,0:T(2,128)(2,1)S(1)} %fusion), channel_id=1, source_target_pairs={{0,2},{2,0},{1,3},{3,1},{4,6},{6,4},{5,7},{7,5},{8,10},{10,8},{9,1... | collective-permute-start | bytes 786440 | tf_op jit(solution)/shard_map/ppermute | solution.py:18
  81.5 2.1 %collective-permute-done.15 = bf16[1,2,256,256]{3,1,2,0:T(2,128)(2,1)S(1)} collective-permute-done((bf16[1,2,256,256]{3,1,2,0:T(2,128)(2,1)S(1)}, bf16[1,2,256,256]{3,1,2,0:T(2,128)(2,1)S(1)}, u32[]{:S(2)}, u32[]{:S(2)}) %collective-permute-start.15) | collective-permute-done | bytes 262176 | tf_op jit(solution)/shard_map/ppermute | solution.py:18
  83.5 4.4 %collective-permute-done.14 = bf16[1,2,256,256]{3,1,2,0:T(2,128)(2,1)S(1)} collective-permute-done((bf16[1,2,256,256]{3,1,2,0:T(2,128)(2,1)S(1)}, bf16[1,2,256,256]{3,1,2,0:T(2,128)(2,1)S(1)}, u32[]{:S(2)}, u32[]{:S(2)}) %collective-permute-start.14) | collective-permute-done | bytes 262176 | tf_op jit(solution)/shard_map/ppermute | solution.py:18
  88.4 3.6 %collective-permute-done.10 = bf16[1,2,256,256]{3,1,2,0:T(2,128)(2,1)S(1)} collective-permute-done((bf16[1,2,256,256]{3,1,2,0:T(2,128)(2,1)S(1)}, bf16[1,2,256,256]{3,1,2,0:T(2,128)(2,1)S(1)}, u32[]{:S(2)}, u32[]{:S(2)}) %collective-permute-start.10) | collective-permute-done | bytes 262176 | tf_op jit(solution)/shard_map/ppermute | solution.py:18
  92.4 1.5 %maximum_bitcast_fusion = f32[2,256,2,256]{3,2,1,0:T(2,128)} fusion(f32[1,2,256,256]{3,1,2,0:T(2,128)S(1)} %fusion.1, f32[1,2,256,256]{3,1,2,0:T(2,128)S(1)} %fusion.3), kind=kLoop, calls=%fused_computation.1 | loop fusion | flops 262144 | bytes 2097152 | tf_op jit(solution)/shard_map/transpose | solution.py:287
  (55 shorter events, 7.4 us)
Async XLA Ops:
  0.0 36.1 %copy-start = (f32[4,256,256]{2,1,0:T(8,128)S(1)}, f32[4,256,256]{2,1,0:T(8,128)}, u32[]{:S(2)}) copy-start(f32[4,256,256]{2,1,0:T(8,128)} %param.9) | copy-start | bytes 3145732
  2.5 8.9 %copy-start.6 = (s32[2,4]{1,0:T(2,128)S(1)}, s32[2,4]{1,0:T(2,128)}, u32[]{:S(2)}) copy-start(s32[2,4]{1,0:T(2,128)} %param.7) | copy-start | bytes 100
  3.1 21.5 %copy-start.1 = (bf16[2,256,2,2,256]{4,1,2,0,3:T(8,128)(2,1)}, bf16[2,256,2,2,256]{4,1,2,0,3:T(8,128)(2,1)S(1)}, u32[]{:S(2)}) copy-start(bf16[2,256,2,2,256]{4,1,2,0,3:T(8,128)(2,1)S(1)} %copy.18) | copy-start | bytes 3145732
  3.2 20.2 %collective-permute-start.4 = (bf16[1,2,256,256]{3,2,1,0:T(8,128)(2,1)S(1)}, bf16[1,2,256,256]{3,2,1,0:T(8,128)(2,1)}, u32[]{:S(2)}, u32[]{:S(2)}) collective-permute-start(bf16[1,2,256,256]{3,2,1,0:T(8,128)(2,1)S(1)} %get-tuple-element.25), channel_id=1, source_target_pairs={{0,2},{2,0},{1,3},{3,1},{4,6},{6,4},{5,7},{7,5},{8,10},{10,8},{9,1... | collective-permute-start | bytes 786440 | tf_op jit(solution)/shard_map/ppermute | solution.py:18
  6.2 10.4 %collective-permute-start.1 = (bf16[1,2,256,256]{3,2,1,0:T(8,128)(2,1)S(1)}, bf16[1,2,256,256]{3,2,1,0:T(8,128)(2,1)S(1)}, u32[]{:S(2)}, u32[]{:S(2)}) collective-permute-start(bf16[1,2,256,256]{3,2,1,0:T(8,128)(2,1)S(1)} %get-tuple-element.25), channel_id=1, source_target_pairs={{0,12},{4,0},{8,4},{12,8},{1,13},{5,1},{9,5},{13,9},{2,14},{6,2},{... | collective-permute-start | bytes 786440 | tf_op jit(solution)/shard_map/ppermute | solution.py:18
  9.8 9.3 %collective-permute-start.3 = (bf16[1,2,256,256]{3,2,1,0:T(8,128)(2,1)S(1)}, bf16[1,2,256,256]{3,2,1,0:T(8,128)(2,1)}, u32[]{:S(2)}, u32[]{:S(2)}) collective-permute-start(bf16[1,2,256,256]{3,2,1,0:T(8,128)(2,1)S(1)} %get-tuple-element.26), channel_id=1, source_target_pairs={{0,2},{2,0},{1,3},{3,1},{4,6},{6,4},{5,7},{7,5},{8,10},{10,8},{9,1... | collective-permute-start | bytes 786440 | tf_op jit(solution)/shard_map/ppermute | solution.py:18
  10.3 12.9 %collective-permute-start = (bf16[1,2,256,256]{3,2,1,0:T(8,128)(2,1)S(1)}, bf16[1,2,256,256]{3,2,1,0:T(8,128)(2,1)S(1)}, u32[]{:S(2)}, u32[]{:S(2)}) collective-permute-start(bf16[1,2,256,256]{3,2,1,0:T(8,128)(2,1)S(1)} %get-tuple-element.26), channel_id=1, source_target_pairs={{0,12},{4,0},{8,4},{12,8},{1,13},{5,1},{9,5},{13,9},{2,14},{6,2},{... | collective-permute-start | bytes 786440 | tf_op jit(solution)/shard_map/ppermute | solution.py:18
  16.5 8.5 %collective-permute-start.7 = (bf16[1,2,256,256]{3,2,1,0:T(8,128)(2,1)S(1)}, bf16[1,2,256,256]{3,2,1,0:T(8,128)(2,1)S(1)}, u32[]{:S(2)}, u32[]{:S(2)}) collective-permute-start(bf16[1,2,256,256]{3,2,1,0:T(8,128)(2,1)S(1)} %collective-permute-done.1), channel_id=1, source_target_pairs={{0,2},{2,0},{1,3},{3,1},{4,6},{6,4},{5,7},{7,5},{8,10},{10,8},{9,1... | collective-permute-start | bytes 786440 | tf_op jit(solution)/shard_map/ppermute | solution.py:18
  19.1 8.3 %collective-permute-start.6 = (bf16[1,2,256,256]{3,2,1,0:T(8,128)(2,1)}, bf16[1,2,256,256]{3,2,1,0:T(8,128)(2,1)S(1)}, u32[]{:S(2)}, u32[]{:S(2)}) collective-permute-start(bf16[1,2,256,256]{3,2,1,0:T(8,128)(2,1)} %collective-permute-done.3), channel_id=1, source_target_pairs={{0,12},{4,0},{8,4},{12,8},{1,13},{5,1},{9,5},{13,9},{2,14},{6,2},{... | collective-permute-start | bytes 786440 | tf_op jit(solution)/shard_map/ppermute | solution.py:18
  23.3 13.7 %copy-start.4 = (bf16[2,2,256,256]{3,2,1,0:T(8,128)(2,1)}, bf16[2,2,256,256]{3,2,1,0:T(8,128)(2,1)S(1)}, u32[]{:S(2)}) copy-start(bf16[2,2,256,256]{3,2,1,0:T(8,128)(2,1)S(1)} %constant_dynamic-update-slice_fusion.nown) | copy-start | bytes 1572868
  23.3 13.7 %collective-permute-start.2 = (bf16[2,2,256,256]{3,2,1,0:T(8,128)(2,1)S(1)}, bf16[2,2,256,256]{3,2,1,0:T(8,128)(2,1)}, u32[]{:S(2)}, u32[]{:S(2)}) collective-permute-start(bf16[2,2,256,256]{3,2,1,0:T(8,128)(2,1)S(1)} %constant_dynamic-update-slice_fusion.nown), channel_id=1, source_target_pairs={{0,1},{1,0},{2,3},{3,2},{4,5},{5,4},{6,7},{7,6},{8,9},{9,8},{10,11... | collective-permute-start | bytes 1572872 | tf_op jit(solution)/shard_map/ppermute | solution.py:18
  24.5 12.5 %copy-start.2 = (bf16[1,2,2,256,256]{4,3,2,1,0:T(8,128)(2,1)}, bf16[1,2,2,256,256]{4,3,2,1,0:T(8,128)(2,1)S(1)}, u32[]{:S(2)}) copy-start(bf16[1,2,2,256,256]{4,3,2,1,0:T(8,128)(2,1)S(1)} %maximum_bitcast_fusion.1.oth) | copy-start | bytes 1572868
  24.6 12.4 %collective-permute-start.5 = (bf16[1,2,2,256,256]{4,3,2,1,0:T(8,128)(2,1)S(1)}, bf16[1,2,2,256,256]{4,3,2,1,0:T(8,128)(2,1)}, u32[]{:S(2)}, u32[]{:S(2)}) collective-permute-start(bf16[1,2,2,256,256]{4,3,2,1,0:T(8,128)(2,1)S(1)} %maximum_bitcast_fusion.1.oth), channel_id=1, source_target_pairs={{0,1},{1,0},{2,3},{3,2},{4,5},{5,4},{6,7},{7,6},{8,9},{9,8},{10,11... | collective-permute-start | bytes 1572872 | tf_op jit(solution)/shard_map/ppermute | solution.py:18
  27.5 9.6 %copy-start.3 = (bf16[1,2,2,256,256]{4,3,2,1,0:T(8,128)(2,1)}, bf16[1,2,2,256,256]{4,3,2,1,0:T(8,128)(2,1)S(1)}, u32[]{:S(2)}) copy-start(bf16[1,2,2,256,256]{4,3,2,1,0:T(8,128)(2,1)S(1)} %maximum_bitcast_fusion.2.noth) | copy-start | bytes 1572868
  27.5 9.5 %collective-permute-start.8 = (bf16[1,2,2,256,256]{4,3,2,1,0:T(8,128)(2,1)S(1)}, bf16[1,2,2,256,256]{4,3,2,1,0:T(8,128)(2,1)S(1)}, u32[]{:S(2)}, u32[]{:S(2)}) collective-permute-start(bf16[1,2,2,256,256]{4,3,2,1,0:T(8,128)(2,1)S(1)} %maximum_bitcast_fusion.2.noth), channel_id=1, source_target_pairs={{0,1},{1,0},{2,3},{3,2},{4,5},{5,4},{6,7},{7,6},{8,9},{9,8},{10,11... | collective-permute-start | bytes 1572872 | tf_op jit(solution)/shard_map/ppermute | solution.py:18
  37.0 0.8 copy-start.5
  59.4 4.5 %collective-permute-start.9 = (bf16[2,4,2,256,256]{4,3,2,1,0:T(8,128)(2,1)}, bf16[2,4,2,256,256]{4,3,2,1,0:T(8,128)(2,1)S(1)}, u32[]{:S(2)}, u32[]{:S(2)}) collective-permute-start(bf16[2,4,2,256,256]{4,3,2,1,0:T(8,128)(2,1)} %get-tuple-element.12), channel_id=1, source_target_pairs={{0,1},{1,0},{2,3},{3,2},{4,5},{5,4},{6,7},{7,6},{8,9},{9,8},{10,11... | collective-permute-start | bytes 6291464 | tf_op jit(solution)/shard_map/ppermute | solution.py:18
  66.7 11.6 %collective-permute-start.13 = (bf16[1,2,256,256]{3,1,2,0:T(2,128)(2,1)S(1)}, bf16[1,2,256,256]{3,1,2,0:T(2,128)(2,1)S(1)}, u32[]{:S(2)}, u32[]{:S(2)}) collective-permute-start(bf16[1,2,256,256]{3,1,2,0:T(2,128)(2,1)S(1)} %bitcast.73), channel_id=1, source_target_pairs={{0,4},{4,8},{8,12},{12,0},{1,5},{5,9},{9,13},{13,1},{2,6},{6,10},{... | collective-permute-start | bytes 786440 | tf_op jit(solution)/shard_map/ppermute | solution.py:18
  67.5 13.5 %collective-permute-start.11 = (bf16[1,2,256,256]{3,1,2,0:T(2,128)(2,1)S(1)}, bf16[1,2,256,256]{3,1,2,0:T(2,128)(2,1)S(1)}, u32[]{:S(2)}, u32[]{:S(2)}) collective-permute-start(bf16[1,2,256,256]{3,1,2,0:T(2,128)(2,1)S(1)} %bitcast.70), channel_id=1, source_target_pairs={{0,2},{2,0},{1,3},{3,1},{4,6},{6,4},{5,7},{7,5},{8,10},{10,8},{9,1... | collective-permute-start | bytes 786440 | tf_op jit(solution)/shard_map/ppermute | solution.py:18
  69.5 14.1 %collective-permute-start.15 = (bf16[1,2,256,256]{3,1,2,0:T(2,128)(2,1)S(1)}, bf16[1,2,256,256]{3,1,2,0:T(2,128)(2,1)S(1)}, u32[]{:S(2)}, u32[]{:S(2)}) collective-permute-start(bf16[1,2,256,256]{3,1,2,0:T(2,128)(2,1)S(1)} %bitcast.71), channel_id=1, source_target_pairs={{0,4},{4,8},{8,12},{12,0},{1,5},{5,9},{9,13},{13,1},{2,6},{6,10},{... | collective-permute-start | bytes 786440 | tf_op jit(solution)/shard_map/ppermute | solution.py:18
  78.6 9.3 %collective-permute-start.14 = (bf16[1,2,256,256]{3,1,2,0:T(2,128)(2,1)S(1)}, bf16[1,2,256,256]{3,1,2,0:T(2,128)(2,1)S(1)}, u32[]{:S(2)}, u32[]{:S(2)}) collective-permute-start(bf16[1,2,256,256]{3,1,2,0:T(2,128)(2,1)S(1)} %fusion), channel_id=1, source_target_pairs={{0,2},{2,0},{1,3},{3,1},{4,6},{6,4},{5,7},{7,5},{8,10},{10,8},{9,1... | collective-permute-start | bytes 786440 | tf_op jit(solution)/shard_map/ppermute | solution.py:18
  80.4 11.5 %collective-permute-start.10 = (bf16[1,2,256,256]{3,1,2,0:T(2,128)(2,1)S(1)}, bf16[1,2,256,256]{3,1,2,0:T(2,128)(2,1)S(1)}, u32[]{:S(2)}, u32[]{:S(2)}) collective-permute-start(bf16[1,2,256,256]{3,1,2,0:T(2,128)(2,1)S(1)} %bitcast.72), channel_id=1, source_target_pairs={{0,2},{2,0},{1,3},{3,1},{4,6},{6,4},{5,7},{7,5},{8,10},{10,8},{9,1... | collective-permute-start | bytes 786440 | tf_op jit(solution)/shard_map/ppermute | solution.py:18
  81.4 10.6 %collective-permute-start.12 = (bf16[1,2,256,256]{3,1,2,0:T(2,128)(2,1)S(1)}, bf16[1,2,256,256]{3,1,2,0:T(2,128)(2,1)S(1)}, u32[]{:S(2)}, u32[]{:S(2)}) collective-permute-start(bf16[1,2,256,256]{3,1,2,0:T(2,128)(2,1)S(1)} %fusion.2), channel_id=1, source_target_pairs={{0,4},{4,8},{8,12},{12,0},{1,5},{5,9},{9,13},{13,1},{2,6},{6,10},{... | collective-permute-start | bytes 786440 | tf_op jit(solution)/shard_map/ppermute | solution.py:18

commit v2 on v1

v2 whole, which is shorter than its diff:
```python
import functools
import math

import jax
import jax.numpy as jnp
import ml_dtypes
import numpy as np
from jax import lax
from jax.experimental import pallas as pl
from jax.experimental.pallas import tpu as pltpu
from jax.sharding import PartitionSpec as P

VMEM_LIMIT = 58 * 1024 * 1024


def passed(array, axis, by):
    peers = lax.axis_size(axis)
    return lax.ppermute(array, axis, [(i, (i + by) % peers) for i in range(peers)])


def base_tables(pix):
    index = np.arange(pix)
    angles = 2.0 * math.pi / pix * (np.outer(index, index) % pix)
    scale = 1.0 / math.sqrt(pix)
    rounded = lambda v: v.astype(np.float32).astype(ml_dtypes.bfloat16)
    wide = lambda v: rounded(v).astype(np.float64)
    w = wide(np.cos(angles) * scale) + 1j * wide(-np.sin(angles) * scale)
    freq = (index + pix // 2) % pix - pix // 2
    h = np.exp(-0.4j * math.pi / pix * (freq * freq))
    planes = []
    for factor in (np.ones_like(h), h, np.conj(h)):
        b = factor[:, None] * w
        planes += [b.real, b.imag]
    stack = np.stack(planes)
    return rounded(np.stack([stack, stack.transpose(0, 2, 1)]))


def prep_kernel(mine, pix, info, base, probe, lefts, rights, psi0):
    bf16 = jnp.bfloat16
    for m in range(mine):
        r0 = info[2 + 4 * m]
        c0 = info[4 + 4 * m]

        def rolled(side, f, shift, axis):
            re = pltpu.roll(base[side, 2 * f].astype(jnp.float32), shift, axis)
            im = pltpu.roll(base[side, 2 * f + 1].astype(jnp.float32), shift, axis)
            return re.astype(bf16), im.astype(bf16)

        def inverse(side, shift, axis):
            re = pltpu.roll(base[side, 0].astype(jnp.float32), shift, axis)
            im = pltpu.roll(base[side, 1].astype(jnp.float32), shift, axis)
            return re.astype(bf16), (-im).astype(bf16)

        for t in range(4):
            re, im = rolled(0, t, r0, 1) if t < 3 else inverse(1, r0, 0)
            lefts[m, t, :, :pix] = re
            lefts[m, t, :, pix:] = im
            re, im = rolled(1, t, c0, 0) if t < 3 else inverse(0, c0, 1)
            rights[m, t, :pix, :] = re
            rights[m, t, pix:, :] = im
        for part in range(2):
            plane = probe[:, part * pix : (part + 1) * pix].astype(jnp.float32)
            plane = pltpu.roll(pltpu.roll(plane, r0, 0), c0, 1)
            psi0[m, part] = plane.astype(bf16)


def main_kernel(groups, depth, mine, pix, pieces, info, *refs):
    count = len(pieces) + 1
    own, operands = refs[0], refs[1:count]
    lefts_any, rights_any, psi0_any, light_any = refs[count : count + 4]
    outs = refs[count + 4 : count + 4 + 4 * groups]
    obj, tp, psi, lefts, rights, light, grads, sems, tab_sems, out_sems = refs[count + 4 + 4 * groups :]
    layers = groups * depth
    rank = info[0]
    core = info[1]
    members = range(mine)

    def layer_of(s, i):
        group = lax.rem(rank - s + groups, groups)
        return group * depth + i

    def table_copies(t):
        return [
            pltpu.make_async_copy(lefts_any.at[:, t], lefts.at[:, t], tab_sems.at[t, 0]),
            pltpu.make_async_copy(rights_any.at[:, t], rights.at[:, t], tab_sems.at[t, 1]),
        ]

    def wait_tables(t):
        for copy in table_copies(t):
            copy.wait()

    psi_copy = pltpu.make_async_copy(psi0_any, psi.at[0], tab_sems.at[4, 0])
    light_copy = pltpu.make_async_copy(light_any, light, tab_sems.at[4, 1])
    psi_copy.start()
    for copy in table_copies(1) + table_copies(3):
        copy.start()
    for i in range(depth):
        j = layer_of(0, i)
        for col in range(2):
            pltpu.make_async_copy(own.at[col, i], obj.at[j, 0, col], sems.at[j, col]).start()
    for (s, start, below, away), ref in zip(pieces, operands):
        for i in range(ref.shape[0]):
            j = layer_of(s, start + i)
            col = (1 - core) if away else core
            at = 2 * below + col
            pltpu.make_async_copy(ref.at[i], obj.at[j, below, col], sems.at[j, at]).start()
    light_copy.start()
    for copy in table_copies(0) + table_copies(2):
        copy.start()

    def wait_object(j):
        for below in range(2):
            for col in range(2):
                pltpu.make_async_copy(own.at[0, 0], obj.at[j, below, col], sems.at[j, 2 * below + col]).wait()

    row_at = lax.broadcasted_iota(jnp.int32, (pix, pix), 0)
    col_at = lax.broadcasted_iota(jnp.int32, (pix, pix), 1)
    r0 = [info[2 + 4 * m] for m in members]
    q = [info[3 + 4 * m] for m in members]
    c0 = [info[4 + 4 * m] for m in members]
    live = [info[5 + 4 * m].astype(jnp.float32) for m in members]
    f32 = jnp.float32
    bf16 = jnp.bfloat16

    def patch(j, m, part):
        right = col_at >= c0[m]
        here = jnp.where(right, obj[j, 0, q[m], part].astype(f32), obj[j, 0, 1 - q[m], part].astype(f32))
        there = jnp.where(right, obj[j, 1, q[m], part].astype(f32), obj[j, 1, 1 - q[m], part].astype(f32))
        return jnp.where(row_at >= r0[m], here, there).astype(bf16)

    def left(m, t, re, im):
        paired = jnp.concatenate(
            [jnp.concatenate([re, im], axis=1), jnp.concatenate([-im, re], axis=1)], axis=0
        )
        out = jnp.dot(lefts[m, t], paired, preferred_element_type=f32)
        return out[:, :pix].astype(bf16), out[:, pix:].astype(bf16)

    def right(m, t, re, im):
        paired = jnp.concatenate(
            [jnp.concatenate([re, -im], axis=1), jnp.concatenate([im, re], axis=1)], axis=0
        )
        out = jnp.dot(paired, rights[m, t], preferred_element_type=f32)
        return out[:pix], out[pix:]

    def both(t, pairs):
        halfway = [left(m, t, re.astype(bf16), im.astype(bf16)) for m, (re, im) in zip(members, pairs)]
        return [right(m, t, re, im) for m, (re, im) in zip(members, halfway)]

    def entrance(j):
        pairs = []
        for m in members:
            tr, ti = patch(j, m, 0), patch(j, m, 1)
            tp[j, m, 0] = tr
            tp[j, m, 1] = ti
            tr, ti = tr.astype(f32), ti.astype(f32)
            pr, pi = psi[j, m, 0].astype(f32), psi[j, m, 1].astype(f32)
            pairs.append((tr * pr - ti * pi, tr * pi + ti * pr))
        return pairs

    psi_copy.wait()
    wait_tables(1)
    wait_tables(3)

    def forward(j, carry):
        wait_object(j)
        spectra = both(1, entrance(j))
        for m, (re, im) in enumerate(both(3, spectra)):
            psi[j + 1, m, 0] = re.astype(bf16)
            psi[j + 1, m, 1] = im.astype(bf16)
        return carry

    lax.fori_loop(0, layers - 1, forward, 0)
    wait_object(layers - 1)
    wait_tables(0)
    light_copy.wait()
    spectra = both(0, entrance(layers - 1))
    tilted = []
    for m, (re, im) in enumerate(spectra):
        excess = (re * re + im * im - light[m]) * live[m]
        tilted.append((excess * re, excess * im))
    exits = both(3, tilted)

    def out_copy(away, below, s, i):
        place = s * depth + i
        out = outs[(away * 2 + below) * groups + s]
        return pltpu.make_async_copy(grads.at[away, below, place], out.at[i], out_sems.at[away, below, place])

    def scatter(j, exits):
        step = lax.rem(rank - j // depth + groups, groups)
        within = lax.rem(j, depth)
        place = step * depth + within
        terms = []
        for m, (re, im) in enumerate(exits):
            pr, pi = psi[j, m, 0].astype(f32), psi[j, m, 1].astype(f32)
            terms.append((pr * re + pi * im, pr * im - pi * re))
        for below in range(2):
            for away in range(2):
                target = (1 - core) if away else core
                for part in range(2):
                    total = None
                    for m in members:
                        rows = (row_at < r0[m]) if below else (row_at >= r0[m])
                        same = target == q[m]
                        low = jnp.where(same, c0[m], 0)
                        high = jnp.where(same, pix, c0[m])
                        mask = rows & (col_at >= low) & (col_at < high)
                        term = jnp.where(mask, terms[m][part], 0.0)
                        total = term if total is None else total + term
                    grads[away, below, place, part] = total.astype(bf16)
        for s in range(groups):

            @pl.when(step == s)
            def _():
                for below in range(2):
                    for away in range(2):
                        out_copy(away, below, s, within).start()

    def wave_grads(j, exits):
        pairs = []
        for m, (re, im) in enumerate(exits):
            tr, ti = tp[j, m, 0].astype(f32), tp[j, m, 1].astype(f32)
            pairs.append((tr * re + ti * im, tr * im - ti * re))
        return pairs

    wait_tables(2)
    hold = tuple(part for pair in exits for part in pair)

    def backward(step, flat):
        j = layers - 1 - step
        exits = [(flat[2 * m], flat[2 * m + 1]) for m in members]
        scatter(j, exits)
        tilted = both(2, wave_grads(j, exits))
        exits = both(3, tilted)
        return tuple(part for pair in exits for part in pair)

    hold = lax.fori_loop(0, layers - 1, backward, hold)
    scatter(0, [(hold[2 * m], hold[2 * m + 1]) for m in members])
    for away in range(2):
        for below in range(2):
            for s in range(groups):
                for i in range(depth):
                    out_copy(away, below, s, i).wait()


def body(object_field, offsets, counts, measured, probe_wave):
    depth, rows, _, cols = object_field.shape
    pix = probe_wave.shape[0]
    slots_here = offsets.shape[1]
    groups = lax.axis_size("slc")
    rank = lax.axis_index("slc").astype(jnp.int32)
    tile = lax.axis_index("tile").astype(jnp.int32)
    core = lax.axis_index("pos").astype(jnp.int32)
    mine = slots_here // groups
    layers = groups * depth
    first = rank * mine
    bf16 = jnp.bfloat16

    off = lax.dynamic_slice(offsets, (jnp.int32(0), first), (2, mine))
    in_tile = core * slots_here + first + jnp.arange(mine, dtype=jnp.int32)
    alive = (in_tile < counts[0]).astype(jnp.int32)
    places = jnp.stack([off[0] - tile * rows, off[1] // pix, off[1] % pix, alive], axis=1)
    info = jnp.concatenate([jnp.stack([rank, core]), places.reshape(-1)])
    light = lax.dynamic_slice(measured, (first, jnp.int32(0), jnp.int32(0)), (mine, pix, pix))

    zero = jnp.int32(0)
    part = lax.dynamic_slice(object_field, (zero, zero, zero, core * pix), (depth, rows, 2, pix))
    part = part.transpose(0, 2, 1, 3)
    half = depth // 2
    lo, hi = part[:half], part[half:]

    steps = range(1, groups)
    here = {(s, 0): passed(lo, "slc", s) for s in steps}
    nown_hi = passed(hi, "tile", -1)
    here |= {(s, half): passed(hi, "slc", s) for s in steps}
    nown_lo = passed(lo, "tile", -1)
    below = {(0, half): nown_hi, (0, 0): nown_lo}
    below |= {(s, 0): passed(here[s, 0], "tile", -1) for s in steps}
    below |= {(s, half): passed(nown_hi, "slc", s) for s in steps}
    pieces, operands = [], []
    for row_block, found in ((0, here), (1, below)):
        for (s, start), array in found.items():
            pieces += [(s, start, row_block, 0), (s, start, row_block, 1)]
            operands += [array, passed(array, "pos", 1)]
    blocks = object_field.reshape(depth, rows, 2, 2, pix).transpose(3, 0, 2, 1, 4)

    smem = pl.BlockSpec(memory_space=pltpu.SMEM)
    vmem = pl.BlockSpec(memory_space=pltpu.VMEM)
    anywhere = pl.BlockSpec(memory_space=pl.ANY)
    lefts, rights, psi0 = pl.pallas_call(
        functools.partial(prep_kernel, mine, pix),
        out_shape=(
            jax.ShapeDtypeStruct((mine, 4, pix, 2 * pix), bf16),
            jax.ShapeDtypeStruct((mine, 4, 2 * pix, pix), bf16),
            jax.ShapeDtypeStruct((mine, 2, pix, pix), bf16),
        ),
        in_specs=[smem, vmem, vmem],
        out_specs=(vmem, vmem, vmem),
        compiler_params=pltpu.CompilerParams(vmem_limit_bytes=VMEM_LIMIT),
        cost_estimate=pl.CostEstimate(flops=8 * 10**9, bytes_accessed=8 * 2**20, transcendentals=0),
        name="tables",
    )(info, jnp.asarray(base_tables(pix)), probe_wave)

    outs = pl.pallas_call(
        functools.partial(main_kernel, groups, depth, mine, pix, tuple(pieces)),
        out_shape=(jax.ShapeDtypeStruct((depth, 2, pix, pix), bf16),) * (4 * groups),
        in_specs=[smem] + [anywhere] * (5 + len(operands)),
        out_specs=(anywhere,) * (4 * groups),
        scratch_shapes=[
            pltpu.VMEM((layers, 2, 2, 2, pix, pix), bf16),
            pltpu.VMEM((layers, mine, 2, pix, pix), bf16),
            pltpu.VMEM((layers, mine, 2, pix, pix), bf16),
            pltpu.VMEM((mine, 4, pix, 2 * pix), bf16),
            pltpu.VMEM((mine, 4, 2 * pix, pix), bf16),
            pltpu.VMEM((mine, pix, pix), jnp.float32),
            pltpu.VMEM((2, 2, layers, 2, pix, pix), bf16),
            pltpu.SemaphoreType.DMA((layers, 4)),
            pltpu.SemaphoreType.DMA((5, 2)),
            pltpu.SemaphoreType.DMA((2, 2, layers)),
        ],
        compiler_params=pltpu.CompilerParams(vmem_limit_bytes=VMEM_LIMIT),
        cost_estimate=pl.CostEstimate(flops=15 * 10**9, bytes_accessed=16 * 2**20, transcendentals=0),
        name="waves",
    )(info, blocks, *operands, lefts, rights, psi0, light)

    wide = lambda v: v.astype(jnp.float32)
    sums = {}
    for s in [*steps, 0]:
        for row_block in (1, 0):
            at = row_block * groups + s
            sums[row_block, s] = wide(outs[at]) + wide(passed(outs[2 * groups + at], "pos", 1))
    rim_lo = sums[1, 0][:half]
    rim_hi = sums[1, 0][half:].astype(bf16)
    tile_lo = sums[0, 0][:half]
    tile_hi = sums[0, 0][half:]
    for s in steps:
        rim, tile_part = sums[1, s], sums[0, s]
        rim_lo += wide(passed(rim[:half].astype(bf16), "slc", -s))
        other_hi = tile_part[half:] + wide(passed(rim[half:].astype(bf16), "tile", 1))
        tile_lo += wide(passed(tile_part[:half].astype(bf16), "slc", -s))
        tile_hi += wide(passed(other_hi.astype(bf16), "slc", -s))
    tile_hi += wide(passed(rim_hi, "tile", 1))
    tile_lo += wide(passed(rim_lo.astype(bf16), "tile", 1))
    return jnp.concatenate([tile_lo, tile_hi]).transpose(0, 2, 1, 3)


def solution(mesh):
    placed = (
        P(("grp", "slc"), "tile", None, None),
        P(None, ("grp", "tile", "pos")),
        P(("grp", "tile")),
        P(("grp", "tile", "pos"), None, None),
        P("grp", None),
    )
    return jax.shard_map(
        body,
        mesh=mesh,
        in_specs=placed,
        out_specs=P(("grp", "slc"), "tile", None, "pos"),
        check_vma=False,
    )
```

time: 94.2 us -> 86.3 us (0.916)
  Pallas kernels: 29.4 us -> 24.3 us
  waiting for transfers between devices: 30.7 us -> 35.4 us
  other arithmetic: 7.21 us -> 2.54 us
  starting transfers between devices: 19.3 us -> 15.8 us
    ppermute x16 -> x22, waiting for transfers between devices: 30.7 us -> 35.4 us  [passed(): lax.ppermute(array, axis, [(i, (i + by) % peers) for i in range(peers)])]
    ppermute x16 -> x22, starting transfers between devices: 19.3 us -> 15.8 us  [passed(): lax.ppermute(array, axis, [(i, (i + by) % peers) for i in range(peers)])]
    unnamed x20 -> x18, local copies, waits for them, and re-layouts: 4.4 us -> 1.16 us
    pallas_call x1, Pallas kernels: 21.6 us -> 18.4 us  [body(): pl.pallas_call(functools.partial(main_kernel, groups, depth, mine, pix, t...]
    convert_element_type x1 -> x0, other arithmetic: 2.22 us -> none  [body(): (keep.astype(jnp.float32) + passed(send, 'pos', 1).astype(jnp.float32)).a...]
    pallas_call x1, Pallas kernels: 7.77 us -> 5.95 us  [body(): pl.pallas_call(functools.partial(prep_kernel, mine, pix), out_shape=(jax....]
    transpose x0 -> x1, local copies, waits for them, and re-layouts: none -> 1.78 us  [body(): return jnp.concatenate([tile_lo, tile_hi]).transpose(0, 2, 1, 3)]
    dynamic_slice x1, local copies, waits for them, and re-layouts: 0.04 us -> 1.5 us  [body(): lax.dynamic_slice(object_field, (zero, zero, zero, core * pix), (depth, r...]
  transfers between devices with their start and end apart: 16 -> 22, of which waited for: 8 -> 8; matrix products, arithmetic and copies ran while one was open for 5% -> 7% of each run, Pallas kernels for 8% -> 7%
where the time goes in v2:
time: 86.3 us; the launch traced here: 86.1 us
  waiting for transfers between devices  35.4 us (41%)
  Pallas kernels  24.3 us (28%)
  starting transfers between devices  15.8 us (18%)
  local copies, waits for them, and re-layouts  6.99 us (8%)
  other arithmetic  2.54 us (3%)
  between operations  0.93 us (1%)
    ppermute x22, waiting for transfers between devices, passed(): lax.ppermute(array, axis, [(i, (i + by) % peers) for i in range(peers)])  35.4 us
    pallas_call x1, Pallas kernels, body(): pl.pallas_call(functools.partial(main_kernel, groups, depth, mine, pix, t...  18.4 us
    ppermute x22, starting transfers between devices, passed(): lax.ppermute(array, axis, [(i, (i + by) % peers) for i in range(peers)])  15.8 us
    pallas_call x1, Pallas kernels, body(): pl.pallas_call(functools.partial(prep_kernel, mine, pix), out_shape=(jax....  5.95 us
    transpose x1, local copies, waits for them, and re-layouts, body(): return jnp.concatenate([tile_lo, tile_hi]).transpose(0, 2, 1, 3)  1.78 us
  transfers between devices with their start and end apart: 22, of which 8 were waited for; matrix products, arithmetic and copies ran while one was open for 7% of the time, Pallas kernels for 7%

profile of v2, /device:TPU:0, one launch (start us, length us, event | category | flops | bytes accessed | tf_op | source)
XLA Modules:
  0.0 86.1 jit_solution(11312584563440170338)
XLA Ops:
  0.0 1.5 %constant_dynamic-slice_fusion.1 = bf16[2,256,2,256]{3,2,1,0:T(2,128)(2,1)S(1)} fusion(bf16[2,256,2,512]{3,2,1,0:T(2,128)(2,1)} %param.6, s32[]{:T(128)S(6)} %select_n.36), kind=kLoop, calls=%fused_computation.24 | loop fusion | bytes 1048580 | tf_op jit(solution)/shard_map/dynamic_slice | solution.py:266
  1.6 5.1 %collective-permute-start.4 = (bf16[1,2,256,256]{3,2,1,0:T(8,128)(2,1)S(1)}, bf16[1,2,256,256]{3,2,1,0:T(8,128)(2,1)S(1)}, u32[]{:S(2)}, u32[]{:S(2)}) collective-permute-start(bf16[1,2,256,256]{3,2,1,0:T(8,128)(2,1)S(1)} %get-tuple-element.33), channel_id=1, source_target_pairs={{0,12},{4,0},{8,4},{12,8},{1,13},{5,1},{9,5},{13,9},{2,14},{6,2},{... | collective-permute-start | bytes 786440 | tf_op jit(solution)/shard_map/ppermute | solution.py:18
  6.7 1.5 %collective-permute-start.2 = (bf16[1,2,256,256]{3,2,1,0:T(8,128)(2,1)S(1)}, bf16[1,2,256,256]{3,2,1,0:T(8,128)(2,1)}, u32[]{:S(2)}, u32[]{:S(2)}) collective-permute-start(bf16[1,2,256,256]{3,2,1,0:T(8,128)(2,1)S(1)} %get-tuple-element.33), channel_id=1, source_target_pairs={{0,2},{2,0},{1,3},{3,1},{4,6},{6,4},{5,7},{7,5},{8,10},{10,8},{9,1... | collective-permute-start | bytes 786440 | tf_op jit(solution)/shard_map/ppermute | solution.py:18
  8.7 0.5 collective-permute-start
  10.0 3.5 %collective-permute-done.4.refs_5_ = bf16[1,2,256,256]{3,2,1,0:T(8,128)(2,1)S(1)} collective-permute-done((bf16[1,2,256,256]{3,2,1,0:T(8,128)(2,1)S(1)}, bf16[1,2,256,256]{3,2,1,0:T(8,128)(2,1)S(1)}, u32[]{:S(2)}, u32[]{:S(2)}) %collective-permute-start.4) | collective-permute-done | bytes 262176 | tf_op jit(solution)/shard_map/ppermute | solution.py:18
  13.5 1.5 %collective-permute-start.10 = (bf16[1,2,256,256]{3,2,1,0:T(8,128)(2,1)S(1)}, bf16[1,2,256,256]{3,2,1,0:T(8,128)(2,1)}, u32[]{:S(2)}, u32[]{:S(2)}) collective-permute-start(bf16[1,2,256,256]{3,2,1,0:T(8,128)(2,1)S(1)} %collective-permute-done.4.refs_5_), channel_id=1, source_target_pairs={{0,2},{2,0},{1,3},{3,1},{4,6},{6,4},{5,7},{7,5},{8,10},{10,8},{9,1... | collective-permute-start | bytes 786440 | tf_op jit(solution)/shard_map/ppermute | solution.py:18
  14.9 6.7 %collective-permute-done.refs_1_ = bf16[1,2,256,256]{3,2,1,0:T(8,128)(2,1)} collective-permute-done((bf16[1,2,256,256]{3,2,1,0:T(8,128)(2,1)S(1)}, bf16[1,2,256,256]{3,2,1,0:T(8,128)(2,1)}, u32[]{:S(2)}, u32[]{:S(2)}) %collective-permute-start) | collective-permute-done | bytes 262176 | tf_op jit(solution)/shard_map/ppermute | solution.py:18
  22.3 0.7 pad_add_fusion.1.info
  23.5 2.3 %collective-permute-done.10.refs_11_ = bf16[1,2,256,256]{3,2,1,0:T(8,128)(2,1)} collective-permute-done((bf16[1,2,256,256]{3,2,1,0:T(8,128)(2,1)S(1)}, bf16[1,2,256,256]{3,2,1,0:T(8,128)(2,1)}, u32[]{:S(2)}, u32[]{:S(2)}) %collective-permute-start.10) | collective-permute-done | bytes 262176 | tf_op jit(solution)/shard_map/ppermute | solution.py:18
  26.4 2.0 %collective-permute-done.8.refs_9_ = bf16[1,2,256,256]{3,2,1,0:T(8,128)(2,1)} collective-permute-done((bf16[1,2,256,256]{3,2,1,0:T(8,128)(2,1)}, bf16[1,2,256,256]{3,2,1,0:T(8,128)(2,1)}, u32[]{:S(2)}, u32[]{:S(2)}) %collective-permute-start.8) | collective-permute-done | bytes 262176 | tf_op jit(solution)/shard_map/ppermute | solution.py:18
  28.4 5.9 %tables.1 = (bf16[2,4,256,512]{3,2,1,0:T(8,128)(2,1)}, bf16[2,4,512,256]{3,2,1,0:T(8,128)(2,1)}, bf16[2,2,256,256]{3,2,1,0:T(8,128)(2,1)}) custom-call(s32[10]{0:T(128)} %pad_add_fusion.1.info, bf16[2,6,256,256]{3,2,1,0:T(8,128)(2,1)} %constant.48.clone.base, bf16[256,512]{1,0:T(8,128)(2,1)} %probe.1), custom_call_target="tpu_custom_call" | custom-call | flops 8000000000 | bytes 8388608 | tf_op jit(solution)/shard_map/tables/pallas_call | solution.py:289
  34.3 1.1 %copy.11 = bf16[2,256,2,512]{1,3,2,0:T(8,128)(2,1)S(1)} copy(bf16[2,256,2,512]{3,2,1,0:T(2,128)(2,1)S(1)} %copy-done.1) | data formatting | bytes 2097152 | tf_op args[0]
  35.4 1.3 %copy.12 = bf16[2,256,2,2,256]{4,1,2,0,3:T(8,128)(2,1)} copy(bf16[2,256,2,2,256]{1,4,3,2,0:T(8,128)(2,1)S(1)} %bitcast.25) | data formatting | bytes 2097152 | tf_op jit(solution)/shard_map/reshape | solution.py:284
  36.7 0.9 constant_dynamic-slice_fusion.refs_16_
  37.6 18.4 %waves.1 = (bf16[2,2,256,256]{3,2,1,0:T(8,128)(2,1)}, bf16[2,2,256,256]{3,2,1,0:T(8,128)(2,1)}, bf16[2,2,256,256]{3,2,1,0:T(8,128)(2,1)}, bf16[2,2,256,256]{3,2,...) custom-call(s32[10]{0:T(128)} %pad_add_fusion.1.info, ...), custom_call_target="tpu_custom_call" | custom-call | flops 15000000512 | bytes 16777216 | tf_op jit(solution)/shard_map/waves/pallas_call | solution.py:303
  56.0 0.6 collective-permute-start.13
  57.2 1.2 %collective-permute-done.13 = bf16[2,2,256,256]{3,2,1,0:T(8,128)(2,1)S(1)} collective-permute-done((bf16[2,2,256,256]{3,2,1,0:T(8,128)(2,1)}, bf16[2,2,256,256]{3,2,1,0:T(8,128)(2,1)S(1)}, u32[]{:S(2)}, u32[]{:S(2)}) %collective-permute-start.13) | collective-permute-done | bytes 524320 | tf_op jit(solution)/shard_map/ppermute | solution.py:18
  58.3 1.1 %convert_add_fusion.1 = f32[2,2,256,256]{3,2,1,0:T(8,128)S(1)} fusion(bf16[2,2,256,256]{3,2,1,0:T(8,128)(2,1)S(1)} %collective-permute-done.13, bf16[2,2,256,256]{3,2,1,0:T(8,128)(2,1)} %get-tuple-element.21), kind=kLoop, calls=%fused_computation.3 | loop fusion | flops 786432 | bytes 2097152 | tf_op jit(solution)/shard_map/add | solution.py:330
  59.5 2.1 %collective-permute-start.14 = (bf16[1,2,256,256]{3,2,1,0:T(8,128)(2,1)S(1)}, bf16[1,2,256,256]{3,2,1,0:T(8,128)(2,1)S(1)}, u32[]{:S(2)}, u32[]{:S(2)}) collective-permute-start(bf16[1,2,256,256]{3,2,1,0:T(8,128)(2,1)S(1)} %slice.81), channel_id=1, source_target_pairs={{0,2},{2,0},{1,3},{3,1},{4,6},{6,4},{5,7},{7,5},{8,10},{10,8},{9,1... | collective-permute-start | bytes 786440 | tf_op jit(solution)/shard_map/ppermute | solution.py:18
  62.2 11.9 %collective-permute-done.17 = bf16[1,2,256,256]{3,2,1,0:T(8,128)(2,1)S(1)} collective-permute-done((bf16[1,2,256,256]{3,2,1,0:T(8,128)(2,1)S(1)}, bf16[1,2,256,256]{3,2,1,0:T(8,128)(2,1)S(1)}, u32[]{:S(2)}, u32[]{:S(2)}) %collective-permute-start.17) | collective-permute-done | bytes 262176 | tf_op jit(solution)/shard_map/ppermute | solution.py:18
  74.3 1.8 %collective-permute-start.20 = (bf16[1,2,256,256]{3,2,1,0:T(8,128)(2,1)S(1)}, bf16[1,2,256,256]{3,2,1,0:T(8,128)(2,1)S(1)}, u32[]{:S(2)}, u32[]{:S(2)}) collective-permute-start(bf16[1,2,256,256]{3,2,1,0:T(8,128)(2,1)S(1)} %fusion), channel_id=1, source_target_pairs={{0,2},{2,0},{1,3},{3,1},{4,6},{6,4},{5,7},{7,5},{8,10},{10,8},{9,1... | collective-permute-start | bytes 786440 | tf_op jit(solution)/shard_map/ppermute | solution.py:18
  76.2 1.4 %collective-permute-done.21 = bf16[1,2,256,256]{3,2,1,0:T(8,128)(2,1)S(1)} collective-permute-done((bf16[1,2,256,256]{3,2,1,0:T(8,128)(2,1)S(1)}, bf16[1,2,256,256]{3,2,1,0:T(8,128)(2,1)S(1)}, u32[]{:S(2)}, u32[]{:S(2)}) %collective-permute-start.21) | collective-permute-done | bytes 262176 | tf_op jit(solution)/shard_map/ppermute | solution.py:18
  77.6 6.4 %collective-permute-done.18 = bf16[1,2,256,256]{3,2,1,0:T(8,128)(2,1)S(1)} collective-permute-done((bf16[1,2,256,256]{3,2,1,0:T(8,128)(2,1)S(1)}, bf16[1,2,256,256]{3,2,1,0:T(8,128)(2,1)S(1)}, u32[]{:S(2)}, u32[]{:S(2)}) %collective-permute-start.18) | collective-permute-done | bytes 262176 | tf_op jit(solution)/shard_map/ppermute | solution.py:18
  84.3 1.8 %copy.14 = f32[2,256,2,256]{3,2,1,0:T(2,128)} copy(f32[2,256,2,256]{3,1,2,0:T(8,128)S(1)} %maximum_bitcast_fusion) | data formatting | bytes 2097152 | tf_op jit(solution)/shard_map/transpose | solution.py:343
  (65 shorter events, 4.0 us)
Async XLA Ops:
  0.0 36.7 %copy-start = (f32[4,256,256]{2,1,0:T(8,128)S(1)}, f32[4,256,256]{2,1,0:T(8,128)}, u32[]{:S(2)}) copy-start(f32[4,256,256]{2,1,0:T(8,128)} %param.9) | copy-start | bytes 3145732
  1.6 11.8 %collective-permute-start.4 = (bf16[1,2,256,256]{3,2,1,0:T(8,128)(2,1)S(1)}, bf16[1,2,256,256]{3,2,1,0:T(8,128)(2,1)S(1)}, u32[]{:S(2)}, u32[]{:S(2)}) collective-permute-start(bf16[1,2,256,256]{3,2,1,0:T(8,128)(2,1)S(1)} %get-tuple-element.33), channel_id=1, source_target_pairs={{0,12},{4,0},{8,4},{12,8},{1,13},{5,1},{9,5},{13,9},{2,14},{6,2},{... | collective-permute-start | bytes 786440 | tf_op jit(solution)/shard_map/ppermute | solution.py:18
  6.7 16.3 %collective-permute-start.2 = (bf16[1,2,256,256]{3,2,1,0:T(8,128)(2,1)S(1)}, bf16[1,2,256,256]{3,2,1,0:T(8,128)(2,1)}, u32[]{:S(2)}, u32[]{:S(2)}) collective-permute-start(bf16[1,2,256,256]{3,2,1,0:T(8,128)(2,1)S(1)} %get-tuple-element.33), channel_id=1, source_target_pairs={{0,2},{2,0},{1,3},{3,1},{4,6},{6,4},{5,7},{7,5},{8,10},{10,8},{9,1... | collective-permute-start | bytes 786440 | tf_op jit(solution)/shard_map/ppermute | solution.py:18
  8.2 14.8 %collective-permute-start.6 = (bf16[1,2,256,256]{3,2,1,0:T(8,128)(2,1)S(1)}, bf16[1,2,256,256]{3,2,1,0:T(8,128)(2,1)}, u32[]{:S(2)}, u32[]{:S(2)}) collective-permute-start(bf16[1,2,256,256]{3,2,1,0:T(8,128)(2,1)S(1)} %get-tuple-element.34), channel_id=1, source_target_pairs={{0,12},{4,0},{8,4},{12,8},{1,13},{5,1},{9,5},{13,9},{2,14},{6,2},{... | collective-permute-start | bytes 786440 | tf_op jit(solution)/shard_map/ppermute | solution.py:18
  8.7 13.0 %collective-permute-start = (bf16[1,2,256,256]{3,2,1,0:T(8,128)(2,1)S(1)}, bf16[1,2,256,256]{3,2,1,0:T(8,128)(2,1)}, u32[]{:S(2)}, u32[]{:S(2)}) collective-permute-start(bf16[1,2,256,256]{3,2,1,0:T(8,128)(2,1)S(1)} %get-tuple-element.34), channel_id=1, source_target_pairs={{0,2},{2,0},{1,3},{3,1},{4,6},{6,4},{5,7},{7,5},{8,10},{10,8},{9,1... | collective-permute-start | bytes 786440 | tf_op jit(solution)/shard_map/ppermute | solution.py:18
  13.5 20.9 %copy-start.6 = (bf16[1,2,256,256]{3,2,1,0:T(8,128)(2,1)}, bf16[1,2,256,256]{3,2,1,0:T(8,128)(2,1)S(1)}, u32[]{:S(2)}) copy-start(bf16[1,2,256,256]{3,2,1,0:T(8,128)(2,1)S(1)} %collective-permute-done.4.refs_5_) | copy-start | bytes 786436
  13.5 12.4 %collective-permute-start.10 = (bf16[1,2,256,256]{3,2,1,0:T(8,128)(2,1)S(1)}, bf16[1,2,256,256]{3,2,1,0:T(8,128)(2,1)}, u32[]{:S(2)}, u32[]{:S(2)}) collective-permute-start(bf16[1,2,256,256]{3,2,1,0:T(8,128)(2,1)S(1)} %collective-permute-done.4.refs_5_), channel_id=1, source_target_pairs={{0,2},{2,0},{1,3},{3,1},{4,6},{6,4},{5,7},{7,5},{8,10},{10,8},{9,1... | collective-permute-start | bytes 786440 | tf_op jit(solution)/shard_map/ppermute | solution.py:18
  14.9 10.9 %collective-permute-start.5 = (bf16[1,2,256,256]{3,2,1,0:T(8,128)(2,1)S(1)}, bf16[1,2,256,256]{3,2,1,0:T(8,128)(2,1)S(1)}, u32[]{:S(2)}, u32[]{:S(2)}) collective-permute-start(bf16[1,2,256,256]{3,2,1,0:T(8,128)(2,1)S(1)} %collective-permute-done.4.refs_5_), channel_id=1, source_target_pairs={{0,1},{1,0},{2,3},{3,2},{4,5},{5,4},{6,7},{7,6},{8,9},{9,8},{10,11... | collective-permute-start | bytes 786440 | tf_op jit(solution)/shard_map/ppermute | solution.py:18
  21.7 6.7 %collective-permute-start.8 = (bf16[1,2,256,256]{3,2,1,0:T(8,128)(2,1)}, bf16[1,2,256,256]{3,2,1,0:T(8,128)(2,1)}, u32[]{:S(2)}, u32[]{:S(2)}) collective-permute-start(bf16[1,2,256,256]{3,2,1,0:T(8,128)(2,1)} %collective-permute-done.refs_1_), channel_id=1, source_target_pairs={{0,12},{4,0},{8,4},{12,8},{1,13},{5,1},{9,5},{13,9},{2,14},{6,2},{... | collective-permute-start | bytes 786440 | tf_op jit(solution)/shard_map/ppermute | solution.py:18
  23.0 14.6 %collective-permute-start.1 = (bf16[1,2,256,256]{3,2,1,0:T(8,128)(2,1)}, bf16[1,2,256,256]{3,2,1,0:T(8,128)(2,1)}, u32[]{:S(2)}, u32[]{:S(2)}) collective-permute-start(bf16[1,2,256,256]{3,2,1,0:T(8,128)(2,1)} %collective-permute-done.refs_1_), channel_id=1, source_target_pairs={{0,1},{1,0},{2,3},{3,2},{4,5},{5,4},{6,7},{7,6},{8,9},{9,8},{10,11... | collective-permute-start | bytes 786440 | tf_op jit(solution)/shard_map/ppermute | solution.py:18
  23.0 14.5 %collective-permute-start.3 = (bf16[1,2,256,256]{3,2,1,0:T(8,128)(2,1)}, bf16[1,2,256,256]{3,2,1,0:T(8,128)(2,1)}, u32[]{:S(2)}, u32[]{:S(2)}) collective-permute-start(bf16[1,2,256,256]{3,2,1,0:T(8,128)(2,1)} %collective-permute-done.2.refs_3_), channel_id=1, source_target_pairs={{0,1},{1,0},{2,3},{3,2},{4,5},{5,4},{6,7},{7,6},{8,9},{9,8},{10,11... | collective-permute-start | bytes 786440 | tf_op jit(solution)/shard_map/ppermute | solution.py:18
  25.8 11.7 %collective-permute-start.7 = (bf16[1,2,256,256]{3,2,1,0:T(8,128)(2,1)}, bf16[1,2,256,256]{3,2,1,0:T(8,128)(2,1)}, u32[]{:S(2)}, u32[]{:S(2)}) collective-permute-start(bf16[1,2,256,256]{3,2,1,0:T(8,128)(2,1)} %collective-permute-done.6.refs_7_), channel_id=1, source_target_pairs={{0,1},{1,0},{2,3},{3,2},{4,5},{5,4},{6,7},{7,6},{8,9},{9,8},{10,11... | collective-permute-start | bytes 786440 | tf_op jit(solution)/shard_map/ppermute | solution.py:18
  25.9 11.7 %collective-permute-start.11 = (bf16[1,2,256,256]{3,2,1,0:T(8,128)(2,1)}, bf16[1,2,256,256]{3,2,1,0:T(8,128)(2,1)}, u32[]{:S(2)}, u32[]{:S(2)}) collective-permute-start(bf16[1,2,256,256]{3,2,1,0:T(8,128)(2,1)} %collective-permute-done.10.refs_11_), channel_id=1, source_target_pairs={{0,1},{1,0},{2,3},{3,2},{4,5},{5,4},{6,7},{7,6},{8,9},{9,8},{10,11... | collective-permute-start | bytes 786440 | tf_op jit(solution)/shard_map/ppermute | solution.py:18
  28.4 9.2 %collective-permute-start.9 = (bf16[1,2,256,256]{3,2,1,0:T(8,128)(2,1)}, bf16[1,2,256,256]{3,2,1,0:T(8,128)(2,1)}, u32[]{:S(2)}, u32[]{:S(2)}) collective-permute-start(bf16[1,2,256,256]{3,2,1,0:T(8,128)(2,1)} %collective-permute-done.8.refs_9_), channel_id=1, source_target_pairs={{0,1},{1,0},{2,3},{3,2},{4,5},{5,4},{6,7},{7,6},{8,9},{9,8},{10,11... | collective-permute-start | bytes 786440 | tf_op jit(solution)/shard_map/ppermute | solution.py:18
  56.0 2.3 %collective-permute-start.13 = (bf16[2,2,256,256]{3,2,1,0:T(8,128)(2,1)}, bf16[2,2,256,256]{3,2,1,0:T(8,128)(2,1)S(1)}, u32[]{:S(2)}, u32[]{:S(2)}) collective-permute-start(bf16[2,2,256,256]{3,2,1,0:T(8,128)(2,1)} %get-tuple-element.22), channel_id=1, source_target_pairs={{0,1},{1,0},{2,3},{3,2},{4,5},{5,4},{6,7},{7,6},{8,9},{9,8},{10,11... | collective-permute-start | bytes 1572872 | tf_op jit(solution)/shard_map/ppermute | solution.py:18
  56.6 5.0 %collective-permute-start.16 = (bf16[2,2,256,256]{3,2,1,0:T(8,128)(2,1)}, bf16[2,2,256,256]{3,2,1,0:T(8,128)(2,1)S(1)}, u32[]{:S(2)}, u32[]{:S(2)}) collective-permute-start(bf16[2,2,256,256]{3,2,1,0:T(8,128)(2,1)} %get-tuple-element.26), channel_id=1, source_target_pairs={{0,1},{1,0},{2,3},{3,2},{4,5},{5,4},{6,7},{7,6},{8,9},{9,8},{10,11... | collective-permute-start | bytes 1572872 | tf_op jit(solution)/shard_map/ppermute | solution.py:18
  56.7 19.4 %collective-permute-start.12 = (bf16[2,2,256,256]{3,2,1,0:T(8,128)(2,1)}, bf16[2,2,256,256]{3,2,1,0:T(8,128)(2,1)S(1)}, u32[]{:S(2)}, u32[]{:S(2)}) collective-permute-start(bf16[2,2,256,256]{3,2,1,0:T(8,128)(2,1)} %get-tuple-element.20), channel_id=1, source_target_pairs={{0,1},{1,0},{2,3},{3,2},{4,5},{5,4},{6,7},{7,6},{8,9},{9,8},{10,11... | collective-permute-start | bytes 1572872 | tf_op jit(solution)/shard_map/ppermute | solution.py:18
  57.1 4.8 %collective-permute-start.15 = (bf16[2,2,256,256]{3,2,1,0:T(8,128)(2,1)}, bf16[2,2,256,256]{3,2,1,0:T(8,128)(2,1)S(1)}, u32[]{:S(2)}, u32[]{:S(2)}) collective-permute-start(bf16[2,2,256,256]{3,2,1,0:T(8,128)(2,1)} %get-tuple-element.24), channel_id=1, source_target_pairs={{0,1},{1,0},{2,3},{3,2},{4,5},{5,4},{6,7},{7,6},{8,9},{9,8},{10,11... | collective-permute-start | bytes 1572872 | tf_op jit(solution)/shard_map/ppermute | solution.py:18
  59.5 16.7 %collective-permute-start.14 = (bf16[1,2,256,256]{3,2,1,0:T(8,128)(2,1)S(1)}, bf16[1,2,256,256]{3,2,1,0:T(8,128)(2,1)S(1)}, u32[]{:S(2)}, u32[]{:S(2)}) collective-permute-start(bf16[1,2,256,256]{3,2,1,0:T(8,128)(2,1)S(1)} %slice.81), channel_id=1, source_target_pairs={{0,2},{2,0},{1,3},{3,1},{4,6},{6,4},{5,7},{7,5},{8,10},{10,8},{9,1... | collective-permute-start | bytes 786440 | tf_op jit(solution)/shard_map/ppermute | solution.py:18
  61.8 12.3 %collective-permute-start.17 = (bf16[1,2,256,256]{3,2,1,0:T(8,128)(2,1)S(1)}, bf16[1,2,256,256]{3,2,1,0:T(8,128)(2,1)S(1)}, u32[]{:S(2)}, u32[]{:S(2)}) collective-permute-start(bf16[1,2,256,256]{3,2,1,0:T(8,128)(2,1)S(1)} %get-tuple-element.31), channel_id=1, source_target_pairs={{0,2},{2,0},{1,3},{3,1},{4,6},{6,4},{5,7},{7,5},{8,10},{10,8},{9,1... | collective-permute-start | bytes 786440 | tf_op jit(solution)/shard_map/ppermute | solution.py:18
  61.9 12.3 %collective-permute-start.19 = (bf16[1,2,256,256]{3,2,1,0:T(8,128)(2,1)S(1)}, bf16[1,2,256,256]{3,2,1,0:T(8,128)(2,1)S(1)}, u32[]{:S(2)}, u32[]{:S(2)}) collective-permute-start(bf16[1,2,256,256]{3,2,1,0:T(8,128)(2,1)S(1)} %get-tuple-element.32), channel_id=1, source_target_pairs={{0,4},{4,8},{8,12},{12,0},{1,5},{5,9},{9,13},{13,1},{2,6},{6,10},{... | collective-permute-start | bytes 786440 | tf_op jit(solution)/shard_map/ppermute | solution.py:18
  62.1 15.5 %collective-permute-start.21 = (bf16[1,2,256,256]{3,2,1,0:T(8,128)(2,1)S(1)}, bf16[1,2,256,256]{3,2,1,0:T(8,128)(2,1)S(1)}, u32[]{:S(2)}, u32[]{:S(2)}) collective-permute-start(bf16[1,2,256,256]{3,2,1,0:T(8,128)(2,1)S(1)} %slice.80), channel_id=1, source_target_pairs={{0,4},{4,8},{8,12},{12,0},{1,5},{5,9},{9,13},{13,1},{2,6},{6,10},{... | collective-permute-start | bytes 786440 | tf_op jit(solution)/shard_map/ppermute | solution.py:18
  74.1 9.9 %collective-permute-start.18 = (bf16[1,2,256,256]{3,2,1,0:T(8,128)(2,1)S(1)}, bf16[1,2,256,256]{3,2,1,0:T(8,128)(2,1)S(1)}, u32[]{:S(2)}, u32[]{:S(2)}) collective-permute-start(bf16[1,2,256,256]{3,2,1,0:T(8,128)(2,1)S(1)} %fusion.2), channel_id=1, source_target_pairs={{0,4},{4,8},{8,12},{12,0},{1,5},{5,9},{9,13},{13,1},{2,6},{6,10},{... | collective-permute-start | bytes 786440 | tf_op jit(solution)/shard_map/ppermute | solution.py:18
  74.3 9.8 %collective-permute-start.20 = (bf16[1,2,256,256]{3,2,1,0:T(8,128)(2,1)S(1)}, bf16[1,2,256,256]{3,2,1,0:T(8,128)(2,1)S(1)}, u32[]{:S(2)}, u32[]{:S(2)}) collective-permute-start(bf16[1,2,256,256]{3,2,1,0:T(8,128)(2,1)S(1)} %fusion), channel_id=1, source_target_pairs={{0,2},{2,0},{1,3},{3,1},{4,6},{6,4},{5,7},{7,5},{8,10},{10,8},{9,1... | collective-permute-start | bytes 786440 | tf_op jit(solution)/shard_map/ppermute | solution.py:18
  (6 other events, 45.3 us)

commit v3 on v2

--- a/solution.py
+++ b/solution.py
@@ -16,6 +16,18 @@
 def passed(array, axis, by):
     peers = lax.axis_size(axis)
     return lax.ppermute(array, axis, [(i, (i + by) % peers) for i in range(peers)])
+
+
+def split_roles(array, tile_by, slc_by, slc_core, with_tile=True):
+    tiles, groups, cores = (lax.axis_size(name) for name in ("tile", "slc", "pos"))
+    at = lambda t, g, c: ((t % tiles) * groups + g % groups) * cores + c
+    pairs = []
+    for t in range(tiles):
+        for g in range(groups):
+            pairs.append((at(t, g, slc_core), at(t, g + slc_by, slc_core)))
+            if with_tile:
+                pairs.append((at(t, g, 1 - slc_core), at(t + tile_by, g, 1 - slc_core)))
+    return lax.ppermute(array, ("tile", "slc", "pos"), pairs)
 
 
 def base_tables(pix):
@@ -64,13 +76,15 @@
             psi0[m, part] = plane.astype(bf16)
 
 
-def main_kernel(groups, depth, mine, pix, pieces, info, *refs):
+def main_kernel(groups, depth, mine, pix, pieces, results, info, *refs):
     count = len(pieces) + 1
     own, operands = refs[0], refs[1:count]
     lefts_any, rights_any, psi0_any, light_any = refs[count : count + 4]
-    outs = refs[count + 4 : count + 4 + 4 * groups]
-    obj, tp, psi, lefts, rights, light, grads, sems, tab_sems, out_sems = refs[count + 4 + 4 * groups :]
+    outs = refs[count + 4 : count + 4 + len(results)]
+    own_out = refs[count + 4 + len(results)]
+    obj, tp, psi, lefts, rights, light, grads, sems, tab_sems, out_sems = refs[count + 5 + len(results) :]
     layers = groups * depth
+    half = depth // 2
     rank = info[0]
     core = info[1]
     members = range(mine)
@@ -90,28 +104,32 @@
             copy.wait()
 
     psi_copy = pltpu.make_async_copy(psi0_any, psi.at[0], tab_sems.at[4, 0])
-    light_copy = pltpu.make_async_copy(light_any, light, tab_sems.at[4, 1])
+    light_copy = pltpu.make_async_copy(light_any.at[pl.ds(rank * mine, mine)], light, tab_sems.at[4, 1])
     psi_copy.start()
     for copy in table_copies(1) + table_copies(3):
         copy.start()
     for i in range(depth):
         j = layer_of(0, i)
-        for col in range(2):
-            pltpu.make_async_copy(own.at[col, i], obj.at[j, 0, col], sems.at[j, col]).start()
-    for (s, start, below, away), ref in zip(pieces, operands):
-        for i in range(ref.shape[0]):
-            j = layer_of(s, start + i)
-            col = (1 - core) if away else core
-            at = 2 * below + col
-            pltpu.make_async_copy(ref.at[i], obj.at[j, below, col], sems.at[j, at]).start()
+        pltpu.make_async_copy(own.at[i], obj.at[j, 0], sems.at[j, 0]).start()
+    for holds, ref in zip(pieces, operands):
+        for c in range(2):
+            if holds[c] is None:
+                continue
+            s, high, below = holds[c]
+
+            @pl.when(core == c)
+            def _():
+                for i in range(half):
+                    j = layer_of(s, high * half + i)
+                    pltpu.make_async_copy(ref.at[i], obj.at[j, below], sems.at[j, below]).start()
+
     light_copy.start()
     for copy in table_copies(0) + table_copies(2):
         copy.start()
 
     def wait_object(j):
         for below in range(2):
-            for col in range(2):
-                pltpu.make_async_copy(own.at[0, 0], obj.at[j, below, col], sems.at[j, 2 * below + col]).wait()
+            pltpu.make_async_copy(own.at[0], obj.at[j, below], sems.at[j, below]).wait()
 
     row_at = lax.broadcasted_iota(jnp.int32, (pix, pix), 0)
     col_at = lax.broadcasted_iota(jnp.int32, (pix, pix), 1)
@@ -124,8 +142,10 @@
 
     def patch(j, m, part):
         right = col_at >= c0[m]
-        here = jnp.where(right, obj[j, 0, q[m], part].astype(f32), obj[j, 0, 1 - q[m], part].astype(f32))
-        there = jnp.where(right, obj[j, 1, q[m], part].astype(f32), obj[j, 1, 1 - q[m], part].astype(f32))
+        at = pl.ds(pl.multiple_of(q[m] * pix, pix), pix)
+        after = pl.ds(pl.multiple_of((1 - q[m]) * pix, pix), pix)
+        here = jnp.where(right, obj[j, 0, part, :, at].astype(f32), obj[j, 0, part, :, after].astype(f32))
+        there = jnp.where(right, obj[j, 1, part, :, at].astype(f32), obj[j, 1, part, :, after].astype(f32))
         return jnp.where(row_at >= r0[m], here, there).astype(bf16)
 
     def left(m, t, re, im):
@@ -180,10 +200,26 @@
         tilted.append((excess * re, excess * im))
     exits = both(3, tilted)
 
-    def out_copy(away, below, s, i):
-        place = s * depth + i
-        out = outs[(away * 2 + below) * groups + s]
-        return pltpu.make_async_copy(grads.at[away, below, place], out.at[i], out_sems.at[away, below, place])
+    def out_copy(below, place, out):
+        return pltpu.make_async_copy(grads.at[below, place], out, out_sems.at[below, place])
+
+    def send_out(step, within):
+        place = step * depth + within
+
+        @pl.when(step == 0)
+        def _():
+            out_copy(0, place, own_out.at[within]).start()
+
+        for takes, ref in zip(results, outs):
+            for c in range(2):
+                if takes[c] is None:
+                    continue
+                s, high, below = takes[c]
+                inside = (within >= half) if high else (within < half)
+
+                @pl.when((core == c) & (step == s) & inside)
+                def _():
+                    out_copy(below, place, ref.at[within - high * half]).start()
 
     def scatter(j, exits):
         step = lax.rem(rank - j // depth + groups, groups)
@@ -194,26 +230,18 @@
             pr, pi = psi[j, m, 0].astype(f32), psi[j, m, 1].astype(f32)
             terms.append((pr * re + pi * im, pr * im - pi * re))
         for below in range(2):
-            for away in range(2):
-                target = (1 - core) if away else core
+            for col in range(2):
                 for part in range(2):
                     total = None
                     for m in members:
                         rows = (row_at < r0[m]) if below else (row_at >= r0[m])
-                        same = target == q[m]
-                        low = jnp.where(same, c0[m], 0)
-                        high = jnp.where(same, pix, c0[m])
+                        low = jnp.where(q[m] == col, c0[m], 0)
+                        high = jnp.where(q[m] == col, pix, c0[m])
                         mask = rows & (col_at >= low) & (col_at < high)
                         term = jnp.where(mask, terms[m][part], 0.0)
                         total = term if total is None else total + term
-                    grads[away, below, place, part] = total.astype(bf16)
-        for s in range(groups):
-
-            @pl.when(step == s)
-            def _():
-                for below in range(2):
-                    for away in range(2):
-                        out_copy(away, below, s, within).start()
+                    grads[below, place, part, :, col * pix : (col + 1) * pix] = total.astype(bf16)
+        send_out(step, within)
 
     def wave_grads(j, exits):
         pairs = []
@@ -235,11 +263,9 @@
 
     hold = lax.fori_loop(0, layers - 1, backward, hold)
     scatter(0, [(hold[2 * m], hold[2 * m + 1]) for m in members])
-    for away in range(2):
-        for below in range(2):
-            for s in range(groups):
-                for i in range(depth):
-                    out_copy(away, below, s, i).wait()
+    for below in range(2):
+        for place in range(layers):
+            out_copy(below, place, own_out.at[0]).wait()
 
 
 def body(object_field, offsets, counts, measured, probe_wave):
@@ -260,28 +286,14 @@
     alive = (in_tile < counts[0]).astype(jnp.int32)
     places = jnp.stack([off[0] - tile * rows, off[1] // pix, off[1] % pix, alive], axis=1)
     info = jnp.concatenate([jnp.stack([rank, core]), places.reshape(-1)])
-    light = lax.dynamic_slice(measured, (first, jnp.int32(0), jnp.int32(0)), (mine, pix, pix))
-
-    zero = jnp.int32(0)
-    part = lax.dynamic_slice(object_field, (zero, zero, zero, core * pix), (depth, rows, 2, pix))
-    part = part.transpose(0, 2, 1, 3)
+
+    planes = object_field.transpose(0, 2, 1, 3)
     half = depth // 2
-    lo, hi = part[:half], part[half:]
-
     steps = range(1, groups)
-    here = {(s, 0): passed(lo, "slc", s) for s in steps}
-    nown_hi = passed(hi, "tile", -1)
-    here |= {(s, half): passed(hi, "slc", s) for s in steps}
-    nown_lo = passed(lo, "tile", -1)
-    below = {(0, half): nown_hi, (0, 0): nown_lo}
-    below |= {(s, 0): passed(here[s, 0], "tile", -1) for s in steps}
-    below |= {(s, half): passed(nown_hi, "slc", s) for s in steps}
-    pieces, operands = [], []
-    for row_block, found in ((0, here), (1, below)):
-        for (s, start), array in found.items():
-            pieces += [(s, start, row_block, 0), (s, start, row_block, 1)]
-            operands += [array, passed(array, "pos", 1)]
-    blocks = object_field.reshape(depth, rows, 2, 2, pix).transpose(3, 0, 2, 1, 4)
+    halves_of = lambda high: lax.dynamic_slice_in_dim(planes, high * half, half, axis=0)
+    first_half, last_half = halves_of(core), halves_of(1 - core)
+    got_first = [split_roles(first_half, -1, s, 0, s == 1) for s in steps]
+    got_last = [split_roles(last_half, -1, s, 0, s == 1) for s in steps]
 
     smem = pl.BlockSpec(memory_space=pltpu.SMEM)
     vmem = pl.BlockSpec(memory_space=pltpu.VMEM)
@@ -300,47 +312,67 @@
         name="tables",
     )(info, jnp.asarray(base_tables(pix)), probe_wave)
 
-    outs = pl.pallas_call(
-        functools.partial(main_kernel, groups, depth, mine, pix, tuple(pieces)),
-        out_shape=(jax.ShapeDtypeStruct((depth, 2, pix, pix), bf16),) * (4 * groups),
+    got_first, lefts, rights, psi0 = lax.optimization_barrier((got_first, lefts, rights, psi0))
+    passed_on = [split_roles(got_first[s - 1], -1, s, 1) for s in steps]
+    pieces, operands = [], []
+    for s in steps:
+        rim_hi, rim_lo = ((0, 1, 1), (0, 0, 1)) if s == 1 else (None, None)
+        for array, holds in (
+            (got_first[s - 1], ((s, 0, 0), rim_hi)),
+            (got_last[s - 1], ((s, 1, 0), rim_lo)),
+            (passed_on[s - 1], ((s, 0, 1), (s, 1, 1))),
+        ):
+            pieces += [holds, holds[::-1]]
+            operands += [array, passed(array, "pos", 1)]
+    results = []
+    for s in steps:
+        rim_hi, rim_lo = ((0, 1, 1), (0, 0, 1)) if s == 1 else (None, None)
+        for holds in (((s, 1, 1), (s, 0, 1)), ((s, 0, 0), rim_hi), ((s, 1, 0), rim_lo)):
+            results += [holds, holds[::-1]]
+
+    half_shape = jax.ShapeDtypeStruct((half, 2, rows, cols), bf16)
+    *outs, own_grads = pl.pallas_call(
+        functools.partial(main_kernel, groups, depth, mine, pix, tuple(pieces), tuple(results)),
+        out_shape=(half_shape,) * len(results) + (jax.ShapeDtypeStruct((depth, 2, rows, cols), bf16),),
         in_specs=[smem] + [anywhere] * (5 + len(operands)),
-        out_specs=(anywhere,) * (4 * groups),
+        out_specs=(anywhere,) * (len(results) + 1),
         scratch_shapes=[
-            pltpu.VMEM((layers, 2, 2, 2, pix, pix), bf16),
+            pltpu.VMEM((layers, 2, 2, pix, cols), bf16),
             pltpu.VMEM((layers, mine, 2, pix, pix), bf16),
             pltpu.VMEM((layers, mine, 2, pix, pix), bf16),
             pltpu.VMEM((mine, 4, pix, 2 * pix), bf16),
             pltpu.VMEM((mine, 4, 2 * pix, pix), bf16),
             pltpu.VMEM((mine, pix, pix), jnp.float32),
-            pltpu.VMEM((2, 2, layers, 2, pix, pix), bf16),
-            pltpu.SemaphoreType.DMA((layers, 4)),
+            pltpu.VMEM((2, layers, 2, pix, cols), bf16),
+            pltpu.SemaphoreType.DMA((layers, 2)),
             pltpu.SemaphoreType.DMA((5, 2)),
-            pltpu.SemaphoreType.DMA((2, 2, layers)),
+            pltpu.SemaphoreType.DMA((2, layers)),
         ],
         compiler_params=pltpu.CompilerParams(vmem_limit_bytes=VMEM_LIMIT),
         cost_estimate=pl.CostEstimate(flops=15 * 10**9, bytes_accessed=16 * 2**20, transcendentals=0),
         name="waves",
-    )(info, blocks, *operands, lefts, rights, psi0, light)
+    )(info, planes, *operands, lefts, rights, psi0, measured)
 
     wide = lambda v: v.astype(jnp.float32)
-    sums = {}
-    for s in [*steps, 0]:
-        for row_block in (1, 0):
-            at = row_block * groups + s
-            sums[row_block, s] = wide(outs[at]) + wide(passed(outs[2 * groups + at], "pos", 1))
-    rim_lo = sums[1, 0][:half]
-    rim_hi = sums[1, 0][half:].astype(bf16)
-    tile_lo = sums[0, 0][:half]
-    tile_hi = sums[0, 0][half:]
-    for s in steps:
-        rim, tile_part = sums[1, s], sums[0, s]
-        rim_lo += wide(passed(rim[:half].astype(bf16), "slc", -s))
-        other_hi = tile_part[half:] + wide(passed(rim[half:].astype(bf16), "tile", 1))
-        tile_lo += wide(passed(tile_part[:half].astype(bf16), "slc", -s))
-        tile_hi += wide(passed(other_hi.astype(bf16), "slc", -s))
-    tile_hi += wide(passed(rim_hi, "tile", 1))
-    tile_lo += wide(passed(rim_lo.astype(bf16), "tile", 1))
-    return jnp.concatenate([tile_lo, tile_hi]).transpose(0, 2, 1, 3)
+    kept = lambda s, which: wide(outs[6 * (s - 1) + 2 * which])
+    twin = lambda s, which: wide(passed(outs[6 * (s - 1) + 2 * which + 1], "pos", 1))
+    rims = {s: (kept(s, 0) + twin(s, 0)).astype(bf16) for s in steps}
+    firsts = {s: (kept(s, 1) + twin(s, 1)).astype(bf16) for s in steps}
+    lasts = {s: kept(s, 2) + twin(s, 2) for s in steps}
+    back = {s: split_roles(rims[s], 1, -s, 1) for s in steps}
+    come_first = sum(wide(split_roles(firsts[s], 1, -s, 0, s == 1)) for s in steps)
+    summed = sum(wide(back[s]) for s in steps)
+    lasts = {s: (lasts[s] + (jnp.where(core == 1, summed, wide(back[s])))).astype(bf16) for s in steps}
+    come_last = sum(wide(split_roles(lasts[s], 1, -s, 0, s == 1)) for s in steps)
+    on_first = jnp.where(core == 0, 1.0, 0.0)
+    own_sum = wide(own_grads) + jnp.concatenate([come_first * on_first, come_first * (1.0 - on_first)])
+    mine_of = lambda v: lax.dynamic_slice_in_dim(v, core * pix, pix, axis=3)
+    twins_of = lambda v: lax.dynamic_slice_in_dim(v, (1 - core) * pix, pix, axis=3)
+    early = mine_of(own_sum) + wide(passed(twins_of(own_sum).astype(bf16), "pos", 1))
+    here = mine_of(come_last)
+    away = wide(passed(twins_of(come_last).astype(bf16), "pos", 1))
+    late = jnp.concatenate([jnp.where(core == 0, away, here), jnp.where(core == 0, here, away)])
+    return (early + late).transpose(0, 2, 1, 3)
 
 
 def solution(mesh):

time: 86.3 us -> 79.8 us (0.925)
  waiting for transfers between devices: 35.4 us -> 27.2 us
  other arithmetic: 2.54 us -> 5.41 us
  local copies, waits for them, and re-layouts: 6.99 us -> 6 us
    ppermute x22 -> x8, waiting for transfers between devices: 35.4 us -> 5.17 us  [passed(): lax.ppermute(array, axis, [(i, (i + by) % peers) for i in range(peers)])]
    ppermute x0 -> x6, waiting for transfers between devices: none -> 22.1 us  [split_roles(): return lax.ppermute(array, ('tile', 'slc', 'pos'), pairs)]
    ppermute x22 -> x8, starting transfers between devices: 15.8 us -> 0.95 us  [passed(): lax.ppermute(array, axis, [(i, (i + by) % peers) for i in range(peers)])]
    ppermute x0 -> x6, starting transfers between devices: none -> 14.8 us  [split_roles(): return lax.ppermute(array, ('tile', 'slc', 'pos'), pairs)]
    convert_element_type x2 -> x4, other arithmetic: 0.12 us -> 2.69 us  [the longest x1 1.18 us: body(): firsts = {s: (kept(s, 1) + twin(s, 1)).astype(bf16) for s in steps}]
    dynamic_slice x2 -> x1, local copies, waits for them, and re-layouts: 2.36 us -> 0.08 us  [body(): lax.dynamic_slice_in_dim(planes, high * half, half, axis=0)]
    convert_element_type x0 -> x2, local copies, waits for them, and re-layouts: none -> 1.63 us  [the longest x1 0.87 us: body(): twins_of(own_sum).astype(bf16)]
    reshape x1 -> x0, local copies, waits for them, and re-layouts: 1.31 us -> none  [body(): object_field.reshape(depth, rows, 2, 2, pix).transpose(3, 0, 2, 1, 4)]
  transfers between devices with their start and end apart: 22 -> 14, of which waited for: 8 -> 7; matrix products, arithmetic and copies ran while one was open for 7% -> 8% of each run, Pallas kernels for 7% -> 7%
where the time goes in v3:
time: 79.8 us; the launch traced here: 79.4 us
  waiting for transfers between devices  27.2 us (34%)
  Pallas kernels  24.2 us (30%)
  starting transfers between devices  15.7 us (20%)
  local copies, waits for them, and re-layouts  6 us (8%)
  other arithmetic  5.41 us (7%)
  between operations  0.86 us (1%)
    ppermute x6, waiting for transfers between devices, split_roles(): return lax.ppermute(array, ('tile', 'slc', 'pos'), pairs)  22.1 us
    pallas_call x1, Pallas kernels, body(): pl.pallas_call(functools.partial(main_kernel, groups, depth, mine, pix, t...  18.3 us
    ppermute x6, starting transfers between devices, split_roles(): return lax.ppermute(array, ('tile', 'slc', 'pos'), pairs)  14.8 us
    pallas_call x1, Pallas kernels, body(): pl.pallas_call(functools.partial(prep_kernel, mine, pix), out_shape=(jax....  5.95 us
    ppermute x8, waiting for transfers between devices, passed(): lax.ppermute(array, axis, [(i, (i + by) % peers) for i in range(peers)])  5.17 us
    unnamed x21, local copies, waits for them, and re-layouts  2.27 us
    transpose x1, local copies, waits for them, and re-layouts, body(): return (early + late).transpose(0, 2, 1, 3)  1.78 us
  transfers between devices with their start and end apart: 14, of which 7 were waited for; matrix products, arithmetic and copies ran while one was open for 8% of the time, Pallas kernels for 7%

profile of v3, /device:TPU:0, one launch (start us, length us, event | category | flops | bytes accessed | tf_op | source)
XLA Modules:
  0.0 79.4 jit_solution(16655096471553315969)
XLA Ops:
  0.0 1.4 %copy.14 = bf16[2,256,2,512]{3,1,2,0:T(8,128)(2,1)S(1)} copy(bf16[2,256,2,512]{3,2,1,0:T(2,128)(2,1)} %param.6) | data formatting | bytes 2097152 | tf_op args[0]
  1.5 3.0 %collective-permute-start = (bf16[1,2,256,512]{3,2,1,0:T(8,128)(2,1)S(1)}, bf16[1,2,256,512]{3,2,1,0:T(8,128)(2,1)S(1)}, u32[]{:S(2)}, u32[]{:S(2)}) collective-permute-start(bf16[1,2,256,512]{3,2,1,0:T(8,128)(2,1)S(1)} %get-tuple-element.38), channel_id=1, source_target_pairs={{0,2},{1,13},{2,0},{3,15},{4,6},{5,1},{6,4},{7,3},{8,10},{9,5},{10... | collective-permute-start | bytes 1572872 | tf_op jit(solution)/shard_map/ppermute | solution.py:30
  5.5 0.7 pad_add_fusion.1.info
  6.2 5.9 %tables.1 = (bf16[2,4,256,512]{3,2,1,0:T(8,128)(2,1)}, bf16[2,4,512,256]{3,2,1,0:T(8,128)(2,1)}, bf16[2,2,256,256]{3,2,1,0:T(8,128)(2,1)}) custom-call(s32[10]{0:T(128)} %pad_add_fusion.1.info, bf16[2,6,256,256]{3,2,1,0:T(8,128)(2,1)} %constant.55.clone.base, bf16[256,512]{1,0:T(8,128)(2,1)} %probe.1), custom_call_target="tpu_custom_call" | custom-call | flops 8000000000 | bytes 8388608 | tf_op jit(solution)/shard_map/tables/pallas_call | solution.py:301
  12.2 4.1 %collective-permute-start.4 = (bf16[1,2,256,512]{3,2,1,0:T(8,128)(2,1)S(1)}, bf16[1,2,256,512]{3,2,1,0:T(8,128)(2,1)S(1)}, u32[]{:S(2)}, u32[]{:S(2)}) collective-permute-start(bf16[1,2,256,512]{3,2,1,0:T(8,128)(2,1)S(1)} %collective-permute-done.refs_1_), channel_id=1, source_target_pairs={{1,3},{0,12},{3,1},{2,14},{5,7},{4,0},{7,5},{6,2},{9,11},{8,4},{11... | collective-permute-start | bytes 1572872 | tf_op jit(solution)/shard_map/ppermute | solution.py:30
  16.3 1.7 %collective-permute-done.2.refs_3_ = bf16[1,2,256,512]{3,2,1,0:T(8,128)(2,1)S(1)} collective-permute-done((bf16[1,2,256,512]{3,2,1,0:T(8,128)(2,1)S(1)}, bf16[1,2,256,512]{3,2,1,0:T(8,128)(2,1)S(1)}, u32[]{:S(2)}, u32[]{:S(2)}) %collective-permute-start.2) | collective-permute-done | bytes 524320 | tf_op jit(solution)/shard_map/ppermute | solution.py:30
  18.3 5.1 %collective-permute-done.4.refs_5_ = bf16[1,2,256,512]{3,2,1,0:T(8,128)(2,1)S(1)} collective-permute-done((bf16[1,2,256,512]{3,2,1,0:T(8,128)(2,1)S(1)}, bf16[1,2,256,512]{3,2,1,0:T(8,128)(2,1)S(1)}, u32[]{:S(2)}, u32[]{:S(2)}) %collective-permute-start.4) | collective-permute-done | bytes 524320 | tf_op jit(solution)/shard_map/ppermute | solution.py:30
  23.4 1.9 %collective-permute-done.5.refs_6_ = bf16[1,2,256,512]{3,2,1,0:T(8,128)(2,1)S(1)} collective-permute-done((bf16[1,2,256,512]{3,2,1,0:T(8,128)(2,1)S(1)}, bf16[1,2,256,512]{3,2,1,0:T(8,128)(2,1)S(1)}, u32[]{:S(2)}, u32[]{:S(2)}) %collective-permute-start.5) | collective-permute-done | bytes 524320 | tf_op jit(solution)/shard_map/ppermute | solution.py:18
  25.4 0.8 %copy-done.9 = bf16[1,2,256,512]{3,2,1,0:T(8,128)(2,1)} copy-done((bf16[1,2,256,512]{3,2,1,0:T(8,128)(2,1)}, bf16[1,2,256,512]{3,2,1,0:T(8,128)(2,1)S(1)}, u32[]{:S(2)}) %copy-start.9) | copy-done | bytes 524312
  26.2 18.3 %waves.1 = (bf16[1,2,256,512]{3,2,1,0:T(8,128)(2,1)}, bf16[1,2,256,512]{3,2,1,0:T(8,128)(2,1)}, bf16[1,2,256,512]{3,2,1,0:T(8,128)(2,1)}, bf16[1,2,256,512]{3,2,...) custom-call(s32[10]{0:T(128)} %pad_add_fusion.1.info, ...), custom_call_target="tpu_custom_call" | custom-call | flops 15000000512 | bytes 16777216 | tf_op jit(solution)/shard_map/waves/pallas_call | solution.py:334
  44.5 0.5 collective-permute-start.6
  45.1 1.5 %collective-permute-done.10 = bf16[1,2,256,512]{3,2,1,0:T(8,128)(2,1)S(1)} collective-permute-done((bf16[1,2,256,512]{3,2,1,0:T(8,128)(2,1)}, bf16[1,2,256,512]{3,2,1,0:T(8,128)(2,1)S(1)}, u32[]{:S(2)}, u32[]{:S(2)}) %collective-permute-start.10) | collective-permute-done | bytes 524320 | tf_op jit(solution)/shard_map/ppermute | solution.py:18
  46.6 1.2 %add_convert_fusion.1 = bf16[1,2,256,512]{3,2,1,0:T(8,128)(2,1)S(1)} fusion(bf16[1,2,256,512]{3,2,1,0:T(8,128)(2,1)S(1)} %collective-permute-done.10, bf16[1,2,256,512]{3,2,1,0:T(8,128)(2,1)} %get-tuple-element.31), kind=kLoop, calls=%fused_computation.6 | loop fusion | flops 1048576 | bytes 1572864 | tf_op jit(solution)/shard_map/convert_element_type | solution.py:359
  47.8 1.1 %collective-permute-start.11 = (bf16[1,2,256,512]{3,2,1,0:T(8,128)(2,1)S(1)}, bf16[1,2,256,512]{3,2,1,0:T(8,128)(2,1)S(1)}, u32[]{:S(2)}, u32[]{:S(2)}) collective-permute-start(bf16[1,2,256,512]{3,2,1,0:T(8,128)(2,1)S(1)} %add_convert_fusion.1), channel_id=1, source_target_pairs={{1,3},{0,4},{3,1},{2,6},{5,7},{4,8},{7,5},{6,10},{9,11},{8,12},{11... | collective-permute-start | bytes 1572872 | tf_op jit(solution)/shard_map/ppermute | solution.py:30
  48.9 1.2 %add_convert_fusion.2 = bf16[1,2,256,512]{3,2,1,0:T(8,128)(2,1)S(1)} fusion(bf16[1,2,256,512]{3,2,1,0:T(8,128)(2,1)S(1)} %collective-permute-done.6, bf16[1,2,256,512]{3,2,1,0:T(8,128)(2,1)} %get-tuple-element.27), kind=kLoop, calls=%fused_computation.8 | loop fusion | flops 1048576 | bytes 1572864 | tf_op jit(solution)/shard_map/convert_element_type | solution.py:360
  50.1 2.4 %collective-permute-start.7 = (bf16[1,2,256,512]{3,2,1,0:T(8,128)(2,1)S(1)}, bf16[1,2,256,512]{3,2,1,0:T(8,128)(2,1)S(1)}, u32[]{:S(2)}, u32[]{:S(2)}) collective-permute-start(bf16[1,2,256,512]{3,2,1,0:T(8,128)(2,1)S(1)} %add_convert_fusion.2), channel_id=1, source_target_pairs={{0,2},{1,5},{2,0},{3,7},{4,6},{5,9},{6,4},{7,11},{8,10},{9,13},{10... | collective-permute-start | bytes 1572872 | tf_op jit(solution)/shard_map/ppermute | solution.py:30
  52.6 9.6 %collective-permute-done.11 = bf16[1,2,256,512]{3,2,1,0:T(8,128)(2,1)S(1)} collective-permute-done((bf16[1,2,256,512]{3,2,1,0:T(8,128)(2,1)S(1)}, bf16[1,2,256,512]{3,2,1,0:T(8,128)(2,1)S(1)}, u32[]{:S(2)}, u32[]{:S(2)}) %collective-permute-start.11) | collective-permute-done | bytes 524320 | tf_op jit(solution)/shard_map/ppermute | solution.py:30
  62.4 4.1 %collective-permute-start.12 = (bf16[1,2,256,512]{3,2,1,0:T(8,128)(2,1)S(1)}, bf16[1,2,256,512]{3,2,1,0:T(8,128)(2,1)S(1)}, u32[]{:S(2)}, u32[]{:S(2)}) collective-permute-start(bf16[1,2,256,512]{3,2,1,0:T(8,128)(2,1)S(1)} %add_convert_fusion), channel_id=1, source_target_pairs={{0,2},{1,5},{2,0},{3,7},{4,6},{5,9},{6,4},{7,11},{8,10},{9,13},{10... | collective-permute-start | bytes 1572872 | tf_op jit(solution)/shard_map/ppermute | solution.py:30
  67.0 0.9 %dynamic-slice_convert_fusion = bf16[2,2,256,256]{3,2,1,0:T(8,128)(2,1)} fusion(f32[2,2,256,512]{3,2,1,0:T(8,128)S(1)} %maximum_add_fusion, s32[]{:T(128)S(6)} %select_n.70), kind=kLoop, calls=%fused_computation.7 | loop fusion | bytes 1048580 | tf_op jit(solution)/shard_map/convert_element_type | solution.py:371
  67.9 5.7 %collective-permute-done.12 = bf16[1,2,256,512]{3,2,1,0:T(8,128)(2,1)S(1)} collective-permute-done((bf16[1,2,256,512]{3,2,1,0:T(8,128)(2,1)S(1)}, bf16[1,2,256,512]{3,2,1,0:T(8,128)(2,1)S(1)}, u32[]{:S(2)}, u32[]{:S(2)}) %collective-permute-start.12) | collective-permute-done | bytes 524320 | tf_op jit(solution)/shard_map/ppermute | solution.py:30
  73.7 0.8 dynamic-slice_convert_fusion.1
  74.5 1.7 %collective-permute-done.13 = bf16[1,2,256,256]{3,2,1,0:T(8,128)(2,1)S(1)} collective-permute-done((bf16[1,2,256,256]{3,2,1,0:T(8,128)(2,1)}, bf16[1,2,256,256]{3,2,1,0:T(8,128)(2,1)S(1)}, u32[]{:S(2)}, u32[]{:S(2)}) %collective-permute-start.13) | collective-permute-done | bytes 262176 | tf_op jit(solution)/shard_map/ppermute | solution.py:18
  76.3 1.3 %fusion = f32[2,256,2,256]{3,1,2,0:T(8,128)S(1)} fusion(f32[1,2,256,256]{3,2,1,0:T(8,128)S(1)} %get-tuple-element.36, f32[1,2,256,256]{3,2,1,0:T(8,128)S(1)} %get-tuple-element.35, bf16[2,2,256,256]{3,2,1,0:T(8,128)(2,1)} %collective-permute-done.8, f32[2,2,256,512]{3,2,1,0:T(8,128)S(1)} %maximum_add_fusion, s32[]{:T(128)S(6)} %select_n.69), kind=kLoop, calls=%fused_computation.4 | loop fusion | flops 1048576 | bytes 3670020 | tf_op jit(solution)/shard_map/transpose | solution.py:375
  77.7 1.8 %copy.11 = f32[2,256,2,256]{3,2,1,0:T(2,128)} copy(f32[2,256,2,256]{3,1,2,0:T(8,128)S(1)} %fusion) | data formatting | bytes 2097152 | tf_op jit(solution)/shard_map/transpose | solution.py:375
  (48 shorter events, 2.0 us)
Async XLA Ops:
  0.0 4.6 %copy-start = (s32[2,4]{1,0:T(2,128)S(1)}, s32[2,4]{1,0:T(2,128)}, u32[]{:S(2)}) copy-start(s32[2,4]{1,0:T(2,128)} %param.7) | copy-start | bytes 100
  1.4 10.7 %copy-start.1 = (bf16[2,256,2,512]{3,1,2,0:T(8,128)(2,1)}, bf16[2,256,2,512]{3,1,2,0:T(8,128)(2,1)S(1)}, u32[]{:S(2)}) copy-start(bf16[2,256,2,512]{3,1,2,0:T(8,128)(2,1)S(1)} %copy.14) | copy-start | bytes 3145732
  1.5 10.6 %collective-permute-start = (bf16[1,2,256,512]{3,2,1,0:T(8,128)(2,1)S(1)}, bf16[1,2,256,512]{3,2,1,0:T(8,128)(2,1)S(1)}, u32[]{:S(2)}, u32[]{:S(2)}) collective-permute-start(bf16[1,2,256,512]{3,2,1,0:T(8,128)(2,1)S(1)} %get-tuple-element.38), channel_id=1, source_target_pairs={{0,2},{1,13},{2,0},{3,15},{4,6},{5,1},{6,4},{7,3},{8,10},{9,5},{10... | collective-permute-start | bytes 1572872 | tf_op jit(solution)/shard_map/ppermute | solution.py:30
  4.5 13.5 %collective-permute-start.2 = (bf16[1,2,256,512]{3,2,1,0:T(8,128)(2,1)S(1)}, bf16[1,2,256,512]{3,2,1,0:T(8,128)(2,1)S(1)}, u32[]{:S(2)}, u32[]{:S(2)}) collective-permute-start(bf16[1,2,256,512]{3,2,1,0:T(8,128)(2,1)S(1)} %get-tuple-element.37), channel_id=1, source_target_pairs={{0,2},{1,13},{2,0},{3,15},{4,6},{5,1},{6,4},{7,3},{8,10},{9,5},{10... | collective-permute-start | bytes 1572872 | tf_op jit(solution)/shard_map/ppermute | solution.py:30
  12.1 13.2 %copy-start.4 = (bf16[1,2,256,512]{3,2,1,0:T(8,128)(2,1)}, bf16[1,2,256,512]{3,2,1,0:T(8,128)(2,1)S(1)}, u32[]{:S(2)}) copy-start(bf16[1,2,256,512]{3,2,1,0:T(8,128)(2,1)S(1)} %collective-permute-done.refs_1_) | copy-start | bytes 1572868
  12.2 11.3 %collective-permute-start.4 = (bf16[1,2,256,512]{3,2,1,0:T(8,128)(2,1)S(1)}, bf16[1,2,256,512]{3,2,1,0:T(8,128)(2,1)S(1)}, u32[]{:S(2)}, u32[]{:S(2)}) collective-permute-start(bf16[1,2,256,512]{3,2,1,0:T(8,128)(2,1)S(1)} %collective-permute-done.refs_1_), channel_id=1, source_target_pairs={{1,3},{0,12},{3,1},{2,14},{5,7},{4,0},{7,5},{6,2},{9,11},{8,4},{11... | collective-permute-start | bytes 1572872 | tf_op jit(solution)/shard_map/ppermute | solution.py:30
  16.3 7.1 %collective-permute-start.1 = (bf16[1,2,256,512]{3,2,1,0:T(8,128)(2,1)S(1)}, bf16[1,2,256,512]{3,2,1,0:T(8,128)(2,1)S(1)}, u32[]{:S(2)}, u32[]{:S(2)}) collective-permute-start(bf16[1,2,256,512]{3,2,1,0:T(8,128)(2,1)S(1)} %collective-permute-done.refs_1_), channel_id=1, source_target_pairs={{0,1},{1,0},{2,3},{3,2},{4,5},{5,4},{6,7},{7,6},{8,9},{9,8},{10,11... | collective-permute-start | bytes 1572872 | tf_op jit(solution)/shard_map/ppermute | solution.py:18
  18.0 7.3 %copy-start.5 = (bf16[1,2,256,512]{3,2,1,0:T(8,128)(2,1)}, bf16[1,2,256,512]{3,2,1,0:T(8,128)(2,1)S(1)}, u32[]{:S(2)}) copy-start(bf16[1,2,256,512]{3,2,1,0:T(8,128)(2,1)S(1)} %collective-permute-done.2.refs_3_) | copy-start | bytes 1572868
  18.0 5.4 %collective-permute-start.3 = (bf16[1,2,256,512]{3,2,1,0:T(8,128)(2,1)S(1)}, bf16[1,2,256,512]{3,2,1,0:T(8,128)(2,1)S(1)}, u32[]{:S(2)}, u32[]{:S(2)}) collective-permute-start(bf16[1,2,256,512]{3,2,1,0:T(8,128)(2,1)S(1)} %collective-permute-done.2.refs_3_), channel_id=1, source_target_pairs={{0,1},{1,0},{2,3},{3,2},{4,5},{5,4},{6,7},{7,6},{8,9},{9,8},{10,11... | collective-permute-start | bytes 1572872 | tf_op jit(solution)/shard_map/ppermute | solution.py:18
  23.4 1.9 %copy-start.6 = (bf16[1,2,256,512]{3,2,1,0:T(8,128)(2,1)}, bf16[1,2,256,512]{3,2,1,0:T(8,128)(2,1)S(1)}, u32[]{:S(2)}) copy-start(bf16[1,2,256,512]{3,2,1,0:T(8,128)(2,1)S(1)} %collective-permute-done.4.refs_5_) | copy-start | bytes 1572868
  23.4 1.9 %collective-permute-start.5 = (bf16[1,2,256,512]{3,2,1,0:T(8,128)(2,1)S(1)}, bf16[1,2,256,512]{3,2,1,0:T(8,128)(2,1)S(1)}, u32[]{:S(2)}, u32[]{:S(2)}) collective-permute-start(bf16[1,2,256,512]{3,2,1,0:T(8,128)(2,1)S(1)} %collective-permute-done.4.refs_5_), channel_id=1, source_target_pairs={{0,1},{1,0},{2,3},{3,2},{4,5},{5,4},{6,7},{7,6},{8,9},{9,8},{10,11... | collective-permute-start | bytes 1572872 | tf_op jit(solution)/shard_map/ppermute | solution.py:18
  23.4 1.9 %copy-start.7 = (bf16[1,2,256,512]{3,2,1,0:T(8,128)(2,1)}, bf16[1,2,256,512]{3,2,1,0:T(8,128)(2,1)S(1)}, u32[]{:S(2)}) copy-start(bf16[1,2,256,512]{3,2,1,0:T(8,128)(2,1)S(1)} %collective-permute-done.1.refs_2_) | copy-start | bytes 1572868
  23.4 1.9 %copy-start.8 = (bf16[1,2,256,512]{3,2,1,0:T(8,128)(2,1)}, bf16[1,2,256,512]{3,2,1,0:T(8,128)(2,1)S(1)}, u32[]{:S(2)}) copy-start(bf16[1,2,256,512]{3,2,1,0:T(8,128)(2,1)S(1)} %collective-permute-done.3.refs_4_) | copy-start | bytes 1572868
  25.3 0.9 %copy-start.9 = (bf16[1,2,256,512]{3,2,1,0:T(8,128)(2,1)}, bf16[1,2,256,512]{3,2,1,0:T(8,128)(2,1)S(1)}, u32[]{:S(2)}) copy-start(bf16[1,2,256,512]{3,2,1,0:T(8,128)(2,1)S(1)} %collective-permute-done.5.refs_6_) | copy-start | bytes 1572868
  44.5 17.7 %copy-start.3 = (bf16[1,2,256,512]{3,2,1,0:T(8,128)(2,1)S(1)}, bf16[1,2,256,512]{3,2,1,0:T(8,128)(2,1)}, u32[]{:S(2)}) copy-start(bf16[1,2,256,512]{3,2,1,0:T(8,128)(2,1)} %get-tuple-element.29) | copy-start | bytes 1572868
  44.5 2.2 %collective-permute-start.10 = (bf16[1,2,256,512]{3,2,1,0:T(8,128)(2,1)}, bf16[1,2,256,512]{3,2,1,0:T(8,128)(2,1)S(1)}, u32[]{:S(2)}, u32[]{:S(2)}) collective-permute-start(bf16[1,2,256,512]{3,2,1,0:T(8,128)(2,1)} %get-tuple-element.32), channel_id=1, source_target_pairs={{0,1},{1,0},{2,3},{3,2},{4,5},{5,4},{6,7},{7,6},{8,9},{9,8},{10,11... | collective-permute-start | bytes 1572872 | tf_op jit(solution)/shard_map/ppermute | solution.py:18
  44.5 4.4 %collective-permute-start.6 = (bf16[1,2,256,512]{3,2,1,0:T(8,128)(2,1)}, bf16[1,2,256,512]{3,2,1,0:T(8,128)(2,1)S(1)}, u32[]{:S(2)}, u32[]{:S(2)}) collective-permute-start(bf16[1,2,256,512]{3,2,1,0:T(8,128)(2,1)} %get-tuple-element.28), channel_id=1, source_target_pairs={{0,1},{1,0},{2,3},{3,2},{4,5},{5,4},{6,7},{7,6},{8,9},{9,8},{10,11... | collective-permute-start | bytes 1572872 | tf_op jit(solution)/shard_map/ppermute | solution.py:18
  45.0 7.5 %collective-permute-start.9 = (bf16[1,2,256,512]{3,2,1,0:T(8,128)(2,1)}, bf16[1,2,256,512]{3,2,1,0:T(8,128)(2,1)S(1)}, u32[]{:S(2)}, u32[]{:S(2)}) collective-permute-start(bf16[1,2,256,512]{3,2,1,0:T(8,128)(2,1)} %get-tuple-element.30), channel_id=1, source_target_pairs={{0,1},{1,0},{2,3},{3,2},{4,5},{5,4},{6,7},{7,6},{8,9},{9,8},{10,11... | collective-permute-start | bytes 1572872 | tf_op jit(solution)/shard_map/ppermute | solution.py:18
  47.8 14.3 %collective-permute-start.11 = (bf16[1,2,256,512]{3,2,1,0:T(8,128)(2,1)S(1)}, bf16[1,2,256,512]{3,2,1,0:T(8,128)(2,1)S(1)}, u32[]{:S(2)}, u32[]{:S(2)}) collective-permute-start(bf16[1,2,256,512]{3,2,1,0:T(8,128)(2,1)S(1)} %add_convert_fusion.1), channel_id=1, source_target_pairs={{1,3},{0,4},{3,1},{2,6},{5,7},{4,8},{7,5},{6,10},{9,11},{8,12},{11... | collective-permute-start | bytes 1572872 | tf_op jit(solution)/shard_map/ppermute | solution.py:30
  50.1 16.3 %collective-permute-start.7 = (bf16[1,2,256,512]{3,2,1,0:T(8,128)(2,1)S(1)}, bf16[1,2,256,512]{3,2,1,0:T(8,128)(2,1)S(1)}, u32[]{:S(2)}, u32[]{:S(2)}) collective-permute-start(bf16[1,2,256,512]{3,2,1,0:T(8,128)(2,1)S(1)} %add_convert_fusion.2), channel_id=1, source_target_pairs={{0,2},{1,5},{2,0},{3,7},{4,6},{5,9},{6,4},{7,11},{8,10},{9,13},{10... | collective-permute-start | bytes 1572872 | tf_op jit(solution)/shard_map/ppermute | solution.py:30
  62.1 4.5 %copy-start.2 = (bf16[2,2,256,512]{3,2,1,0:T(8,128)(2,1)S(1)}, bf16[2,2,256,512]{3,2,1,0:T(8,128)(2,1)}, u32[]{:S(2)}) copy-start(bf16[2,2,256,512]{3,2,1,0:T(8,128)(2,1)} %get-tuple-element.26) | copy-start | bytes 3145732
  62.4 11.2 %collective-permute-start.12 = (bf16[1,2,256,512]{3,2,1,0:T(8,128)(2,1)S(1)}, bf16[1,2,256,512]{3,2,1,0:T(8,128)(2,1)S(1)}, u32[]{:S(2)}, u32[]{:S(2)}) collective-permute-start(bf16[1,2,256,512]{3,2,1,0:T(8,128)(2,1)S(1)} %add_convert_fusion), channel_id=1, source_target_pairs={{0,2},{1,5},{2,0},{3,7},{4,6},{5,9},{6,4},{7,11},{8,10},{9,13},{10... | collective-permute-start | bytes 1572872 | tf_op jit(solution)/shard_map/ppermute | solution.py:30
  67.9 8.4 %collective-permute-start.8 = (bf16[2,2,256,256]{3,2,1,0:T(8,128)(2,1)}, bf16[2,2,256,256]{3,2,1,0:T(8,128)(2,1)}, u32[]{:S(2)}, u32[]{:S(2)}) collective-permute-start(bf16[2,2,256,256]{3,2,1,0:T(8,128)(2,1)} %dynamic-slice_convert_fusion), channel_id=1, source_target_pairs={{0,1},{1,0},{2,3},{3,2},{4,5},{5,4},{6,7},{7,6},{8,9},{9,8},{10,11... | collective-permute-start | bytes 1572872 | tf_op jit(solution)/shard_map/ppermute | solution.py:18
  74.5 1.7 %collective-permute-start.13 = (bf16[1,2,256,256]{3,2,1,0:T(8,128)(2,1)}, bf16[1,2,256,256]{3,2,1,0:T(8,128)(2,1)S(1)}, u32[]{:S(2)}, u32[]{:S(2)}) collective-permute-start(bf16[1,2,256,256]{3,2,1,0:T(8,128)(2,1)} %dynamic-slice_convert_fusion.1), channel_id=1, source_target_pairs={{0,1},{1,0},{2,3},{3,2},{4,5},{5,4},{6,7},{7,6},{8,9},{9,8},{10,11... | collective-permute-start | bytes 786440 | tf_op jit(solution)/shard_map/ppermute | solution.py:18

commit v4 on v3

--- a/solution.py
+++ b/solution.py
@@ -41,39 +41,65 @@
     h = np.exp(-0.4j * math.pi / pix * (freq * freq))
     planes = []
     for factor in (np.ones_like(h), h, np.conj(h)):
-        b = factor[:, None] * w
+        b = (factor[:, None] * w)[np.concatenate([index[::2], index[1::2]])]
         planes += [b.real, b.imag]
     stack = np.stack(planes)
     return rounded(np.stack([stack, stack.transpose(0, 2, 1)]))
 
 
-def prep_kernel(mine, pix, info, base, probe, lefts, rights, psi0):
-    bf16 = jnp.bfloat16
+def prep_kernel(mine, pix, info, base, probe, measured, lefts, rights, psi0, light):
+    bf16, f32 = jnp.bfloat16, jnp.float32
+    mid = pix // 2
+
+    def rolled(side, f, shift, axis):
+        found = []
+        for part in range(2):
+            whole = pltpu.roll(base[side, 2 * f + part].astype(f32), shift, axis)
+            found.append(whole[:, :mid] if axis else whole[:mid])
+        return found
+
+    def put(ref, m, t, re, im, by_rows, from_left):
+        for odd in range(2):
+            at = slice(odd * mid, (odd + 1) * mid)
+            re_part, im_part = (re[at], im[at]) if by_rows else (re[:, at], im[:, at])
+            upper, lower = (-im_part, im_part) if from_left else (im_part, -im_part)
+            ref[m, t, odd, :mid, :mid] = re_part.astype(bf16)
+            ref[m, t, odd, :mid, mid:] = upper.astype(bf16)
+            ref[m, t, odd, mid:, :mid] = lower.astype(bf16)
+            ref[m, t, odd, mid:, mid:] = re_part.astype(bf16)
+
+    row_at = lax.broadcasted_iota(jnp.int32, (pix, pix), 0)
+    col_at = lax.broadcasted_iota(jnp.int32, (pix, pix), 1)
+    order = lambda at: jnp.where(at < mid, 2 * at, 2 * at - (pix - 1))
+    pick_rows = (col_at == order(row_at)).astype(f32).astype(bf16)
+    pick_cols = (row_at == order(col_at)).astype(f32).astype(bf16)
+
+    def exact(values, product):
+        total = None
+        for _ in range(3):
+            term = values.astype(bf16)
+            values = values - term.astype(f32)
+            moved = product(term)
+            total = moved if total is None else total + moved
+        return total
+
     for m in range(mine):
         r0 = info[2 + 4 * m]
         c0 = info[4 + 4 * m]
-
-        def rolled(side, f, shift, axis):
-            re = pltpu.roll(base[side, 2 * f].astype(jnp.float32), shift, axis)
-            im = pltpu.roll(base[side, 2 * f + 1].astype(jnp.float32), shift, axis)
-            return re.astype(bf16), im.astype(bf16)
-
-        def inverse(side, shift, axis):
-            re = pltpu.roll(base[side, 0].astype(jnp.float32), shift, axis)
-            im = pltpu.roll(base[side, 1].astype(jnp.float32), shift, axis)
-            return re.astype(bf16), (-im).astype(bf16)
-
-        for t in range(4):
-            re, im = rolled(0, t, r0, 1) if t < 3 else inverse(1, r0, 0)
-            lefts[m, t, :, :pix] = re
-            lefts[m, t, :, pix:] = im
-            re, im = rolled(1, t, c0, 0) if t < 3 else inverse(0, c0, 1)
-            rights[m, t, :pix, :] = re
-            rights[m, t, pix:, :] = im
+        for t in range(3):
+            put(lefts, m, t, *rolled(0, t, r0, 1), True, True)
+            put(rights, m, t, *rolled(1, t, c0, 0), False, False)
+        re, im = rolled(1, 0, r0, 0)
+        put(lefts, m, 3, re, -im, False, True)
+        re, im = rolled(0, 0, c0, 1)
+        put(rights, m, 3, re, -im, True, False)
         for part in range(2):
-            plane = probe[:, part * pix : (part + 1) * pix].astype(jnp.float32)
+            plane = probe[:, part * pix : (part + 1) * pix].astype(f32)
             plane = pltpu.roll(pltpu.roll(plane, r0, 0), c0, 1)
             psi0[m, part] = plane.astype(bf16)
+        seen = measured[info[0] * mine + m]
+        seen = exact(seen, lambda v: jnp.dot(pick_rows, v, preferred_element_type=f32))
+        light[m] = exact(seen, lambda v: jnp.dot(v, pick_cols, preferred_element_type=f32))
 
 
 def main_kernel(groups, depth, mine, pix, pieces, results, info, *refs):
@@ -104,7 +130,7 @@
             copy.wait()
 
     psi_copy = pltpu.make_async_copy(psi0_any, psi.at[0], tab_sems.at[4, 0])
-    light_copy = pltpu.make_async_copy(light_any.at[pl.ds(rank * mine, mine)], light, tab_sems.at[4, 1])
+    light_copy = pltpu.make_async_copy(light_any, light, tab_sems.at[4, 1])
     psi_copy.start()
     for copy in table_copies(1) + table_copies(3):
         copy.start()
@@ -148,23 +174,45 @@
         there = jnp.where(right, obj[j, 1, part, :, at].astype(f32), obj[j, 1, part, :, after].astype(f32))
         return jnp.where(row_at >= r0[m], here, there).astype(bf16)
 
-    def left(m, t, re, im):
-        paired = jnp.concatenate(
-            [jnp.concatenate([re, im], axis=1), jnp.concatenate([-im, re], axis=1)], axis=0
-        )
-        out = jnp.dot(lefts[m, t], paired, preferred_element_type=f32)
-        return out[:, :pix].astype(bf16), out[:, pix:].astype(bf16)
-
-    def right(m, t, re, im):
-        paired = jnp.concatenate(
-            [jnp.concatenate([re, -im], axis=1), jnp.concatenate([im, re], axis=1)], axis=0
-        )
-        out = jnp.dot(paired, rights[m, t], preferred_element_type=f32)
-        return out[:pix], out[pix:]
-
-    def both(t, pairs):
-        halfway = [left(m, t, re.astype(bf16), im.astype(bf16)) for m, (re, im) in zip(members, pairs)]
-        return [right(m, t, re, im) for m, (re, im) in zip(members, halfway)]
+    mid = pix // 2
+    cat = lambda parts, axis: jnp.concatenate(parts, axis=axis)
+
+    def product(a, b):
+        return jnp.dot(a, b, preferred_element_type=f32)
+
+    def spectrum_of(t, pairs):
+        halfway = []
+        for m, (re, im) in zip(members, pairs):
+            plus = cat([re[:mid] + re[mid:], im[:mid] + im[mid:]], 0).astype(bf16)
+            minus = cat([re[:mid] - re[mid:], im[:mid] - im[mid:]], 0).astype(bf16)
+            halfway.append((product(lefts[m, t, 0], plus), product(lefts[m, t, 1], minus)))
+        found = []
+        for m, groups_of_rows in zip(members, halfway):
+            plus = cat([cat([g[:mid, :mid] + g[:mid, mid:], g[mid:, :mid] + g[mid:, mid:]], 1) for g in groups_of_rows], 0)
+            minus = cat([cat([g[:mid, :mid] - g[:mid, mid:], g[mid:, :mid] - g[mid:, mid:]], 1) for g in groups_of_rows], 0)
+            found.append((product(plus.astype(bf16), rights[m, t, 0]), product(minus.astype(bf16), rights[m, t, 1])))
+        return found
+
+    def wave_of(spectra):
+        halfway = []
+        for m, (even, odd) in zip(members, spectra):
+            even, odd = even.astype(bf16), odd.astype(bf16)
+            terms = []
+            for half_at in range(2):
+                at = slice(half_at * mid, (half_at + 1) * mid)
+                stacked = cat([cat([even[at, :mid], odd[at, :mid]], 1), cat([even[at, mid:], odd[at, mid:]], 1)], 0)
+                terms.append(product(lefts[m, 3, half_at], stacked))
+            halfway.append(((terms[0] + terms[1]).astype(bf16), (terms[0] - terms[1]).astype(bf16)))
+        found = []
+        for m, blocks in zip(members, halfway):
+            terms = []
+            for half_at in range(2):
+                at = slice(half_at * mid, (half_at + 1) * mid)
+                rows = cat([cat([b[:mid, at], b[mid:, at]], 1) for b in blocks], 0)
+                terms.append(product(rows, rights[m, 3, half_at]))
+            near, far = terms[0] + terms[1], terms[0] - terms[1]
+            found.append((cat([near[:, :mid], far[:, :mid]], 1), cat([near[:, mid:], far[:, mid:]], 1)))
+        return found
 
     def entrance(j):
         pairs = []
@@ -183,8 +231,8 @@
 
     def forward(j, carry):
         wait_object(j)
-        spectra = both(1, entrance(j))
-        for m, (re, im) in enumerate(both(3, spectra)):
+        spectra = spectrum_of(1, entrance(j))
+        for m, (re, im) in enumerate(wave_of(spectra)):
             psi[j + 1, m, 0] = re.astype(bf16)
             psi[j + 1, m, 1] = im.astype(bf16)
         return carry
@@ -193,12 +241,16 @@
     wait_object(layers - 1)
     wait_tables(0)
     light_copy.wait()
-    spectra = both(0, entrance(layers - 1))
+    spectra = spectrum_of(0, entrance(layers - 1))
     tilted = []
-    for m, (re, im) in enumerate(spectra):
-        excess = (re * re + im * im - light[m]) * live[m]
-        tilted.append((excess * re, excess * im))
-    exits = both(3, tilted)
+    for m, parts in enumerate(spectra):
+        scaled = []
+        for odd, values in enumerate(parts):
+            re, im = values[:, :mid], values[:, mid:]
+            excess = (re * re + im * im - light[m, :, odd * mid : (odd + 1) * mid]) * live[m]
+            scaled.append(cat([excess * re, excess * im], 1))
+        tilted.append(tuple(scaled))
+    exits = wave_of(tilted)
 
     def out_copy(below, place, out):
         return pltpu.make_async_copy(grads.at[below, place], out, out_sems.at[below, place])
@@ -257,8 +309,7 @@
         j = layers - 1 - step
         exits = [(flat[2 * m], flat[2 * m + 1]) for m in members]
         scatter(j, exits)
-        tilted = both(2, wave_grads(j, exits))
-        exits = both(3, tilted)
+        exits = wave_of(spectrum_of(2, wave_grads(j, exits)))
         return tuple(part for pair in exits for part in pair)
 
     hold = lax.fori_loop(0, layers - 1, backward, hold)
@@ -298,21 +349,25 @@
     smem = pl.BlockSpec(memory_space=pltpu.SMEM)
     vmem = pl.BlockSpec(memory_space=pltpu.VMEM)
     anywhere = pl.BlockSpec(memory_space=pl.ANY)
-    lefts, rights, psi0 = pl.pallas_call(
+    tables_shape = jax.ShapeDtypeStruct((mine, 4, 2, pix, pix), bf16)
+    lefts, rights, psi0, light = pl.pallas_call(
         functools.partial(prep_kernel, mine, pix),
         out_shape=(
-            jax.ShapeDtypeStruct((mine, 4, pix, 2 * pix), bf16),
-            jax.ShapeDtypeStruct((mine, 4, 2 * pix, pix), bf16),
+            tables_shape,
+            tables_shape,
             jax.ShapeDtypeStruct((mine, 2, pix, pix), bf16),
+            jax.ShapeDtypeStruct((mine, pix, pix), jnp.float32),
         ),
-        in_specs=[smem, vmem, vmem],
-        out_specs=(vmem, vmem, vmem),
+        in_specs=[smem, vmem, vmem, vmem],
+        out_specs=(vmem,) * 4,
         compiler_params=pltpu.CompilerParams(vmem_limit_bytes=VMEM_LIMIT),
         cost_estimate=pl.CostEstimate(flops=8 * 10**9, bytes_accessed=8 * 2**20, transcendentals=0),
         name="tables",
-    )(info, jnp.asarray(base_tables(pix)), probe_wave)
-
-    got_first, lefts, rights, psi0 = lax.optimization_barrier((got_first, lefts, rights, psi0))
+    )(info, jnp.asarray(base_tables(pix)), probe_wave, measured)
+
+    got_first, lefts, rights, psi0, light = lax.optimization_barrier(
+        (got_first, lefts, rights, psi0, light)
+    )
     passed_on = [split_roles(got_first[s - 1], -1, s, 1) for s in steps]
     pieces, operands = [], []
     for s in steps:
@@ -340,8 +395,8 @@
             pltpu.VMEM((layers, 2, 2, pix, cols), bf16),
             pltpu.VMEM((layers, mine, 2, pix, pix), bf16),
             pltpu.VMEM((layers, mine, 2, pix, pix), bf16),
-            pltpu.VMEM((mine, 4, pix, 2 * pix), bf16),
-            pltpu.VMEM((mine, 4, 2 * pix, pix), bf16),
+            pltpu.VMEM((mine, 4, 2, pix, pix), bf16),
+            pltpu.VMEM((mine, 4, 2, pix, pix), bf16),
             pltpu.VMEM((mine, pix, pix), jnp.float32),
             pltpu.VMEM((2, layers, 2, pix, cols), bf16),
             pltpu.SemaphoreType.DMA((layers, 2)),
@@ -351,7 +406,7 @@
         compiler_params=pltpu.CompilerParams(vmem_limit_bytes=VMEM_LIMIT),
         cost_estimate=pl.CostEstimate(flops=15 * 10**9, bytes_accessed=16 * 2**20, transcendentals=0),
         name="waves",
-    )(info, planes, *operands, lefts, rights, psi0, measured)
+    )(info, planes, *operands, lefts, rights, psi0, light)
 
     wide = lambda v: v.astype(jnp.float32)
     kept = lambda s, which: wide(outs[6 * (s - 1) + 2 * which])

time: 79.8 us -> 77.6 us (0.972)
  Pallas kernels: 24.2 us -> 22.5 us
    pallas_call x1, Pallas kernels: 18.3 us -> 15.7 us  [body(): pl.pallas_call(functools.partial(main_kernel, groups, depth, mine, pix, t...]
    pallas_call x1, Pallas kernels: 5.95 us -> 6.82 us  [body(): pl.pallas_call(functools.partial(prep_kernel, mine, pix), out_shape=(tabl...]
  transfers between devices with their start and end apart: 14 -> 14, of which waited for: 7 -> 7; matrix products, arithmetic and copies ran while one was open for 8% -> 8% of each run, Pallas kernels for 7% -> 9%
where the time goes in v4:
time: 77.6 us; the launch traced here: 77.3 us
  waiting for transfers between devices  26.8 us (35%)
  Pallas kernels  22.5 us (29%)
  starting transfers between devices  15.7 us (20%)
  local copies, waits for them, and re-layouts  6 us (8%)
  other arithmetic  5.4 us (7%)
  between operations  0.86 us (1%)
    ppermute x6, waiting for transfers between devices, split_roles(): return lax.ppermute(array, ('tile', 'slc', 'pos'), pairs)  21.7 us
    pallas_call x1, Pallas kernels, body(): pl.pallas_call(functools.partial(main_kernel, groups, depth, mine, pix, t...  15.7 us
    ppermute x6, starting transfers between devices, split_roles(): return lax.ppermute(array, ('tile', 'slc', 'pos'), pairs)  14.4 us
    pallas_call x1, Pallas kernels, body(): pl.pallas_call(functools.partial(prep_kernel, mine, pix), out_shape=(tabl...  6.82 us
    ppermute x8, waiting for transfers between devices, passed(): lax.ppermute(array, axis, [(i, (i + by) % peers) for i in range(peers)])  5.17 us
    unnamed x21, local copies, waits for them, and re-layouts  2.27 us
    transpose x1, local copies, waits for them, and re-layouts, body(): return (early + late).transpose(0, 2, 1, 3)  1.78 us
  transfers between devices with their start and end apart: 14, of which 7 were waited for; matrix products, arithmetic and copies ran while one was open for 8% of the time, Pallas kernels for 9%

profile of v4, /device:TPU:0, one launch (start us, length us, event | category | flops | bytes accessed | tf_op | source)
XLA Modules:
  0.0 77.3 jit_solution(7794099452872436711)
XLA Ops:
  0.0 1.4 %copy.14 = bf16[2,256,2,512]{3,1,2,0:T(8,128)(2,1)S(1)} copy(bf16[2,256,2,512]{3,2,1,0:T(2,128)(2,1)} %param.6) | data formatting | bytes 2097152 | tf_op args[0]
  1.5 3.0 %collective-permute-start = (bf16[1,2,256,512]{3,2,1,0:T(8,128)(2,1)S(1)}, bf16[1,2,256,512]{3,2,1,0:T(8,128)(2,1)S(1)}, u32[]{:S(2)}, u32[]{:S(2)}) collective-permute-start(bf16[1,2,256,512]{3,2,1,0:T(8,128)(2,1)S(1)} %get-tuple-element.42), channel_id=1, source_target_pairs={{0,2},{1,13},{2,0},{3,15},{4,6},{5,1},{6,4},{7,3},{8,10},{9,5},{10... | collective-permute-start | bytes 1572872 | tf_op jit(solution)/shard_map/ppermute | solution.py:30
  5.5 0.6 pad_add_fusion.1.info
  6.2 6.8 %tables.1 = (bf16[2,4,2,256,256]{4,3,2,1,0:T(8,128)(2,1)}, bf16[2,4,2,256,256]{4,3,2,1,0:T(8,128)(2,1)}, bf16[2,2,256,256]{3,2,1,0:T(8,128)(2,1)}, f32[2,256,256]{2,1,0:T(8,128)}) custom-call(s32[10]{0:T(128)} %pad_add_fusion.1.info, bf16[2,6,256,256]{3,2,1,0:T(8,128)(2,1)} %constant.55.clone.base, bf16[256,512]{1,0:T(8,128)(2,1)} %probe.1, ...), custom_call_target="tpu_custom_call" | custom-call | flops 8000000000 | bytes 8388608 | tf_op jit(solution)/shard_map/tables/pallas_call | solution.py:353
  13.0 4.1 %collective-permute-start.4 = (bf16[1,2,256,512]{3,2,1,0:T(8,128)(2,1)S(1)}, bf16[1,2,256,512]{3,2,1,0:T(8,128)(2,1)S(1)}, u32[]{:S(2)}, u32[]{:S(2)}) collective-permute-start(bf16[1,2,256,512]{3,2,1,0:T(8,128)(2,1)S(1)} %collective-permute-done.refs_1_), channel_id=1, source_target_pairs={{1,3},{0,12},{3,1},{2,14},{5,7},{4,0},{7,5},{6,2},{9,11},{8,4},{11... | collective-permute-start | bytes 1572872 | tf_op jit(solution)/shard_map/ppermute | solution.py:30
  17.3 0.6 collective-permute-start.3
  17.9 5.9 %collective-permute-done.4.refs_5_ = bf16[1,2,256,512]{3,2,1,0:T(8,128)(2,1)S(1)} collective-permute-done((bf16[1,2,256,512]{3,2,1,0:T(8,128)(2,1)S(1)}, bf16[1,2,256,512]{3,2,1,0:T(8,128)(2,1)S(1)}, u32[]{:S(2)}, u32[]{:S(2)}) %collective-permute-start.4) | collective-permute-done | bytes 524320 | tf_op jit(solution)/shard_map/ppermute | solution.py:30
  23.9 1.9 %collective-permute-done.5.refs_6_ = bf16[1,2,256,512]{3,2,1,0:T(8,128)(2,1)S(1)} collective-permute-done((bf16[1,2,256,512]{3,2,1,0:T(8,128)(2,1)S(1)}, bf16[1,2,256,512]{3,2,1,0:T(8,128)(2,1)S(1)}, u32[]{:S(2)}, u32[]{:S(2)}) %collective-permute-start.5) | collective-permute-done | bytes 524320 | tf_op jit(solution)/shard_map/ppermute | solution.py:18
  25.8 0.8 %copy-done.9 = bf16[1,2,256,512]{3,2,1,0:T(8,128)(2,1)} copy-done((bf16[1,2,256,512]{3,2,1,0:T(8,128)(2,1)}, bf16[1,2,256,512]{3,2,1,0:T(8,128)(2,1)S(1)}, u32[]{:S(2)}) %copy-start.9) | copy-done | bytes 524312
  26.6 15.7 %waves.1 = (bf16[1,2,256,512]{3,2,1,0:T(8,128)(2,1)}, bf16[1,2,256,512]{3,2,1,0:T(8,128)(2,1)}, bf16[1,2,256,512]{3,2,1,0:T(8,128)(2,1)}, bf16[1,2,256,512]{3,2,...) custom-call(s32[10]{0:T(128)} %pad_add_fusion.1.info, ...), custom_call_target="tpu_custom_call" | custom-call | flops 15000000512 | bytes 16777216 | tf_op jit(solution)/shard_map/waves/pallas_call | solution.py:389
  42.4 0.5 collective-permute-start.6
  42.9 1.5 %collective-permute-done.10 = bf16[1,2,256,512]{3,2,1,0:T(8,128)(2,1)S(1)} collective-permute-done((bf16[1,2,256,512]{3,2,1,0:T(8,128)(2,1)}, bf16[1,2,256,512]{3,2,1,0:T(8,128)(2,1)S(1)}, u32[]{:S(2)}, u32[]{:S(2)}) %collective-permute-start.10) | collective-permute-done | bytes 524320 | tf_op jit(solution)/shard_map/ppermute | solution.py:18
  44.5 1.2 %add_convert_fusion.1 = bf16[1,2,256,512]{3,2,1,0:T(8,128)(2,1)S(1)} fusion(bf16[1,2,256,512]{3,2,1,0:T(8,128)(2,1)S(1)} %collective-permute-done.10, bf16[1,2,256,512]{3,2,1,0:T(8,128)(2,1)} %get-tuple-element.35), kind=kLoop, calls=%fused_computation.6 | loop fusion | flops 1048576 | bytes 1572864 | tf_op jit(solution)/shard_map/convert_element_type | solution.py:414
  45.7 0.7 collective-permute-start.11
  46.3 1.2 %add_convert_fusion.2 = bf16[1,2,256,512]{3,2,1,0:T(8,128)(2,1)S(1)} fusion(bf16[1,2,256,512]{3,2,1,0:T(8,128)(2,1)S(1)} %collective-permute-done.6, bf16[1,2,256,512]{3,2,1,0:T(8,128)(2,1)} %get-tuple-element.31), kind=kLoop, calls=%fused_computation.8 | loop fusion | flops 1048576 | bytes 1572864 | tf_op jit(solution)/shard_map/convert_element_type | solution.py:415
  47.5 2.4 %collective-permute-start.7 = (bf16[1,2,256,512]{3,2,1,0:T(8,128)(2,1)S(1)}, bf16[1,2,256,512]{3,2,1,0:T(8,128)(2,1)S(1)}, u32[]{:S(2)}, u32[]{:S(2)}) collective-permute-start(bf16[1,2,256,512]{3,2,1,0:T(8,128)(2,1)S(1)} %add_convert_fusion.2), channel_id=1, source_target_pairs={{0,2},{1,5},{2,0},{3,7},{4,6},{5,9},{6,4},{7,11},{8,10},{9,13},{10... | collective-permute-start | bytes 1572872 | tf_op jit(solution)/shard_map/ppermute | solution.py:30
  49.9 10.0 %collective-permute-done.11 = bf16[1,2,256,512]{3,2,1,0:T(8,128)(2,1)S(1)} collective-permute-done((bf16[1,2,256,512]{3,2,1,0:T(8,128)(2,1)S(1)}, bf16[1,2,256,512]{3,2,1,0:T(8,128)(2,1)S(1)}, u32[]{:S(2)}, u32[]{:S(2)}) %collective-permute-start.11) | collective-permute-done | bytes 524320 | tf_op jit(solution)/shard_map/ppermute | solution.py:30
  60.1 4.1 %collective-permute-start.12 = (bf16[1,2,256,512]{3,2,1,0:T(8,128)(2,1)S(1)}, bf16[1,2,256,512]{3,2,1,0:T(8,128)(2,1)S(1)}, u32[]{:S(2)}, u32[]{:S(2)}) collective-permute-start(bf16[1,2,256,512]{3,2,1,0:T(8,128)(2,1)S(1)} %add_convert_fusion), channel_id=1, source_target_pairs={{0,2},{1,5},{2,0},{3,7},{4,6},{5,9},{6,4},{7,11},{8,10},{9,13},{10... | collective-permute-start | bytes 1572872 | tf_op jit(solution)/shard_map/ppermute | solution.py:30
  64.9 0.9 %dynamic-slice_convert_fusion = bf16[2,2,256,256]{3,2,1,0:T(8,128)(2,1)} fusion(f32[2,2,256,512]{3,2,1,0:T(8,128)S(1)} %maximum_add_fusion, s32[]{:T(128)S(6)} %select_n.70), kind=kLoop, calls=%fused_computation.7 | loop fusion | bytes 1048580 | tf_op jit(solution)/shard_map/convert_element_type | solution.py:426
  65.7 5.7 %collective-permute-done.12 = bf16[1,2,256,512]{3,2,1,0:T(8,128)(2,1)S(1)} collective-permute-done((bf16[1,2,256,512]{3,2,1,0:T(8,128)(2,1)S(1)}, bf16[1,2,256,512]{3,2,1,0:T(8,128)(2,1)S(1)}, u32[]{:S(2)}, u32[]{:S(2)}) %collective-permute-start.12) | collective-permute-done | bytes 524320 | tf_op jit(solution)/shard_map/ppermute | solution.py:30
  71.5 0.8 dynamic-slice_convert_fusion.1
  72.3 1.7 %collective-permute-done.13 = bf16[1,2,256,256]{3,2,1,0:T(8,128)(2,1)S(1)} collective-permute-done((bf16[1,2,256,256]{3,2,1,0:T(8,128)(2,1)}, bf16[1,2,256,256]{3,2,1,0:T(8,128)(2,1)S(1)}, u32[]{:S(2)}, u32[]{:S(2)}) %collective-permute-start.13) | collective-permute-done | bytes 262176 | tf_op jit(solution)/shard_map/ppermute | solution.py:18
  74.1 1.3 %fusion = f32[2,256,2,256]{3,1,2,0:T(8,128)S(1)} fusion(f32[1,2,256,256]{3,2,1,0:T(8,128)S(1)} %get-tuple-element.40, f32[1,2,256,256]{3,2,1,0:T(8,128)S(1)} %get-tuple-element.39, bf16[2,2,256,256]{3,2,1,0:T(8,128)(2,1)} %collective-permute-done.8, f32[2,2,256,512]{3,2,1,0:T(8,128)S(1)} %maximum_add_fusion, s32[]{:T(128)S(6)} %select_n.69), kind=kLoop, calls=%fused_computation.4 | loop fusion | flops 1048576 | bytes 3670020 | tf_op jit(solution)/shard_map/transpose | solution.py:430
  75.5 1.8 %copy.11 = f32[2,256,2,256]{3,2,1,0:T(2,128)} copy(f32[2,256,2,256]{3,1,2,0:T(8,128)S(1)} %fusion) | data formatting | bytes 2097152 | tf_op jit(solution)/shard_map/transpose | solution.py:430
  (48 shorter events, 1.8 us)
Async XLA Ops:
  0.0 4.6 %copy-start = (s32[2,4]{1,0:T(2,128)S(1)}, s32[2,4]{1,0:T(2,128)}, u32[]{:S(2)}) copy-start(s32[2,4]{1,0:T(2,128)} %param.7) | copy-start | bytes 100
  1.4 11.6 %copy-start.1 = (bf16[2,256,2,512]{3,1,2,0:T(8,128)(2,1)}, bf16[2,256,2,512]{3,1,2,0:T(8,128)(2,1)S(1)}, u32[]{:S(2)}) copy-start(bf16[2,256,2,512]{3,1,2,0:T(8,128)(2,1)S(1)} %copy.14) | copy-start | bytes 3145732
  1.5 11.5 %collective-permute-start = (bf16[1,2,256,512]{3,2,1,0:T(8,128)(2,1)S(1)}, bf16[1,2,256,512]{3,2,1,0:T(8,128)(2,1)S(1)}, u32[]{:S(2)}, u32[]{:S(2)}) collective-permute-start(bf16[1,2,256,512]{3,2,1,0:T(8,128)(2,1)S(1)} %get-tuple-element.42), channel_id=1, source_target_pairs={{0,2},{1,13},{2,0},{3,15},{4,6},{5,1},{6,4},{7,3},{8,10},{9,5},{10... | collective-permute-start | bytes 1572872 | tf_op jit(solution)/shard_map/ppermute | solution.py:30
  4.5 12.8 %collective-permute-start.2 = (bf16[1,2,256,512]{3,2,1,0:T(8,128)(2,1)S(1)}, bf16[1,2,256,512]{3,2,1,0:T(8,128)(2,1)S(1)}, u32[]{:S(2)}, u32[]{:S(2)}) collective-permute-start(bf16[1,2,256,512]{3,2,1,0:T(8,128)(2,1)S(1)} %get-tuple-element.41), channel_id=1, source_target_pairs={{0,2},{1,13},{2,0},{3,15},{4,6},{5,1},{6,4},{7,3},{8,10},{9,5},{10... | collective-permute-start | bytes 1572872 | tf_op jit(solution)/shard_map/ppermute | solution.py:30
  13.0 12.8 %copy-start.4 = (bf16[1,2,256,512]{3,2,1,0:T(8,128)(2,1)}, bf16[1,2,256,512]{3,2,1,0:T(8,128)(2,1)S(1)}, u32[]{:S(2)}) copy-start(bf16[1,2,256,512]{3,2,1,0:T(8,128)(2,1)S(1)} %collective-permute-done.refs_1_) | copy-start | bytes 1572868
  13.0 10.8 %collective-permute-start.4 = (bf16[1,2,256,512]{3,2,1,0:T(8,128)(2,1)S(1)}, bf16[1,2,256,512]{3,2,1,0:T(8,128)(2,1)S(1)}, u32[]{:S(2)}, u32[]{:S(2)}) collective-permute-start(bf16[1,2,256,512]{3,2,1,0:T(8,128)(2,1)S(1)} %collective-permute-done.refs_1_), channel_id=1, source_target_pairs={{1,3},{0,12},{3,1},{2,14},{5,7},{4,0},{7,5},{6,2},{9,11},{8,4},{11... | collective-permute-start | bytes 1572872 | tf_op jit(solution)/shard_map/ppermute | solution.py:30
  17.2 6.7 %collective-permute-start.1 = (bf16[1,2,256,512]{3,2,1,0:T(8,128)(2,1)S(1)}, bf16[1,2,256,512]{3,2,1,0:T(8,128)(2,1)S(1)}, u32[]{:S(2)}, u32[]{:S(2)}) collective-permute-start(bf16[1,2,256,512]{3,2,1,0:T(8,128)(2,1)S(1)} %collective-permute-done.refs_1_), channel_id=1, source_target_pairs={{0,1},{1,0},{2,3},{3,2},{4,5},{5,4},{6,7},{7,6},{8,9},{9,8},{10,11... | collective-permute-start | bytes 1572872 | tf_op jit(solution)/shard_map/ppermute | solution.py:18
  17.3 8.5 %copy-start.5 = (bf16[1,2,256,512]{3,2,1,0:T(8,128)(2,1)}, bf16[1,2,256,512]{3,2,1,0:T(8,128)(2,1)S(1)}, u32[]{:S(2)}) copy-start(bf16[1,2,256,512]{3,2,1,0:T(8,128)(2,1)S(1)} %collective-permute-done.2.refs_3_) | copy-start | bytes 1572868
  17.3 6.6 %collective-permute-start.3 = (bf16[1,2,256,512]{3,2,1,0:T(8,128)(2,1)S(1)}, bf16[1,2,256,512]{3,2,1,0:T(8,128)(2,1)S(1)}, u32[]{:S(2)}, u32[]{:S(2)}) collective-permute-start(bf16[1,2,256,512]{3,2,1,0:T(8,128)(2,1)S(1)} %collective-permute-done.2.refs_3_), channel_id=1, source_target_pairs={{0,1},{1,0},{2,3},{3,2},{4,5},{5,4},{6,7},{7,6},{8,9},{9,8},{10,11... | collective-permute-start | bytes 1572872 | tf_op jit(solution)/shard_map/ppermute | solution.py:18
  23.9 1.9 %copy-start.6 = (bf16[1,2,256,512]{3,2,1,0:T(8,128)(2,1)}, bf16[1,2,256,512]{3,2,1,0:T(8,128)(2,1)S(1)}, u32[]{:S(2)}) copy-start(bf16[1,2,256,512]{3,2,1,0:T(8,128)(2,1)S(1)} %collective-permute-done.4.refs_5_) | copy-start | bytes 1572868
  23.9 1.9 %collective-permute-start.5 = (bf16[1,2,256,512]{3,2,1,0:T(8,128)(2,1)S(1)}, bf16[1,2,256,512]{3,2,1,0:T(8,128)(2,1)S(1)}, u32[]{:S(2)}, u32[]{:S(2)}) collective-permute-start(bf16[1,2,256,512]{3,2,1,0:T(8,128)(2,1)S(1)} %collective-permute-done.4.refs_5_), channel_id=1, source_target_pairs={{0,1},{1,0},{2,3},{3,2},{4,5},{5,4},{6,7},{7,6},{8,9},{9,8},{10,11... | collective-permute-start | bytes 1572872 | tf_op jit(solution)/shard_map/ppermute | solution.py:18
  23.9 1.9 %copy-start.7 = (bf16[1,2,256,512]{3,2,1,0:T(8,128)(2,1)}, bf16[1,2,256,512]{3,2,1,0:T(8,128)(2,1)S(1)}, u32[]{:S(2)}) copy-start(bf16[1,2,256,512]{3,2,1,0:T(8,128)(2,1)S(1)} %collective-permute-done.1.refs_2_) | copy-start | bytes 1572868
  23.9 1.9 %copy-start.8 = (bf16[1,2,256,512]{3,2,1,0:T(8,128)(2,1)}, bf16[1,2,256,512]{3,2,1,0:T(8,128)(2,1)S(1)}, u32[]{:S(2)}) copy-start(bf16[1,2,256,512]{3,2,1,0:T(8,128)(2,1)S(1)} %collective-permute-done.3.refs_4_) | copy-start | bytes 1572868
  25.8 0.9 %copy-start.9 = (bf16[1,2,256,512]{3,2,1,0:T(8,128)(2,1)}, bf16[1,2,256,512]{3,2,1,0:T(8,128)(2,1)S(1)}, u32[]{:S(2)}) copy-start(bf16[1,2,256,512]{3,2,1,0:T(8,128)(2,1)S(1)} %collective-permute-done.5.refs_6_) | copy-start | bytes 1572868
  42.3 17.6 %copy-start.3 = (bf16[1,2,256,512]{3,2,1,0:T(8,128)(2,1)S(1)}, bf16[1,2,256,512]{3,2,1,0:T(8,128)(2,1)}, u32[]{:S(2)}) copy-start(bf16[1,2,256,512]{3,2,1,0:T(8,128)(2,1)} %get-tuple-element.33) | copy-start | bytes 1572868
  42.3 2.2 %collective-permute-start.10 = (bf16[1,2,256,512]{3,2,1,0:T(8,128)(2,1)}, bf16[1,2,256,512]{3,2,1,0:T(8,128)(2,1)S(1)}, u32[]{:S(2)}, u32[]{:S(2)}) collective-permute-start(bf16[1,2,256,512]{3,2,1,0:T(8,128)(2,1)} %get-tuple-element.36), channel_id=1, source_target_pairs={{0,1},{1,0},{2,3},{3,2},{4,5},{5,4},{6,7},{7,6},{8,9},{9,8},{10,11... | collective-permute-start | bytes 1572872 | tf_op jit(solution)/shard_map/ppermute | solution.py:18
  42.4 3.9 %collective-permute-start.6 = (bf16[1,2,256,512]{3,2,1,0:T(8,128)(2,1)}, bf16[1,2,256,512]{3,2,1,0:T(8,128)(2,1)S(1)}, u32[]{:S(2)}, u32[]{:S(2)}) collective-permute-start(bf16[1,2,256,512]{3,2,1,0:T(8,128)(2,1)} %get-tuple-element.32), channel_id=1, source_target_pairs={{0,1},{1,0},{2,3},{3,2},{4,5},{5,4},{6,7},{7,6},{8,9},{9,8},{10,11... | collective-permute-start | bytes 1572872 | tf_op jit(solution)/shard_map/ppermute | solution.py:18
  42.9 7.1 %collective-permute-start.9 = (bf16[1,2,256,512]{3,2,1,0:T(8,128)(2,1)}, bf16[1,2,256,512]{3,2,1,0:T(8,128)(2,1)S(1)}, u32[]{:S(2)}, u32[]{:S(2)}) collective-permute-start(bf16[1,2,256,512]{3,2,1,0:T(8,128)(2,1)} %get-tuple-element.34), channel_id=1, source_target_pairs={{0,1},{1,0},{2,3},{3,2},{4,5},{5,4},{6,7},{7,6},{8,9},{9,8},{10,11... | collective-permute-start | bytes 1572872 | tf_op jit(solution)/shard_map/ppermute | solution.py:18
  45.7 14.2 %collective-permute-start.11 = (bf16[1,2,256,512]{3,2,1,0:T(8,128)(2,1)S(1)}, bf16[1,2,256,512]{3,2,1,0:T(8,128)(2,1)S(1)}, u32[]{:S(2)}, u32[]{:S(2)}) collective-permute-start(bf16[1,2,256,512]{3,2,1,0:T(8,128)(2,1)S(1)} %add_convert_fusion.1), channel_id=1, source_target_pairs={{1,3},{0,4},{3,1},{2,6},{5,7},{4,8},{7,5},{6,10},{9,11},{8,12},{11... | collective-permute-start | bytes 1572872 | tf_op jit(solution)/shard_map/ppermute | solution.py:30
  47.5 16.7 %collective-permute-start.7 = (bf16[1,2,256,512]{3,2,1,0:T(8,128)(2,1)S(1)}, bf16[1,2,256,512]{3,2,1,0:T(8,128)(2,1)S(1)}, u32[]{:S(2)}, u32[]{:S(2)}) collective-permute-start(bf16[1,2,256,512]{3,2,1,0:T(8,128)(2,1)S(1)} %add_convert_fusion.2), channel_id=1, source_target_pairs={{0,2},{1,5},{2,0},{3,7},{4,6},{5,9},{6,4},{7,11},{8,10},{9,13},{10... | collective-permute-start | bytes 1572872 | tf_op jit(solution)/shard_map/ppermute | solution.py:30
  59.9 4.6 %copy-start.2 = (bf16[2,2,256,512]{3,2,1,0:T(8,128)(2,1)S(1)}, bf16[2,2,256,512]{3,2,1,0:T(8,128)(2,1)}, u32[]{:S(2)}) copy-start(bf16[2,2,256,512]{3,2,1,0:T(8,128)(2,1)} %get-tuple-element.30) | copy-start | bytes 3145732
  60.1 11.3 %collective-permute-start.12 = (bf16[1,2,256,512]{3,2,1,0:T(8,128)(2,1)S(1)}, bf16[1,2,256,512]{3,2,1,0:T(8,128)(2,1)S(1)}, u32[]{:S(2)}, u32[]{:S(2)}) collective-permute-start(bf16[1,2,256,512]{3,2,1,0:T(8,128)(2,1)S(1)} %add_convert_fusion), channel_id=1, source_target_pairs={{0,2},{1,5},{2,0},{3,7},{4,6},{5,9},{6,4},{7,11},{8,10},{9,13},{10... | collective-permute-start | bytes 1572872 | tf_op jit(solution)/shard_map/ppermute | solution.py:30
  65.7 8.4 %collective-permute-start.8 = (bf16[2,2,256,256]{3,2,1,0:T(8,128)(2,1)}, bf16[2,2,256,256]{3,2,1,0:T(8,128)(2,1)}, u32[]{:S(2)}, u32[]{:S(2)}) collective-permute-start(bf16[2,2,256,256]{3,2,1,0:T(8,128)(2,1)} %dynamic-slice_convert_fusion), channel_id=1, source_target_pairs={{0,1},{1,0},{2,3},{3,2},{4,5},{5,4},{6,7},{7,6},{8,9},{9,8},{10,11... | collective-permute-start | bytes 1572872 | tf_op jit(solution)/shard_map/ppermute | solution.py:18
  72.3 1.7 %collective-permute-start.13 = (bf16[1,2,256,256]{3,2,1,0:T(8,128)(2,1)}, bf16[1,2,256,256]{3,2,1,0:T(8,128)(2,1)S(1)}, u32[]{:S(2)}, u32[]{:S(2)}) collective-permute-start(bf16[1,2,256,256]{3,2,1,0:T(8,128)(2,1)} %dynamic-slice_convert_fusion.1), channel_id=1, source_target_pairs={{0,1},{1,0},{2,3},{3,2},{4,5},{5,4},{6,7},{7,6},{8,9},{9,8},{10,11... | collective-permute-start | bytes 786440 | tf_op jit(solution)/shard_map/ppermute | solution.py:18

commit v5 on v4

--- a/solution.py
+++ b/solution.py
@@ -47,7 +47,7 @@
     return rounded(np.stack([stack, stack.transpose(0, 2, 1)]))
 
 
-def prep_kernel(mine, pix, info, base, probe, measured, lefts, rights, psi0, light):
+def table_kernel(mine, pix, info, base, lefts, rights):
     bf16, f32 = jnp.bfloat16, jnp.float32
     mid = pix // 2
 
@@ -67,21 +67,6 @@
             ref[m, t, odd, :mid, mid:] = upper.astype(bf16)
             ref[m, t, odd, mid:, :mid] = lower.astype(bf16)
             ref[m, t, odd, mid:, mid:] = re_part.astype(bf16)
-
-    row_at = lax.broadcasted_iota(jnp.int32, (pix, pix), 0)
-    col_at = lax.broadcasted_iota(jnp.int32, (pix, pix), 1)
-    order = lambda at: jnp.where(at < mid, 2 * at, 2 * at - (pix - 1))
-    pick_rows = (col_at == order(row_at)).astype(f32).astype(bf16)
-    pick_cols = (row_at == order(col_at)).astype(f32).astype(bf16)
-
-    def exact(values, product):
-        total = None
-        for _ in range(3):
-            term = values.astype(bf16)
-            values = values - term.astype(f32)
-            moved = product(term)
-            total = moved if total is None else total + moved
-        return total
 
     for m in range(mine):
         r0 = info[2 + 4 * m]
@@ -93,6 +78,29 @@
         put(lefts, m, 3, re, -im, False, True)
         re, im = rolled(0, 0, c0, 1)
         put(rights, m, 3, re, -im, True, False)
+
+
+def slot_kernel(mine, pix, info, probe, measured, psi0, light):
+    bf16, f32 = jnp.bfloat16, jnp.float32
+    mid = pix // 2
+    row_at = lax.broadcasted_iota(jnp.int32, (pix, pix), 0)
+    col_at = lax.broadcasted_iota(jnp.int32, (pix, pix), 1)
+    order = lambda at: jnp.where(at < mid, 2 * at, 2 * at - (pix - 1))
+    pick_rows = (col_at == order(row_at)).astype(f32).astype(bf16)
+    pick_cols = (row_at == order(col_at)).astype(f32).astype(bf16)
+
+    def exact(values, product):
+        total = None
+        for _ in range(3):
+            term = values.astype(bf16)
+            values = values - term.astype(f32)
+            moved = product(term)
+            total = moved if total is None else total + moved
+        return total
+
+    for m in range(mine):
+        r0 = info[2 + 4 * m]
+        c0 = info[4 + 4 * m]
         for part in range(2):
             plane = probe[:, part * pix : (part + 1) * pix].astype(f32)
             plane = pltpu.roll(pltpu.roll(plane, r0, 0), c0, 1)
@@ -107,8 +115,8 @@
     own, operands = refs[0], refs[1:count]
     lefts_any, rights_any, psi0_any, light_any = refs[count : count + 4]
     outs = refs[count + 4 : count + 4 + len(results)]
-    own_out = refs[count + 4 + len(results)]
-    obj, tp, psi, lefts, rights, light, grads, sems, tab_sems, out_sems = refs[count + 5 + len(results) :]
+    own_keep, own_send = refs[count + 4 + len(results) : count + 6 + len(results)]
+    obj, tp, psi, lefts, rights, light, grads, sems, tab_sems, out_sems = refs[count + 6 + len(results) :]
     layers = groups * depth
     half = depth // 2
     rank = info[0]
@@ -255,12 +263,21 @@
     def out_copy(below, place, out):
         return pltpu.make_async_copy(grads.at[below, place], out, out_sems.at[below, place])
 
+    def own_copies(i):
+        copies = []
+        for away, out in enumerate((own_keep, own_send)):
+            at = pl.multiple_of(((1 - core) if away else core) * pix, pix)
+            columns = grads.at[0, i, :, :, pl.ds(at, pix)]
+            copies.append(pltpu.make_async_copy(columns, out.at[i], out_sems.at[2 * away, i]))
+        return copies
+
     def send_out(step, within):
         place = step * depth + within
 
         @pl.when(step == 0)
         def _():
-            out_copy(0, place, own_out.at[within]).start()
+            for copy in own_copies(within):
+                copy.start()
 
         for takes, ref in zip(results, outs):
             for c in range(2):
@@ -281,18 +298,22 @@
         for m, (re, im) in enumerate(exits):
             pr, pi = psi[j, m, 0].astype(f32), psi[j, m, 1].astype(f32)
             terms.append((pr * re + pi * im, pr * im - pi * re))
-        for below in range(2):
-            for col in range(2):
-                for part in range(2):
-                    total = None
-                    for m in members:
-                        rows = (row_at < r0[m]) if below else (row_at >= r0[m])
-                        low = jnp.where(q[m] == col, c0[m], 0)
-                        high = jnp.where(q[m] == col, pix, c0[m])
-                        mask = rows & (col_at >= low) & (col_at < high)
-                        term = jnp.where(mask, terms[m][part], 0.0)
-                        total = term if total is None else total + term
-                    grads[below, place, part, :, col * pix : (col + 1) * pix] = total.astype(bf16)
+        for part in range(2):
+            total = [[None, None], [None, None]]
+            for m in members:
+                value = terms[m][part]
+                after = jnp.where(col_at >= c0[m], value, 0.0)
+                before = value - after
+                by_col = [jnp.where(q[m] == 0, after, before), jnp.where(q[m] == 0, before, after)]
+                for col in range(2):
+                    below = jnp.where(row_at < r0[m], by_col[col], 0.0)
+                    for row_block, found in ((0, by_col[col] - below), (1, below)):
+                        so_far = total[row_block][col]
+                        total[row_block][col] = found if so_far is None else so_far + found
+            for row_block in range(2):
+                for col in range(2):
+                    values = total[row_block][col].astype(bf16)
+                    grads[row_block, place, part, :, col * pix : (col + 1) * pix] = values
         send_out(step, within)
 
     def wave_grads(j, exits):
@@ -315,8 +336,11 @@
     hold = lax.fori_loop(0, layers - 1, backward, hold)
     scatter(0, [(hold[2 * m], hold[2 * m + 1]) for m in members])
     for below in range(2):
-        for place in range(layers):
-            out_copy(below, place, own_out.at[0]).wait()
+        for place in range(0 if below else depth, layers):
+            out_copy(below, place, outs[0].at[0]).wait()
+    for i in range(depth):
+        for copy in own_copies(i):
+            copy.wait()
 
 
 def body(object_field, offsets, counts, measured, probe_wave):
@@ -343,32 +367,38 @@
     steps = range(1, groups)
     halves_of = lambda high: lax.dynamic_slice_in_dim(planes, high * half, half, axis=0)
     first_half, last_half = halves_of(core), halves_of(1 - core)
-    got_first = [split_roles(first_half, -1, s, 0, s == 1) for s in steps]
-    got_last = [split_roles(last_half, -1, s, 0, s == 1) for s in steps]
-
     smem = pl.BlockSpec(memory_space=pltpu.SMEM)
     vmem = pl.BlockSpec(memory_space=pltpu.VMEM)
     anywhere = pl.BlockSpec(memory_space=pl.ANY)
     tables_shape = jax.ShapeDtypeStruct((mine, 4, 2, pix, pix), bf16)
-    lefts, rights, psi0, light = pl.pallas_call(
-        functools.partial(prep_kernel, mine, pix),
+    params = pltpu.CompilerParams(vmem_limit_bytes=VMEM_LIMIT)
+    lefts, rights = pl.pallas_call(
+        functools.partial(table_kernel, mine, pix),
+        out_shape=(tables_shape, tables_shape),
+        in_specs=[smem, vmem],
+        out_specs=(vmem, vmem),
+        compiler_params=params,
+        cost_estimate=pl.CostEstimate(flops=5 * 10**9, bytes_accessed=8 * 2**20, transcendentals=0),
+        name="tables",
+    )(info, jnp.asarray(base_tables(pix)))
+    psi0, light = pl.pallas_call(
+        functools.partial(slot_kernel, mine, pix),
         out_shape=(
-            tables_shape,
-            tables_shape,
             jax.ShapeDtypeStruct((mine, 2, pix, pix), bf16),
             jax.ShapeDtypeStruct((mine, pix, pix), jnp.float32),
         ),
-        in_specs=[smem, vmem, vmem, vmem],
-        out_specs=(vmem,) * 4,
-        compiler_params=pltpu.CompilerParams(vmem_limit_bytes=VMEM_LIMIT),
-        cost_estimate=pl.CostEstimate(flops=8 * 10**9, bytes_accessed=8 * 2**20, transcendentals=0),
-        name="tables",
-    )(info, jnp.asarray(base_tables(pix)), probe_wave, measured)
-
-    got_first, lefts, rights, psi0, light = lax.optimization_barrier(
-        (got_first, lefts, rights, psi0, light)
-    )
+        in_specs=[smem, vmem, vmem],
+        out_specs=(vmem, vmem),
+        compiler_params=params,
+        cost_estimate=pl.CostEstimate(flops=2 * 10**9, bytes_accessed=2 * 2**20, transcendentals=0),
+        name="slots",
+    )(info, probe_wave, measured)
+
+    got_first = [split_roles(first_half, -1, s, 0, s == 1) for s in steps]
+    last_half, lefts, rights = lax.optimization_barrier((last_half, lefts, rights))
+    got_last = [split_roles(last_half, -1, s, 0, s == 1) for s in steps]
     passed_on = [split_roles(got_first[s - 1], -1, s, 1) for s in steps]
+    got_last, psi0, light = lax.optimization_barrier((got_last, psi0, light))
     pieces, operands = [], []
     for s in steps:
         rim_hi, rim_lo = ((0, 1, 1), (0, 0, 1)) if s == 1 else (None, None)
@@ -386,11 +416,11 @@
             results += [holds, holds[::-1]]
 
     half_shape = jax.ShapeDtypeStruct((half, 2, rows, cols), bf16)
-    *outs, own_grads = pl.pallas_call(
+    *outs, own_keep, own_send = pl.pallas_call(
         functools.partial(main_kernel, groups, depth, mine, pix, tuple(pieces), tuple(results)),
-        out_shape=(half_shape,) * len(results) + (jax.ShapeDtypeStruct((depth, 2, rows, cols), bf16),),
+        out_shape=(half_shape,) * len(results) + (jax.ShapeDtypeStruct((depth, 2, rows, pix), bf16),) * 2,
         in_specs=[smem] + [anywhere] * (5 + len(operands)),
-        out_specs=(anywhere,) * (len(results) + 1),
+        out_specs=(anywhere,) * (len(results) + 2),
         scratch_shapes=[
             pltpu.VMEM((layers, 2, 2, pix, cols), bf16),
             pltpu.VMEM((layers, mine, 2, pix, pix), bf16),
@@ -401,7 +431,7 @@
             pltpu.VMEM((2, layers, 2, pix, cols), bf16),
             pltpu.SemaphoreType.DMA((layers, 2)),
             pltpu.SemaphoreType.DMA((5, 2)),
-            pltpu.SemaphoreType.DMA((2, layers)),
+            pltpu.SemaphoreType.DMA((3, layers)),
         ],
         compiler_params=pltpu.CompilerParams(vmem_limit_bytes=VMEM_LIMIT),
         cost_estimate=pl.CostEstimate(flops=15 * 10**9, bytes_accessed=16 * 2**20, transcendentals=0),
@@ -412,22 +442,28 @@
     kept = lambda s, which: wide(outs[6 * (s - 1) + 2 * which])
     twin = lambda s, which: wide(passed(outs[6 * (s - 1) + 2 * which + 1], "pos", 1))
     rims = {s: (kept(s, 0) + twin(s, 0)).astype(bf16) for s in steps}
+    back = {s: split_roles(rims[s], 1, -s, 1) for s in steps}
     firsts = {s: (kept(s, 1) + twin(s, 1)).astype(bf16) for s in steps}
     lasts = {s: kept(s, 2) + twin(s, 2) for s in steps}
-    back = {s: split_roles(rims[s], 1, -s, 1) for s in steps}
-    come_first = sum(wide(split_roles(firsts[s], 1, -s, 0, s == 1)) for s in steps)
+    early = (wide(own_keep) + wide(passed(own_send, "pos", 1))).transpose(0, 2, 1, 3)
+    back, firsts, lasts = lax.optimization_barrier((back, firsts, lasts))
+    come_first = [split_roles(firsts[s], 1, -s, 0, s == 1) for s in steps]
     summed = sum(wide(back[s]) for s in steps)
-    lasts = {s: (lasts[s] + (jnp.where(core == 1, summed, wide(back[s])))).astype(bf16) for s in steps}
-    come_last = sum(wide(split_roles(lasts[s], 1, -s, 0, s == 1)) for s in steps)
-    on_first = jnp.where(core == 0, 1.0, 0.0)
-    own_sum = wide(own_grads) + jnp.concatenate([come_first * on_first, come_first * (1.0 - on_first)])
+    lasts = {s: (lasts[s] + jnp.where(core == 1, summed, wide(back[s]))).astype(bf16) for s in steps}
+    come_last = [split_roles(lasts[s], 1, -s, 0, s == 1) for s in steps]
+    come_first, early = lax.optimization_barrier((come_first, early))
+    come_first = sum(map(wide, come_first)).astype(bf16)
+    come_last = sum(map(wide, come_last)).astype(bf16)
     mine_of = lambda v: lax.dynamic_slice_in_dim(v, core * pix, pix, axis=3)
     twins_of = lambda v: lax.dynamic_slice_in_dim(v, (1 - core) * pix, pix, axis=3)
-    early = mine_of(own_sum) + wide(passed(twins_of(own_sum).astype(bf16), "pos", 1))
-    here = mine_of(come_last)
-    away = wide(passed(twins_of(come_last).astype(bf16), "pos", 1))
-    late = jnp.concatenate([jnp.where(core == 0, away, here), jnp.where(core == 0, here, away)])
-    return (early + late).transpose(0, 2, 1, 3)
+    in_place = lambda v: v.transpose(0, 2, 1, 3)
+    here_first, here_last = in_place(mine_of(come_first)), in_place(mine_of(come_last))
+    away_first = in_place(passed(twins_of(come_first), "pos", 1))
+    away_last = in_place(passed(twins_of(come_last), "pos", 1))
+    one = wide(here_first) + wide(away_last)
+    other = wide(here_last) + wide(away_first)
+    late = jnp.concatenate([jnp.where(core == 0, one, other), jnp.where(core == 0, other, one)])
+    return early + late
 
 
 def solution(mesh):

time: 77.6 us -> 81.5 us (1.050)
  waiting for transfers between devices: 26.8 us -> 32.4 us
  starting transfers between devices: 15.7 us -> 13 us
  Pallas kernels: 22.5 us -> 23.8 us
    ppermute x6, waiting for transfers between devices: 21.7 us -> 27.3 us  [split_roles(): return lax.ppermute(array, ('tile', 'slc', 'pos'), pairs)]
    ppermute x6, starting transfers between devices: 14.4 us -> 9.66 us  [split_roles(): return lax.ppermute(array, ('tile', 'slc', 'pos'), pairs)]
    ppermute x8 -> x9, starting transfers between devices: 1.29 us -> 3.34 us  [passed(): lax.ppermute(array, axis, [(i, (i + by) % peers) for i in range(peers)])]
    dynamic_slice x0 -> x2, local copies, waits for them, and re-layouts: none -> 1.93 us  [body(): lax.dynamic_slice_in_dim(v, (1 - core) * pix, pix, axis=3)]
    add x0 -> x1, local copies, waits for them, and re-layouts: none -> 1.78 us  [body(): return early + late]
    transpose x1 -> x0, local copies, waits for them, and re-layouts: 1.78 us -> none  [body(): return (early + late).transpose(0, 2, 1, 3)]
    convert_element_type x2 -> x0, local copies, waits for them, and re-layouts: 1.63 us -> none  [the longest x1 0.87 us: body(): twins_of(own_sum).astype(bf16)]
    pallas_call x1 -> x2, Pallas kernels: 6.82 us -> 8.34 us  [the longest x1 4.9 us: body(): pl.pallas_call(functools.partial(table_kernel, mine, pix), out_shape=(tab...]
  transfers between devices with their start and end apart: 14 -> 15, of which waited for: 7 -> 10; matrix products, arithmetic and copies ran while one was open for 8% -> 7% of each run, Pallas kernels for 9% -> 10%
where the time goes in v5:
time: 81.5 us; the launch traced here: 81.1 us
  waiting for transfers between devices  32.4 us (40%)
  Pallas kernels  23.8 us (29%)
  starting transfers between devices  13 us (16%)
  local copies, waits for them, and re-layouts  6.32 us (8%)
  other arithmetic  4.76 us (6%)
  between operations  0.84 us (1%)
    ppermute x6, waiting for transfers between devices, split_roles(): return lax.ppermute(array, ('tile', 'slc', 'pos'), pairs)  27.3 us
    pallas_call x1, Pallas kernels, body(): pl.pallas_call(functools.partial(main_kernel, groups, depth, mine, pix, t...  15.5 us
    ppermute x6, starting transfers between devices, split_roles(): return lax.ppermute(array, ('tile', 'slc', 'pos'), pairs)  9.66 us
    ppermute x9, waiting for transfers between devices, passed(): lax.ppermute(array, axis, [(i, (i + by) % peers) for i in range(peers)])  5.13 us
    pallas_call x1, Pallas kernels, body(): pl.pallas_call(functools.partial(table_kernel, mine, pix), out_shape=(tab...  4.9 us
    pallas_call x1, Pallas kernels, body(): pl.pallas_call(functools.partial(slot_kernel, mine, pix), out_shape=(jax....  3.44 us
    ppermute x9, starting transfers between devices, passed(): lax.ppermute(array, axis, [(i, (i + by) % peers) for i in range(peers)])  3.34 us
    unnamed x21, local copies, waits for them, and re-layouts  2.28 us
  transfers between devices with their start and end apart: 15, of which 10 were waited for; matrix products, arithmetic and copies ran while one was open for 7% of the time, Pallas kernels for 10%

profile of v5, /device:TPU:0, one launch (start us, length us, event | category | flops | bytes accessed | tf_op | source)
XLA Modules:
  0.0 81.1 jit_solution(5665502815281966591)
XLA Ops:
  0.0 1.4 %copy.14 = bf16[2,256,2,512]{3,1,2,0:T(8,128)(2,1)S(1)} copy(bf16[2,256,2,512]{3,2,1,0:T(2,128)(2,1)} %param.6) | data formatting | bytes 2097152 | tf_op args[0]
  1.5 3.0 %collective-permute-start = (bf16[1,2,256,512]{3,2,1,0:T(8,128)(2,1)S(1)}, bf16[1,2,256,512]{3,2,1,0:T(8,128)(2,1)S(1)}, u32[]{:S(2)}, u32[]{:S(2)}) collective-permute-start(bf16[1,2,256,512]{3,2,1,0:T(8,128)(2,1)S(1)} %get-tuple-element.56), channel_id=1, source_target_pairs={{0,2},{1,13},{2,0},{3,15},{4,6},{5,1},{6,4},{7,3},{8,10},{9,5},{10... | collective-permute-start | bytes 1572872 | tf_op jit(solution)/shard_map/ppermute | solution.py:30
  6.1 4.9 %tables.1 = (bf16[2,4,2,256,256]{4,3,2,1,0:T(8,128)(2,1)}, bf16[2,4,2,256,256]{4,3,2,1,0:T(8,128)(2,1)}) custom-call(s32[10]{0:T(128)} %pad_add_fusion.1.info, bf16[2,6,256,256]{3,2,1,0:T(8,128)(2,1)} %constant.51.clone.base), custom_call_target="tpu_custom_call" | custom-call | flops 5000000000 | bytes 8388608 | tf_op jit(solution)/shard_map/tables/pallas_call | solution.py:375
  11.7 4.1 %collective-permute-start.4 = (bf16[1,2,256,512]{3,2,1,0:T(8,128)(2,1)S(1)}, bf16[1,2,256,512]{3,2,1,0:T(8,128)(2,1)S(1)}, u32[]{:S(2)}, u32[]{:S(2)}) collective-permute-start(bf16[1,2,256,512]{3,2,1,0:T(8,128)(2,1)S(1)} %collective-permute-done.refs_1_), channel_id=1, source_target_pairs={{1,3},{0,12},{3,1},{2,14},{5,7},{4,0},{7,5},{6,2},{9,11},{8,4},{11... | collective-permute-start | bytes 1572872 | tf_op jit(solution)/shard_map/ppermute | solution.py:30
  15.8 3.4 %slots.1 = (bf16[2,2,256,256]{3,2,1,0:T(8,128)(2,1)}, f32[2,256,256]{2,1,0:T(8,128)}) custom-call(s32[10]{0:T(128)} %pad_add_fusion.1.info, bf16[256,512]{1,0:T(8,128)(2,1)} %probe.1, f32[4,256,256]{2,1,0:T(8,128)} %measured.1), custom_call_target="tpu_custom_call" | custom-call | flops 2000000000 | bytes 2097152 | tf_op jit(solution)/shard_map/slots/pallas_call | solution.py:384
  19.2 5.7 %collective-permute-done.2.refs_3_ = bf16[1,2,256,512]{3,2,1,0:T(8,128)(2,1)S(1)} collective-permute-done((bf16[1,2,256,512]{3,2,1,0:T(8,128)(2,1)S(1)}, bf16[1,2,256,512]{3,2,1,0:T(8,128)(2,1)S(1)}, u32[]{:S(2)}, u32[]{:S(2)}) %collective-permute-start.2) | collective-permute-done | bytes 524320 | tf_op jit(solution)/shard_map/ppermute | solution.py:30
  24.9 1.6 %collective-permute-start.3 = (bf16[1,2,256,512]{3,2,1,0:T(8,128)(2,1)S(1)}, bf16[1,2,256,512]{3,2,1,0:T(8,128)(2,1)S(1)}, u32[]{:S(2)}, u32[]{:S(2)}) collective-permute-start(bf16[1,2,256,512]{3,2,1,0:T(8,128)(2,1)S(1)} %collective-permute-done.2.refs_3_), channel_id=1, source_target_pairs={{0,1},{1,0},{2,3},{3,2},{4,5},{5,4},{6,7},{7,6},{8,9},{9,8},{10,11... | collective-permute-start | bytes 1572872 | tf_op jit(solution)/shard_map/ppermute | solution.py:18
  27.1 1.0 %collective-permute-done.3.refs_4_ = bf16[1,2,256,512]{3,2,1,0:T(8,128)(2,1)S(1)} collective-permute-done((bf16[1,2,256,512]{3,2,1,0:T(8,128)(2,1)S(1)}, bf16[1,2,256,512]{3,2,1,0:T(8,128)(2,1)S(1)}, u32[]{:S(2)}, u32[]{:S(2)}) %collective-permute-start.3) | collective-permute-done | bytes 524320 | tf_op jit(solution)/shard_map/ppermute | solution.py:18
  28.1 0.7 collective-permute-done.1.refs_2_
  28.8 0.7 collective-permute-done.5.refs_6_
  29.7 0.8 copy-done.9
  30.4 15.5 %waves.1 = (bf16[1,2,256,512]{3,2,1,0:T(8,128)(2,1)}, bf16[1,2,256,512]{3,2,1,0:T(8,128)(2,1)}, bf16[1,2,256,512]{3,2,1,0:T(8,128)(2,1)}, bf16[1,2,256,512]{3,2,...) custom-call(s32[10]{0:T(128)} %pad_add_fusion.1.info, ...), custom_call_target="tpu_custom_call" | custom-call | flops 15000000512 | bytes 16777216 | tf_op jit(solution)/shard_map/waves/pallas_call | solution.py:419
  47.0 1.1 %collective-permute-done.6 = bf16[1,2,256,512]{3,2,1,0:T(8,128)(2,1)S(1)} collective-permute-done((bf16[1,2,256,512]{3,2,1,0:T(8,128)(2,1)}, bf16[1,2,256,512]{3,2,1,0:T(8,128)(2,1)S(1)}, u32[]{:S(2)}, u32[]{:S(2)}) %collective-permute-start.6) | collective-permute-done | bytes 524320 | tf_op jit(solution)/shard_map/ppermute | solution.py:18
  48.1 1.2 %add_convert_fusion.2 = bf16[1,2,256,512]{3,2,1,0:T(8,128)(2,1)S(1)} fusion(bf16[1,2,256,512]{3,2,1,0:T(8,128)(2,1)S(1)} %collective-permute-done.6, bf16[1,2,256,512]{3,2,1,0:T(8,128)(2,1)} %get-tuple-element.38), kind=kLoop, calls=%fused_computation.5 | loop fusion | flops 1048576 | bytes 1572864 | tf_op jit(solution)/shard_map/convert_element_type | solution.py:444
  49.7 1.2 %add_convert_fusion.1 = bf16[1,2,256,512]{3,2,1,0:T(8,128)(2,1)S(1)} fusion(bf16[1,2,256,512]{3,2,1,0:T(8,128)(2,1)S(1)} %collective-permute-done.8, bf16[1,2,256,512]{3,2,1,0:T(8,128)(2,1)} %get-tuple-element.40), kind=kLoop, calls=%fused_computation.4 | loop fusion | flops 1048576 | bytes 1572864 | tf_op jit(solution)/shard_map/convert_element_type | solution.py:446
  51.1 9.3 %collective-permute-done.7 = bf16[1,2,256,512]{3,2,1,0:T(8,128)(2,1)S(1)} collective-permute-done((bf16[1,2,256,512]{3,2,1,0:T(8,128)(2,1)S(1)}, bf16[1,2,256,512]{3,2,1,0:T(8,128)(2,1)S(1)}, u32[]{:S(2)}, u32[]{:S(2)}) %collective-permute-start.7) | collective-permute-done | bytes 524320 | tf_op jit(solution)/shard_map/ppermute | solution.py:30
  60.5 2.0 %collective-permute-start.12 = (bf16[1,2,256,512]{3,2,1,0:T(8,128)(2,1)S(1)}, bf16[1,2,256,512]{3,2,1,0:T(8,128)(2,1)}, u32[]{:S(2)}, u32[]{:S(2)}) collective-permute-start(bf16[1,2,256,512]{3,2,1,0:T(8,128)(2,1)S(1)} %add_convert_fusion), channel_id=1, source_target_pairs={{0,2},{1,5},{2,0},{3,7},{4,6},{5,9},{6,4},{7,11},{8,10},{9,13},{10... | collective-permute-start | bytes 1572872 | tf_op jit(solution)/shard_map/ppermute | solution.py:30
  62.7 7.1 %collective-permute-done.12 = bf16[1,2,256,512]{3,2,1,0:T(8,128)(2,1)} collective-permute-done((bf16[1,2,256,512]{3,2,1,0:T(8,128)(2,1)S(1)}, bf16[1,2,256,512]{3,2,1,0:T(8,128)(2,1)}, u32[]{:S(2)}, u32[]{:S(2)}) %collective-permute-start.12) | collective-permute-done | bytes 524320 | tf_op jit(solution)/shard_map/ppermute | solution.py:30
  69.8 1.0 %constant_dynamic-slice_fusion.1 = bf16[1,2,256,256]{3,2,1,0:T(8,128)(2,1)S(1)} fusion(bf16[1,2,256,512]{3,2,1,0:T(8,128)(2,1)} %collective-permute-done.12, s32[]{:T(128)S(6)} %select_n.72), kind=kLoop, calls=%fused_computation.17 | loop fusion | bytes 524292 | tf_op jit(solution)/shard_map/dynamic_slice | solution.py:458
  70.9 4.6 %collective-permute-done.10 = bf16[1,2,256,512]{3,2,1,0:T(8,128)(2,1)} collective-permute-done((bf16[1,2,256,512]{3,2,1,0:T(8,128)(2,1)S(1)}, bf16[1,2,256,512]{3,2,1,0:T(8,128)(2,1)}, u32[]{:S(2)}, u32[]{:S(2)}) %collective-permute-start.10) | collective-permute-done | bytes 524320 | tf_op jit(solution)/shard_map/ppermute | solution.py:30
  75.5 1.0 %constant_dynamic-slice_fusion = bf16[1,2,256,256]{3,2,1,0:T(8,128)(2,1)S(1)} fusion(bf16[1,2,256,512]{3,2,1,0:T(8,128)(2,1)} %collective-permute-done.10, s32[]{:T(128)S(6)} %select_n.72), kind=kLoop, calls=%fused_computation.16 | loop fusion | bytes 524292 | tf_op jit(solution)/shard_map/dynamic_slice | solution.py:458
  76.5 1.5 %collective-permute-done.14 = bf16[1,2,256,256]{3,2,1,0:T(8,128)(2,1)S(1)} collective-permute-done((bf16[1,2,256,256]{3,2,1,0:T(8,128)(2,1)S(1)}, bf16[1,2,256,256]{3,2,1,0:T(8,128)(2,1)S(1)}, u32[]{:S(2)}, u32[]{:S(2)}) %collective-permute-start.14) | collective-permute-done | bytes 262176 | tf_op jit(solution)/shard_map/ppermute | solution.py:18
  78.0 1.2 %select_bitcast_fusion.1 = (f32[1,256,2,256]{3,1,2,0:T(8,128)S(1)}, f32[1,256,2,256]{3,1,2,0:T(8,128)S(1)}) fusion(bf16[1,2,256,256]{3,2,1,0:T(8,128)(2,1)S(1)} %collective-permute-done.13, bf16[1,2,256,256]{3,2,1,0:T(8,128)(2,1)S(1)} %collective-permute-done.14, pred[]{:T(512)S(6)} %eq.4, bf16[1,2,256,512]{3,2,1,0:T(8,128)(2,1)} %collective-permute-done.12, ...), kind=kLoop, calls=%fused_computation.7 | loop fusion | flops 1048576 | bytes 2097157 | tf_op jit(solution)/shard_map/jit(_where)/select_n | solution.py:465
  79.4 1.8 %copy.11 = f32[2,256,2,256]{3,2,1,0:T(2,128)} copy(f32[2,256,2,256]{3,1,2,0:T(8,128)S(1)} %maximum_add_fusion) | data formatting | bytes 2097152 | tf_op jit(solution)/shard_map/add | solution.py:466
  (50 shorter events, 4.5 us)
Async XLA Ops:
  0.0 4.5 %copy-start = (s32[2,4]{1,0:T(2,128)S(1)}, s32[2,4]{1,0:T(2,128)}, u32[]{:S(2)}) copy-start(s32[2,4]{1,0:T(2,128)} %param.7) | copy-start | bytes 100
  1.4 9.6 %copy-start.1 = (bf16[2,256,2,512]{3,1,2,0:T(8,128)(2,1)}, bf16[2,256,2,512]{3,1,2,0:T(8,128)(2,1)S(1)}, u32[]{:S(2)}) copy-start(bf16[2,256,2,512]{3,1,2,0:T(8,128)(2,1)S(1)} %copy.14) | copy-start | bytes 3145732
  1.5 10.2 %collective-permute-start = (bf16[1,2,256,512]{3,2,1,0:T(8,128)(2,1)S(1)}, bf16[1,2,256,512]{3,2,1,0:T(8,128)(2,1)S(1)}, u32[]{:S(2)}, u32[]{:S(2)}) collective-permute-start(bf16[1,2,256,512]{3,2,1,0:T(8,128)(2,1)S(1)} %get-tuple-element.56), channel_id=1, source_target_pairs={{0,2},{1,13},{2,0},{3,15},{4,6},{5,1},{6,4},{7,3},{8,10},{9,5},{10... | collective-permute-start | bytes 1572872 | tf_op jit(solution)/shard_map/ppermute | solution.py:30
  11.0 13.9 %collective-permute-start.2 = (bf16[1,2,256,512]{3,2,1,0:T(8,128)(2,1)S(1)}, bf16[1,2,256,512]{3,2,1,0:T(8,128)(2,1)S(1)}, u32[]{:S(2)}, u32[]{:S(2)}) collective-permute-start(bf16[1,2,256,512]{3,2,1,0:T(8,128)(2,1)S(1)} %get-tuple-element.30), channel_id=1, source_target_pairs={{0,2},{1,13},{2,0},{3,15},{4,6},{5,1},{6,4},{7,3},{8,10},{9,5},{10... | collective-permute-start | bytes 1572872 | tf_op jit(solution)/shard_map/ppermute | solution.py:30
  11.7 14.9 %copy-start.4 = (bf16[1,2,256,512]{3,2,1,0:T(8,128)(2,1)}, bf16[1,2,256,512]{3,2,1,0:T(8,128)(2,1)S(1)}, u32[]{:S(2)}) copy-start(bf16[1,2,256,512]{3,2,1,0:T(8,128)(2,1)S(1)} %collective-permute-done.refs_1_) | copy-start | bytes 1572868
  11.7 15.0 %collective-permute-start.4 = (bf16[1,2,256,512]{3,2,1,0:T(8,128)(2,1)S(1)}, bf16[1,2,256,512]{3,2,1,0:T(8,128)(2,1)S(1)}, u32[]{:S(2)}, u32[]{:S(2)}) collective-permute-start(bf16[1,2,256,512]{3,2,1,0:T(8,128)(2,1)S(1)} %collective-permute-done.refs_1_), channel_id=1, source_target_pairs={{1,3},{0,12},{3,1},{2,14},{5,7},{4,0},{7,5},{6,2},{9,11},{8,4},{11... | collective-permute-start | bytes 1572872 | tf_op jit(solution)/shard_map/ppermute | solution.py:30
  24.9 4.7 %copy-start.5 = (bf16[1,2,256,512]{3,2,1,0:T(8,128)(2,1)}, bf16[1,2,256,512]{3,2,1,0:T(8,128)(2,1)S(1)}, u32[]{:S(2)}) copy-start(bf16[1,2,256,512]{3,2,1,0:T(8,128)(2,1)S(1)} %collective-permute-done.2.refs_3_) | copy-start | bytes 1572868
  24.9 3.1 %collective-permute-start.3 = (bf16[1,2,256,512]{3,2,1,0:T(8,128)(2,1)S(1)}, bf16[1,2,256,512]{3,2,1,0:T(8,128)(2,1)S(1)}, u32[]{:S(2)}, u32[]{:S(2)}) collective-permute-start(bf16[1,2,256,512]{3,2,1,0:T(8,128)(2,1)S(1)} %collective-permute-done.2.refs_3_), channel_id=1, source_target_pairs={{0,1},{1,0},{2,3},{3,2},{4,5},{5,4},{6,7},{7,6},{8,9},{9,8},{10,11... | collective-permute-start | bytes 1572872 | tf_op jit(solution)/shard_map/ppermute | solution.py:18
  26.6 2.3 %collective-permute-start.1 = (bf16[1,2,256,512]{3,2,1,0:T(8,128)(2,1)S(1)}, bf16[1,2,256,512]{3,2,1,0:T(8,128)(2,1)S(1)}, u32[]{:S(2)}, u32[]{:S(2)}) collective-permute-start(bf16[1,2,256,512]{3,2,1,0:T(8,128)(2,1)S(1)} %collective-permute-done.refs_1_), channel_id=1, source_target_pairs={{0,1},{1,0},{2,3},{3,2},{4,5},{5,4},{6,7},{7,6},{8,9},{9,8},{10,11... | collective-permute-start | bytes 1572872 | tf_op jit(solution)/shard_map/ppermute | solution.py:18
  26.6 3.0 %copy-start.6 = (bf16[1,2,256,512]{3,2,1,0:T(8,128)(2,1)}, bf16[1,2,256,512]{3,2,1,0:T(8,128)(2,1)S(1)}, u32[]{:S(2)}) copy-start(bf16[1,2,256,512]{3,2,1,0:T(8,128)(2,1)S(1)} %collective-permute-done.4.refs_5_) | copy-start | bytes 1572868
  26.6 3.0 %collective-permute-start.5 = (bf16[1,2,256,512]{3,2,1,0:T(8,128)(2,1)S(1)}, bf16[1,2,256,512]{3,2,1,0:T(8,128)(2,1)S(1)}, u32[]{:S(2)}, u32[]{:S(2)}) collective-permute-start(bf16[1,2,256,512]{3,2,1,0:T(8,128)(2,1)S(1)} %collective-permute-done.4.refs_5_), channel_id=1, source_target_pairs={{0,1},{1,0},{2,3},{3,2},{4,5},{5,4},{6,7},{7,6},{8,9},{9,8},{10,11... | collective-permute-start | bytes 1572872 | tf_op jit(solution)/shard_map/ppermute | solution.py:18
  28.1 1.5 %copy-start.7 = (bf16[1,2,256,512]{3,2,1,0:T(8,128)(2,1)}, bf16[1,2,256,512]{3,2,1,0:T(8,128)(2,1)S(1)}, u32[]{:S(2)}) copy-start(bf16[1,2,256,512]{3,2,1,0:T(8,128)(2,1)S(1)} %collective-permute-done.3.refs_4_) | copy-start | bytes 1572868
  29.6 0.9 %copy-start.9 = (bf16[1,2,256,512]{3,2,1,0:T(8,128)(2,1)}, bf16[1,2,256,512]{3,2,1,0:T(8,128)(2,1)S(1)}, u32[]{:S(2)}) copy-start(bf16[1,2,256,512]{3,2,1,0:T(8,128)(2,1)S(1)} %collective-permute-done.5.refs_6_) | copy-start | bytes 1572868
  45.9 5.0 %copy-start.3 = (bf16[1,2,256,512]{3,2,1,0:T(8,128)(2,1)S(1)}, bf16[1,2,256,512]{3,2,1,0:T(8,128)(2,1)}, u32[]{:S(2)}) copy-start(bf16[1,2,256,512]{3,2,1,0:T(8,128)(2,1)} %get-tuple-element.42) | copy-start | bytes 1572868
  45.9 2.2 %collective-permute-start.6 = (bf16[1,2,256,512]{3,2,1,0:T(8,128)(2,1)}, bf16[1,2,256,512]{3,2,1,0:T(8,128)(2,1)S(1)}, u32[]{:S(2)}, u32[]{:S(2)}) collective-permute-start(bf16[1,2,256,512]{3,2,1,0:T(8,128)(2,1)} %get-tuple-element.39), channel_id=1, source_target_pairs={{0,1},{1,0},{2,3},{3,2},{4,5},{5,4},{6,7},{7,6},{8,9},{9,8},{10,11... | collective-permute-start | bytes 1572872 | tf_op jit(solution)/shard_map/ppermute | solution.py:18
  46.2 3.5 %collective-permute-start.8 = (bf16[1,2,256,512]{3,2,1,0:T(8,128)(2,1)}, bf16[1,2,256,512]{3,2,1,0:T(8,128)(2,1)S(1)}, u32[]{:S(2)}, u32[]{:S(2)}) collective-permute-start(bf16[1,2,256,512]{3,2,1,0:T(8,128)(2,1)} %get-tuple-element.41), channel_id=1, source_target_pairs={{0,1},{1,0},{2,3},{3,2},{4,5},{5,4},{6,7},{7,6},{8,9},{9,8},{10,11... | collective-permute-start | bytes 1572872 | tf_op jit(solution)/shard_map/ppermute | solution.py:18
  46.5 4.4 %collective-permute-start.9 = (bf16[1,2,256,512]{3,2,1,0:T(8,128)(2,1)}, bf16[1,2,256,512]{3,2,1,0:T(8,128)(2,1)S(1)}, u32[]{:S(2)}, u32[]{:S(2)}) collective-permute-start(bf16[1,2,256,512]{3,2,1,0:T(8,128)(2,1)} %get-tuple-element.43), channel_id=1, source_target_pairs={{0,1},{1,0},{2,3},{3,2},{4,5},{5,4},{6,7},{7,6},{8,9},{9,8},{10,11... | collective-permute-start | bytes 1572872 | tf_op jit(solution)/shard_map/ppermute | solution.py:18
  46.7 15.9 %collective-permute-start.11 = (bf16[2,2,256,256]{3,2,1,0:T(8,128)(2,1)}, bf16[2,2,256,256]{3,2,1,0:T(8,128)(2,1)S(1)}, u32[]{:S(2)}, u32[]{:S(2)}) collective-permute-start(bf16[2,2,256,256]{3,2,1,0:T(8,128)(2,1)} %get-tuple-element.46), channel_id=1, source_target_pairs={{0,1},{1,0},{2,3},{3,2},{4,5},{5,4},{6,7},{7,6},{8,9},{9,8},{10,11... | collective-permute-start | bytes 1572872 | tf_op jit(solution)/shard_map/ppermute | solution.py:18
  49.3 11.0 %collective-permute-start.7 = (bf16[1,2,256,512]{3,2,1,0:T(8,128)(2,1)S(1)}, bf16[1,2,256,512]{3,2,1,0:T(8,128)(2,1)S(1)}, u32[]{:S(2)}, u32[]{:S(2)}) collective-permute-start(bf16[1,2,256,512]{3,2,1,0:T(8,128)(2,1)S(1)} %add_convert_fusion.2), channel_id=1, source_target_pairs={{1,3},{0,4},{3,1},{2,6},{5,7},{4,8},{7,5},{6,10},{9,11},{8,12},{11... | collective-permute-start | bytes 1572872 | tf_op jit(solution)/shard_map/ppermute | solution.py:30
  50.9 11.7 %copy-start.2 = (bf16[2,2,256,256]{3,2,1,0:T(8,128)(2,1)S(1)}, bf16[2,2,256,256]{3,2,1,0:T(8,128)(2,1)}, u32[]{:S(2)}) copy-start(bf16[2,2,256,256]{3,2,1,0:T(8,128)(2,1)} %get-tuple-element.45) | copy-start | bytes 1572868
  60.5 9.3 %collective-permute-start.12 = (bf16[1,2,256,512]{3,2,1,0:T(8,128)(2,1)S(1)}, bf16[1,2,256,512]{3,2,1,0:T(8,128)(2,1)}, u32[]{:S(2)}, u32[]{:S(2)}) collective-permute-start(bf16[1,2,256,512]{3,2,1,0:T(8,128)(2,1)S(1)} %add_convert_fusion), channel_id=1, source_target_pairs={{0,2},{1,5},{2,0},{3,7},{4,6},{5,9},{6,4},{7,11},{8,10},{9,13},{10... | collective-permute-start | bytes 1572872 | tf_op jit(solution)/shard_map/ppermute | solution.py:30
  62.5 13.0 %collective-permute-start.10 = (bf16[1,2,256,512]{3,2,1,0:T(8,128)(2,1)S(1)}, bf16[1,2,256,512]{3,2,1,0:T(8,128)(2,1)}, u32[]{:S(2)}, u32[]{:S(2)}) collective-permute-start(bf16[1,2,256,512]{3,2,1,0:T(8,128)(2,1)S(1)} %add_convert_fusion.1), channel_id=1, source_target_pairs={{0,2},{1,5},{2,0},{3,7},{4,6},{5,9},{6,4},{7,11},{8,10},{9,13},{10... | collective-permute-start | bytes 1572872 | tf_op jit(solution)/shard_map/ppermute | solution.py:30
  70.8 5.7 %collective-permute-start.13 = (bf16[1,2,256,256]{3,2,1,0:T(8,128)(2,1)S(1)}, bf16[1,2,256,256]{3,2,1,0:T(8,128)(2,1)S(1)}, u32[]{:S(2)}, u32[]{:S(2)}) collective-permute-start(bf16[1,2,256,256]{3,2,1,0:T(8,128)(2,1)S(1)} %constant_dynamic-slice_fusion.1), channel_id=1, source_target_pairs={{0,1},{1,0},{2,3},{3,2},{4,5},{5,4},{6,7},{7,6},{8,9},{9,8},{10,11... | collective-permute-start | bytes 786440 | tf_op jit(solution)/shard_map/ppermute | solution.py:18
  76.4 1.6 %collective-permute-start.14 = (bf16[1,2,256,256]{3,2,1,0:T(8,128)(2,1)S(1)}, bf16[1,2,256,256]{3,2,1,0:T(8,128)(2,1)S(1)}, u32[]{:S(2)}, u32[]{:S(2)}) collective-permute-start(bf16[1,2,256,256]{3,2,1,0:T(8,128)(2,1)S(1)} %constant_dynamic-slice_fusion), channel_id=1, source_target_pairs={{0,1},{1,0},{2,3},{3,2},{4,5},{5,4},{6,7},{7,6},{8,9},{9,8},{10,11... | collective-permute-start | bytes 786440 | tf_op jit(solution)/shard_map/ppermute | solution.py:18
  (1 other events, 0.8 us)

commit v6 on v4

--- a/solution.py
+++ b/solution.py
@@ -10,7 +10,7 @@
 from jax.experimental.pallas import tpu as pltpu
 from jax.sharding import PartitionSpec as P
 
-VMEM_LIMIT = 58 * 1024 * 1024
+VMEM_LIMIT = 38 * 1024 * 1024
 
 
 def passed(array, axis, by):
@@ -47,7 +47,7 @@
     return rounded(np.stack([stack, stack.transpose(0, 2, 1)]))
 
 
-def prep_kernel(mine, pix, info, base, probe, measured, lefts, rights, psi0, light):
+def prep_kernel(mine, pix, info, base, probe, measured, lefts, rights, psi0, light, masks):
     bf16, f32 = jnp.bfloat16, jnp.float32
     mid = pix // 2
 
@@ -97,6 +97,13 @@
             plane = probe[:, part * pix : (part + 1) * pix].astype(f32)
             plane = pltpu.roll(pltpu.roll(plane, r0, 0), c0, 1)
             psi0[m, part] = plane.astype(bf16)
+        for below in range(2):
+            rows = (row_at < r0) if below else (row_at >= r0)
+            for col in range(2):
+                low = jnp.where(info[3 + 4 * m] == col, c0, 0)
+                high = jnp.where(info[3 + 4 * m] == col, pix, c0)
+                inside = rows & (col_at >= low) & (col_at < high)
+                masks[m, below, col] = jnp.where(inside, 1.0, 0.0).astype(bf16)
         seen = measured[info[0] * mine + m]
         seen = exact(seen, lambda v: jnp.dot(pick_rows, v, preferred_element_type=f32))
         light[m] = exact(seen, lambda v: jnp.dot(v, pick_cols, preferred_element_type=f32))
@@ -105,10 +112,10 @@
 def main_kernel(groups, depth, mine, pix, pieces, results, info, *refs):
     count = len(pieces) + 1
     own, operands = refs[0], refs[1:count]
-    lefts_any, rights_any, psi0_any, light_any = refs[count : count + 4]
-    outs = refs[count + 4 : count + 4 + len(results)]
-    own_out = refs[count + 4 + len(results)]
-    obj, tp, psi, lefts, rights, light, grads, sems, tab_sems, out_sems = refs[count + 5 + len(results) :]
+    lefts_any, rights_any, psi0_any, light_any, masks_any = refs[count : count + 5]
+    outs = refs[count + 5 : count + 5 + len(results)]
+    own_out = refs[count + 5 + len(results)]
+    obj, tp, psi, lefts, rights, light, masks, grads, sems, tab_sems, out_sems = refs[count + 6 + len(results) :]
     layers = groups * depth
     half = depth // 2
     rank = info[0]
@@ -131,7 +138,9 @@
 
     psi_copy = pltpu.make_async_copy(psi0_any, psi.at[0], tab_sems.at[4, 0])
     light_copy = pltpu.make_async_copy(light_any, light, tab_sems.at[4, 1])
+    mask_copy = pltpu.make_async_copy(masks_any, masks, tab_sems.at[5, 0])
     psi_copy.start()
+    mask_copy.start()
     for copy in table_copies(1) + table_copies(3):
         copy.start()
     for i in range(depth):
@@ -157,22 +166,17 @@
         for below in range(2):
             pltpu.make_async_copy(own.at[0], obj.at[j, below], sems.at[j, below]).wait()
 
-    row_at = lax.broadcasted_iota(jnp.int32, (pix, pix), 0)
-    col_at = lax.broadcasted_iota(jnp.int32, (pix, pix), 1)
-    r0 = [info[2 + 4 * m] for m in members]
-    q = [info[3 + 4 * m] for m in members]
-    c0 = [info[4 + 4 * m] for m in members]
     live = [info[5 + 4 * m].astype(jnp.float32) for m in members]
     f32 = jnp.float32
     bf16 = jnp.bfloat16
 
     def patch(j, m, part):
-        right = col_at >= c0[m]
-        at = pl.ds(pl.multiple_of(q[m] * pix, pix), pix)
-        after = pl.ds(pl.multiple_of((1 - q[m]) * pix, pix), pix)
-        here = jnp.where(right, obj[j, 0, part, :, at].astype(f32), obj[j, 0, part, :, after].astype(f32))
-        there = jnp.where(right, obj[j, 1, part, :, at].astype(f32), obj[j, 1, part, :, after].astype(f32))
-        return jnp.where(row_at >= r0[m], here, there).astype(bf16)
+        total = None
+        for below in range(2):
+            for col in range(2):
+                term = obj[j, below, part, :, col * pix : (col + 1) * pix] * masks[m, below, col]
+                total = term if total is None else total + term
+        return total
 
     mid = pix // 2
     cat = lambda parts, axis: jnp.concatenate(parts, axis=axis)
@@ -220,12 +224,12 @@
             tr, ti = patch(j, m, 0), patch(j, m, 1)
             tp[j, m, 0] = tr
             tp[j, m, 1] = ti
-            tr, ti = tr.astype(f32), ti.astype(f32)
-            pr, pi = psi[j, m, 0].astype(f32), psi[j, m, 1].astype(f32)
-            pairs.append((tr * pr - ti * pi, tr * pi + ti * pr))
+            pr, pi = psi[j, m, 0], psi[j, m, 1]
+            pairs.append(((tr * pr - ti * pi).astype(f32), (tr * pi + ti * pr).astype(f32)))
         return pairs
 
     psi_copy.wait()
+    mask_copy.wait()
     wait_tables(1)
     wait_tables(3)
 
@@ -279,27 +283,25 @@
         place = step * depth + within
         terms = []
         for m, (re, im) in enumerate(exits):
-            pr, pi = psi[j, m, 0].astype(f32), psi[j, m, 1].astype(f32)
+            re, im = re.astype(bf16), im.astype(bf16)
+            pr, pi = psi[j, m, 0], psi[j, m, 1]
             terms.append((pr * re + pi * im, pr * im - pi * re))
         for below in range(2):
             for col in range(2):
                 for part in range(2):
                     total = None
                     for m in members:
-                        rows = (row_at < r0[m]) if below else (row_at >= r0[m])
-                        low = jnp.where(q[m] == col, c0[m], 0)
-                        high = jnp.where(q[m] == col, pix, c0[m])
-                        mask = rows & (col_at >= low) & (col_at < high)
-                        term = jnp.where(mask, terms[m][part], 0.0)
+                        term = terms[m][part] * masks[m, below, col]
                         total = term if total is None else total + term
-                    grads[below, place, part, :, col * pix : (col + 1) * pix] = total.astype(bf16)
+                    grads[below, place, part, :, col * pix : (col + 1) * pix] = total
         send_out(step, within)
 
     def wave_grads(j, exits):
         pairs = []
         for m, (re, im) in enumerate(exits):
-            tr, ti = tp[j, m, 0].astype(f32), tp[j, m, 1].astype(f32)
-            pairs.append((tr * re + ti * im, tr * im - ti * re))
+            re, im = re.astype(bf16), im.astype(bf16)
+            tr, ti = tp[j, m, 0], tp[j, m, 1]
+            pairs.append(((tr * re + ti * im).astype(f32), (tr * im - ti * re).astype(f32)))
         return pairs
 
     wait_tables(2)
@@ -350,23 +352,24 @@
     vmem = pl.BlockSpec(memory_space=pltpu.VMEM)
     anywhere = pl.BlockSpec(memory_space=pl.ANY)
     tables_shape = jax.ShapeDtypeStruct((mine, 4, 2, pix, pix), bf16)
-    lefts, rights, psi0, light = pl.pallas_call(
+    lefts, rights, psi0, light, masks = pl.pallas_call(
         functools.partial(prep_kernel, mine, pix),
         out_shape=(
             tables_shape,
             tables_shape,
             jax.ShapeDtypeStruct((mine, 2, pix, pix), bf16),
             jax.ShapeDtypeStruct((mine, pix, pix), jnp.float32),
+            jax.ShapeDtypeStruct((mine, 2, 2, pix, pix), bf16),
         ),
         in_specs=[smem, vmem, vmem, vmem],
-        out_specs=(vmem,) * 4,
+        out_specs=(vmem,) * 5,
         compiler_params=pltpu.CompilerParams(vmem_limit_bytes=VMEM_LIMIT),
         cost_estimate=pl.CostEstimate(flops=8 * 10**9, bytes_accessed=8 * 2**20, transcendentals=0),
         name="tables",
     )(info, jnp.asarray(base_tables(pix)), probe_wave, measured)
 
-    got_first, lefts, rights, psi0, light = lax.optimization_barrier(
-        (got_first, lefts, rights, psi0, light)
+    got_first, lefts, rights, psi0, light, masks = lax.optimization_barrier(
+        (got_first, lefts, rights, psi0, light, masks)
     )
     passed_on = [split_roles(got_first[s - 1], -1, s, 1) for s in steps]
     pieces, operands = [], []
@@ -389,7 +392,7 @@
     *outs, own_grads = pl.pallas_call(
         functools.partial(main_kernel, groups, depth, mine, pix, tuple(pieces), tuple(results)),
         out_shape=(half_shape,) * len(results) + (jax.ShapeDtypeStruct((depth, 2, rows, cols), bf16),),
-        in_specs=[smem] + [anywhere] * (5 + len(operands)),
+        in_specs=[smem] + [anywhere] * (6 + len(operands)),
         out_specs=(anywhere,) * (len(results) + 1),
         scratch_shapes=[
             pltpu.VMEM((layers, 2, 2, pix, cols), bf16),
@@ -398,15 +401,16 @@
             pltpu.VMEM((mine, 4, 2, pix, pix), bf16),
             pltpu.VMEM((mine, 4, 2, pix, pix), bf16),
             pltpu.VMEM((mine, pix, pix), jnp.float32),
+            pltpu.VMEM((mine, 2, 2, pix, pix), bf16),
             pltpu.VMEM((2, layers, 2, pix, cols), bf16),
             pltpu.SemaphoreType.DMA((layers, 2)),
-            pltpu.SemaphoreType.DMA((5, 2)),
+            pltpu.SemaphoreType.DMA((6, 2)),
             pltpu.SemaphoreType.DMA((2, layers)),
         ],
         compiler_params=pltpu.CompilerParams(vmem_limit_bytes=VMEM_LIMIT),
         cost_estimate=pl.CostEstimate(flops=15 * 10**9, bytes_accessed=16 * 2**20, transcendentals=0),
         name="waves",
-    )(info, planes, *operands, lefts, rights, psi0, light)
+    )(info, planes, *operands, lefts, rights, psi0, light, masks)
 
     wide = lambda v: v.astype(jnp.float32)
     kept = lambda s, which: wide(outs[6 * (s - 1) + 2 * which])

time: 77.6 us -> 74 us (0.954)
  Pallas kernels: 22.5 us -> 15.7 us
  waiting for transfers between devices: 26.8 us -> 32.1 us
  starting transfers between devices: 15.7 us -> 10.5 us
  local copies, waits for them, and re-layouts: 6 us -> 10.8 us
  other arithmetic: 5.4 us -> 3.88 us
    ppermute x6, waiting for transfers between devices: 21.7 us -> 26.8 us  [split_roles(): return lax.ppermute(array, ('tile', 'slc', 'pos'), pairs)]
    ppermute x6, starting transfers between devices: 14.4 us -> 9.8 us  [split_roles(): return lax.ppermute(array, ('tile', 'slc', 'pos'), pairs)]
    pallas_call x1, Pallas kernels: 15.7 us -> 11.2 us  [body(): pl.pallas_call(functools.partial(main_kernel, groups, depth, mine, pix, t...]
    unnamed x21 -> x17, local copies, waits for them, and re-layouts: 2.27 us -> 6.08 us
    pallas_call x1, Pallas kernels: 6.82 us -> 4.49 us  [body(): pl.pallas_call(functools.partial(prep_kernel, mine, pix), out_shape=(tabl...]
    convert_element_type x1, other arithmetic: 0.21 us -> 1.41 us  [body(): (lasts[s] + jnp.where(core == 1, summed, wide(back[s]))).astype(bf16)]
    convert_element_type x1, other arithmetic: 1.18 us -> 0.14 us  [body(): firsts = {s: (kept(s, 1) + twin(s, 1)).astype(bf16) for s in steps}]
    convert_element_type x1, other arithmetic: 1.18 us -> 0.14 us  [body(): rims = {s: (kept(s, 0) + twin(s, 0)).astype(bf16) for s in steps}]
  transfers between devices with their start and end apart: 14 -> 14, of which waited for: 7 -> 9; matrix products, arithmetic and copies ran while one was open for 8% -> 6% of each run, Pallas kernels for 9% -> 6%
where the time goes in v6:
time: 74 us; the launch traced here: 73.7 us
  waiting for transfers between devices  32.1 us (43%)
  Pallas kernels  15.7 us (21%)
  local copies, waits for them, and re-layouts  10.8 us (15%)
  starting transfers between devices  10.5 us (14%)
  other arithmetic  3.88 us (5%)
  between operations  0.81 us (1%)
    ppermute x6, waiting for transfers between devices, split_roles(): return lax.ppermute(array, ('tile', 'slc', 'pos'), pairs)  26.8 us
    pallas_call x1, Pallas kernels, body(): pl.pallas_call(functools.partial(main_kernel, groups, depth, mine, pix, t...  11.2 us
    ppermute x6, starting transfers between devices, split_roles(): return lax.ppermute(array, ('tile', 'slc', 'pos'), pairs)  9.8 us
    unnamed x17, local copies, waits for them, and re-layouts  6.08 us
    ppermute x8, waiting for transfers between devices, passed(): lax.ppermute(array, axis, [(i, (i + by) % peers) for i in range(peers)])  5.24 us
    pallas_call x1, Pallas kernels, body(): pl.pallas_call(functools.partial(prep_kernel, mine, pix), out_shape=(tabl...  4.49 us
    transpose x1, local copies, waits for them, and re-layouts, body(): return (early + late).transpose(0, 2, 1, 3)  1.78 us
  transfers between devices with their start and end apart: 14, of which 9 were waited for; matrix products, arithmetic and copies ran while one was open for 6% of the time, Pallas kernels for 6%

profile of v6, /device:TPU:0, one launch (start us, length us, event | category | flops | bytes accessed | tf_op | source)
XLA Modules:
  0.0 73.7 jit_solution(15881147106538337169)
XLA Ops:
  0.0 1.5 %copy.14 = bf16[2,256,2,512]{3,1,2,0:T(8,128)(2,1)S(1)} copy(bf16[2,256,2,512]{3,2,1,0:T(2,128)(2,1)} %param.6) | data formatting | bytes 2097152 | tf_op args[0]
  1.5 1.1 %dynamic-slice_bitcast_fusion = (bf16[1,2,256,512]{3,2,1,0:T(8,128)(2,1)}, bf16[1,2,256,512]{3,2,1,0:T(8,128)(2,1)}) fusion(bf16[2,256,2,512]{3,1,2,0:T(8,128)(2,1)S(1)} %copy.14, s32[]{:T(128)S(6)} %select_n.67, s32[]{:T(128)S(6)} %select_n.66), kind=kLoop, calls=%fused_computation.12 | loop fusion | bytes 2097160 | tf_op jit(solution)/shard_map/dynamic_slice | solution.py:346
  2.6 2.9 %collective-permute-start = (bf16[1,2,256,512]{3,2,1,0:T(8,128)(2,1)}, bf16[1,2,256,512]{3,2,1,0:T(8,128)(2,1)S(1)}, u32[]{:S(2)}, u32[]{:S(2)}) collective-permute-start(bf16[1,2,256,512]{3,2,1,0:T(8,128)(2,1)} %get-tuple-element.46), channel_id=1, source_target_pairs={{0,2},{1,13},{2,0},{3,15},{4,6},{5,1},{6,4},{7,3},{8,10},{9,5},{10... | collective-permute-start | bytes 1572872 | tf_op jit(solution)/shard_map/ppermute | solution.py:30
  6.6 1.4 %copy-done.5 = bf16[2,6,256,256]{3,2,1,0:T(8,128)(2,1)S(1)} copy-done((bf16[2,6,256,256]{3,2,1,0:T(8,128)(2,1)S(1)}, bf16[2,6,256,256]{3,2,1,0:T(8,128)(2,1)}, u32[]{:S(2)}) %copy-start.5) | copy-done | bytes 1572888
  8.0 4.5 %tables.1 = (bf16[2,4,2,256,256]{4,3,2,1,0:T(8,128)(2,1)S(1)}, bf16[2,4,2,256,256]{4,3,2,1,0:T(8,128)(2,1)S(1)}, bf16[2,2,256,256]{3,2,1,0:T(8,128)(2,1)S(1)}, f...) custom-call(s32[10]{0:T(128)S(1)} %pad_add_fusion.1.info, bf16[2,6,256,256]{3,2,1,0:T(8,128)(2,1)S(1)} %copy-done.5, ...), custom_call_target="tpu_custom_call" | custom-call | flops 8000000000 | bytes 8388608 | tf_op jit(solution)/shard_map/tables/pallas_call | solution.py:355
  12.9 4.1 %collective-permute-start.4 = (bf16[1,2,256,512]{3,2,1,0:T(8,128)(2,1)S(1)}, bf16[1,2,256,512]{3,2,1,0:T(8,128)(2,1)S(1)}, u32[]{:S(2)}, u32[]{:S(2)}) collective-permute-start(bf16[1,2,256,512]{3,2,1,0:T(8,128)(2,1)S(1)} %collective-permute-done.refs_1_), channel_id=1, source_target_pairs={{1,3},{0,12},{3,1},{2,14},{5,7},{4,0},{7,5},{6,2},{9,11},{8,4},{11... | collective-permute-start | bytes 1572872 | tf_op jit(solution)/shard_map/ppermute | solution.py:30
  17.0 3.1 %collective-permute-done.2.refs_3_ = bf16[1,2,256,512]{3,2,1,0:T(8,128)(2,1)S(1)} collective-permute-done((bf16[1,2,256,512]{3,2,1,0:T(8,128)(2,1)}, bf16[1,2,256,512]{3,2,1,0:T(8,128)(2,1)S(1)}, u32[]{:S(2)}, u32[]{:S(2)}) %collective-permute-start.2) | collective-permute-done | bytes 524320 | tf_op jit(solution)/shard_map/ppermute | solution.py:30
  20.1 0.8 %copy-done.2 = bf16[1,2,256,512]{3,2,1,0:T(8,128)(2,1)} copy-done((bf16[1,2,256,512]{3,2,1,0:T(8,128)(2,1)}, bf16[1,2,256,512]{3,2,1,0:T(8,128)(2,1)S(1)}, u32[]{:S(2)}) %copy-start.2) | copy-done | bytes 524312
  20.9 3.7 %collective-permute-done.4.refs_5_ = bf16[1,2,256,512]{3,2,1,0:T(8,128)(2,1)S(1)} collective-permute-done((bf16[1,2,256,512]{3,2,1,0:T(8,128)(2,1)S(1)}, bf16[1,2,256,512]{3,2,1,0:T(8,128)(2,1)S(1)}, u32[]{:S(2)}, u32[]{:S(2)}) %collective-permute-start.4) | collective-permute-done | bytes 524320 | tf_op jit(solution)/shard_map/ppermute | solution.py:30
  24.6 1.9 %collective-permute-done.5.refs_6_ = bf16[1,2,256,512]{3,2,1,0:T(8,128)(2,1)S(1)} collective-permute-done((bf16[1,2,256,512]{3,2,1,0:T(8,128)(2,1)S(1)}, bf16[1,2,256,512]{3,2,1,0:T(8,128)(2,1)S(1)}, u32[]{:S(2)}, u32[]{:S(2)}) %collective-permute-start.5) | collective-permute-done | bytes 524320 | tf_op jit(solution)/shard_map/ppermute | solution.py:18
  26.6 1.0 %copy-done.3 = bf16[1,2,256,512]{3,2,1,0:T(8,128)(2,1)S(1)} copy-done((bf16[1,2,256,512]{3,2,1,0:T(8,128)(2,1)S(1)}, bf16[1,2,256,512]{3,2,1,0:T(8,128)(2,1)}, u32[]{:S(2)}) %copy-start.3) | copy-done | bytes 524312
  27.6 11.2 %waves.1 = (bf16[1,2,256,512]{3,2,1,0:T(8,128)(2,1)S(1)}, bf16[1,2,256,512]{3,2,1,0:T(8,128)(2,1)S(1)}, bf16[1,2,256,512]{3,2,1,0:T(8,128)(2,1)S(1)}, bf16[1,2,2...) custom-call(s32[10]{0:T(128)S(1)} %pad_add_fusion.1.info, ...), custom_call_target="tpu_custom_call" | custom-call | flops 15000000512 | bytes 16777216 | tf_op jit(solution)/shard_map/waves/pallas_call | solution.py:392
  39.4 1.3 %collective-permute-done.10 = bf16[1,2,256,512]{3,2,1,0:T(8,128)(2,1)S(1)} collective-permute-done((bf16[1,2,256,512]{3,2,1,0:T(8,128)(2,1)S(1)}, bf16[1,2,256,512]{3,2,1,0:T(8,128)(2,1)S(1)}, u32[]{:S(2)}, u32[]{:S(2)}) %collective-permute-start.10) | collective-permute-done | bytes 524320 | tf_op jit(solution)/shard_map/ppermute | solution.py:18
  40.9 1.1 %collective-permute-start.11 = (bf16[1,2,256,512]{3,2,1,0:T(8,128)(2,1)S(1)}, bf16[1,2,256,512]{3,2,1,0:T(8,128)(2,1)}, u32[]{:S(2)}, u32[]{:S(2)}) collective-permute-start(bf16[1,2,256,512]{3,2,1,0:T(8,128)(2,1)S(1)} %add_convert_fusion.1), channel_id=1, source_target_pairs={{1,3},{0,4},{3,1},{2,6},{5,7},{4,8},{7,5},{6,10},{9,11},{8,12},{11... | collective-permute-start | bytes 1572872 | tf_op jit(solution)/shard_map/ppermute | solution.py:30
  42.4 0.8 %collective-permute-start.7 = (bf16[1,2,256,512]{3,2,1,0:T(8,128)(2,1)S(1)}, bf16[1,2,256,512]{3,2,1,0:T(8,128)(2,1)S(1)}, u32[]{:S(2)}, u32[]{:S(2)}) collective-permute-start(bf16[1,2,256,512]{3,2,1,0:T(8,128)(2,1)S(1)} %add_convert_fusion.2), channel_id=1, source_target_pairs={{0,2},{1,5},{2,0},{3,7},{4,6},{5,9},{6,4},{7,11},{8,10},{9,13},{10... | collective-permute-start | bytes 1572872 | tf_op jit(solution)/shard_map/ppermute | solution.py:30
  43.2 14.0 %collective-permute-done.11 = bf16[1,2,256,512]{3,2,1,0:T(8,128)(2,1)} collective-permute-done((bf16[1,2,256,512]{3,2,1,0:T(8,128)(2,1)S(1)}, bf16[1,2,256,512]{3,2,1,0:T(8,128)(2,1)}, u32[]{:S(2)}, u32[]{:S(2)}) %collective-permute-start.11) | collective-permute-done | bytes 524320 | tf_op jit(solution)/shard_map/ppermute | solution.py:30
  57.2 1.4 %add_convert_fusion = bf16[1,2,256,512]{3,2,1,0:T(8,128)(2,1)S(1)} fusion(bf16[1,2,256,512]{3,2,1,0:T(8,128)(2,1)} %collective-permute-done.11, bf16[1,2,256,512]{3,2,1,0:T(8,128)(2,1)} %collective-permute-done.9, bf16[1,2,256,512]{3,2,1,0:T(8,128)(2,1)S(1)} %get-tuple-element.37), kind=kLoop, calls=%fused_computation.5 | loop fusion | flops 1572864 | bytes 2097152 | tf_op jit(solution)/shard_map/convert_element_type | solution.py:424
  58.6 0.8 %collective-permute-start.12 = (bf16[1,2,256,512]{3,2,1,0:T(8,128)(2,1)S(1)}, bf16[1,2,256,512]{3,2,1,0:T(8,128)(2,1)S(1)}, u32[]{:S(2)}, u32[]{:S(2)}) collective-permute-start(bf16[1,2,256,512]{3,2,1,0:T(8,128)(2,1)S(1)} %add_convert_fusion), channel_id=1, source_target_pairs={{0,2},{1,5},{2,0},{3,7},{4,6},{5,9},{6,4},{7,11},{8,10},{9,13},{10... | collective-permute-start | bytes 1572872 | tf_op jit(solution)/shard_map/ppermute | solution.py:30
  59.9 1.3 %copy-done.6 = f32[2,2,256,512]{3,2,1,0:T(8,128)} copy-done((f32[2,2,256,512]{3,2,1,0:T(8,128)}, f32[2,2,256,512]{3,2,1,0:T(8,128)S(1)}, u32[]{:S(2)}) %copy-start.6) | copy-done | bytes 2097176
  61.3 0.9 %dynamic-slice_convert_fusion = bf16[2,2,256,256]{3,2,1,0:T(8,128)(2,1)} fusion(f32[2,2,256,512]{3,2,1,0:T(8,128)S(1)} %maximum_add_fusion, s32[]{:T(128)S(6)} %select_n.70), kind=kLoop, calls=%fused_computation.7 | loop fusion | bytes 1048580 | tf_op jit(solution)/shard_map/convert_element_type | solution.py:430
  62.1 5.7 %collective-permute-done.12 = bf16[1,2,256,512]{3,2,1,0:T(8,128)(2,1)S(1)} collective-permute-done((bf16[1,2,256,512]{3,2,1,0:T(8,128)(2,1)S(1)}, bf16[1,2,256,512]{3,2,1,0:T(8,128)(2,1)S(1)}, u32[]{:S(2)}, u32[]{:S(2)}) %collective-permute-start.12) | collective-permute-done | bytes 524320 | tf_op jit(solution)/shard_map/ppermute | solution.py:30
  68.7 1.7 %collective-permute-done.13 = bf16[1,2,256,256]{3,2,1,0:T(8,128)(2,1)S(1)} collective-permute-done((bf16[1,2,256,256]{3,2,1,0:T(8,128)(2,1)}, bf16[1,2,256,256]{3,2,1,0:T(8,128)(2,1)S(1)}, u32[]{:S(2)}, u32[]{:S(2)}) %collective-permute-start.13) | collective-permute-done | bytes 262176 | tf_op jit(solution)/shard_map/ppermute | solution.py:18
  70.6 1.3 %fusion = f32[2,256,2,256]{3,1,2,0:T(8,128)S(1)} fusion(f32[1,2,256,256]{3,2,1,0:T(8,128)S(1)} %get-tuple-element.44, f32[1,2,256,256]{3,2,1,0:T(8,128)S(1)} %get-tuple-element.43, bf16[2,2,256,256]{3,2,1,0:T(8,128)(2,1)} %collective-permute-done.8, f32[2,2,256,512]{3,2,1,0:T(8,128)S(1)} %copy-done.7, s32[]{:T(128)S(6)} %select_n.69), kind=kLoop, calls=%fused_computation.4 | loop fusion | flops 1048576 | bytes 3670020 | tf_op jit(solution)/shard_map/transpose | solution.py:434
  71.9 1.8 %copy.11 = f32[2,256,2,256]{3,2,1,0:T(2,128)} copy(f32[2,256,2,256]{3,1,2,0:T(8,128)S(1)} %fusion) | data formatting | bytes 2097152 | tf_op jit(solution)/shard_map/transpose | solution.py:434
  (44 shorter events, 3.5 us)
Async XLA Ops:
  0.0 5.6 %copy-start = (s32[2,4]{1,0:T(2,128)S(1)}, s32[2,4]{1,0:T(2,128)}, u32[]{:S(2)}) copy-start(s32[2,4]{1,0:T(2,128)} %param.7) | copy-start | bytes 100
  0.0 6.6 %copy-start.1 = (f32[4,256,256]{2,1,0:T(8,128)S(1)}, f32[4,256,256]{2,1,0:T(8,128)}, u32[]{:S(2)}) copy-start(f32[4,256,256]{2,1,0:T(8,128)} %measured.1) | copy-start | bytes 3145732
  0.0 6.6 %copy-start.4 = (bf16[256,512]{1,0:T(8,128)(2,1)S(1)}, bf16[256,512]{1,0:T(8,128)(2,1)}, u32[]{:S(2)}) copy-start(bf16[256,512]{1,0:T(8,128)(2,1)} %probe.1) | copy-start | bytes 786436
  2.6 10.3 %collective-permute-start = (bf16[1,2,256,512]{3,2,1,0:T(8,128)(2,1)}, bf16[1,2,256,512]{3,2,1,0:T(8,128)(2,1)S(1)}, u32[]{:S(2)}, u32[]{:S(2)}) collective-permute-start(bf16[1,2,256,512]{3,2,1,0:T(8,128)(2,1)} %get-tuple-element.46), channel_id=1, source_target_pairs={{0,2},{1,13},{2,0},{3,15},{4,6},{5,1},{6,4},{7,3},{8,10},{9,5},{10... | collective-permute-start | bytes 1572872 | tf_op jit(solution)/shard_map/ppermute | solution.py:30
  5.5 14.6 %collective-permute-start.2 = (bf16[1,2,256,512]{3,2,1,0:T(8,128)(2,1)}, bf16[1,2,256,512]{3,2,1,0:T(8,128)(2,1)S(1)}, u32[]{:S(2)}, u32[]{:S(2)}) collective-permute-start(bf16[1,2,256,512]{3,2,1,0:T(8,128)(2,1)} %get-tuple-element.45), channel_id=1, source_target_pairs={{0,2},{1,13},{2,0},{3,15},{4,6},{5,1},{6,4},{7,3},{8,10},{9,5},{10... | collective-permute-start | bytes 1572872 | tf_op jit(solution)/shard_map/ppermute | solution.py:30
  6.6 1.4 %copy-start.5 = (bf16[2,6,256,256]{3,2,1,0:T(8,128)(2,1)S(1)}, bf16[2,6,256,256]{3,2,1,0:T(8,128)(2,1)}, u32[]{:S(2)}) copy-start(bf16[2,6,256,256]{3,2,1,0:T(8,128)(2,1)} %constant.55.clone.base) | copy-start | bytes 4718596
  12.9 11.8 %collective-permute-start.4 = (bf16[1,2,256,512]{3,2,1,0:T(8,128)(2,1)S(1)}, bf16[1,2,256,512]{3,2,1,0:T(8,128)(2,1)S(1)}, u32[]{:S(2)}, u32[]{:S(2)}) collective-permute-start(bf16[1,2,256,512]{3,2,1,0:T(8,128)(2,1)S(1)} %collective-permute-done.refs_1_), channel_id=1, source_target_pairs={{1,3},{0,12},{3,1},{2,14},{5,7},{4,0},{7,5},{6,2},{9,11},{8,4},{11... | collective-permute-start | bytes 1572872 | tf_op jit(solution)/shard_map/ppermute | solution.py:30
  17.0 7.6 %collective-permute-start.1 = (bf16[1,2,256,512]{3,2,1,0:T(8,128)(2,1)S(1)}, bf16[1,2,256,512]{3,2,1,0:T(8,128)(2,1)S(1)}, u32[]{:S(2)}, u32[]{:S(2)}) collective-permute-start(bf16[1,2,256,512]{3,2,1,0:T(8,128)(2,1)S(1)} %collective-permute-done.refs_1_), channel_id=1, source_target_pairs={{0,1},{1,0},{2,3},{3,2},{4,5},{5,4},{6,7},{7,6},{8,9},{9,8},{10,11... | collective-permute-start | bytes 1572872 | tf_op jit(solution)/shard_map/ppermute | solution.py:18
  20.1 4.5 %collective-permute-start.3 = (bf16[1,2,256,512]{3,2,1,0:T(8,128)(2,1)S(1)}, bf16[1,2,256,512]{3,2,1,0:T(8,128)(2,1)S(1)}, u32[]{:S(2)}, u32[]{:S(2)}) collective-permute-start(bf16[1,2,256,512]{3,2,1,0:T(8,128)(2,1)S(1)} %collective-permute-done.2.refs_3_), channel_id=1, source_target_pairs={{0,1},{1,0},{2,3},{3,2},{4,5},{5,4},{6,7},{7,6},{8,9},{9,8},{10,11... | collective-permute-start | bytes 1572872 | tf_op jit(solution)/shard_map/ppermute | solution.py:18
  20.1 0.8 %copy-start.2 = (bf16[1,2,256,512]{3,2,1,0:T(8,128)(2,1)}, bf16[1,2,256,512]{3,2,1,0:T(8,128)(2,1)S(1)}, u32[]{:S(2)}) copy-start(bf16[1,2,256,512]{3,2,1,0:T(8,128)(2,1)S(1)} %collective-permute-done.2.refs_3_) | copy-start | bytes 1572868
  24.6 1.9 %collective-permute-start.5 = (bf16[1,2,256,512]{3,2,1,0:T(8,128)(2,1)S(1)}, bf16[1,2,256,512]{3,2,1,0:T(8,128)(2,1)S(1)}, u32[]{:S(2)}, u32[]{:S(2)}) collective-permute-start(bf16[1,2,256,512]{3,2,1,0:T(8,128)(2,1)S(1)} %collective-permute-done.4.refs_5_), channel_id=1, source_target_pairs={{0,1},{1,0},{2,3},{3,2},{4,5},{5,4},{6,7},{7,6},{8,9},{9,8},{10,11... | collective-permute-start | bytes 1572872 | tf_op jit(solution)/shard_map/ppermute | solution.py:18
  26.5 1.0 %copy-start.3 = (bf16[1,2,256,512]{3,2,1,0:T(8,128)(2,1)S(1)}, bf16[1,2,256,512]{3,2,1,0:T(8,128)(2,1)}, u32[]{:S(2)}) copy-start(bf16[1,2,256,512]{3,2,1,0:T(8,128)(2,1)} %copy-done.2) | copy-start | bytes 1572868
  38.8 2.0 %collective-permute-start.10 = (bf16[1,2,256,512]{3,2,1,0:T(8,128)(2,1)S(1)}, bf16[1,2,256,512]{3,2,1,0:T(8,128)(2,1)S(1)}, u32[]{:S(2)}, u32[]{:S(2)}) collective-permute-start(bf16[1,2,256,512]{3,2,1,0:T(8,128)(2,1)S(1)} %get-tuple-element.40), channel_id=1, source_target_pairs={{0,1},{1,0},{2,3},{3,2},{4,5},{5,4},{6,7},{7,6},{8,9},{9,8},{10,11... | collective-permute-start | bytes 1572872 | tf_op jit(solution)/shard_map/ppermute | solution.py:18
  38.9 3.4 %collective-permute-start.6 = (bf16[1,2,256,512]{3,2,1,0:T(8,128)(2,1)S(1)}, bf16[1,2,256,512]{3,2,1,0:T(8,128)(2,1)S(1)}, u32[]{:S(2)}, u32[]{:S(2)}) collective-permute-start(bf16[1,2,256,512]{3,2,1,0:T(8,128)(2,1)S(1)} %get-tuple-element.36), channel_id=1, source_target_pairs={{0,1},{1,0},{2,3},{3,2},{4,5},{5,4},{6,7},{7,6},{8,9},{9,8},{10,11... | collective-permute-start | bytes 1572872 | tf_op jit(solution)/shard_map/ppermute | solution.py:18
  39.4 3.9 %collective-permute-start.9 = (bf16[1,2,256,512]{3,2,1,0:T(8,128)(2,1)}, bf16[1,2,256,512]{3,2,1,0:T(8,128)(2,1)}, u32[]{:S(2)}, u32[]{:S(2)}) collective-permute-start(bf16[1,2,256,512]{3,2,1,0:T(8,128)(2,1)} %get-tuple-element.38), channel_id=1, source_target_pairs={{0,1},{1,0},{2,3},{3,2},{4,5},{5,4},{6,7},{7,6},{8,9},{9,8},{10,11... | collective-permute-start | bytes 1572872 | tf_op jit(solution)/shard_map/ppermute | solution.py:18
  40.9 16.3 %collective-permute-start.11 = (bf16[1,2,256,512]{3,2,1,0:T(8,128)(2,1)S(1)}, bf16[1,2,256,512]{3,2,1,0:T(8,128)(2,1)}, u32[]{:S(2)}, u32[]{:S(2)}) collective-permute-start(bf16[1,2,256,512]{3,2,1,0:T(8,128)(2,1)S(1)} %add_convert_fusion.1), channel_id=1, source_target_pairs={{1,3},{0,4},{3,1},{2,6},{5,7},{4,8},{7,5},{6,10},{9,11},{8,12},{11... | collective-permute-start | bytes 1572872 | tf_op jit(solution)/shard_map/ppermute | solution.py:30
  42.4 17.0 %collective-permute-start.7 = (bf16[1,2,256,512]{3,2,1,0:T(8,128)(2,1)S(1)}, bf16[1,2,256,512]{3,2,1,0:T(8,128)(2,1)S(1)}, u32[]{:S(2)}, u32[]{:S(2)}) collective-permute-start(bf16[1,2,256,512]{3,2,1,0:T(8,128)(2,1)S(1)} %add_convert_fusion.2), channel_id=1, source_target_pairs={{0,2},{1,5},{2,0},{3,7},{4,6},{5,9},{6,4},{7,11},{8,10},{9,13},{10... | collective-permute-start | bytes 1572872 | tf_op jit(solution)/shard_map/ppermute | solution.py:30
  58.6 9.2 %collective-permute-start.12 = (bf16[1,2,256,512]{3,2,1,0:T(8,128)(2,1)S(1)}, bf16[1,2,256,512]{3,2,1,0:T(8,128)(2,1)S(1)}, u32[]{:S(2)}, u32[]{:S(2)}) collective-permute-start(bf16[1,2,256,512]{3,2,1,0:T(8,128)(2,1)S(1)} %add_convert_fusion), channel_id=1, source_target_pairs={{0,2},{1,5},{2,0},{3,7},{4,6},{5,9},{6,4},{7,11},{8,10},{9,13},{10... | collective-permute-start | bytes 1572872 | tf_op jit(solution)/shard_map/ppermute | solution.py:30
  59.9 1.3 %copy-start.6 = (f32[2,2,256,512]{3,2,1,0:T(8,128)}, f32[2,2,256,512]{3,2,1,0:T(8,128)S(1)}, u32[]{:S(2)}) copy-start(f32[2,2,256,512]{3,2,1,0:T(8,128)S(1)} %maximum_add_fusion) | copy-start | bytes 6291460
  62.1 8.5 %copy-start.7 = (f32[2,2,256,512]{3,2,1,0:T(8,128)S(1)}, f32[2,2,256,512]{3,2,1,0:T(8,128)}, u32[]{:S(2)}) copy-start(f32[2,2,256,512]{3,2,1,0:T(8,128)} %copy-done.6) | copy-start | bytes 6291460
  62.1 8.4 %collective-permute-start.8 = (bf16[2,2,256,256]{3,2,1,0:T(8,128)(2,1)}, bf16[2,2,256,256]{3,2,1,0:T(8,128)(2,1)}, u32[]{:S(2)}, u32[]{:S(2)}) collective-permute-start(bf16[2,2,256,256]{3,2,1,0:T(8,128)(2,1)} %dynamic-slice_convert_fusion), channel_id=1, source_target_pairs={{0,1},{1,0},{2,3},{3,2},{4,5},{5,4},{6,7},{7,6},{8,9},{9,8},{10,11... | collective-permute-start | bytes 1572872 | tf_op jit(solution)/shard_map/ppermute | solution.py:18
  68.7 1.7 %collective-permute-start.13 = (bf16[1,2,256,256]{3,2,1,0:T(8,128)(2,1)}, bf16[1,2,256,256]{3,2,1,0:T(8,128)(2,1)S(1)}, u32[]{:S(2)}, u32[]{:S(2)}) collective-permute-start(bf16[1,2,256,256]{3,2,1,0:T(8,128)(2,1)} %dynamic-slice_convert_fusion.1), channel_id=1, source_target_pairs={{0,1},{1,0},{2,3},{3,2},{4,5},{5,4},{6,7},{7,6},{8,9},{9,8},{10,11... | collective-permute-start | bytes 786440 | tf_op jit(solution)/shard_map/ppermute | solution.py:18

commit v7 on v6

--- a/solution.py
+++ b/solution.py
@@ -109,13 +109,12 @@
         light[m] = exact(seen, lambda v: jnp.dot(v, pick_cols, preferred_element_type=f32))
 
 
-def main_kernel(groups, depth, mine, pix, pieces, results, info, *refs):
+def main_kernel(groups, depth, mine, pix, pieces, info, *refs):
     count = len(pieces) + 1
     own, operands = refs[0], refs[1:count]
     lefts_any, rights_any, psi0_any, light_any, masks_any = refs[count : count + 5]
-    outs = refs[count + 5 : count + 5 + len(results)]
-    own_out = refs[count + 5 + len(results)]
-    obj, tp, psi, lefts, rights, light, masks, grads, sems, tab_sems, out_sems = refs[count + 6 + len(results) :]
+    outs = refs[count + 5 : count + 5 + 4 * groups]
+    obj, tp, psi, lefts, rights, light, masks, grads, sems, tab_sems, out_sems = refs[count + 5 + 4 * groups :]
     layers = groups * depth
     half = depth // 2
     rank = info[0]
@@ -256,26 +255,24 @@
         tilted.append(tuple(scaled))
     exits = wave_of(tilted)
 
-    def out_copy(below, place, out):
-        return pltpu.make_async_copy(grads.at[below, place], out, out_sems.at[below, place])
+    def out_copies(s, i):
+        place = s * depth + i
+        copies = []
+        for away in range(2):
+            at = pl.multiple_of(((1 - core) if away else core) * pix, pix)
+            for below in range(2):
+                out = outs[(away * 2 + below) * groups + s]
+                columns = grads.at[below, place, :, :, pl.ds(at, pix)]
+                copies.append(pltpu.make_async_copy(columns, out.at[i], out_sems.at[away * 2 + below, place]))
+        return copies
 
     def send_out(step, within):
-        place = step * depth + within
-
-        @pl.when(step == 0)
-        def _():
-            out_copy(0, place, own_out.at[within]).start()
-
-        for takes, ref in zip(results, outs):
-            for c in range(2):
-                if takes[c] is None:
-                    continue
-                s, high, below = takes[c]
-                inside = (within >= half) if high else (within < half)
-
-                @pl.when((core == c) & (step == s) & inside)
-                def _():
-                    out_copy(below, place, ref.at[within - high * half]).start()
+        for s in range(groups):
+
+            @pl.when(step == s)
+            def _():
+                for copy in out_copies(s, within):
+                    copy.start()
 
     def scatter(j, exits):
         step = lax.rem(rank - j // depth + groups, groups)
@@ -316,9 +313,10 @@
 
     hold = lax.fori_loop(0, layers - 1, backward, hold)
     scatter(0, [(hold[2 * m], hold[2 * m + 1]) for m in members])
-    for below in range(2):
-        for place in range(layers):
-            out_copy(below, place, own_out.at[0]).wait()
+    for s in range(groups):
+        for i in range(depth):
+            for copy in out_copies(s, i):
+                copy.wait()
 
 
 def body(object_field, offsets, counts, measured, probe_wave):
@@ -382,18 +380,12 @@
         ):
             pieces += [holds, holds[::-1]]
             operands += [array, passed(array, "pos", 1)]
-    results = []
-    for s in steps:
-        rim_hi, rim_lo = ((0, 1, 1), (0, 0, 1)) if s == 1 else (None, None)
-        for holds in (((s, 1, 1), (s, 0, 1)), ((s, 0, 0), rim_hi), ((s, 1, 0), rim_lo)):
-            results += [holds, holds[::-1]]
-
-    half_shape = jax.ShapeDtypeStruct((half, 2, rows, cols), bf16)
-    *outs, own_grads = pl.pallas_call(
-        functools.partial(main_kernel, groups, depth, mine, pix, tuple(pieces), tuple(results)),
-        out_shape=(half_shape,) * len(results) + (jax.ShapeDtypeStruct((depth, 2, rows, cols), bf16),),
+
+    outs = pl.pallas_call(
+        functools.partial(main_kernel, groups, depth, mine, pix, tuple(pieces)),
+        out_shape=(jax.ShapeDtypeStruct((depth, 2, rows, pix), bf16),) * (4 * groups),
         in_specs=[smem] + [anywhere] * (6 + len(operands)),
-        out_specs=(anywhere,) * (len(results) + 1),
+        out_specs=(anywhere,) * (4 * groups),
         scratch_shapes=[
             pltpu.VMEM((layers, 2, 2, pix, cols), bf16),
             pltpu.VMEM((layers, mine, 2, pix, pix), bf16),
@@ -405,7 +397,7 @@
             pltpu.VMEM((2, layers, 2, pix, cols), bf16),
             pltpu.SemaphoreType.DMA((layers, 2)),
             pltpu.SemaphoreType.DMA((6, 2)),
-            pltpu.SemaphoreType.DMA((2, layers)),
+            pltpu.SemaphoreType.DMA((4, layers)),
         ],
         compiler_params=pltpu.CompilerParams(vmem_limit_bytes=VMEM_LIMIT),
         cost_estimate=pl.CostEstimate(flops=15 * 10**9, bytes_accessed=16 * 2**20, transcendentals=0),
@@ -413,25 +405,24 @@
     )(info, planes, *operands, lefts, rights, psi0, light, masks)
 
     wide = lambda v: v.astype(jnp.float32)
-    kept = lambda s, which: wide(outs[6 * (s - 1) + 2 * which])
-    twin = lambda s, which: wide(passed(outs[6 * (s - 1) + 2 * which + 1], "pos", 1))
-    rims = {s: (kept(s, 0) + twin(s, 0)).astype(bf16) for s in steps}
-    firsts = {s: (kept(s, 1) + twin(s, 1)).astype(bf16) for s in steps}
-    lasts = {s: kept(s, 2) + twin(s, 2) for s in steps}
-    back = {s: split_roles(rims[s], 1, -s, 1) for s in steps}
-    come_first = sum(wide(split_roles(firsts[s], 1, -s, 0, s == 1)) for s in steps)
-    summed = sum(wide(back[s]) for s in steps)
-    lasts = {s: (lasts[s] + (jnp.where(core == 1, summed, wide(back[s])))).astype(bf16) for s in steps}
-    come_last = sum(wide(split_roles(lasts[s], 1, -s, 0, s == 1)) for s in steps)
-    on_first = jnp.where(core == 0, 1.0, 0.0)
-    own_sum = wide(own_grads) + jnp.concatenate([come_first * on_first, come_first * (1.0 - on_first)])
-    mine_of = lambda v: lax.dynamic_slice_in_dim(v, core * pix, pix, axis=3)
-    twins_of = lambda v: lax.dynamic_slice_in_dim(v, (1 - core) * pix, pix, axis=3)
-    early = mine_of(own_sum) + wide(passed(twins_of(own_sum).astype(bf16), "pos", 1))
-    here = mine_of(come_last)
-    away = wide(passed(twins_of(come_last).astype(bf16), "pos", 1))
-    late = jnp.concatenate([jnp.where(core == 0, away, here), jnp.where(core == 0, here, away)])
-    return (early + late).transpose(0, 2, 1, 3)
+    sums = {}
+    for s in [*steps, 0]:
+        for row_block in (1, 0):
+            at = row_block * groups + s
+            sums[row_block, s] = wide(outs[at]) + wide(passed(outs[2 * groups + at], "pos", 1))
+    rim_lo = sums[1, 0][:half]
+    rim_hi = sums[1, 0][half:].astype(bf16)
+    tile_lo = sums[0, 0][:half]
+    tile_hi = sums[0, 0][half:]
+    for s in steps:
+        rim, tile_part = sums[1, s], sums[0, s]
+        rim_lo += wide(passed(rim[:half].astype(bf16), "slc", -s))
+        other_hi = tile_part[half:] + wide(passed(rim[half:].astype(bf16), "tile", 1))
+        tile_lo += wide(passed(tile_part[:half].astype(bf16), "slc", -s))
+        tile_hi += wide(passed(other_hi.astype(bf16), "slc", -s))
+    tile_hi += wide(passed(rim_hi, "tile", 1))
+    tile_lo += wide(passed(rim_lo.astype(bf16), "tile", 1))
+    return jnp.concatenate([tile_lo, tile_hi]).transpose(0, 2, 1, 3)
 
 
 def solution(mesh):

time: 74 us -> 70.1 us (0.947)
  local copies, waits for them, and re-layouts: 10.8 us -> 6.09 us
  starting transfers between devices: 10.5 us -> 15 us
  other arithmetic: 3.88 us -> 0.92 us
  Pallas kernels: 15.7 us -> 14.9 us
    ppermute x8 -> x13, waiting for transfers between devices: 5.24 us -> 20.1 us  [passed(): lax.ppermute(array, axis, [(i, (i + by) % peers) for i in range(peers)])]
    ppermute x6 -> x3, waiting for transfers between devices: 26.8 us -> 12.2 us  [split_roles(): return lax.ppermute(array, ('tile', 'slc', 'pos'), pairs)]
    ppermute x8 -> x13, starting transfers between devices: 0.66 us -> 7.89 us  [passed(): lax.ppermute(array, axis, [(i, (i + by) % peers) for i in range(peers)])]
    unnamed x17 -> x9, local copies, waits for them, and re-layouts: 6.08 us -> 2.92 us
    ppermute x6 -> x3, starting transfers between devices: 9.8 us -> 7.11 us  [split_roles(): return lax.ppermute(array, ('tile', 'slc', 'pos'), pairs)]
    convert_element_type x4 -> x2, other arithmetic: 1.8 us -> 0.12 us  [the longest x1 0.06 us: body(): tile_lo += wide(passed(rim_lo.astype(bf16), 'tile', 1))]
    convert_element_type x2 -> x0, local copies, waits for them, and re-layouts: 1.62 us -> none  [the longest x1 0.86 us: body(): twins_of(own_sum).astype(bf16)]
    transpose x1, other arithmetic: 1.33 us -> 0.07 us  [body(): return jnp.concatenate([tile_lo, tile_hi]).transpose(0, 2, 1, 3)]
  transfers between devices with their start and end apart: 14 -> 16, of which waited for: 9 -> 7; matrix products, arithmetic and copies ran while one was open for 6% -> 2% of each run, Pallas kernels for 6% -> 6%
where the time goes in v7:
time: 70.1 us; the launch traced here: 70 us
  waiting for transfers between devices  32.2 us (46%)
  starting transfers between devices  15 us (21%)
  Pallas kernels  14.9 us (21%)
  local copies, waits for them, and re-layouts  6.09 us (9%)
  other arithmetic  0.92 us (1%)
  between operations  0.82 us (1%)
    ppermute x13, waiting for transfers between devices, passed(): lax.ppermute(array, axis, [(i, (i + by) % peers) for i in range(peers)])  20.1 us
    ppermute x3, waiting for transfers between devices, split_roles(): return lax.ppermute(array, ('tile', 'slc', 'pos'), pairs)  12.2 us
    pallas_call x1, Pallas kernels, body(): pl.pallas_call(functools.partial(main_kernel, groups, depth, mine, pix, t...  10.4 us
    ppermute x13, starting transfers between devices, passed(): lax.ppermute(array, axis, [(i, (i + by) % peers) for i in range(peers)])  7.89 us
    ppermute x3, starting transfers between devices, split_roles(): return lax.ppermute(array, ('tile', 'slc', 'pos'), pairs)  7.11 us
    pallas_call x1, Pallas kernels, body(): pl.pallas_call(functools.partial(prep_kernel, mine, pix), out_shape=(tabl...  4.49 us
    unnamed x9, local copies, waits for them, and re-layouts  2.92 us
    transpose x1, local copies, waits for them, and re-layouts, body(): return jnp.concatenate([tile_lo, tile_hi]).transpose(0, 2, 1, 3)  1.78 us
  transfers between devices with their start and end apart: 16, of which 7 were waited for; matrix products, arithmetic and copies ran while one was open for 2% of the time, Pallas kernels for 6%

profile of v7, /device:TPU:0, one launch (start us, length us, event | category | flops | bytes accessed | tf_op | source)
XLA Modules:
  0.0 70.0 jit_solution(18245759843457719760)
XLA Ops:
  0.0 1.5 %copy.14 = bf16[2,256,2,512]{3,1,2,0:T(8,128)(2,1)S(1)} copy(bf16[2,256,2,512]{3,2,1,0:T(2,128)(2,1)} %param.6) | data formatting | bytes 2097152 | tf_op args[0]
  1.5 1.1 %dynamic-slice_bitcast_fusion = (bf16[1,2,256,512]{3,2,1,0:T(8,128)(2,1)}, bf16[1,2,256,512]{3,2,1,0:T(8,128)(2,1)}) fusion(bf16[2,256,2,512]{3,1,2,0:T(8,128)(2,1)S(1)} %copy.14, s32[]{:T(128)S(6)} %select_n.39, s32[]{:T(128)S(6)} %select_n.38), kind=kLoop, calls=%fused_computation.15 | loop fusion | bytes 2097160 | tf_op jit(solution)/shard_map/dynamic_slice | solution.py:344
  2.6 2.9 %collective-permute-start.2 = (bf16[1,2,256,512]{3,2,1,0:T(8,128)(2,1)}, bf16[1,2,256,512]{3,2,1,0:T(8,128)(2,1)S(1)}, u32[]{:S(2)}, u32[]{:S(2)}) collective-permute-start(bf16[1,2,256,512]{3,2,1,0:T(8,128)(2,1)} %get-tuple-element.47), channel_id=1, source_target_pairs={{0,2},{1,13},{2,0},{3,15},{4,6},{5,1},{6,4},{7,3},{8,10},{9,5},{10... | collective-permute-start | bytes 1572872 | tf_op jit(solution)/shard_map/ppermute | solution.py:30
  6.6 1.4 %copy-done.3 = bf16[2,6,256,256]{3,2,1,0:T(8,128)(2,1)S(1)} copy-done((bf16[2,6,256,256]{3,2,1,0:T(8,128)(2,1)S(1)}, bf16[2,6,256,256]{3,2,1,0:T(8,128)(2,1)}, u32[]{:S(2)}) %copy-start.3) | copy-done | bytes 1572888
  8.0 4.5 %tables.1 = (bf16[2,4,2,256,256]{4,3,2,1,0:T(8,128)(2,1)S(1)}, bf16[2,4,2,256,256]{4,3,2,1,0:T(8,128)(2,1)S(1)}, bf16[2,2,256,256]{3,2,1,0:T(8,128)(2,1)S(1)}, f...) custom-call(s32[10]{0:T(128)S(1)} %pad_add_fusion.1.info, bf16[2,6,256,256]{3,2,1,0:T(8,128)(2,1)S(1)} %copy-done.3, ...), custom_call_target="tpu_custom_call" | custom-call | flops 8000000000 | bytes 8388608 | tf_op jit(solution)/shard_map/tables/pallas_call | solution.py:353
  12.5 6.0 %collective-permute-done.refs_1_ = bf16[1,2,256,512]{3,2,1,0:T(8,128)(2,1)S(1)} collective-permute-done((bf16[1,2,256,512]{3,2,1,0:T(8,128)(2,1)}, bf16[1,2,256,512]{3,2,1,0:T(8,128)(2,1)S(1)}, u32[]{:S(2)}, u32[]{:S(2)}) %collective-permute-start) | collective-permute-done | bytes 524320 | tf_op jit(solution)/shard_map/ppermute | solution.py:30
  18.5 4.1 %collective-permute-start.4 = (bf16[1,2,256,512]{3,2,1,0:T(8,128)(2,1)S(1)}, bf16[1,2,256,512]{3,2,1,0:T(8,128)(2,1)S(1)}, u32[]{:S(2)}, u32[]{:S(2)}) collective-permute-start(bf16[1,2,256,512]{3,2,1,0:T(8,128)(2,1)S(1)} %collective-permute-done.refs_1_), channel_id=1, source_target_pairs={{1,3},{0,12},{3,1},{2,14},{5,7},{4,0},{7,5},{6,2},{9,11},{8,4},{11... | collective-permute-start | bytes 1572872 | tf_op jit(solution)/shard_map/ppermute | solution.py:30
  22.6 0.5 collective-permute-start.3
  23.1 6.2 %collective-permute-done.4.refs_5_ = bf16[1,2,256,512]{3,2,1,0:T(8,128)(2,1)S(1)} collective-permute-done((bf16[1,2,256,512]{3,2,1,0:T(8,128)(2,1)S(1)}, bf16[1,2,256,512]{3,2,1,0:T(8,128)(2,1)S(1)}, u32[]{:S(2)}, u32[]{:S(2)}) %collective-permute-start.4) | collective-permute-done | bytes 524320 | tf_op jit(solution)/shard_map/ppermute | solution.py:30
  29.3 1.9 %collective-permute-done.5.refs_6_ = bf16[1,2,256,512]{3,2,1,0:T(8,128)(2,1)S(1)} collective-permute-done((bf16[1,2,256,512]{3,2,1,0:T(8,128)(2,1)S(1)}, bf16[1,2,256,512]{3,2,1,0:T(8,128)(2,1)S(1)}, u32[]{:S(2)}, u32[]{:S(2)}) %collective-permute-start.5) | collective-permute-done | bytes 524320 | tf_op jit(solution)/shard_map/ppermute | solution.py:18
  31.2 10.4 %waves.1 = (bf16[2,2,256,256]{3,2,1,0:T(8,128)(2,1)S(1)}, bf16[2,2,256,256]{3,2,1,0:T(8,128)(2,1)S(1)}, bf16[2,2,256,256]{3,2,1,0:T(8,128)(2,1)S(1)}, bf16[2,2,2...) custom-call(s32[10]{0:T(128)S(1)} %pad_add_fusion.1.info, ...), custom_call_target="tpu_custom_call" | custom-call | flops 15000000512 | bytes 16777216 | tf_op jit(solution)/shard_map/waves/pallas_call | solution.py:384
  41.8 0.4 collective-permute-start.10
  42.3 0.4 collective-permute-start.9
  42.7 0.9 %collective-permute-done.7 = bf16[2,2,256,256]{3,2,1,0:T(8,128)(2,1)S(1)} collective-permute-done((bf16[2,2,256,256]{3,2,1,0:T(8,128)(2,1)S(1)}, bf16[2,2,256,256]{3,2,1,0:T(8,128)(2,1)S(1)}, u32[]{:S(2)}, u32[]{:S(2)}) %collective-permute-start.7) | collective-permute-done | bytes 524320 | tf_op jit(solution)/shard_map/ppermute | solution.py:18
  43.8 1.6 %collective-permute-start.8 = (bf16[1,2,256,256]{3,2,1,0:T(8,128)(2,1)S(1)}, bf16[1,2,256,256]{3,2,1,0:T(8,128)(2,1)S(1)}, u32[]{:S(2)}, u32[]{:S(2)}) collective-permute-start(bf16[1,2,256,256]{3,2,1,0:T(8,128)(2,1)S(1)} %slice.71), channel_id=1, source_target_pairs={{0,2},{2,0},{1,3},{3,1},{4,6},{6,4},{5,7},{7,5},{8,10},{10,8},{9,1... | collective-permute-start | bytes 786440 | tf_op jit(solution)/shard_map/ppermute | solution.py:18
  45.5 0.6 collective-permute-start.11
  46.1 0.5 collective-permute-start.13
  46.7 1.6 %collective-permute-start.15 = (bf16[1,2,256,256]{3,2,1,0:T(8,128)(2,1)S(1)}, bf16[1,2,256,256]{3,2,1,0:T(8,128)(2,1)S(1)}, u32[]{:S(2)}, u32[]{:S(2)}) collective-permute-start(bf16[1,2,256,256]{3,2,1,0:T(8,128)(2,1)S(1)} %slice.70), channel_id=1, source_target_pairs={{0,4},{4,8},{8,12},{12,0},{1,5},{5,9},{9,13},{13,1},{2,6},{6,10},{... | collective-permute-start | bytes 786440 | tf_op jit(solution)/shard_map/ppermute | solution.py:18
  48.4 9.4 %collective-permute-done.11 = bf16[1,2,256,256]{3,2,1,0:T(8,128)(2,1)S(1)} collective-permute-done((bf16[1,2,256,256]{3,2,1,0:T(8,128)(2,1)S(1)}, bf16[1,2,256,256]{3,2,1,0:T(8,128)(2,1)S(1)}, u32[]{:S(2)}, u32[]{:S(2)}) %collective-permute-start.11) | collective-permute-done | bytes 262176 | tf_op jit(solution)/shard_map/ppermute | solution.py:18
  57.9 0.5 collective-permute-start.12
  58.4 1.5 %collective-permute-start.14 = (bf16[1,2,256,256]{3,2,1,0:T(8,128)(2,1)S(1)}, bf16[1,2,256,256]{3,2,1,0:T(8,128)(2,1)S(1)}, u32[]{:S(2)}, u32[]{:S(2)}) collective-permute-start(bf16[1,2,256,256]{3,2,1,0:T(8,128)(2,1)S(1)} %fusion), channel_id=1, source_target_pairs={{0,2},{2,0},{1,3},{3,1},{4,6},{6,4},{5,7},{7,5},{8,10},{10,8},{9,1... | collective-permute-start | bytes 786440 | tf_op jit(solution)/shard_map/ppermute | solution.py:18
  60.1 2.2 %collective-permute-done.15 = bf16[1,2,256,256]{3,2,1,0:T(8,128)(2,1)S(1)} collective-permute-done((bf16[1,2,256,256]{3,2,1,0:T(8,128)(2,1)S(1)}, bf16[1,2,256,256]{3,2,1,0:T(8,128)(2,1)S(1)}, u32[]{:S(2)}, u32[]{:S(2)}) %collective-permute-start.15) | collective-permute-done | bytes 262176 | tf_op jit(solution)/shard_map/ppermute | solution.py:18
  62.3 5.6 %collective-permute-done.12 = bf16[1,2,256,256]{3,2,1,0:T(8,128)(2,1)S(1)} collective-permute-done((bf16[1,2,256,256]{3,2,1,0:T(8,128)(2,1)S(1)}, bf16[1,2,256,256]{3,2,1,0:T(8,128)(2,1)S(1)}, u32[]{:S(2)}, u32[]{:S(2)}) %collective-permute-start.12) | collective-permute-done | bytes 262176 | tf_op jit(solution)/shard_map/ppermute | solution.py:18
  68.2 1.8 %copy.11 = f32[2,256,2,256]{3,2,1,0:T(2,128)} copy(f32[2,256,2,256]{3,1,2,0:T(8,128)S(1)} %maximum_bitcast_fusion) | data formatting | bytes 2097152 | tf_op jit(solution)/shard_map/transpose | solution.py:425
  (41 shorter events, 1.6 us)
Async XLA Ops:
  0.0 6.2 %copy-start = (s32[2,4]{1,0:T(2,128)S(1)}, s32[2,4]{1,0:T(2,128)}, u32[]{:S(2)}) copy-start(s32[2,4]{1,0:T(2,128)} %param.7) | copy-start | bytes 100
  0.0 6.6 %copy-start.1 = (f32[4,256,256]{2,1,0:T(8,128)S(1)}, f32[4,256,256]{2,1,0:T(8,128)}, u32[]{:S(2)}) copy-start(f32[4,256,256]{2,1,0:T(8,128)} %measured.1) | copy-start | bytes 3145732
  0.0 6.6 %copy-start.2 = (bf16[256,512]{1,0:T(8,128)(2,1)S(1)}, bf16[256,512]{1,0:T(8,128)(2,1)}, u32[]{:S(2)}) copy-start(bf16[256,512]{1,0:T(8,128)(2,1)} %probe.1) | copy-start | bytes 786436
  2.6 20.1 %collective-permute-start.2 = (bf16[1,2,256,512]{3,2,1,0:T(8,128)(2,1)}, bf16[1,2,256,512]{3,2,1,0:T(8,128)(2,1)S(1)}, u32[]{:S(2)}, u32[]{:S(2)}) collective-permute-start(bf16[1,2,256,512]{3,2,1,0:T(8,128)(2,1)} %get-tuple-element.47), channel_id=1, source_target_pairs={{0,2},{1,13},{2,0},{3,15},{4,6},{5,1},{6,4},{7,3},{8,10},{9,5},{10... | collective-permute-start | bytes 1572872 | tf_op jit(solution)/shard_map/ppermute | solution.py:30
  5.5 13.0 %collective-permute-start = (bf16[1,2,256,512]{3,2,1,0:T(8,128)(2,1)}, bf16[1,2,256,512]{3,2,1,0:T(8,128)(2,1)S(1)}, u32[]{:S(2)}, u32[]{:S(2)}) collective-permute-start(bf16[1,2,256,512]{3,2,1,0:T(8,128)(2,1)} %get-tuple-element.48), channel_id=1, source_target_pairs={{0,2},{1,13},{2,0},{3,15},{4,6},{5,1},{6,4},{7,3},{8,10},{9,5},{10... | collective-permute-start | bytes 1572872 | tf_op jit(solution)/shard_map/ppermute | solution.py:30
  6.6 1.4 %copy-start.3 = (bf16[2,6,256,256]{3,2,1,0:T(8,128)(2,1)S(1)}, bf16[2,6,256,256]{3,2,1,0:T(8,128)(2,1)}, u32[]{:S(2)}) copy-start(bf16[2,6,256,256]{3,2,1,0:T(8,128)(2,1)} %constant.49.clone.base) | copy-start | bytes 4718596
  18.5 10.8 %collective-permute-start.4 = (bf16[1,2,256,512]{3,2,1,0:T(8,128)(2,1)S(1)}, bf16[1,2,256,512]{3,2,1,0:T(8,128)(2,1)S(1)}, u32[]{:S(2)}, u32[]{:S(2)}) collective-permute-start(bf16[1,2,256,512]{3,2,1,0:T(8,128)(2,1)S(1)} %collective-permute-done.refs_1_), channel_id=1, source_target_pairs={{1,3},{0,12},{3,1},{2,14},{5,7},{4,0},{7,5},{6,2},{9,11},{8,4},{11... | collective-permute-start | bytes 1572872 | tf_op jit(solution)/shard_map/ppermute | solution.py:30
  22.6 6.7 %collective-permute-start.1 = (bf16[1,2,256,512]{3,2,1,0:T(8,128)(2,1)S(1)}, bf16[1,2,256,512]{3,2,1,0:T(8,128)(2,1)S(1)}, u32[]{:S(2)}, u32[]{:S(2)}) collective-permute-start(bf16[1,2,256,512]{3,2,1,0:T(8,128)(2,1)S(1)} %collective-permute-done.refs_1_), channel_id=1, source_target_pairs={{0,1},{1,0},{2,3},{3,2},{4,5},{5,4},{6,7},{7,6},{8,9},{9,8},{10,11... | collective-permute-start | bytes 1572872 | tf_op jit(solution)/shard_map/ppermute | solution.py:18
  22.6 6.7 %collective-permute-start.3 = (bf16[1,2,256,512]{3,2,1,0:T(8,128)(2,1)S(1)}, bf16[1,2,256,512]{3,2,1,0:T(8,128)(2,1)S(1)}, u32[]{:S(2)}, u32[]{:S(2)}) collective-permute-start(bf16[1,2,256,512]{3,2,1,0:T(8,128)(2,1)S(1)} %collective-permute-done.2.refs_3_), channel_id=1, source_target_pairs={{0,1},{1,0},{2,3},{3,2},{4,5},{5,4},{6,7},{7,6},{8,9},{9,8},{10,11... | collective-permute-start | bytes 1572872 | tf_op jit(solution)/shard_map/ppermute | solution.py:18
  29.3 1.9 %collective-permute-start.5 = (bf16[1,2,256,512]{3,2,1,0:T(8,128)(2,1)S(1)}, bf16[1,2,256,512]{3,2,1,0:T(8,128)(2,1)S(1)}, u32[]{:S(2)}, u32[]{:S(2)}) collective-permute-start(bf16[1,2,256,512]{3,2,1,0:T(8,128)(2,1)S(1)} %collective-permute-done.4.refs_5_), channel_id=1, source_target_pairs={{0,1},{1,0},{2,3},{3,2},{4,5},{5,4},{6,7},{7,6},{8,9},{9,8},{10,11... | collective-permute-start | bytes 1572872 | tf_op jit(solution)/shard_map/ppermute | solution.py:18
  41.6 2.0 %collective-permute-start.7 = (bf16[2,2,256,256]{3,2,1,0:T(8,128)(2,1)S(1)}, bf16[2,2,256,256]{3,2,1,0:T(8,128)(2,1)S(1)}, u32[]{:S(2)}, u32[]{:S(2)}) collective-permute-start(bf16[2,2,256,256]{3,2,1,0:T(8,128)(2,1)S(1)} %get-tuple-element.38), channel_id=1, source_target_pairs={{0,1},{1,0},{2,3},{3,2},{4,5},{5,4},{6,7},{7,6},{8,9},{9,8},{10,11... | collective-permute-start | bytes 1572872 | tf_op jit(solution)/shard_map/ppermute | solution.py:18
  41.8 3.5 %collective-permute-start.10 = (bf16[2,2,256,256]{3,2,1,0:T(8,128)(2,1)S(1)}, bf16[2,2,256,256]{3,2,1,0:T(8,128)(2,1)S(1)}, u32[]{:S(2)}, u32[]{:S(2)}) collective-permute-start(bf16[2,2,256,256]{3,2,1,0:T(8,128)(2,1)S(1)} %get-tuple-element.42), channel_id=1, source_target_pairs={{0,1},{1,0},{2,3},{3,2},{4,5},{5,4},{6,7},{7,6},{8,9},{9,8},{10,11... | collective-permute-start | bytes 1572872 | tf_op jit(solution)/shard_map/ppermute | solution.py:18
  42.2 17.8 %collective-permute-start.6 = (bf16[2,2,256,256]{3,2,1,0:T(8,128)(2,1)S(1)}, bf16[2,2,256,256]{3,2,1,0:T(8,128)(2,1)S(1)}, u32[]{:S(2)}, u32[]{:S(2)}) collective-permute-start(bf16[2,2,256,256]{3,2,1,0:T(8,128)(2,1)S(1)} %get-tuple-element.36), channel_id=1, source_target_pairs={{0,1},{1,0},{2,3},{3,2},{4,5},{5,4},{6,7},{7,6},{8,9},{9,8},{10,11... | collective-permute-start | bytes 1572872 | tf_op jit(solution)/shard_map/ppermute | solution.py:18
  42.3 4.3 %collective-permute-start.9 = (bf16[2,2,256,256]{3,2,1,0:T(8,128)(2,1)S(1)}, bf16[2,2,256,256]{3,2,1,0:T(8,128)(2,1)S(1)}, u32[]{:S(2)}, u32[]{:S(2)}) collective-permute-start(bf16[2,2,256,256]{3,2,1,0:T(8,128)(2,1)S(1)} %get-tuple-element.40), channel_id=1, source_target_pairs={{0,1},{1,0},{2,3},{3,2},{4,5},{5,4},{6,7},{7,6},{8,9},{9,8},{10,11... | collective-permute-start | bytes 1572872 | tf_op jit(solution)/shard_map/ppermute | solution.py:18
  43.8 16.3 %collective-permute-start.8 = (bf16[1,2,256,256]{3,2,1,0:T(8,128)(2,1)S(1)}, bf16[1,2,256,256]{3,2,1,0:T(8,128)(2,1)S(1)}, u32[]{:S(2)}, u32[]{:S(2)}) collective-permute-start(bf16[1,2,256,256]{3,2,1,0:T(8,128)(2,1)S(1)} %slice.71), channel_id=1, source_target_pairs={{0,2},{2,0},{1,3},{3,1},{4,6},{6,4},{5,7},{7,5},{8,10},{10,8},{9,1... | collective-permute-start | bytes 786440 | tf_op jit(solution)/shard_map/ppermute | solution.py:18
  45.5 12.3 %collective-permute-start.11 = (bf16[1,2,256,256]{3,2,1,0:T(8,128)(2,1)S(1)}, bf16[1,2,256,256]{3,2,1,0:T(8,128)(2,1)S(1)}, u32[]{:S(2)}, u32[]{:S(2)}) collective-permute-start(bf16[1,2,256,256]{3,2,1,0:T(8,128)(2,1)S(1)} %get-tuple-element.51), channel_id=1, source_target_pairs={{0,2},{2,0},{1,3},{3,1},{4,6},{6,4},{5,7},{7,5},{8,10},{10,8},{9,1... | collective-permute-start | bytes 786440 | tf_op jit(solution)/shard_map/ppermute | solution.py:18
  46.1 12.3 %collective-permute-start.13 = (bf16[1,2,256,256]{3,2,1,0:T(8,128)(2,1)S(1)}, bf16[1,2,256,256]{3,2,1,0:T(8,128)(2,1)S(1)}, u32[]{:S(2)}, u32[]{:S(2)}) collective-permute-start(bf16[1,2,256,256]{3,2,1,0:T(8,128)(2,1)S(1)} %get-tuple-element.52), channel_id=1, source_target_pairs={{0,4},{4,8},{8,12},{12,0},{1,5},{5,9},{9,13},{13,1},{2,6},{6,10},{... | collective-permute-start | bytes 786440 | tf_op jit(solution)/shard_map/ppermute | solution.py:18
  46.7 15.6 %collective-permute-start.15 = (bf16[1,2,256,256]{3,2,1,0:T(8,128)(2,1)S(1)}, bf16[1,2,256,256]{3,2,1,0:T(8,128)(2,1)S(1)}, u32[]{:S(2)}, u32[]{:S(2)}) collective-permute-start(bf16[1,2,256,256]{3,2,1,0:T(8,128)(2,1)S(1)} %slice.70), channel_id=1, source_target_pairs={{0,4},{4,8},{8,12},{12,0},{1,5},{5,9},{9,13},{13,1},{2,6},{6,10},{... | collective-permute-start | bytes 786440 | tf_op jit(solution)/shard_map/ppermute | solution.py:18
  57.9 10.1 %collective-permute-start.12 = (bf16[1,2,256,256]{3,2,1,0:T(8,128)(2,1)S(1)}, bf16[1,2,256,256]{3,2,1,0:T(8,128)(2,1)S(1)}, u32[]{:S(2)}, u32[]{:S(2)}) collective-permute-start(bf16[1,2,256,256]{3,2,1,0:T(8,128)(2,1)S(1)} %fusion.2), channel_id=1, source_target_pairs={{0,4},{4,8},{8,12},{12,0},{1,5},{5,9},{9,13},{13,1},{2,6},{6,10},{... | collective-permute-start | bytes 786440 | tf_op jit(solution)/shard_map/ppermute | solution.py:18
  58.4 9.5 %collective-permute-start.14 = (bf16[1,2,256,256]{3,2,1,0:T(8,128)(2,1)S(1)}, bf16[1,2,256,256]{3,2,1,0:T(8,128)(2,1)S(1)}, u32[]{:S(2)}, u32[]{:S(2)}) collective-permute-start(bf16[1,2,256,256]{3,2,1,0:T(8,128)(2,1)S(1)} %fusion), channel_id=1, source_target_pairs={{0,2},{2,0},{1,3},{3,1},{4,6},{6,4},{5,7},{7,5},{8,10},{10,8},{9,1... | collective-permute-start | bytes 786440 | tf_op jit(solution)/shard_map/ppermute | solution.py:18

commit v8 on v7

--- a/solution.py
+++ b/solution.py
@@ -342,9 +342,9 @@
     half = depth // 2
     steps = range(1, groups)
     halves_of = lambda high: lax.dynamic_slice_in_dim(planes, high * half, half, axis=0)
+    planes, info = lax.optimization_barrier((planes, info))
     first_half, last_half = halves_of(core), halves_of(1 - core)
     got_first = [split_roles(first_half, -1, s, 0, s == 1) for s in steps]
-    got_last = [split_roles(last_half, -1, s, 0, s == 1) for s in steps]
 
     smem = pl.BlockSpec(memory_space=pltpu.SMEM)
     vmem = pl.BlockSpec(memory_space=pltpu.VMEM)
@@ -366,9 +366,10 @@
         name="tables",
     )(info, jnp.asarray(base_tables(pix)), probe_wave, measured)
 
-    got_first, lefts, rights, psi0, light, masks = lax.optimization_barrier(
-        (got_first, lefts, rights, psi0, light, masks)
+    last_half, lefts, rights, psi0, light, masks = lax.optimization_barrier(
+        (last_half, lefts, rights, psi0, light, masks)
     )
+    got_last = [split_roles(last_half, -1, s, 0, s == 1) for s in steps]
     passed_on = [split_roles(got_first[s - 1], -1, s, 1) for s in steps]
     pieces, operands = [], []
     for s in steps:

time: 70.1 us -> 65.8 us (0.939)
  waiting for transfers between devices: 32.2 us -> 28.5 us
  local copies, waits for them, and re-layouts: 6.09 us -> 3.71 us
  starting transfers between devices: 15 us -> 16.8 us
    ppermute x3, waiting for transfers between devices: 12.2 us -> 9 us  [split_roles(): return lax.ppermute(array, ('tile', 'slc', 'pos'), pairs)]
    unnamed x9, local copies, waits for them, and re-layouts: 2.92 us -> 1.52 us
    ppermute x3, starting transfers between devices: 7.11 us -> 8.44 us  [split_roles(): return lax.ppermute(array, ('tile', 'slc', 'pos'), pairs)]
    dynamic_slice x1, local copies, waits for them, and re-layouts: 1.05 us -> 0.07 us  [body(): lax.dynamic_slice_in_dim(planes, high * half, half, axis=0)]
  transfers between devices with their start and end apart: 16 -> 16, of which waited for: 7 -> 8; matrix products, arithmetic and copies ran while one was open for 2% -> 1% of each run, Pallas kernels for 6% -> 7%
where the time goes in v8:
time: 65.8 us; the launch traced here: 65.6 us
  waiting for transfers between devices  28.5 us (43%)
  starting transfers between devices  16.8 us (26%)
  Pallas kernels  14.9 us (23%)
  local copies, waits for them, and re-layouts  3.71 us (6%)
  other arithmetic  0.92 us (1%)
  between operations  0.83 us (1%)
    ppermute x13, waiting for transfers between devices, passed(): lax.ppermute(array, axis, [(i, (i + by) % peers) for i in range(peers)])  19.5 us
    pallas_call x1, Pallas kernels, body(): pl.pallas_call(functools.partial(main_kernel, groups, depth, mine, pix, t...  10.4 us
    ppermute x3, waiting for transfers between devices, split_roles(): return lax.ppermute(array, ('tile', 'slc', 'pos'), pairs)  9 us
    ppermute x3, starting transfers between devices, split_roles(): return lax.ppermute(array, ('tile', 'slc', 'pos'), pairs)  8.44 us
    ppermute x13, starting transfers between devices, passed(): lax.ppermute(array, axis, [(i, (i + by) % peers) for i in range(peers)])  8.32 us
    pallas_call x1, Pallas kernels, body(): pl.pallas_call(functools.partial(prep_kernel, mine, pix), out_shape=(tabl...  4.49 us
    transpose x1, local copies, waits for them, and re-layouts, body(): return jnp.concatenate([tile_lo, tile_hi]).transpose(0, 2, 1, 3)  1.78 us
    unnamed x9, local copies, waits for them, and re-layouts  1.52 us
  transfers between devices with their start and end apart: 16, of which 8 were waited for; matrix products, arithmetic and copies ran while one was open for 1% of the time, Pallas kernels for 7%

profile of v8, /device:TPU:0, one launch (start us, length us, event | category | flops | bytes accessed | tf_op | source)
XLA Modules:
  0.0 65.6 jit_solution(16370386607381187027)
XLA Ops:
  1.0 1.5 %copy.11 = bf16[2,256,2,512]{3,1,2,0:T(8,128)(2,1)S(1)} copy(bf16[2,256,2,512]{3,2,1,0:T(2,128)(2,1)} %param.6) | data formatting | bytes 2097152 | tf_op args[0]
  2.7 3.0 %collective-permute-start = (bf16[1,2,256,512]{3,2,1,0:T(8,128)(2,1)S(1)}, bf16[1,2,256,512]{3,2,1,0:T(8,128)(2,1)S(1)}, u32[]{:S(2)}, u32[]{:S(2)}) collective-permute-start(bf16[1,2,256,512]{3,2,1,0:T(8,128)(2,1)S(1)} %get-tuple-element.52), channel_id=1, source_target_pairs={{0,2},{1,13},{2,0},{3,15},{4,6},{5,1},{6,4},{7,3},{8,10},{9,5},{10... | collective-permute-start | bytes 1572872 | tf_op jit(solution)/shard_map/ppermute | solution.py:30
  5.7 4.5 %tables.1 = (bf16[2,4,2,256,256]{4,3,2,1,0:T(8,128)(2,1)S(1)}, bf16[2,4,2,256,256]{4,3,2,1,0:T(8,128)(2,1)S(1)}, bf16[2,2,256,256]{3,2,1,0:T(8,128)(2,1)S(1)}, f...) custom-call(s32[10]{0:T(128)S(1)} %pad_add_fusion.1.info, bf16[2,6,256,256]{3,2,1,0:T(8,128)(2,1)S(1)} %copy-done.3, ...), custom_call_target="tpu_custom_call" | custom-call | flops 8000000000 | bytes 8388608 | tf_op jit(solution)/shard_map/tables/pallas_call | solution.py:353
  10.2 1.3 %collective-permute-start.2 = (bf16[1,2,256,512]{3,2,1,0:T(8,128)(2,1)S(1)}, bf16[1,2,256,512]{3,2,1,0:T(8,128)(2,1)S(1)}, u32[]{:S(2)}, u32[]{:S(2)}) collective-permute-start(bf16[1,2,256,512]{3,2,1,0:T(8,128)(2,1)S(1)} %get-tuple-element.33), channel_id=1, source_target_pairs={{0,2},{1,13},{2,0},{3,15},{4,6},{5,1},{6,4},{7,3},{8,10},{9,5},{10... | collective-permute-start | bytes 1572872 | tf_op jit(solution)/shard_map/ppermute | solution.py:30
  11.5 1.3 %collective-permute-done.refs_1_ = bf16[1,2,256,512]{3,2,1,0:T(8,128)(2,1)S(1)} collective-permute-done((bf16[1,2,256,512]{3,2,1,0:T(8,128)(2,1)S(1)}, bf16[1,2,256,512]{3,2,1,0:T(8,128)(2,1)S(1)}, u32[]{:S(2)}, u32[]{:S(2)}) %collective-permute-start) | collective-permute-done | bytes 524320 | tf_op jit(solution)/shard_map/ppermute | solution.py:30
  12.8 4.1 %collective-permute-start.4 = (bf16[1,2,256,512]{3,2,1,0:T(8,128)(2,1)S(1)}, bf16[1,2,256,512]{3,2,1,0:T(8,128)(2,1)S(1)}, u32[]{:S(2)}, u32[]{:S(2)}) collective-permute-start(bf16[1,2,256,512]{3,2,1,0:T(8,128)(2,1)S(1)} %collective-permute-done.refs_1_), channel_id=1, source_target_pairs={{1,3},{0,12},{3,1},{2,14},{5,7},{4,0},{7,5},{6,2},{9,11},{8,4},{11... | collective-permute-start | bytes 1572872 | tf_op jit(solution)/shard_map/ppermute | solution.py:30
  16.9 5.7 %collective-permute-done.2.refs_3_ = bf16[1,2,256,512]{3,2,1,0:T(8,128)(2,1)S(1)} collective-permute-done((bf16[1,2,256,512]{3,2,1,0:T(8,128)(2,1)S(1)}, bf16[1,2,256,512]{3,2,1,0:T(8,128)(2,1)S(1)}, u32[]{:S(2)}, u32[]{:S(2)}) %collective-permute-start.2) | collective-permute-done | bytes 524320 | tf_op jit(solution)/shard_map/ppermute | solution.py:30
  22.7 1.1 %collective-permute-start.3 = (bf16[1,2,256,512]{3,2,1,0:T(8,128)(2,1)S(1)}, bf16[1,2,256,512]{3,2,1,0:T(8,128)(2,1)S(1)}, u32[]{:S(2)}, u32[]{:S(2)}) collective-permute-start(bf16[1,2,256,512]{3,2,1,0:T(8,128)(2,1)S(1)} %collective-permute-done.2.refs_3_), channel_id=1, source_target_pairs={{0,1},{1,0},{2,3},{3,2},{4,5},{5,4},{6,7},{7,6},{8,9},{9,8},{10,11... | collective-permute-start | bytes 1572872 | tf_op jit(solution)/shard_map/ppermute | solution.py:18
  23.8 1.9 %collective-permute-done.4.refs_5_ = bf16[1,2,256,512]{3,2,1,0:T(8,128)(2,1)S(1)} collective-permute-done((bf16[1,2,256,512]{3,2,1,0:T(8,128)(2,1)S(1)}, bf16[1,2,256,512]{3,2,1,0:T(8,128)(2,1)S(1)}, u32[]{:S(2)}, u32[]{:S(2)}) %collective-permute-start.4) | collective-permute-done | bytes 524320 | tf_op jit(solution)/shard_map/ppermute | solution.py:30
  25.7 1.9 %collective-permute-done.5.refs_6_ = bf16[1,2,256,512]{3,2,1,0:T(8,128)(2,1)S(1)} collective-permute-done((bf16[1,2,256,512]{3,2,1,0:T(8,128)(2,1)S(1)}, bf16[1,2,256,512]{3,2,1,0:T(8,128)(2,1)S(1)}, u32[]{:S(2)}, u32[]{:S(2)}) %collective-permute-start.5) | collective-permute-done | bytes 524320 | tf_op jit(solution)/shard_map/ppermute | solution.py:18
  27.6 10.4 %waves.1 = (bf16[2,2,256,256]{3,2,1,0:T(8,128)(2,1)S(1)}, bf16[2,2,256,256]{3,2,1,0:T(8,128)(2,1)S(1)}, bf16[2,2,256,256]{3,2,1,0:T(8,128)(2,1)S(1)}, bf16[2,2,2...) custom-call(s32[10]{0:T(128)S(1)} %pad_add_fusion.1.info, ...), custom_call_target="tpu_custom_call" | custom-call | flops 15000000512 | bytes 16777216 | tf_op jit(solution)/shard_map/waves/pallas_call | solution.py:385
  38.2 0.4 collective-permute-start.10
  38.7 0.4 collective-permute-start.9
  39.1 0.9 %collective-permute-done.7 = bf16[2,2,256,256]{3,2,1,0:T(8,128)(2,1)S(1)} collective-permute-done((bf16[2,2,256,256]{3,2,1,0:T(8,128)(2,1)S(1)}, bf16[2,2,256,256]{3,2,1,0:T(8,128)(2,1)S(1)}, u32[]{:S(2)}, u32[]{:S(2)}) %collective-permute-start.7) | collective-permute-done | bytes 524320 | tf_op jit(solution)/shard_map/ppermute | solution.py:18
  40.2 1.5 %collective-permute-start.8 = (bf16[1,2,256,256]{3,2,1,0:T(8,128)(2,1)S(1)}, bf16[1,2,256,256]{3,2,1,0:T(8,128)(2,1)S(1)}, u32[]{:S(2)}, u32[]{:S(2)}) collective-permute-start(bf16[1,2,256,256]{3,2,1,0:T(8,128)(2,1)S(1)} %slice.71), channel_id=1, source_target_pairs={{0,2},{2,0},{1,3},{3,1},{4,6},{6,4},{5,7},{7,5},{8,10},{10,8},{9,1... | collective-permute-start | bytes 786440 | tf_op jit(solution)/shard_map/ppermute | solution.py:18
  41.9 0.6 collective-permute-start.11
  42.5 0.4 collective-permute-start.13
  43.1 1.6 %collective-permute-start.15 = (bf16[1,2,256,256]{3,2,1,0:T(8,128)(2,1)S(1)}, bf16[1,2,256,256]{3,2,1,0:T(8,128)(2,1)S(1)}, u32[]{:S(2)}, u32[]{:S(2)}) collective-permute-start(bf16[1,2,256,256]{3,2,1,0:T(8,128)(2,1)S(1)} %slice.70), channel_id=1, source_target_pairs={{0,4},{4,8},{8,12},{12,0},{1,5},{5,9},{9,13},{13,1},{2,6},{6,10},{... | collective-permute-start | bytes 786440 | tf_op jit(solution)/shard_map/ppermute | solution.py:18
  44.7 9.5 %collective-permute-done.11 = bf16[1,2,256,256]{3,2,1,0:T(8,128)(2,1)S(1)} collective-permute-done((bf16[1,2,256,256]{3,2,1,0:T(8,128)(2,1)S(1)}, bf16[1,2,256,256]{3,2,1,0:T(8,128)(2,1)S(1)}, u32[]{:S(2)}, u32[]{:S(2)}) %collective-permute-start.11) | collective-permute-done | bytes 262176 | tf_op jit(solution)/shard_map/ppermute | solution.py:18
  54.2 0.6 collective-permute-start.12
  54.9 1.3 %collective-permute-start.14 = (bf16[1,2,256,256]{3,2,1,0:T(8,128)(2,1)S(1)}, bf16[1,2,256,256]{3,2,1,0:T(8,128)(2,1)S(1)}, u32[]{:S(2)}, u32[]{:S(2)}) collective-permute-start(bf16[1,2,256,256]{3,2,1,0:T(8,128)(2,1)S(1)} %fusion), channel_id=1, source_target_pairs={{0,2},{2,0},{1,3},{3,1},{4,6},{6,4},{5,7},{7,5},{8,10},{10,8},{9,1... | collective-permute-start | bytes 786440 | tf_op jit(solution)/shard_map/ppermute | solution.py:18
  56.4 1.6 %collective-permute-done.15 = bf16[1,2,256,256]{3,2,1,0:T(8,128)(2,1)S(1)} collective-permute-done((bf16[1,2,256,256]{3,2,1,0:T(8,128)(2,1)S(1)}, bf16[1,2,256,256]{3,2,1,0:T(8,128)(2,1)S(1)}, u32[]{:S(2)}, u32[]{:S(2)}) %collective-permute-start.15) | collective-permute-done | bytes 262176 | tf_op jit(solution)/shard_map/ppermute | solution.py:18
  58.0 5.7 %collective-permute-done.12 = bf16[1,2,256,256]{3,2,1,0:T(8,128)(2,1)S(1)} collective-permute-done((bf16[1,2,256,256]{3,2,1,0:T(8,128)(2,1)S(1)}, bf16[1,2,256,256]{3,2,1,0:T(8,128)(2,1)S(1)}, u32[]{:S(2)}, u32[]{:S(2)}) %collective-permute-start.12) | collective-permute-done | bytes 262176 | tf_op jit(solution)/shard_map/ppermute | solution.py:18
  63.8 1.8 %copy.9 = f32[2,256,2,256]{3,2,1,0:T(2,128)} copy(f32[2,256,2,256]{3,1,2,0:T(8,128)S(1)} %maximum_bitcast_fusion) | data formatting | bytes 2097152 | tf_op jit(solution)/shard_map/transpose | solution.py:426
  (41 shorter events, 1.7 us)
Async XLA Ops:
  0.0 0.7 %copy-start = (s32[2,4]{1,0:T(2,128)S(1)}, s32[2,4]{1,0:T(2,128)}, u32[]{:S(2)}) copy-start(s32[2,4]{1,0:T(2,128)} %param.7) | copy-start | bytes 100
  1.0 4.7 %copy-start.1 = (f32[4,256,256]{2,1,0:T(8,128)S(1)}, f32[4,256,256]{2,1,0:T(8,128)}, u32[]{:S(2)}) copy-start(f32[4,256,256]{2,1,0:T(8,128)} %measured.1) | copy-start | bytes 3145732
  1.0 4.7 %copy-start.2 = (bf16[256,512]{1,0:T(8,128)(2,1)S(1)}, bf16[256,512]{1,0:T(8,128)(2,1)}, u32[]{:S(2)}) copy-start(bf16[256,512]{1,0:T(8,128)(2,1)} %probe.1) | copy-start | bytes 786436
  2.6 3.1 %copy-start.3 = (bf16[2,6,256,256]{3,2,1,0:T(8,128)(2,1)S(1)}, bf16[2,6,256,256]{3,2,1,0:T(8,128)(2,1)}, u32[]{:S(2)}) copy-start(bf16[2,6,256,256]{3,2,1,0:T(8,128)(2,1)} %constant.49.clone.base) | copy-start | bytes 4718596
  2.7 10.2 %collective-permute-start = (bf16[1,2,256,512]{3,2,1,0:T(8,128)(2,1)S(1)}, bf16[1,2,256,512]{3,2,1,0:T(8,128)(2,1)S(1)}, u32[]{:S(2)}, u32[]{:S(2)}) collective-permute-start(bf16[1,2,256,512]{3,2,1,0:T(8,128)(2,1)S(1)} %get-tuple-element.52), channel_id=1, source_target_pairs={{0,2},{1,13},{2,0},{3,15},{4,6},{5,1},{6,4},{7,3},{8,10},{9,5},{10... | collective-permute-start | bytes 1572872 | tf_op jit(solution)/shard_map/ppermute | solution.py:30
  10.2 12.5 %collective-permute-start.2 = (bf16[1,2,256,512]{3,2,1,0:T(8,128)(2,1)S(1)}, bf16[1,2,256,512]{3,2,1,0:T(8,128)(2,1)S(1)}, u32[]{:S(2)}, u32[]{:S(2)}) collective-permute-start(bf16[1,2,256,512]{3,2,1,0:T(8,128)(2,1)S(1)} %get-tuple-element.33), channel_id=1, source_target_pairs={{0,2},{1,13},{2,0},{3,15},{4,6},{5,1},{6,4},{7,3},{8,10},{9,5},{10... | collective-permute-start | bytes 1572872 | tf_op jit(solution)/shard_map/ppermute | solution.py:30
  12.8 12.9 %collective-permute-start.4 = (bf16[1,2,256,512]{3,2,1,0:T(8,128)(2,1)S(1)}, bf16[1,2,256,512]{3,2,1,0:T(8,128)(2,1)S(1)}, u32[]{:S(2)}, u32[]{:S(2)}) collective-permute-start(bf16[1,2,256,512]{3,2,1,0:T(8,128)(2,1)S(1)} %collective-permute-done.refs_1_), channel_id=1, source_target_pairs={{1,3},{0,12},{3,1},{2,14},{5,7},{4,0},{7,5},{6,2},{9,11},{8,4},{11... | collective-permute-start | bytes 1572872 | tf_op jit(solution)/shard_map/ppermute | solution.py:30
  16.9 8.8 %collective-permute-start.1 = (bf16[1,2,256,512]{3,2,1,0:T(8,128)(2,1)S(1)}, bf16[1,2,256,512]{3,2,1,0:T(8,128)(2,1)S(1)}, u32[]{:S(2)}, u32[]{:S(2)}) collective-permute-start(bf16[1,2,256,512]{3,2,1,0:T(8,128)(2,1)S(1)} %collective-permute-done.refs_1_), channel_id=1, source_target_pairs={{0,1},{1,0},{2,3},{3,2},{4,5},{5,4},{6,7},{7,6},{8,9},{9,8},{10,11... | collective-permute-start | bytes 1572872 | tf_op jit(solution)/shard_map/ppermute | solution.py:18
  22.7 3.0 %collective-permute-start.3 = (bf16[1,2,256,512]{3,2,1,0:T(8,128)(2,1)S(1)}, bf16[1,2,256,512]{3,2,1,0:T(8,128)(2,1)S(1)}, u32[]{:S(2)}, u32[]{:S(2)}) collective-permute-start(bf16[1,2,256,512]{3,2,1,0:T(8,128)(2,1)S(1)} %collective-permute-done.2.refs_3_), channel_id=1, source_target_pairs={{0,1},{1,0},{2,3},{3,2},{4,5},{5,4},{6,7},{7,6},{8,9},{9,8},{10,11... | collective-permute-start | bytes 1572872 | tf_op jit(solution)/shard_map/ppermute | solution.py:18
  25.7 1.9 %collective-permute-start.5 = (bf16[1,2,256,512]{3,2,1,0:T(8,128)(2,1)S(1)}, bf16[1,2,256,512]{3,2,1,0:T(8,128)(2,1)S(1)}, u32[]{:S(2)}, u32[]{:S(2)}) collective-permute-start(bf16[1,2,256,512]{3,2,1,0:T(8,128)(2,1)S(1)} %collective-permute-done.4.refs_5_), channel_id=1, source_target_pairs={{0,1},{1,0},{2,3},{3,2},{4,5},{5,4},{6,7},{7,6},{8,9},{9,8},{10,11... | collective-permute-start | bytes 1572872 | tf_op jit(solution)/shard_map/ppermute | solution.py:18
  38.0 2.0 %collective-permute-start.7 = (bf16[2,2,256,256]{3,2,1,0:T(8,128)(2,1)S(1)}, bf16[2,2,256,256]{3,2,1,0:T(8,128)(2,1)S(1)}, u32[]{:S(2)}, u32[]{:S(2)}) collective-permute-start(bf16[2,2,256,256]{3,2,1,0:T(8,128)(2,1)S(1)} %get-tuple-element.42), channel_id=1, source_target_pairs={{0,1},{1,0},{2,3},{3,2},{4,5},{5,4},{6,7},{7,6},{8,9},{9,8},{10,11... | collective-permute-start | bytes 1572872 | tf_op jit(solution)/shard_map/ppermute | solution.py:18
  38.2 3.5 %collective-permute-start.10 = (bf16[2,2,256,256]{3,2,1,0:T(8,128)(2,1)S(1)}, bf16[2,2,256,256]{3,2,1,0:T(8,128)(2,1)S(1)}, u32[]{:S(2)}, u32[]{:S(2)}) collective-permute-start(bf16[2,2,256,256]{3,2,1,0:T(8,128)(2,1)S(1)} %get-tuple-element.46), channel_id=1, source_target_pairs={{0,1},{1,0},{2,3},{3,2},{4,5},{5,4},{6,7},{7,6},{8,9},{9,8},{10,11... | collective-permute-start | bytes 1572872 | tf_op jit(solution)/shard_map/ppermute | solution.py:18
  38.6 17.6 %collective-permute-start.6 = (bf16[2,2,256,256]{3,2,1,0:T(8,128)(2,1)S(1)}, bf16[2,2,256,256]{3,2,1,0:T(8,128)(2,1)S(1)}, u32[]{:S(2)}, u32[]{:S(2)}) collective-permute-start(bf16[2,2,256,256]{3,2,1,0:T(8,128)(2,1)S(1)} %get-tuple-element.40), channel_id=1, source_target_pairs={{0,1},{1,0},{2,3},{3,2},{4,5},{5,4},{6,7},{7,6},{8,9},{9,8},{10,11... | collective-permute-start | bytes 1572872 | tf_op jit(solution)/shard_map/ppermute | solution.py:18
  38.7 4.2 %collective-permute-start.9 = (bf16[2,2,256,256]{3,2,1,0:T(8,128)(2,1)S(1)}, bf16[2,2,256,256]{3,2,1,0:T(8,128)(2,1)S(1)}, u32[]{:S(2)}, u32[]{:S(2)}) collective-permute-start(bf16[2,2,256,256]{3,2,1,0:T(8,128)(2,1)S(1)} %get-tuple-element.44), channel_id=1, source_target_pairs={{0,1},{1,0},{2,3},{3,2},{4,5},{5,4},{6,7},{7,6},{8,9},{9,8},{10,11... | collective-permute-start | bytes 1572872 | tf_op jit(solution)/shard_map/ppermute | solution.py:18
  40.2 16.2 %collective-permute-start.8 = (bf16[1,2,256,256]{3,2,1,0:T(8,128)(2,1)S(1)}, bf16[1,2,256,256]{3,2,1,0:T(8,128)(2,1)S(1)}, u32[]{:S(2)}, u32[]{:S(2)}) collective-permute-start(bf16[1,2,256,256]{3,2,1,0:T(8,128)(2,1)S(1)} %slice.71), channel_id=1, source_target_pairs={{0,2},{2,0},{1,3},{3,1},{4,6},{6,4},{5,7},{7,5},{8,10},{10,8},{9,1... | collective-permute-start | bytes 786440 | tf_op jit(solution)/shard_map/ppermute | solution.py:18
  41.9 12.3 %collective-permute-start.11 = (bf16[1,2,256,256]{3,2,1,0:T(8,128)(2,1)S(1)}, bf16[1,2,256,256]{3,2,1,0:T(8,128)(2,1)S(1)}, u32[]{:S(2)}, u32[]{:S(2)}) collective-permute-start(bf16[1,2,256,256]{3,2,1,0:T(8,128)(2,1)S(1)} %get-tuple-element.53), channel_id=1, source_target_pairs={{0,2},{2,0},{1,3},{3,1},{4,6},{6,4},{5,7},{7,5},{8,10},{10,8},{9,1... | collective-permute-start | bytes 786440 | tf_op jit(solution)/shard_map/ppermute | solution.py:18
  42.5 12.3 %collective-permute-start.13 = (bf16[1,2,256,256]{3,2,1,0:T(8,128)(2,1)S(1)}, bf16[1,2,256,256]{3,2,1,0:T(8,128)(2,1)S(1)}, u32[]{:S(2)}, u32[]{:S(2)}) collective-permute-start(bf16[1,2,256,256]{3,2,1,0:T(8,128)(2,1)S(1)} %get-tuple-element.54), channel_id=1, source_target_pairs={{0,4},{4,8},{8,12},{12,0},{1,5},{5,9},{9,13},{13,1},{2,6},{6,10},{... | collective-permute-start | bytes 786440 | tf_op jit(solution)/shard_map/ppermute | solution.py:18
  43.1 14.9 %collective-permute-start.15 = (bf16[1,2,256,256]{3,2,1,0:T(8,128)(2,1)S(1)}, bf16[1,2,256,256]{3,2,1,0:T(8,128)(2,1)S(1)}, u32[]{:S(2)}, u32[]{:S(2)}) collective-permute-start(bf16[1,2,256,256]{3,2,1,0:T(8,128)(2,1)S(1)} %slice.70), channel_id=1, source_target_pairs={{0,4},{4,8},{8,12},{12,0},{1,5},{5,9},{9,13},{13,1},{2,6},{6,10},{... | collective-permute-start | bytes 786440 | tf_op jit(solution)/shard_map/ppermute | solution.py:18
  54.2 9.4 %collective-permute-start.12 = (bf16[1,2,256,256]{3,2,1,0:T(8,128)(2,1)S(1)}, bf16[1,2,256,256]{3,2,1,0:T(8,128)(2,1)S(1)}, u32[]{:S(2)}, u32[]{:S(2)}) collective-permute-start(bf16[1,2,256,256]{3,2,1,0:T(8,128)(2,1)S(1)} %fusion.2), channel_id=1, source_target_pairs={{0,4},{4,8},{8,12},{12,0},{1,5},{5,9},{9,13},{13,1},{2,6},{6,10},{... | collective-permute-start | bytes 786440 | tf_op jit(solution)/shard_map/ppermute | solution.py:18
  54.9 8.7 %collective-permute-start.14 = (bf16[1,2,256,256]{3,2,1,0:T(8,128)(2,1)S(1)}, bf16[1,2,256,256]{3,2,1,0:T(8,128)(2,1)S(1)}, u32[]{:S(2)}, u32[]{:S(2)}) collective-permute-start(bf16[1,2,256,256]{3,2,1,0:T(8,128)(2,1)S(1)} %fusion), channel_id=1, source_target_pairs={{0,2},{2,0},{1,3},{3,1},{4,6},{6,4},{5,7},{7,5},{8,10},{10,8},{9,1... | collective-permute-start | bytes 786440 | tf_op jit(solution)/shard_map/ppermute | solution.py:18

commit v9 on v8

--- a/solution.py
+++ b/solution.py
@@ -411,6 +411,9 @@
         for row_block in (1, 0):
             at = row_block * groups + s
             sums[row_block, s] = wide(outs[at]) + wide(passed(outs[2 * groups + at], "pos", 1))
+    for s in steps:
+        ready = lax.optimization_barrier((sums[0, s], sums[1, 0], sums[0, 0]))
+        sums[0, s], sums[1, 0], sums[0, 0] = ready
     rim_lo = sums[1, 0][:half]
     rim_hi = sums[1, 0][half:].astype(bf16)
     tile_lo = sums[0, 0][:half]

time: 65.8 us -> 65 us (0.988)
  starting transfers between devices: 16.8 us -> 15.5 us
    ppermute x13, starting transfers between devices: 8.32 us -> 7.06 us  [passed(): lax.ppermute(array, axis, [(i, (i + by) % peers) for i in range(peers)])]
  transfers between devices with their start and end apart: 16 -> 16, of which waited for: 8 -> 10; matrix products, arithmetic and copies ran while one was open for 1% -> 1% of each run, Pallas kernels for 7% -> 7%
where the time goes in v9:
time: 65 us; the launch traced here: 64.8 us
  waiting for transfers between devices  29 us (45%)
  starting transfers between devices  15.5 us (24%)
  Pallas kernels  14.9 us (23%)
  local copies, waits for them, and re-layouts  3.71 us (6%)
  other arithmetic  0.92 us (1%)
  between operations  0.82 us (1%)
    ppermute x13, waiting for transfers between devices, passed(): lax.ppermute(array, axis, [(i, (i + by) % peers) for i in range(peers)])  20 us
    pallas_call x1, Pallas kernels, body(): pl.pallas_call(functools.partial(main_kernel, groups, depth, mine, pix, t...  10.4 us
    ppermute x3, waiting for transfers between devices, split_roles(): return lax.ppermute(array, ('tile', 'slc', 'pos'), pairs)  9 us
    ppermute x3, starting transfers between devices, split_roles(): return lax.ppermute(array, ('tile', 'slc', 'pos'), pairs)  8.44 us
    ppermute x13, starting transfers between devices, passed(): lax.ppermute(array, axis, [(i, (i + by) % peers) for i in range(peers)])  7.06 us
    pallas_call x1, Pallas kernels, body(): pl.pallas_call(functools.partial(prep_kernel, mine, pix), out_shape=(tabl...  4.49 us
    transpose x1, local copies, waits for them, and re-layouts, body(): return jnp.concatenate([tile_lo, tile_hi]).transpose(0, 2, 1, 3)  1.78 us
    unnamed x9, local copies, waits for them, and re-layouts  1.52 us
  transfers between devices with their start and end apart: 16, of which 10 were waited for; matrix products, arithmetic and copies ran while one was open for 1% of the time, Pallas kernels for 7%

profile of v9, /device:TPU:0, one launch (start us, length us, event | category | flops | bytes accessed | tf_op | source)
XLA Modules:
  0.0 64.8 jit_solution(369917806434355456)
XLA Ops:
  1.0 1.5 %copy.11 = bf16[2,256,2,512]{3,1,2,0:T(8,128)(2,1)S(1)} copy(bf16[2,256,2,512]{3,2,1,0:T(2,128)(2,1)} %param.6) | data formatting | bytes 2097152 | tf_op args[0]
  2.7 3.0 %collective-permute-start = (bf16[1,2,256,512]{3,2,1,0:T(8,128)(2,1)S(1)}, bf16[1,2,256,512]{3,2,1,0:T(8,128)(2,1)S(1)}, u32[]{:S(2)}, u32[]{:S(2)}) collective-permute-start(bf16[1,2,256,512]{3,2,1,0:T(8,128)(2,1)S(1)} %get-tuple-element.58), channel_id=1, source_target_pairs={{0,2},{1,13},{2,0},{3,15},{4,6},{5,1},{6,4},{7,3},{8,10},{9,5},{10... | collective-permute-start | bytes 1572872 | tf_op jit(solution)/shard_map/ppermute | solution.py:30
  5.7 4.5 %tables.1 = (bf16[2,4,2,256,256]{4,3,2,1,0:T(8,128)(2,1)S(1)}, bf16[2,4,2,256,256]{4,3,2,1,0:T(8,128)(2,1)S(1)}, bf16[2,2,256,256]{3,2,1,0:T(8,128)(2,1)S(1)}, f...) custom-call(s32[10]{0:T(128)S(1)} %pad_add_fusion.1.info, bf16[2,6,256,256]{3,2,1,0:T(8,128)(2,1)S(1)} %copy-done.3, ...), custom_call_target="tpu_custom_call" | custom-call | flops 8000000000 | bytes 8388608 | tf_op jit(solution)/shard_map/tables/pallas_call | solution.py:353
  10.2 1.3 %collective-permute-start.2 = (bf16[1,2,256,512]{3,2,1,0:T(8,128)(2,1)S(1)}, bf16[1,2,256,512]{3,2,1,0:T(8,128)(2,1)S(1)}, u32[]{:S(2)}, u32[]{:S(2)}) collective-permute-start(bf16[1,2,256,512]{3,2,1,0:T(8,128)(2,1)S(1)} %get-tuple-element.36), channel_id=1, source_target_pairs={{0,2},{1,13},{2,0},{3,15},{4,6},{5,1},{6,4},{7,3},{8,10},{9,5},{10... | collective-permute-start | bytes 1572872 | tf_op jit(solution)/shard_map/ppermute | solution.py:30
  11.5 1.3 %collective-permute-done.refs_1_ = bf16[1,2,256,512]{3,2,1,0:T(8,128)(2,1)S(1)} collective-permute-done((bf16[1,2,256,512]{3,2,1,0:T(8,128)(2,1)S(1)}, bf16[1,2,256,512]{3,2,1,0:T(8,128)(2,1)S(1)}, u32[]{:S(2)}, u32[]{:S(2)}) %collective-permute-start) | collective-permute-done | bytes 524320 | tf_op jit(solution)/shard_map/ppermute | solution.py:30
  12.8 4.1 %collective-permute-start.4 = (bf16[1,2,256,512]{3,2,1,0:T(8,128)(2,1)S(1)}, bf16[1,2,256,512]{3,2,1,0:T(8,128)(2,1)S(1)}, u32[]{:S(2)}, u32[]{:S(2)}) collective-permute-start(bf16[1,2,256,512]{3,2,1,0:T(8,128)(2,1)S(1)} %collective-permute-done.refs_1_), channel_id=1, source_target_pairs={{1,3},{0,12},{3,1},{2,14},{5,7},{4,0},{7,5},{6,2},{9,11},{8,4},{11... | collective-permute-start | bytes 1572872 | tf_op jit(solution)/shard_map/ppermute | solution.py:30
  16.9 5.7 %collective-permute-done.2.refs_3_ = bf16[1,2,256,512]{3,2,1,0:T(8,128)(2,1)S(1)} collective-permute-done((bf16[1,2,256,512]{3,2,1,0:T(8,128)(2,1)S(1)}, bf16[1,2,256,512]{3,2,1,0:T(8,128)(2,1)S(1)}, u32[]{:S(2)}, u32[]{:S(2)}) %collective-permute-start.2) | collective-permute-done | bytes 524320 | tf_op jit(solution)/shard_map/ppermute | solution.py:30
  22.7 1.1 %collective-permute-start.3 = (bf16[1,2,256,512]{3,2,1,0:T(8,128)(2,1)S(1)}, bf16[1,2,256,512]{3,2,1,0:T(8,128)(2,1)S(1)}, u32[]{:S(2)}, u32[]{:S(2)}) collective-permute-start(bf16[1,2,256,512]{3,2,1,0:T(8,128)(2,1)S(1)} %collective-permute-done.2.refs_3_), channel_id=1, source_target_pairs={{0,1},{1,0},{2,3},{3,2},{4,5},{5,4},{6,7},{7,6},{8,9},{9,8},{10,11... | collective-permute-start | bytes 1572872 | tf_op jit(solution)/shard_map/ppermute | solution.py:18
  23.8 1.9 %collective-permute-done.4.refs_5_ = bf16[1,2,256,512]{3,2,1,0:T(8,128)(2,1)S(1)} collective-permute-done((bf16[1,2,256,512]{3,2,1,0:T(8,128)(2,1)S(1)}, bf16[1,2,256,512]{3,2,1,0:T(8,128)(2,1)S(1)}, u32[]{:S(2)}, u32[]{:S(2)}) %collective-permute-start.4) | collective-permute-done | bytes 524320 | tf_op jit(solution)/shard_map/ppermute | solution.py:30
  25.7 1.9 %collective-permute-done.5.refs_6_ = bf16[1,2,256,512]{3,2,1,0:T(8,128)(2,1)S(1)} collective-permute-done((bf16[1,2,256,512]{3,2,1,0:T(8,128)(2,1)S(1)}, bf16[1,2,256,512]{3,2,1,0:T(8,128)(2,1)S(1)}, u32[]{:S(2)}, u32[]{:S(2)}) %collective-permute-start.5) | collective-permute-done | bytes 524320 | tf_op jit(solution)/shard_map/ppermute | solution.py:18
  27.6 10.4 %waves.1 = (bf16[2,2,256,256]{3,2,1,0:T(8,128)(2,1)S(1)}, bf16[2,2,256,256]{3,2,1,0:T(8,128)(2,1)S(1)}, bf16[2,2,256,256]{3,2,1,0:T(8,128)(2,1)S(1)}, bf16[2,2,2...) custom-call(s32[10]{0:T(128)S(1)} %pad_add_fusion.1.info, ...), custom_call_target="tpu_custom_call" | custom-call | flops 15000000512 | bytes 16777216 | tf_op jit(solution)/shard_map/waves/pallas_call | solution.py:385
  38.2 0.4 collective-permute-start.6
  38.7 0.4 collective-permute-start.8
  39.1 0.9 %collective-permute-done.10 = bf16[2,2,256,256]{3,2,1,0:T(8,128)(2,1)S(1)} collective-permute-done((bf16[2,2,256,256]{3,2,1,0:T(8,128)(2,1)S(1)}, bf16[2,2,256,256]{3,2,1,0:T(8,128)(2,1)S(1)}, u32[]{:S(2)}, u32[]{:S(2)}) %collective-permute-start.10) | collective-permute-done | bytes 524320 | tf_op jit(solution)/shard_map/ppermute | solution.py:18
  40.2 1.5 %collective-permute-start.11 = (bf16[1,2,256,256]{3,2,1,0:T(8,128)(2,1)S(1)}, bf16[1,2,256,256]{3,2,1,0:T(8,128)(2,1)S(1)}, u32[]{:S(2)}, u32[]{:S(2)}) collective-permute-start(bf16[1,2,256,256]{3,2,1,0:T(8,128)(2,1)S(1)} %get-tuple-element.59), channel_id=1, source_target_pairs={{0,2},{2,0},{1,3},{3,1},{4,6},{6,4},{5,7},{7,5},{8,10},{10,8},{9,1... | collective-permute-start | bytes 786440 | tf_op jit(solution)/shard_map/ppermute | solution.py:18
  42.4 1.5 %collective-permute-start.15 = (bf16[1,2,256,256]{3,2,1,0:T(8,128)(2,1)S(1)}, bf16[1,2,256,256]{3,2,1,0:T(8,128)(2,1)S(1)}, u32[]{:S(2)}, u32[]{:S(2)}) collective-permute-start(bf16[1,2,256,256]{3,2,1,0:T(8,128)(2,1)S(1)} %slice.58), channel_id=1, source_target_pairs={{0,4},{4,8},{8,12},{12,0},{1,5},{5,9},{9,13},{13,1},{2,6},{6,10},{... | collective-permute-start | bytes 786440 | tf_op jit(solution)/shard_map/ppermute | solution.py:18
  43.9 0.9 %collective-permute-start.9 = (bf16[1,2,256,256]{3,2,1,0:T(8,128)(2,1)S(1)}, bf16[1,2,256,256]{3,2,1,0:T(8,128)(2,1)S(1)}, u32[]{:S(2)}, u32[]{:S(2)}) collective-permute-start(bf16[1,2,256,256]{3,2,1,0:T(8,128)(2,1)S(1)} %slice.59), channel_id=1, source_target_pairs={{0,2},{2,0},{1,3},{3,1},{4,6},{6,4},{5,7},{7,5},{8,10},{10,8},{9,1... | collective-permute-start | bytes 786440 | tf_op jit(solution)/shard_map/ppermute | solution.py:18
  44.8 4.6 %collective-permute-done.11 = bf16[1,2,256,256]{3,2,1,0:T(8,128)(2,1)S(1)} collective-permute-done((bf16[1,2,256,256]{3,2,1,0:T(8,128)(2,1)S(1)}, bf16[1,2,256,256]{3,2,1,0:T(8,128)(2,1)S(1)}, u32[]{:S(2)}, u32[]{:S(2)}) %collective-permute-start.11) | collective-permute-done | bytes 262176 | tf_op jit(solution)/shard_map/ppermute | solution.py:18
  49.5 0.2 collective-permute-start.12
  49.7 3.0 %collective-permute-done.13 = bf16[1,2,256,256]{3,2,1,0:T(8,128)(2,1)S(1)} collective-permute-done((bf16[1,2,256,256]{3,2,1,0:T(8,128)(2,1)S(1)}, bf16[1,2,256,256]{3,2,1,0:T(8,128)(2,1)S(1)}, u32[]{:S(2)}, u32[]{:S(2)}) %collective-permute-start.13) | collective-permute-done | bytes 262176 | tf_op jit(solution)/shard_map/ppermute | solution.py:18
  52.8 0.6 collective-permute-start.14
  53.4 4.9 %collective-permute-done.15 = bf16[1,2,256,256]{3,2,1,0:T(8,128)(2,1)S(1)} collective-permute-done((bf16[1,2,256,256]{3,2,1,0:T(8,128)(2,1)S(1)}, bf16[1,2,256,256]{3,2,1,0:T(8,128)(2,1)S(1)}, u32[]{:S(2)}, u32[]{:S(2)}) %collective-permute-start.15) | collective-permute-done | bytes 262176 | tf_op jit(solution)/shard_map/ppermute | solution.py:18
  58.3 4.5 %collective-permute-done.12 = bf16[1,2,256,256]{3,2,1,0:T(8,128)(2,1)S(1)} collective-permute-done((bf16[1,2,256,256]{3,2,1,0:T(8,128)(2,1)S(1)}, bf16[1,2,256,256]{3,2,1,0:T(8,128)(2,1)S(1)}, u32[]{:S(2)}, u32[]{:S(2)}) %collective-permute-start.12) | collective-permute-done | bytes 262176 | tf_op jit(solution)/shard_map/ppermute | solution.py:18
  63.1 1.8 %copy.9 = f32[2,256,2,256]{3,2,1,0:T(2,128)} copy(f32[2,256,2,256]{3,1,2,0:T(8,128)S(1)} %maximum_bitcast_fusion) | data formatting | bytes 2097152 | tf_op jit(solution)/shard_map/transpose | solution.py:429
  (41 shorter events, 2.0 us)
Async XLA Ops:
  0.0 0.7 %copy-start = (s32[2,4]{1,0:T(2,128)S(1)}, s32[2,4]{1,0:T(2,128)}, u32[]{:S(2)}) copy-start(s32[2,4]{1,0:T(2,128)} %param.7) | copy-start | bytes 100
  1.0 4.7 %copy-start.1 = (f32[4,256,256]{2,1,0:T(8,128)S(1)}, f32[4,256,256]{2,1,0:T(8,128)}, u32[]{:S(2)}) copy-start(f32[4,256,256]{2,1,0:T(8,128)} %measured.1) | copy-start | bytes 3145732
  1.0 4.7 %copy-start.2 = (bf16[256,512]{1,0:T(8,128)(2,1)S(1)}, bf16[256,512]{1,0:T(8,128)(2,1)}, u32[]{:S(2)}) copy-start(bf16[256,512]{1,0:T(8,128)(2,1)} %probe.1) | copy-start | bytes 786436
  2.6 3.1 %copy-start.3 = (bf16[2,6,256,256]{3,2,1,0:T(8,128)(2,1)S(1)}, bf16[2,6,256,256]{3,2,1,0:T(8,128)(2,1)}, u32[]{:S(2)}) copy-start(bf16[2,6,256,256]{3,2,1,0:T(8,128)(2,1)} %constant.49.clone.base) | copy-start | bytes 4718596
  2.7 10.2 %collective-permute-start = (bf16[1,2,256,512]{3,2,1,0:T(8,128)(2,1)S(1)}, bf16[1,2,256,512]{3,2,1,0:T(8,128)(2,1)S(1)}, u32[]{:S(2)}, u32[]{:S(2)}) collective-permute-start(bf16[1,2,256,512]{3,2,1,0:T(8,128)(2,1)S(1)} %get-tuple-element.58), channel_id=1, source_target_pairs={{0,2},{1,13},{2,0},{3,15},{4,6},{5,1},{6,4},{7,3},{8,10},{9,5},{10... | collective-permute-start | bytes 1572872 | tf_op jit(solution)/shard_map/ppermute | solution.py:30
  10.2 12.5 %collective-permute-start.2 = (bf16[1,2,256,512]{3,2,1,0:T(8,128)(2,1)S(1)}, bf16[1,2,256,512]{3,2,1,0:T(8,128)(2,1)S(1)}, u32[]{:S(2)}, u32[]{:S(2)}) collective-permute-start(bf16[1,2,256,512]{3,2,1,0:T(8,128)(2,1)S(1)} %get-tuple-element.36), channel_id=1, source_target_pairs={{0,2},{1,13},{2,0},{3,15},{4,6},{5,1},{6,4},{7,3},{8,10},{9,5},{10... | collective-permute-start | bytes 1572872 | tf_op jit(solution)/shard_map/ppermute | solution.py:30
  12.8 12.9 %collective-permute-start.4 = (bf16[1,2,256,512]{3,2,1,0:T(8,128)(2,1)S(1)}, bf16[1,2,256,512]{3,2,1,0:T(8,128)(2,1)S(1)}, u32[]{:S(2)}, u32[]{:S(2)}) collective-permute-start(bf16[1,2,256,512]{3,2,1,0:T(8,128)(2,1)S(1)} %collective-permute-done.refs_1_), channel_id=1, source_target_pairs={{1,3},{0,12},{3,1},{2,14},{5,7},{4,0},{7,5},{6,2},{9,11},{8,4},{11... | collective-permute-start | bytes 1572872 | tf_op jit(solution)/shard_map/ppermute | solution.py:30
  16.9 8.8 %collective-permute-start.1 = (bf16[1,2,256,512]{3,2,1,0:T(8,128)(2,1)S(1)}, bf16[1,2,256,512]{3,2,1,0:T(8,128)(2,1)S(1)}, u32[]{:S(2)}, u32[]{:S(2)}) collective-permute-start(bf16[1,2,256,512]{3,2,1,0:T(8,128)(2,1)S(1)} %collective-permute-done.refs_1_), channel_id=1, source_target_pairs={{0,1},{1,0},{2,3},{3,2},{4,5},{5,4},{6,7},{7,6},{8,9},{9,8},{10,11... | collective-permute-start | bytes 1572872 | tf_op jit(solution)/shard_map/ppermute | solution.py:18
  22.7 3.0 %collective-permute-start.3 = (bf16[1,2,256,512]{3,2,1,0:T(8,128)(2,1)S(1)}, bf16[1,2,256,512]{3,2,1,0:T(8,128)(2,1)S(1)}, u32[]{:S(2)}, u32[]{:S(2)}) collective-permute-start(bf16[1,2,256,512]{3,2,1,0:T(8,128)(2,1)S(1)} %collective-permute-done.2.refs_3_), channel_id=1, source_target_pairs={{0,1},{1,0},{2,3},{3,2},{4,5},{5,4},{6,7},{7,6},{8,9},{9,8},{10,11... | collective-permute-start | bytes 1572872 | tf_op jit(solution)/shard_map/ppermute | solution.py:18
  25.7 1.9 %collective-permute-start.5 = (bf16[1,2,256,512]{3,2,1,0:T(8,128)(2,1)S(1)}, bf16[1,2,256,512]{3,2,1,0:T(8,128)(2,1)S(1)}, u32[]{:S(2)}, u32[]{:S(2)}) collective-permute-start(bf16[1,2,256,512]{3,2,1,0:T(8,128)(2,1)S(1)} %collective-permute-done.4.refs_5_), channel_id=1, source_target_pairs={{0,1},{1,0},{2,3},{3,2},{4,5},{5,4},{6,7},{7,6},{8,9},{9,8},{10,11... | collective-permute-start | bytes 1572872 | tf_op jit(solution)/shard_map/ppermute | solution.py:18
  38.0 2.0 %collective-permute-start.10 = (bf16[2,2,256,256]{3,2,1,0:T(8,128)(2,1)S(1)}, bf16[2,2,256,256]{3,2,1,0:T(8,128)(2,1)S(1)}, u32[]{:S(2)}, u32[]{:S(2)}) collective-permute-start(bf16[2,2,256,256]{3,2,1,0:T(8,128)(2,1)S(1)} %get-tuple-element.52), channel_id=1, source_target_pairs={{0,1},{1,0},{2,3},{3,2},{4,5},{5,4},{6,7},{7,6},{8,9},{9,8},{10,11... | collective-permute-start | bytes 1572872 | tf_op jit(solution)/shard_map/ppermute | solution.py:18
  38.2 3.6 %collective-permute-start.6 = (bf16[2,2,256,256]{3,2,1,0:T(8,128)(2,1)S(1)}, bf16[2,2,256,256]{3,2,1,0:T(8,128)(2,1)S(1)}, u32[]{:S(2)}, u32[]{:S(2)}) collective-permute-start(bf16[2,2,256,256]{3,2,1,0:T(8,128)(2,1)S(1)} %get-tuple-element.43), channel_id=1, source_target_pairs={{0,1},{1,0},{2,3},{3,2},{4,5},{5,4},{6,7},{7,6},{8,9},{9,8},{10,11... | collective-permute-start | bytes 1572872 | tf_op jit(solution)/shard_map/ppermute | solution.py:18
  38.6 3.4 %collective-permute-start.7 = (bf16[2,2,256,256]{3,2,1,0:T(8,128)(2,1)S(1)}, bf16[2,2,256,256]{3,2,1,0:T(8,128)(2,1)S(1)}, u32[]{:S(2)}, u32[]{:S(2)}) collective-permute-start(bf16[2,2,256,256]{3,2,1,0:T(8,128)(2,1)S(1)} %get-tuple-element.45), channel_id=1, source_target_pairs={{0,1},{1,0},{2,3},{3,2},{4,5},{5,4},{6,7},{7,6},{8,9},{9,8},{10,11... | collective-permute-start | bytes 1572872 | tf_op jit(solution)/shard_map/ppermute | solution.py:18
  38.7 3.5 %collective-permute-start.8 = (bf16[2,2,256,256]{3,2,1,0:T(8,128)(2,1)S(1)}, bf16[2,2,256,256]{3,2,1,0:T(8,128)(2,1)S(1)}, u32[]{:S(2)}, u32[]{:S(2)}) collective-permute-start(bf16[2,2,256,256]{3,2,1,0:T(8,128)(2,1)S(1)} %get-tuple-element.47), channel_id=1, source_target_pairs={{0,1},{1,0},{2,3},{3,2},{4,5},{5,4},{6,7},{7,6},{8,9},{9,8},{10,11... | collective-permute-start | bytes 1572872 | tf_op jit(solution)/shard_map/ppermute | solution.py:18
  40.2 9.2 %collective-permute-start.11 = (bf16[1,2,256,256]{3,2,1,0:T(8,128)(2,1)S(1)}, bf16[1,2,256,256]{3,2,1,0:T(8,128)(2,1)S(1)}, u32[]{:S(2)}, u32[]{:S(2)}) collective-permute-start(bf16[1,2,256,256]{3,2,1,0:T(8,128)(2,1)S(1)} %get-tuple-element.59), channel_id=1, source_target_pairs={{0,2},{2,0},{1,3},{3,1},{4,6},{6,4},{5,7},{7,5},{8,10},{10,8},{9,1... | collective-permute-start | bytes 786440 | tf_op jit(solution)/shard_map/ppermute | solution.py:18
  41.7 11.0 %collective-permute-start.13 = (bf16[1,2,256,256]{3,2,1,0:T(8,128)(2,1)S(1)}, bf16[1,2,256,256]{3,2,1,0:T(8,128)(2,1)S(1)}, u32[]{:S(2)}, u32[]{:S(2)}) collective-permute-start(bf16[1,2,256,256]{3,2,1,0:T(8,128)(2,1)S(1)} %get-tuple-element.60), channel_id=1, source_target_pairs={{0,4},{4,8},{8,12},{12,0},{1,5},{5,9},{9,13},{13,1},{2,6},{6,10},{... | collective-permute-start | bytes 786440 | tf_op jit(solution)/shard_map/ppermute | solution.py:18
  42.4 15.9 %collective-permute-start.15 = (bf16[1,2,256,256]{3,2,1,0:T(8,128)(2,1)S(1)}, bf16[1,2,256,256]{3,2,1,0:T(8,128)(2,1)S(1)}, u32[]{:S(2)}, u32[]{:S(2)}) collective-permute-start(bf16[1,2,256,256]{3,2,1,0:T(8,128)(2,1)S(1)} %slice.58), channel_id=1, source_target_pairs={{0,4},{4,8},{8,12},{12,0},{1,5},{5,9},{9,13},{13,1},{2,6},{6,10},{... | collective-permute-start | bytes 786440 | tf_op jit(solution)/shard_map/ppermute | solution.py:18
  43.9 14.4 %collective-permute-start.9 = (bf16[1,2,256,256]{3,2,1,0:T(8,128)(2,1)S(1)}, bf16[1,2,256,256]{3,2,1,0:T(8,128)(2,1)S(1)}, u32[]{:S(2)}, u32[]{:S(2)}) collective-permute-start(bf16[1,2,256,256]{3,2,1,0:T(8,128)(2,1)S(1)} %slice.59), channel_id=1, source_target_pairs={{0,2},{2,0},{1,3},{3,1},{4,6},{6,4},{5,7},{7,5},{8,10},{10,8},{9,1... | collective-permute-start | bytes 786440 | tf_op jit(solution)/shard_map/ppermute | solution.py:18
  49.5 13.4 %collective-permute-start.12 = (bf16[1,2,256,256]{3,2,1,0:T(8,128)(2,1)S(1)}, bf16[1,2,256,256]{3,2,1,0:T(8,128)(2,1)S(1)}, u32[]{:S(2)}, u32[]{:S(2)}) collective-permute-start(bf16[1,2,256,256]{3,2,1,0:T(8,128)(2,1)S(1)} %add_convert_fusion.2), channel_id=1, source_target_pairs={{0,4},{4,8},{8,12},{12,0},{1,5},{5,9},{9,13},{13,1},{2,6},{6,10},{... | collective-permute-start | bytes 786440 | tf_op jit(solution)/shard_map/ppermute | solution.py:18
  52.8 10.1 %collective-permute-start.14 = (bf16[1,2,256,256]{3,2,1,0:T(8,128)(2,1)S(1)}, bf16[1,2,256,256]{3,2,1,0:T(8,128)(2,1)S(1)}, u32[]{:S(2)}, u32[]{:S(2)}) collective-permute-start(bf16[1,2,256,256]{3,2,1,0:T(8,128)(2,1)S(1)} %add_convert_fusion.1), channel_id=1, source_target_pairs={{0,2},{2,0},{1,3},{3,1},{4,6},{6,4},{5,7},{7,5},{8,10},{10,8},{9,1... | collective-permute-start | bytes 786440 | tf_op jit(solution)/shard_map/ppermute | solution.py:18

commit v10 on v9

--- a/solution.py
+++ b/solution.py
@@ -186,6 +186,7 @@
     def spectrum_of(t, pairs):
         halfway = []
         for m, (re, im) in zip(members, pairs):
+            re, im = re.astype(bf16), im.astype(bf16)
             plus = cat([re[:mid] + re[mid:], im[:mid] + im[mid:]], 0).astype(bf16)
             minus = cat([re[:mid] - re[mid:], im[:mid] - im[mid:]], 0).astype(bf16)
             halfway.append((product(lefts[m, t, 0], plus), product(lefts[m, t, 1], minus)))

time: 65 us -> 64.8 us (level)
  no operation moved by 1% of the time
where the time goes in v10:
time: 64.8 us; the launch traced here: 64.6 us
  waiting for transfers between devices  28.9 us (45%)
  starting transfers between devices  15.6 us (24%)
  Pallas kernels  14.7 us (23%)
  local copies, waits for them, and re-layouts  3.71 us (6%)
  other arithmetic  0.92 us (1%)
  between operations  0.82 us (1%)
    ppermute x13, waiting for transfers between devices, passed(): lax.ppermute(array, axis, [(i, (i + by) % peers) for i in range(peers)])  19.9 us
    pallas_call x1, Pallas kernels, body(): pl.pallas_call(functools.partial(main_kernel, groups, depth, mine, pix, t...  10.2 us
    ppermute x3, waiting for transfers between devices, split_roles(): return lax.ppermute(array, ('tile', 'slc', 'pos'), pairs)  9 us
    ppermute x3, starting transfers between devices, split_roles(): return lax.ppermute(array, ('tile', 'slc', 'pos'), pairs)  8.44 us
    ppermute x13, starting transfers between devices, passed(): lax.ppermute(array, axis, [(i, (i + by) % peers) for i in range(peers)])  7.15 us
    pallas_call x1, Pallas kernels, body(): pl.pallas_call(functools.partial(prep_kernel, mine, pix), out_shape=(tabl...  4.49 us
    transpose x1, local copies, waits for them, and re-layouts, body(): return jnp.concatenate([tile_lo, tile_hi]).transpose(0, 2, 1, 3)  1.78 us
    unnamed x9, local copies, waits for them, and re-layouts  1.52 us
  transfers between devices with their start and end apart: 16, of which 10 were waited for; matrix products, arithmetic and copies ran while one was open for 1% of the time, Pallas kernels for 7%

profile of v10, /device:TPU:0, one launch (start us, length us, event | category | flops | bytes accessed | tf_op | source)
XLA Modules:
  0.0 64.6 jit_solution(5290265404299637968)
XLA Ops:
  1.0 1.5 %copy.11 = bf16[2,256,2,512]{3,1,2,0:T(8,128)(2,1)S(1)} copy(bf16[2,256,2,512]{3,2,1,0:T(2,128)(2,1)} %param.6) | data formatting | bytes 2097152 | tf_op args[0]
  2.7 3.0 %collective-permute-start = (bf16[1,2,256,512]{3,2,1,0:T(8,128)(2,1)S(1)}, bf16[1,2,256,512]{3,2,1,0:T(8,128)(2,1)S(1)}, u32[]{:S(2)}, u32[]{:S(2)}) collective-permute-start(bf16[1,2,256,512]{3,2,1,0:T(8,128)(2,1)S(1)} %get-tuple-element.58), channel_id=1, source_target_pairs={{0,2},{1,13},{2,0},{3,15},{4,6},{5,1},{6,4},{7,3},{8,10},{9,5},{10... | collective-permute-start | bytes 1572872 | tf_op jit(solution)/shard_map/ppermute | solution.py:30
  5.7 4.5 %tables.1 = (bf16[2,4,2,256,256]{4,3,2,1,0:T(8,128)(2,1)S(1)}, bf16[2,4,2,256,256]{4,3,2,1,0:T(8,128)(2,1)S(1)}, bf16[2,2,256,256]{3,2,1,0:T(8,128)(2,1)S(1)}, f...) custom-call(s32[10]{0:T(128)S(1)} %pad_add_fusion.1.info, bf16[2,6,256,256]{3,2,1,0:T(8,128)(2,1)S(1)} %copy-done.3, ...), custom_call_target="tpu_custom_call" | custom-call | flops 8000000000 | bytes 8388608 | tf_op jit(solution)/shard_map/tables/pallas_call | solution.py:354
  10.2 1.3 %collective-permute-start.2 = (bf16[1,2,256,512]{3,2,1,0:T(8,128)(2,1)S(1)}, bf16[1,2,256,512]{3,2,1,0:T(8,128)(2,1)S(1)}, u32[]{:S(2)}, u32[]{:S(2)}) collective-permute-start(bf16[1,2,256,512]{3,2,1,0:T(8,128)(2,1)S(1)} %get-tuple-element.36), channel_id=1, source_target_pairs={{0,2},{1,13},{2,0},{3,15},{4,6},{5,1},{6,4},{7,3},{8,10},{9,5},{10... | collective-permute-start | bytes 1572872 | tf_op jit(solution)/shard_map/ppermute | solution.py:30
  11.5 1.3 %collective-permute-done.refs_1_ = bf16[1,2,256,512]{3,2,1,0:T(8,128)(2,1)S(1)} collective-permute-done((bf16[1,2,256,512]{3,2,1,0:T(8,128)(2,1)S(1)}, bf16[1,2,256,512]{3,2,1,0:T(8,128)(2,1)S(1)}, u32[]{:S(2)}, u32[]{:S(2)}) %collective-permute-start) | collective-permute-done | bytes 524320 | tf_op jit(solution)/shard_map/ppermute | solution.py:30
  12.8 4.1 %collective-permute-start.4 = (bf16[1,2,256,512]{3,2,1,0:T(8,128)(2,1)S(1)}, bf16[1,2,256,512]{3,2,1,0:T(8,128)(2,1)S(1)}, u32[]{:S(2)}, u32[]{:S(2)}) collective-permute-start(bf16[1,2,256,512]{3,2,1,0:T(8,128)(2,1)S(1)} %collective-permute-done.refs_1_), channel_id=1, source_target_pairs={{1,3},{0,12},{3,1},{2,14},{5,7},{4,0},{7,5},{6,2},{9,11},{8,4},{11... | collective-permute-start | bytes 1572872 | tf_op jit(solution)/shard_map/ppermute | solution.py:30
  16.9 5.7 %collective-permute-done.2.refs_3_ = bf16[1,2,256,512]{3,2,1,0:T(8,128)(2,1)S(1)} collective-permute-done((bf16[1,2,256,512]{3,2,1,0:T(8,128)(2,1)S(1)}, bf16[1,2,256,512]{3,2,1,0:T(8,128)(2,1)S(1)}, u32[]{:S(2)}, u32[]{:S(2)}) %collective-permute-start.2) | collective-permute-done | bytes 524320 | tf_op jit(solution)/shard_map/ppermute | solution.py:30
  22.7 1.1 %collective-permute-start.3 = (bf16[1,2,256,512]{3,2,1,0:T(8,128)(2,1)S(1)}, bf16[1,2,256,512]{3,2,1,0:T(8,128)(2,1)S(1)}, u32[]{:S(2)}, u32[]{:S(2)}) collective-permute-start(bf16[1,2,256,512]{3,2,1,0:T(8,128)(2,1)S(1)} %collective-permute-done.2.refs_3_), channel_id=1, source_target_pairs={{0,1},{1,0},{2,3},{3,2},{4,5},{5,4},{6,7},{7,6},{8,9},{9,8},{10,11... | collective-permute-start | bytes 1572872 | tf_op jit(solution)/shard_map/ppermute | solution.py:18
  23.8 1.9 %collective-permute-done.4.refs_5_ = bf16[1,2,256,512]{3,2,1,0:T(8,128)(2,1)S(1)} collective-permute-done((bf16[1,2,256,512]{3,2,1,0:T(8,128)(2,1)S(1)}, bf16[1,2,256,512]{3,2,1,0:T(8,128)(2,1)S(1)}, u32[]{:S(2)}, u32[]{:S(2)}) %collective-permute-start.4) | collective-permute-done | bytes 524320 | tf_op jit(solution)/shard_map/ppermute | solution.py:30
  25.7 1.9 %collective-permute-done.5.refs_6_ = bf16[1,2,256,512]{3,2,1,0:T(8,128)(2,1)S(1)} collective-permute-done((bf16[1,2,256,512]{3,2,1,0:T(8,128)(2,1)S(1)}, bf16[1,2,256,512]{3,2,1,0:T(8,128)(2,1)S(1)}, u32[]{:S(2)}, u32[]{:S(2)}) %collective-permute-start.5) | collective-permute-done | bytes 524320 | tf_op jit(solution)/shard_map/ppermute | solution.py:18
  27.6 10.2 %waves.1 = (bf16[2,2,256,256]{3,2,1,0:T(8,128)(2,1)S(1)}, bf16[2,2,256,256]{3,2,1,0:T(8,128)(2,1)S(1)}, bf16[2,2,256,256]{3,2,1,0:T(8,128)(2,1)S(1)}, bf16[2,2,2...) custom-call(s32[10]{0:T(128)S(1)} %pad_add_fusion.1.info, ...), custom_call_target="tpu_custom_call" | custom-call | flops 15000000512 | bytes 16777216 | tf_op jit(solution)/shard_map/waves/pallas_call | solution.py:386
  38.0 0.4 collective-permute-start.6
  38.5 0.4 collective-permute-start.8
  38.9 0.9 %collective-permute-done.10 = bf16[2,2,256,256]{3,2,1,0:T(8,128)(2,1)S(1)} collective-permute-done((bf16[2,2,256,256]{3,2,1,0:T(8,128)(2,1)S(1)}, bf16[2,2,256,256]{3,2,1,0:T(8,128)(2,1)S(1)}, u32[]{:S(2)}, u32[]{:S(2)}) %collective-permute-start.10) | collective-permute-done | bytes 524320 | tf_op jit(solution)/shard_map/ppermute | solution.py:18
  40.0 1.6 %collective-permute-start.11 = (bf16[1,2,256,256]{3,2,1,0:T(8,128)(2,1)S(1)}, bf16[1,2,256,256]{3,2,1,0:T(8,128)(2,1)S(1)}, u32[]{:S(2)}, u32[]{:S(2)}) collective-permute-start(bf16[1,2,256,256]{3,2,1,0:T(8,128)(2,1)S(1)} %get-tuple-element.59), channel_id=1, source_target_pairs={{0,2},{2,0},{1,3},{3,1},{4,6},{6,4},{5,7},{7,5},{8,10},{10,8},{9,1... | collective-permute-start | bytes 786440 | tf_op jit(solution)/shard_map/ppermute | solution.py:18
  42.2 1.5 %collective-permute-start.15 = (bf16[1,2,256,256]{3,2,1,0:T(8,128)(2,1)S(1)}, bf16[1,2,256,256]{3,2,1,0:T(8,128)(2,1)S(1)}, u32[]{:S(2)}, u32[]{:S(2)}) collective-permute-start(bf16[1,2,256,256]{3,2,1,0:T(8,128)(2,1)S(1)} %slice.58), channel_id=1, source_target_pairs={{0,4},{4,8},{8,12},{12,0},{1,5},{5,9},{9,13},{13,1},{2,6},{6,10},{... | collective-permute-start | bytes 786440 | tf_op jit(solution)/shard_map/ppermute | solution.py:18
  43.7 0.9 %collective-permute-start.9 = (bf16[1,2,256,256]{3,2,1,0:T(8,128)(2,1)S(1)}, bf16[1,2,256,256]{3,2,1,0:T(8,128)(2,1)S(1)}, u32[]{:S(2)}, u32[]{:S(2)}) collective-permute-start(bf16[1,2,256,256]{3,2,1,0:T(8,128)(2,1)S(1)} %slice.59), channel_id=1, source_target_pairs={{0,2},{2,0},{1,3},{3,1},{4,6},{6,4},{5,7},{7,5},{8,10},{10,8},{9,1... | collective-permute-start | bytes 786440 | tf_op jit(solution)/shard_map/ppermute | solution.py:18
  44.6 4.6 %collective-permute-done.11 = bf16[1,2,256,256]{3,2,1,0:T(8,128)(2,1)S(1)} collective-permute-done((bf16[1,2,256,256]{3,2,1,0:T(8,128)(2,1)S(1)}, bf16[1,2,256,256]{3,2,1,0:T(8,128)(2,1)S(1)}, u32[]{:S(2)}, u32[]{:S(2)}) %collective-permute-start.11) | collective-permute-done | bytes 262176 | tf_op jit(solution)/shard_map/ppermute | solution.py:18
  49.2 0.3 collective-permute-start.12
  49.5 3.0 %collective-permute-done.13 = bf16[1,2,256,256]{3,2,1,0:T(8,128)(2,1)S(1)} collective-permute-done((bf16[1,2,256,256]{3,2,1,0:T(8,128)(2,1)S(1)}, bf16[1,2,256,256]{3,2,1,0:T(8,128)(2,1)S(1)}, u32[]{:S(2)}, u32[]{:S(2)}) %collective-permute-start.13) | collective-permute-done | bytes 262176 | tf_op jit(solution)/shard_map/ppermute | solution.py:18
  52.6 0.6 collective-permute-start.14
  53.2 4.9 %collective-permute-done.15 = bf16[1,2,256,256]{3,2,1,0:T(8,128)(2,1)S(1)} collective-permute-done((bf16[1,2,256,256]{3,2,1,0:T(8,128)(2,1)S(1)}, bf16[1,2,256,256]{3,2,1,0:T(8,128)(2,1)S(1)}, u32[]{:S(2)}, u32[]{:S(2)}) %collective-permute-start.15) | collective-permute-done | bytes 262176 | tf_op jit(solution)/shard_map/ppermute | solution.py:18
  58.1 4.5 %collective-permute-done.12 = bf16[1,2,256,256]{3,2,1,0:T(8,128)(2,1)S(1)} collective-permute-done((bf16[1,2,256,256]{3,2,1,0:T(8,128)(2,1)S(1)}, bf16[1,2,256,256]{3,2,1,0:T(8,128)(2,1)S(1)}, u32[]{:S(2)}, u32[]{:S(2)}) %collective-permute-start.12) | collective-permute-done | bytes 262176 | tf_op jit(solution)/shard_map/ppermute | solution.py:18
  62.8 1.8 %copy.9 = f32[2,256,2,256]{3,2,1,0:T(2,128)} copy(f32[2,256,2,256]{3,1,2,0:T(8,128)S(1)} %maximum_bitcast_fusion) | data formatting | bytes 2097152 | tf_op jit(solution)/shard_map/transpose | solution.py:430
  (41 shorter events, 2.0 us)
Async XLA Ops:
  0.0 0.7 %copy-start = (s32[2,4]{1,0:T(2,128)S(1)}, s32[2,4]{1,0:T(2,128)}, u32[]{:S(2)}) copy-start(s32[2,4]{1,0:T(2,128)} %param.7) | copy-start | bytes 100
  1.0 4.7 %copy-start.1 = (f32[4,256,256]{2,1,0:T(8,128)S(1)}, f32[4,256,256]{2,1,0:T(8,128)}, u32[]{:S(2)}) copy-start(f32[4,256,256]{2,1,0:T(8,128)} %measured.1) | copy-start | bytes 3145732
  1.0 4.7 %copy-start.2 = (bf16[256,512]{1,0:T(8,128)(2,1)S(1)}, bf16[256,512]{1,0:T(8,128)(2,1)}, u32[]{:S(2)}) copy-start(bf16[256,512]{1,0:T(8,128)(2,1)} %probe.1) | copy-start | bytes 786436
  2.6 3.1 %copy-start.3 = (bf16[2,6,256,256]{3,2,1,0:T(8,128)(2,1)S(1)}, bf16[2,6,256,256]{3,2,1,0:T(8,128)(2,1)}, u32[]{:S(2)}) copy-start(bf16[2,6,256,256]{3,2,1,0:T(8,128)(2,1)} %constant.49.clone.base) | copy-start | bytes 4718596
  2.7 10.2 %collective-permute-start = (bf16[1,2,256,512]{3,2,1,0:T(8,128)(2,1)S(1)}, bf16[1,2,256,512]{3,2,1,0:T(8,128)(2,1)S(1)}, u32[]{:S(2)}, u32[]{:S(2)}) collective-permute-start(bf16[1,2,256,512]{3,2,1,0:T(8,128)(2,1)S(1)} %get-tuple-element.58), channel_id=1, source_target_pairs={{0,2},{1,13},{2,0},{3,15},{4,6},{5,1},{6,4},{7,3},{8,10},{9,5},{10... | collective-permute-start | bytes 1572872 | tf_op jit(solution)/shard_map/ppermute | solution.py:30
  10.2 12.5 %collective-permute-start.2 = (bf16[1,2,256,512]{3,2,1,0:T(8,128)(2,1)S(1)}, bf16[1,2,256,512]{3,2,1,0:T(8,128)(2,1)S(1)}, u32[]{:S(2)}, u32[]{:S(2)}) collective-permute-start(bf16[1,2,256,512]{3,2,1,0:T(8,128)(2,1)S(1)} %get-tuple-element.36), channel_id=1, source_target_pairs={{0,2},{1,13},{2,0},{3,15},{4,6},{5,1},{6,4},{7,3},{8,10},{9,5},{10... | collective-permute-start | bytes 1572872 | tf_op jit(solution)/shard_map/ppermute | solution.py:30
  12.8 12.9 %collective-permute-start.4 = (bf16[1,2,256,512]{3,2,1,0:T(8,128)(2,1)S(1)}, bf16[1,2,256,512]{3,2,1,0:T(8,128)(2,1)S(1)}, u32[]{:S(2)}, u32[]{:S(2)}) collective-permute-start(bf16[1,2,256,512]{3,2,1,0:T(8,128)(2,1)S(1)} %collective-permute-done.refs_1_), channel_id=1, source_target_pairs={{1,3},{0,12},{3,1},{2,14},{5,7},{4,0},{7,5},{6,2},{9,11},{8,4},{11... | collective-permute-start | bytes 1572872 | tf_op jit(solution)/shard_map/ppermute | solution.py:30
  16.9 8.8 %collective-permute-start.1 = (bf16[1,2,256,512]{3,2,1,0:T(8,128)(2,1)S(1)}, bf16[1,2,256,512]{3,2,1,0:T(8,128)(2,1)S(1)}, u32[]{:S(2)}, u32[]{:S(2)}) collective-permute-start(bf16[1,2,256,512]{3,2,1,0:T(8,128)(2,1)S(1)} %collective-permute-done.refs_1_), channel_id=1, source_target_pairs={{0,1},{1,0},{2,3},{3,2},{4,5},{5,4},{6,7},{7,6},{8,9},{9,8},{10,11... | collective-permute-start | bytes 1572872 | tf_op jit(solution)/shard_map/ppermute | solution.py:18
  22.7 3.0 %collective-permute-start.3 = (bf16[1,2,256,512]{3,2,1,0:T(8,128)(2,1)S(1)}, bf16[1,2,256,512]{3,2,1,0:T(8,128)(2,1)S(1)}, u32[]{:S(2)}, u32[]{:S(2)}) collective-permute-start(bf16[1,2,256,512]{3,2,1,0:T(8,128)(2,1)S(1)} %collective-permute-done.2.refs_3_), channel_id=1, source_target_pairs={{0,1},{1,0},{2,3},{3,2},{4,5},{5,4},{6,7},{7,6},{8,9},{9,8},{10,11... | collective-permute-start | bytes 1572872 | tf_op jit(solution)/shard_map/ppermute | solution.py:18
  25.7 1.9 %collective-permute-start.5 = (bf16[1,2,256,512]{3,2,1,0:T(8,128)(2,1)S(1)}, bf16[1,2,256,512]{3,2,1,0:T(8,128)(2,1)S(1)}, u32[]{:S(2)}, u32[]{:S(2)}) collective-permute-start(bf16[1,2,256,512]{3,2,1,0:T(8,128)(2,1)S(1)} %collective-permute-done.4.refs_5_), channel_id=1, source_target_pairs={{0,1},{1,0},{2,3},{3,2},{4,5},{5,4},{6,7},{7,6},{8,9},{9,8},{10,11... | collective-permute-start | bytes 1572872 | tf_op jit(solution)/shard_map/ppermute | solution.py:18
  37.8 2.0 %collective-permute-start.10 = (bf16[2,2,256,256]{3,2,1,0:T(8,128)(2,1)S(1)}, bf16[2,2,256,256]{3,2,1,0:T(8,128)(2,1)S(1)}, u32[]{:S(2)}, u32[]{:S(2)}) collective-permute-start(bf16[2,2,256,256]{3,2,1,0:T(8,128)(2,1)S(1)} %get-tuple-element.52), channel_id=1, source_target_pairs={{0,1},{1,0},{2,3},{3,2},{4,5},{5,4},{6,7},{7,6},{8,9},{9,8},{10,11... | collective-permute-start | bytes 1572872 | tf_op jit(solution)/shard_map/ppermute | solution.py:18
  38.0 3.6 %collective-permute-start.6 = (bf16[2,2,256,256]{3,2,1,0:T(8,128)(2,1)S(1)}, bf16[2,2,256,256]{3,2,1,0:T(8,128)(2,1)S(1)}, u32[]{:S(2)}, u32[]{:S(2)}) collective-permute-start(bf16[2,2,256,256]{3,2,1,0:T(8,128)(2,1)S(1)} %get-tuple-element.43), channel_id=1, source_target_pairs={{0,1},{1,0},{2,3},{3,2},{4,5},{5,4},{6,7},{7,6},{8,9},{9,8},{10,11... | collective-permute-start | bytes 1572872 | tf_op jit(solution)/shard_map/ppermute | solution.py:18
  38.4 3.4 %collective-permute-start.7 = (bf16[2,2,256,256]{3,2,1,0:T(8,128)(2,1)S(1)}, bf16[2,2,256,256]{3,2,1,0:T(8,128)(2,1)S(1)}, u32[]{:S(2)}, u32[]{:S(2)}) collective-permute-start(bf16[2,2,256,256]{3,2,1,0:T(8,128)(2,1)S(1)} %get-tuple-element.45), channel_id=1, source_target_pairs={{0,1},{1,0},{2,3},{3,2},{4,5},{5,4},{6,7},{7,6},{8,9},{9,8},{10,11... | collective-permute-start | bytes 1572872 | tf_op jit(solution)/shard_map/ppermute | solution.py:18
  38.5 3.5 %collective-permute-start.8 = (bf16[2,2,256,256]{3,2,1,0:T(8,128)(2,1)S(1)}, bf16[2,2,256,256]{3,2,1,0:T(8,128)(2,1)S(1)}, u32[]{:S(2)}, u32[]{:S(2)}) collective-permute-start(bf16[2,2,256,256]{3,2,1,0:T(8,128)(2,1)S(1)} %get-tuple-element.47), channel_id=1, source_target_pairs={{0,1},{1,0},{2,3},{3,2},{4,5},{5,4},{6,7},{7,6},{8,9},{9,8},{10,11... | collective-permute-start | bytes 1572872 | tf_op jit(solution)/shard_map/ppermute | solution.py:18
  40.0 9.2 %collective-permute-start.11 = (bf16[1,2,256,256]{3,2,1,0:T(8,128)(2,1)S(1)}, bf16[1,2,256,256]{3,2,1,0:T(8,128)(2,1)S(1)}, u32[]{:S(2)}, u32[]{:S(2)}) collective-permute-start(bf16[1,2,256,256]{3,2,1,0:T(8,128)(2,1)S(1)} %get-tuple-element.59), channel_id=1, source_target_pairs={{0,2},{2,0},{1,3},{3,1},{4,6},{6,4},{5,7},{7,5},{8,10},{10,8},{9,1... | collective-permute-start | bytes 786440 | tf_op jit(solution)/shard_map/ppermute | solution.py:18
  41.5 11.0 %collective-permute-start.13 = (bf16[1,2,256,256]{3,2,1,0:T(8,128)(2,1)S(1)}, bf16[1,2,256,256]{3,2,1,0:T(8,128)(2,1)S(1)}, u32[]{:S(2)}, u32[]{:S(2)}) collective-permute-start(bf16[1,2,256,256]{3,2,1,0:T(8,128)(2,1)S(1)} %get-tuple-element.60), channel_id=1, source_target_pairs={{0,4},{4,8},{8,12},{12,0},{1,5},{5,9},{9,13},{13,1},{2,6},{6,10},{... | collective-permute-start | bytes 786440 | tf_op jit(solution)/shard_map/ppermute | solution.py:18
  42.2 15.9 %collective-permute-start.15 = (bf16[1,2,256,256]{3,2,1,0:T(8,128)(2,1)S(1)}, bf16[1,2,256,256]{3,2,1,0:T(8,128)(2,1)S(1)}, u32[]{:S(2)}, u32[]{:S(2)}) collective-permute-start(bf16[1,2,256,256]{3,2,1,0:T(8,128)(2,1)S(1)} %slice.58), channel_id=1, source_target_pairs={{0,4},{4,8},{8,12},{12,0},{1,5},{5,9},{9,13},{13,1},{2,6},{6,10},{... | collective-permute-start | bytes 786440 | tf_op jit(solution)/shard_map/ppermute | solution.py:18
  43.7 14.4 %collective-permute-start.9 = (bf16[1,2,256,256]{3,2,1,0:T(8,128)(2,1)S(1)}, bf16[1,2,256,256]{3,2,1,0:T(8,128)(2,1)S(1)}, u32[]{:S(2)}, u32[]{:S(2)}) collective-permute-start(bf16[1,2,256,256]{3,2,1,0:T(8,128)(2,1)S(1)} %slice.59), channel_id=1, source_target_pairs={{0,2},{2,0},{1,3},{3,1},{4,6},{6,4},{5,7},{7,5},{8,10},{10,8},{9,1... | collective-permute-start | bytes 786440 | tf_op jit(solution)/shard_map/ppermute | solution.py:18
  49.2 13.4 %collective-permute-start.12 = (bf16[1,2,256,256]{3,2,1,0:T(8,128)(2,1)S(1)}, bf16[1,2,256,256]{3,2,1,0:T(8,128)(2,1)S(1)}, u32[]{:S(2)}, u32[]{:S(2)}) collective-permute-start(bf16[1,2,256,256]{3,2,1,0:T(8,128)(2,1)S(1)} %add_convert_fusion.2), channel_id=1, source_target_pairs={{0,4},{4,8},{8,12},{12,0},{1,5},{5,9},{9,13},{13,1},{2,6},{6,10},{... | collective-permute-start | bytes 786440 | tf_op jit(solution)/shard_map/ppermute | solution.py:18
  52.6 10.1 %collective-permute-start.14 = (bf16[1,2,256,256]{3,2,1,0:T(8,128)(2,1)S(1)}, bf16[1,2,256,256]{3,2,1,0:T(8,128)(2,1)S(1)}, u32[]{:S(2)}, u32[]{:S(2)}) collective-permute-start(bf16[1,2,256,256]{3,2,1,0:T(8,128)(2,1)S(1)} %add_convert_fusion.1), channel_id=1, source_target_pairs={{0,2},{2,0},{1,3},{3,1},{4,6},{6,4},{5,7},{7,5},{8,10},{10,8},{9,1... | collective-permute-start | bytes 786440 | tf_op jit(solution)/shard_map/ppermute | solution.py:18
